TPU v7x, 256 devices: a whole 4x4x8 slice. The times are simulated.
256 devices in a mesh: dp: 32 (over x, y, core), proto: 8 (over z).
Axes of the slice: x: 4, y: 4, z: 8, core: 2. Of those that a mesh axis runs over, the one named last changes fastest.
Arguments:
- student_crops: bfloat16 [4096, 256], P('dp'), may hold values from -0.6 to 0.6
- teacher_crops: bfloat16 [4096, 256], P('dp'), may hold values from -5 to 5
- student_patches: bfloat16 [32768, 256], P('dp'), may hold values from -0.6 to 0.6
- teacher_patches: bfloat16 [32768, 256], P('dp'), may hold values from -5 to 5
- patch_mask: int32 [128, 96], P('dp'), may hold values from 0 to 255, as said below
- student_protos: bfloat16 [256, 65536], P(None, 'proto'), may hold values from -0.6 to 0.6
- teacher_protos: bfloat16 [256, 65536], P(None, 'proto'), may hold values from -5 to 5
Outputs:
- proto_grad: float32 [256, 65536], P('dp', 'proto')
- crop_grad: float32 [4096, 256], P(('dp', 'proto'))
- patch_grad: float32 [32768, 256], P(('dp', 'proto'))
Inputs may be any that keep to these rules, and one draw needn't show every extreme that they name: `patch_mask`: each row holds 96 different patch positions of one image.
All inputs are finite; a program needn't handle non-finite values.
Results may differ from a plain program's by a relative error of at most 0.0052.
Values sent between devices are 32-bit elements; how exact they have to be, the bound alone decides.
No kernel may reach another device: no remote copies, remote signals or barrier semaphores. Data moves between devices by JAX's collectives and lax.ppermute only.
A program may use at most 128 MiB of HBM per device.

v0:
```python
import jax
import jax.numpy as jnp
from jax import lax
from jax.sharding import PartitionSpec as P

ITERS = 3


EPS = 1e-06
TEACHER_TEMP = 0.07
STUDENT_TEMP = 0.1
LOSS_SCALE = 256.0


def unit_rows(x):
    xf = x.astype(jnp.float32)
    inv = lax.rsqrt(jnp.sum(xf * xf, axis=-1, keepdims=True) + EPS)
    return (xf * inv, inv)


def unit_cols(w):
    wf = w.astype(jnp.float32)
    inv = lax.rsqrt(jnp.sum(wf * wf, axis=0, keepdims=True) + EPS)
    return (wf * inv, inv)


def col_part(rowscale, exponent_matrix):
    return jnp.sum(rowscale[:, None] * exponent_matrix.astype(jnp.float32), axis=0)


def row_part(exponent_matrix, colscale):
    return jnp.sum(exponent_matrix.astype(jnp.float32) * colscale[None, :], axis=1)


def balance_apart(exponent_matrix):
    rowscale = jnp.ones((exponent_matrix.shape[0],), jnp.float32)
    colscale = jnp.ones((exponent_matrix.shape[1],), jnp.float32)
    for step in range(ITERS):
        colscale = 1.0 / lax.psum(col_part(rowscale, exponent_matrix), "dp")
        rowscale = 1.0 / lax.psum(row_part(exponent_matrix, colscale), "proto")
    return (rowscale, colscale)


def norm_back(xf, inv, fgrad):
    return (fgrad - xf * jnp.sum(xf * fgrad, axis=-1, keepdims=True)) * inv


def local(
    student_crops,
    teacher_crops,
    student_patches,
    teacher_patches,
    patch_mask,
    student_protos,
    teacher_protos,
):
    images, masked = patch_mask.shape
    patches = student_patches.shape[0] // images
    width = student_crops.shape[1]
    flat = (jnp.arange(images, dtype=jnp.int32)[:, None] * patches + patch_mask).reshape(-1)
    crop_f, crop_inv = unit_rows(student_crops)
    student_dino = crop_f.astype(jnp.bfloat16)
    teacher_dino = unit_rows(teacher_crops)[0].astype(jnp.bfloat16)
    student_ibot = unit_rows(jnp.take(student_patches, flat, axis=0))[0].astype(jnp.bfloat16)
    teacher_ibot = unit_rows(jnp.take(teacher_patches, flat, axis=0))[0].astype(jnp.bfloat16)
    wnorm, winv = unit_cols(student_protos)
    student_w = wnorm.astype(jnp.bfloat16)
    teacher_w = unit_cols(teacher_protos)[0].astype(jnp.bfloat16)
    exponent_global = jnp.exp(
        jnp.dot(teacher_dino, teacher_w, preferred_element_type=jnp.float32) / TEACHER_TEMP
    ).astype(jnp.bfloat16)
    exponent_patchwise = jnp.exp(
        jnp.dot(teacher_ibot, teacher_w, preferred_element_type=jnp.float32) / TEACHER_TEMP
    ).astype(jnp.bfloat16)
    row_count_global, column_count_global = balance_apart(exponent_global)
    row_count_patchwise, column_count_patchwise = balance_apart(exponent_patchwise)
    score_dino = jnp.dot(student_dino, student_w, preferred_element_type=jnp.float32) / STUDENT_TEMP
    score_ibot = jnp.dot(student_ibot, student_w, preferred_element_type=jnp.float32) / STUDENT_TEMP
    total_dino, total_ibot = lax.psum(
        (jnp.sum(jnp.exp(score_dino), axis=1), jnp.sum(jnp.exp(score_ibot), axis=1)), "proto"
    )
    prob_dino = jnp.exp(score_dino - jnp.log(total_dino)[:, None])
    prob_ibot = jnp.exp(score_ibot - jnp.log(total_ibot)[:, None])
    target_dino = (
        row_count_global[:, None]
        * exponent_global.astype(jnp.float32)
        * column_count_global[None, :]
    )
    target_ibot = (
        row_count_patchwise[:, None]
        * exponent_patchwise.astype(jnp.float32)
        * column_count_patchwise[None, :]
    )
    grad_dino = (LOSS_SCALE * (prob_dino - target_dino) / STUDENT_TEMP).astype(jnp.bfloat16)
    grad_ibot = (LOSS_SCALE * (prob_ibot - target_ibot) / STUDENT_TEMP).astype(jnp.bfloat16)
    dp_size = lax.axis_size("dp")
    own_rows = width // dp_size
    row_start = lax.axis_index("dp") * own_rows
    shard = lax.psum_scatter(
        jnp.einsum("rb,rk->bk", student_dino, grad_dino, preferred_element_type=jnp.float32)
        + jnp.einsum("rb,rk->bk", student_ibot, grad_ibot, preferred_element_type=jnp.float32),
        "dp",
        scatter_dimension=0,
        tiled=True,
    )
    wslice = lax.dynamic_slice_in_dim(wnorm, row_start, own_rows, 0)
    coldot = lax.psum(jnp.sum(wslice * shard, axis=0, keepdims=True), "dp")
    proto_grad = (shard - wslice * coldot) * winv
    fgrad_dino = jnp.einsum("rk,bk->rb", grad_dino, student_w, preferred_element_type=jnp.float32)
    fgrad_ibot = jnp.einsum("rk,bk->rb", grad_ibot, student_w, preferred_element_type=jnp.float32)
    dense = jnp.zeros(student_patches.shape, jnp.float32).at[flat].add(fgrad_ibot)
    proto_size = lax.axis_size("proto")
    crop_share = student_crops.shape[0] // proto_size
    patch_share = student_patches.shape[0] // proto_size
    stacked = jnp.concatenate(
        [
            fgrad_dino.reshape(proto_size, crop_share, width),
            dense.reshape(proto_size, patch_share, width),
        ],
        axis=1,
    )
    stacked = stacked.reshape(proto_size * (crop_share + patch_share), width)
    mine_rows = crop_share + patch_share
    summed = lax.psum(stacked, "proto")
    mine = lax.dynamic_slice_in_dim(summed, lax.axis_index("proto") * mine_rows, mine_rows, 0)
    proto_index = lax.axis_index("proto")
    crop_x = lax.dynamic_slice_in_dim(crop_f, proto_index * crop_share, crop_share, 0)
    crop_scale = lax.dynamic_slice_in_dim(crop_inv, proto_index * crop_share, crop_share, 0)
    crop_grad = norm_back(crop_x, crop_scale, mine[:crop_share])
    patch_rows = lax.dynamic_slice_in_dim(
        student_patches, proto_index * patch_share, patch_share, 0
    )
    patch_x, patch_scale = unit_rows(patch_rows)
    patch_grad = norm_back(patch_x, patch_scale, mine[crop_share:])
    return (proto_grad, crop_grad, patch_grad)


def solution(mesh):
    in_specs = (
        P("dp", None),
        P("dp", None),
        P("dp", None),
        P("dp", None),
        P("dp", None),
        P(None, "proto"),
        P(None, "proto"),
    )
    out_specs = (P("dp", "proto"), P(("dp", "proto"), None), P(("dp", "proto"), None))
    return jax.shard_map(local, mesh=mesh, in_specs=in_specs, out_specs=out_specs, check_vma=False)
```

profile of v0, /device:TPU:32, one launch (start us, length us, event | category | flops | bytes accessed | tf_op | source)
XLA Modules:
  0.0 754.3 jit_solution(15434015217802872534)
XLA Ops:
  8.2 2.8 gather_fusion
  11.0 2.1 gather_fusion.1
  13.0 3.2 fusion.12
  16.7 5.5 convert_reduce_fusion
  22.2 2.2 convert_reduce_fusion.1
  24.6 3.2 fusion.11
  28.0 6.0 exponential_reduce_fusion
  34.0 99.1 %all-reduce.17.cloned.1.call-done = (f32[8192]{0:T(1024)}, f32[8192]{0:T(1024)}) async-done(((f32[8192]{0:T(1024)}, f32[8192]{0:T(1024)}), (f32[8192]{0:T(1024)}, f32[8192]{0:T(1024)})) %all-reduce.17.cloned.1.call-update) | async-done | bytes 65552 | tf_op jit(solution)/shard_map/psum | solution.py:39
  134.6 4.2 fusion
  139.3 16.2 %all-reduce.5 = (f32[128]{0:T(128)S(1)}, f32[384]{0:T(512)S(1)}) all-reduce(f32[128]{0:T(128)S(1)} %fusion.14, f32[384]{0:T(512)S(1)} %fusion), channel_id=1, replica_groups=mesh['dp'=32,'proto'=8] {'proto'}, use_global_device_ids=true, to_apply=%region_9.10 | all-reduce | flops 512 | bytes 4096 | tf_op jit(solution)/shard_map/psum | solution.py:40
  155.6 5.2 fusion.1
  162.0 5.7 exponential_reduce_fusion.1
  167.8 98.1 %all-reduce.15.cloned.1.call-done = (f32[8192]{0:T(1024)}, f32[8192]{0:T(1024)}) async-done(((f32[8192]{0:T(1024)}, f32[8192]{0:T(1024)}), (f32[8192]{0:T(1024)}, f32[8192]{0:T(1024)})) %all-reduce.15.cloned.1.call-update) | async-done | bytes 65552 | tf_op jit(solution)/shard_map/psum | solution.py:39
  266.7 4.2 fusion.2
  271.4 16.1 %all-reduce.4 = (f32[128]{0:T(128)S(1)}, f32[384]{0:T(512)S(1)}) all-reduce(f32[128]{0:T(128)S(1)} %fusion.16, f32[384]{0:T(512)S(1)} %fusion.2), channel_id=1, replica_groups=mesh['dp'=32,'proto'=8] {'proto'}, use_global_device_ids=true, to_apply=%region_13.14 | all-reduce | flops 512 | bytes 4096 | tf_op jit(solution)/shard_map/psum | solution.py:40
  287.5 5.2 fusion.3
  293.9 103.8 %all-reduce.13.cloned.1.call-done = (f32[8192]{0:T(1024)}, f32[8192]{0:T(1024)}) async-done(((f32[8192]{0:T(1024)}, f32[8192]{0:T(1024)}), (f32[8192]{0:T(1024)}, f32[8192]{0:T(1024)})) %all-reduce.13.cloned.1.call-update) | async-done | bytes 65552 | tf_op jit(solution)/shard_map/psum | solution.py:39
  398.5 4.2 fusion.4
  403.2 16.5 %all-reduce.3 = (f32[128]{0:T(128)S(1)}, f32[128]{0:T(128)S(1)}, f32[384]{0:T(512)S(1)}, f32[384]{0:T(512)S(1)}) all-reduce(f32[128]{0:T(128)S(1)} %fusion.18, f32[128]{0:T(128)S(1)} %get-tuple-element.24, f32[384]{0:T(512)S(1)} %fusion.4, f32[384]{0:T(512)S(1)} %get-tuple-element.26), channel_id=1, replica_groups=mesh['dp'=32,'proto'=8] {'proto'}, use_global_device_ids=true, to_apply=%region_17.18 | all-reduce | flops 1024 | bytes 8192 | tf_op jit(solution)/shard_map/psum | solution.py:40
  419.8 8.5 %fusion.8 = bf16[384,8192]{1,0:T(8,128)(2,1)S(1)} fusion(bf16[384,8192]{1,0:T(8,128)(2,1)} %get-tuple-element.23, f32[384,8192]{1,0:T(8,128)} %get-tuple-element.27, f32[384]{0:T(512)S(1)} %broadcast_divide_fusion.6, f32[8192]{0:T(1024)S(1)} %broadcast_divide_fusion, f32[384]{0:T(512)S(1)} %log.7), kind=kLoop, calls=%fused_computation.18 | loop fusion | flops 22020096 | bytes 25201664 | tf_op jit(solution)/shard_map/convert_element_type | solution.py:95
  428.4 1.8 fusion.26
  435.5 1.5 fusion.28
  437.0 3.6 scatter_custom_fusion
  440.6 2.3 pad_maximum_fusion
  444.6 8.8 %convolution_add_fusion = f32[256,8192]{1,0:T(8,128)} fusion(f32[256,8192]{1,0:T(8,128)S(1)} %fusion.51, bf16[384,8192]{1,0:T(8,128)(2,1)} %copy-done.4, f32[384]{0:T(512)S(1)} %get-tuple-element.29, bf16[384,256]{1,0:T(8,128)(2,1)S(1)} %gather_fusion, pred[384]{0:T(512)(128)(4,1)S(1)} %compare_and_fusion), kind=kOutput, calls=%fused_computation.22 | convolution fusion | flops 1613103104 | bytes 23267200 | tf_op jit(solution)/shard_map/rb,rk->bk/dot_general | solution.py:101
  454.6 6.5 convert_multiply_fusion.8
  461.1 56.0 %all-reduce.11.cloned.1.call-done = f32[1152,256]{1,0:T(8,128)} async-done(((f32[1152,256]{1,0:T(8,128)}), f32[1152,256]{1,0:T(8,128)}) %all-reduce.11.cloned.1.call-update) | async-done | bytes 1179664 | tf_op jit(solution)/shard_map/psum | solution.py:124
  519.0 1.4 subtract_multiply_fusion.1
  520.4 1.7 fusion.44
  522.1 98.4 %reduce-scatter.2.cloned.1.call-done = f32[8,8192]{1,0:T(8,128)} async-done(((f32[256,8192]{1,0:T(8,128)}), f32[8,8192]{1,0:T(8,128)}) %reduce-scatter.2.cloned.1.call-update) | async-done | bytes 262160 | tf_op jit(solution)/shard_map/reduce_scatter | solution.py:99
  621.7 124.3 %psum.126 = f32[8192]{0:T(1024)S(1)} all-reduce(f32[8192]{0:T(1024)S(1)} %multiply_reduce_fusion), channel_id=1, replica_groups=mesh['dp'=32,'proto'=8] {'dp'}, use_global_device_ids=true, to_apply=%region_36.38 | all-reduce | flops 8192 | bytes 65536 | tf_op jit(solution)/shard_map/psum | solution.py:107
  746.0 1.8 subtract_multiply_fusion
  (80 shorter events, 19.9 us)
Async XLA Ops:
  7.2 3.8 copy-start
  7.2 9.1 %copy-start.10 = (bf16[128,256]{1,0:T(8,128)(2,1)S(1)}, bf16[128,256]{1,0:T(8,128)(2,1)}, u32[]{:S(2)}) copy-start(bf16[128,256]{1,0:T(8,128)(2,1)} %param.10) | copy-start | bytes 196612
  7.2 125.9 %all-reduce.17.cloned.1.call-start = ((), (), s32[]{:S(2)}) async-start(), calls=%async_computation.5 | async-start | bytes 131072 | tf_op jit(solution)/shard_map/psum | solution.py:39
  13.0 3.7 copy-start.8
  24.5 3.3 copy-start.9
  24.5 241.4 %all-reduce.15.cloned.1.call-start = ((), (), s32[]{:S(2)}) async-start(), calls=%async_computation.4 | async-start | bytes 131072 | tf_op jit(solution)/shard_map/psum | solution.py:39
  24.5 3.5 copy-start.2
  161.9 235.8 %all-reduce.13.cloned.1.call-start = ((), (), s32[]{:S(2)}) async-start(), calls=%async_computation.3 | async-start | bytes 131072 | tf_op jit(solution)/shard_map/psum | solution.py:39
  265.9 5.0 copy-start.11
  293.8 223.3 %all-reduce.11.cloned.1.call-start = ((), (), s32[]{:S(2)}) async-start(), calls=%async_computation.2 | async-start | bytes 2359296 | tf_op jit(solution)/shard_map/psum | solution.py:124
  397.7 5.0 copy-start.12
  419.8 8.6 %copy-start.3 = (bf16[256,8192]{1,0:T(8,128)(2,1)S(1)}, bf16[256,8192]{1,0:T(8,128)(2,1)}, u32[]{:S(2)}) copy-start(bf16[256,8192]{1,0:T(8,128)(2,1)} %param.14) | copy-start | bytes 12582916
  428.3 3.2 copy-start.4
  428.3 4.5 copy-start.5
  434.1 1.4 copy-start.6
  437.0 6.3 copy-start.7
  442.9 177.6 %reduce-scatter.2.cloned.1.call-start = ((), (), s32[]{:S(2)}) async-start(), calls=%async_computation.1 | async-start | bytes 8650752 | tf_op jit(solution)/shard_map/reduce_scatter | solution.py:99
  454.6 293.2 %copy-start.1 = (bf16[1024,256]{1,0:T(8,128)(2,1)S(1)}, bf16[1024,256]{1,0:T(8,128)(2,1)}, u32[]{:S(2)}) copy-start(bf16[1024,256]{1,0:T(8,128)(2,1)} %param.12) | copy-start | bytes 1572868
Sparse Core Ops, SparseCore 0:
  24.6 108.4 all-reduce.16
  162.1 103.7 all-reduce.14
  293.9 103.7 all-reduce.12
  443.1 74.0 all-reduce.10
  521.5 99.0 reduce-scatter.1
where the time goes:
time: 755 us; the launch traced here: 754 us
  waiting for transfers between devices  456 us (60%)
  blocking collectives  173 us (23%)
  other arithmetic  68.8 us (9%)
  matrix products  33 us (4%)
  between operations  14.1 us (2%)
  local copies, waits for them, and re-layouts  9.19 us (1%)
    psum x3, waiting for transfers between devices, balance_apart(): colscale = 1.0 / lax.psum(col_part(rowscale, exponent_matrix), 'dp')  301 us
    psum x1, blocking collectives, local(): coldot = lax.psum(jnp.sum(wslice * shard, axis=0, keepdims=True), 'dp')  124 us
    reduce_scatter x1, waiting for transfers between devices, local(): lax.psum_scatter(jnp.einsum('rb,rk->bk', student_dino, grad_dino, preferr...  98.4 us
    psum x1, waiting for transfers between devices, local(): summed = lax.psum(stacked, 'proto')  56 us
    psum x3, blocking collectives, balance_apart(): rowscale = 1.0 / lax.psum(row_part(exponent_matrix, colscale), 'proto')  48.8 us
  transfers between devices with their start and end apart: 5, of which 5 were waited for; matrix products, arithmetic and copies ran while one was open for 5% of the time, Pallas kernels for 0%

commit v1 on v0

v1 whole, which is shorter than its diff:
```python
import functools

import jax
import jax.numpy as jnp
from jax import lax
from jax.experimental import pallas as pl
from jax.experimental.pallas import tpu as pltpu
from jax.sharding import Mesh, PartitionSpec as P

ITERS = 3
EPS = 1e-06
TEACHER_TEMP = 0.07
STUDENT_TEMP = 0.1
LOSS_SCALE = 256.0
GRAD_SCALE = LOSS_SCALE / STUDENT_TEMP
LOG2E = 1.4426950408889634

BN = 512
RB = 128
F32 = jnp.float32
BF16 = jnp.bfloat16
VMEM_LIMIT = 48 * 1024 * 1024


def params():
    return pltpu.CompilerParams(
        dimension_semantics=("arbitrary",), vmem_limit_bytes=VMEM_LIMIT
    )


def unit(x):
    xf = x.astype(F32)
    return xf * lax.rsqrt(jnp.sum(xf * xf, axis=-1, keepdims=True) + EPS)


def unit_cols(w):
    wf = w.astype(F32)
    inv = lax.rsqrt(jnp.sum(wf * wf, axis=0, keepdims=True) + EPS)
    return wf * inv, inv


def prep_kernel(images, patches, masked, crops, patch_rows, mask, out):
    count = crops.shape[0]
    out[:count, :] = unit(crops[...])
    for i in range(images):
        place = lax.broadcasted_iota(jnp.int32, (masked, patches), 1)
        chosen = (place == mask[i * masked : (i + 1) * masked, :]).astype(F32).astype(BF16)
        rows = jnp.dot(
            chosen, patch_rows[i * patches : (i + 1) * patches, :], preferred_element_type=F32
        )
        out[count + i * masked : count + (i + 1) * masked, :] = unit(rows)


def prep(crops, patch_rows, mask_col, images, masked):
    patches = patch_rows.shape[0] // images
    count = crops.shape[0] + images * masked
    return pl.pallas_call(
        functools.partial(prep_kernel, images, patches, masked),
        out_shape=jax.ShapeDtypeStruct((count, crops.shape[1]), F32),
        compiler_params=pltpu.CompilerParams(vmem_limit_bytes=VMEM_LIMIT),
    )(crops, patch_rows, mask_col)


def place_rows(core, own, other, dest):
    half = own.shape[0]
    first = pl.multiple_of(core * half, half)
    second = pl.multiple_of((1 - core) * half, half)
    dest[pl.ds(first, half), :] = own[...].astype(dest.dtype)
    dest[pl.ds(second, half), :] = other[...].astype(dest.dtype)


def row_groups(half, crops):
    groups = []
    for base in (0, half):
        groups.append((base, base + crops, 0))
        groups.append((base + crops, base + half, 1))
    return groups


def put_columns(step, heads, out):
    copies = out.shape[0]
    per_head = out.shape[1] // 2
    for head in range(2):
        for t in range(BN // 128):
            piece = heads[head][:, 128 * t : 128 * (t + 1)]
            out[:, pl.ds(head * per_head + step * (BN // 128) + t, 1), :] = jnp.broadcast_to(
                piece[None], (copies, 1, 128)
            )


def teacher_kernel(groups, idx, own, other, protos, expo, sums, feats):
    step = pl.program_id(0)

    @pl.when(step == 0)
    def _():
        place_rows(idx[0], own, other, feats)

    w = unit_cols(protos[...])[0].astype(BF16)
    heads = [jnp.zeros((1, BN), F32), jnp.zeros((1, BN), F32)]
    for start, stop, head in groups:
        score = jnp.dot(feats[start:stop, :], w, preferred_element_type=F32)
        e = jnp.exp2(score * (LOG2E / TEACHER_TEMP)).astype(BF16)
        expo[start:stop, :] = e
        heads[head] = heads[head] + jnp.sum(e.astype(F32), axis=0, keepdims=True)
    put_columns(step, heads, sums)


def teacher_pass(idx, own, other, protos, groups, columns, copies):
    half, width = own.shape
    steps = columns // BN
    return pl.pallas_call(
        functools.partial(teacher_kernel, groups),
        grid_spec=pltpu.PrefetchScalarGridSpec(
            num_scalar_prefetch=1,
            grid=(steps,),
            in_specs=[
                pl.BlockSpec((half, width), lambda j, idx: (0, 0)),
                pl.BlockSpec((half, width), lambda j, idx: (0, 0)),
                pl.BlockSpec((width, BN), lambda j, idx: (0, idx[0] * steps + j)),
            ],
            out_specs=[
                pl.BlockSpec((2 * half, BN), lambda j, idx: (0, j)),
                pl.BlockSpec((copies, 2 * columns // 128, 128), lambda j, idx: (0, 0, 0)),
            ],
            scratch_shapes=[pltpu.VMEM((2 * half, width), BF16)],
        ),
        out_shape=[
            jax.ShapeDtypeStruct((2 * half, columns), BF16),
            jax.ShapeDtypeStruct((copies, 2 * columns // 128, 128), F32),
        ],
        compiler_params=params(),
    )(idx, own, other, protos)


def denominator_kernel(steps, idx, own, other, protos, total, feats, acc):
    step = pl.program_id(0)

    @pl.when(step == 0)
    def _():
        place_rows(idx[0], own, other, feats)
        acc[...] = jnp.zeros_like(acc)

    w = unit_cols(protos[...])[0].astype(BF16)
    rows = feats.shape[0]
    for start in range(0, rows, 256):
        score = jnp.dot(feats[start : start + 256, :], w, preferred_element_type=F32)
        p = jnp.exp2(score * (LOG2E / STUDENT_TEMP))
        part = p[:, :128]
        for t in range(1, BN // 128):
            part = part + p[:, 128 * t : 128 * (t + 1)]
        acc[start : start + 256, :] += part

    @pl.when(step == steps - 1)
    def _():
        for t in range(rows // 128):
            turned = jnp.transpose(acc[128 * t : 128 * (t + 1), :])
            total[t : t + 1, :] = jnp.sum(turned, axis=0, keepdims=True)


def denominator_pass(idx, own, other, protos, columns):
    half, width = own.shape
    steps = columns // BN
    rows = 2 * half
    return pl.pallas_call(
        functools.partial(denominator_kernel, steps),
        grid_spec=pltpu.PrefetchScalarGridSpec(
            num_scalar_prefetch=1,
            grid=(steps,),
            in_specs=[
                pl.BlockSpec((half, width), lambda j, idx: (0, 0)),
                pl.BlockSpec((half, width), lambda j, idx: (0, 0)),
                pl.BlockSpec((width, BN), lambda j, idx: (0, idx[0] * steps + j)),
            ],
            out_specs=pl.BlockSpec((rows // 128, 128), lambda j, idx: (0, 0)),
            scratch_shapes=[pltpu.VMEM((rows, width), BF16), pltpu.VMEM((rows, 128), F32)],
        ),
        out_shape=jax.ShapeDtypeStruct((rows // 128, 128), F32),
        compiler_params=params(),
    )(idx, own, other, protos)


def row_kernel(per_half, crop_blocks, columns, extra, expo, colparts, *refs):
    if extra:
        total, out, colscale = refs
    else:
        out, colscale = refs
    step = pl.program_id(0)
    copies = out.shape[0]
    rows8 = expo.shape[0]
    per_head = columns // 128

    @pl.when(step == 0)
    def _():
        colscale[...] = 1.0 / jnp.sum(colparts[...], axis=0)
        if extra:
            count = total.shape[0]
            out[:, count:, :] = jnp.broadcast_to(total[...][None], (copies, count, 128))

    head = jnp.where(lax.rem(step, per_half) < crop_blocks, 0, 1)

    def chunk(k, acc):
        e = expo[:, pl.ds(pl.multiple_of(k * 128, 128), 128)].astype(F32)
        return acc + e * colscale[pl.ds(head * per_head + k, 1), :]

    acc = lax.fori_loop(0, per_head, chunk, jnp.zeros((rows8, 128), F32), unroll=8)
    sums = jnp.sum(jnp.transpose(acc), axis=0, keepdims=True)
    out[:, pl.ds(step, 1), :] = jnp.broadcast_to(sums[None], (copies, 1, 128))


def row_pass(expo, colparts, total, half, crops, copies):
    rows, columns = expo.shape
    sublanes = rows // 128
    extra = total is not None
    in_specs = [
        pl.BlockSpec((RB, columns), lambda i: (i, 0)),
        pl.BlockSpec(colparts.shape, lambda i: (0, 0, 0)),
    ]
    args = [expo, colparts]
    if extra:
        in_specs.append(pl.BlockSpec(total.shape, lambda i: (0, 0)))
        args.append(total)
    out_shape = (copies, sublanes * (2 if extra else 1), 128)
    return pl.pallas_call(
        functools.partial(row_kernel, half // RB, crops // RB, columns, extra),
        grid=(rows // RB,),
        in_specs=in_specs,
        out_specs=pl.BlockSpec(out_shape, lambda i: (0, 0, 0)),
        out_shape=jax.ShapeDtypeStruct(out_shape, F32),
        scratch_shapes=[pltpu.VMEM((2 * columns // 128, 128), F32)],
        compiler_params=params(),
    )(*args)


def spread_rows(values, dest):
    for t in range(values.shape[0]):
        line = jnp.broadcast_to(values[t : t + 1, :], (128, 128))
        dest[128 * t : 128 * (t + 1), :] = jnp.transpose(line)


def column_kernel(groups, expo, rowparts, out, rowscale):
    step = pl.program_id(0)
    rows = expo.shape[0]

    @pl.when(step == 0)
    def _():
        spread_rows(1.0 / jnp.sum(rowparts[:, : rows // 128, :], axis=0), rowscale)

    def group(start, stop):
        def body(i, acc):
            at = pl.multiple_of(start + i * 16, 16)
            e = expo[pl.ds(at, 16), :].astype(F32)
            r = rowscale[pl.ds(at, 16), :]
            m = e * jnp.concatenate([r] * (BN // 128), axis=1)
            return acc + (m[:8, :] + m[8:, :])

        acc = lax.fori_loop(0, (stop - start) // 16, body, jnp.zeros((8, BN), F32), unroll=8)
        return jnp.sum(acc, axis=0, keepdims=True)

    heads = [jnp.zeros((1, BN), F32), jnp.zeros((1, BN), F32)]
    for start, stop, head in groups:
        heads[head] = heads[head] + group(start, stop)
    put_columns(step, heads, out)


def column_pass(expo, rowparts, groups, copies):
    rows, columns = expo.shape
    out_shape = (copies, 2 * columns // 128, 128)
    return pl.pallas_call(
        functools.partial(column_kernel, groups),
        grid=(columns // BN,),
        in_specs=[
            pl.BlockSpec((rows, BN), lambda j: (0, j)),
            pl.BlockSpec(rowparts.shape, lambda j: (0, 0, 0)),
        ],
        out_specs=pl.BlockSpec(out_shape, lambda j: (0, 0, 0)),
        out_shape=jax.ShapeDtypeStruct(out_shape, F32),
        scratch_shapes=[pltpu.VMEM((rows, 128), F32)],
        compiler_params=params(),
    )(expo, rowparts)


def grad_kernel(groups, steps, nx, ny, idx, own, other, protos, expo, colparts, rowparts, totals, *refs):
    first = refs[:nx]
    second = refs[nx : nx + ny]
    fown, fother, winv_out, feats, feats_t, colscale, rowscale, shift, gbuf, wsum, facc = refs[nx + ny :]
    step = pl.program_id(0)
    rows, width = feats.shape
    half = rows // 2
    sub = rows // 128
    per_head = colscale.shape[0] // 2

    @pl.when(step == 0)
    def _():
        place_rows(idx[0], own, other, feats)
        feats_t[...] = jnp.transpose(feats[...].astype(F32)).astype(BF16)
        colscale[...] = 1.0 / jnp.sum(colparts[...], axis=0)
        spread_rows(GRAD_SCALE / jnp.sum(rowparts[:, :sub, :], axis=0), rowscale)
        denominators = jnp.sum(totals[:, sub : 2 * sub, :], axis=0)
        spread_rows(jnp.log2(GRAD_SCALE / denominators), shift)
        facc[...] = jnp.zeros_like(facc)

    wnorm, winv = unit_cols(protos[...])
    w = wnorm.astype(BF16)
    winv_out[...] = winv
    wide = BN // 128
    scales = []
    for head in range(2):
        base = head * per_head + step * wide
        scales.append(
            jnp.concatenate([colscale[pl.ds(base + t, 1), :] for t in range(wide)], axis=1)
        )
    for start, stop, head in groups:
        score = jnp.dot(feats[start:stop, :], w, preferred_element_type=F32)
        shifts = jnp.concatenate([shift[start:stop, :]] * wide, axis=1)
        prob = jnp.exp2(score * (LOG2E / STUDENT_TEMP) + shifts)
        rs = jnp.concatenate([rowscale[start:stop, :]] * wide, axis=1)
        target = rs * expo[start:stop, :].astype(F32) * scales[head]
        gbuf[start:stop, :] = (prob - target).astype(BF16)
    wsum[...] = jnp.dot(feats_t[...], gbuf[...], preferred_element_type=F32)
    facc[...] += lax.dot_general(
        gbuf[...], w, (((1,), (1,)), ((), ())), preferred_element_type=F32
    )
    coldot = jnp.broadcast_to(jnp.sum(wnorm * wsum[...], axis=0, keepdims=True), (8, BN))

    @pl.when(step < steps // 2)
    def _():
        part = width // nx
        for s in range(nx):
            at = pl.multiple_of(lax.rem(idx[1] + s, nx) * part, part)
            first[s][:part, :] = wsum[pl.ds(at, part), :]
            first[s][part:, :] = coldot

    @pl.when(step >= steps // 2)
    def _():
        part = width // (nx * ny)
        for s in range(ny):
            dest = lax.rem(idx[2] + s, ny)
            for q in range(nx):
                at = pl.multiple_of((q * ny + dest) * part, part)
                second[s][q * part : (q + 1) * part, :] = wsum[pl.ds(at, part), :]
            second[s][nx * part :, :] = coldot

    @pl.when(step == steps - 1)
    def _():
        mine = pl.multiple_of(idx[0] * half, half)
        theirs = pl.multiple_of((1 - idx[0]) * half, half)
        fown[...] = facc[pl.ds(mine, half), :]
        fother[...] = facc[pl.ds(theirs, half), :]


def grad_pass(idx, own, other, protos, expo, colparts, rowparts, totals, groups, nx, ny):
    half, width = own.shape
    rows, columns = expo.shape
    steps = columns // BN
    mid = steps // 2
    whole = lambda shape: pl.BlockSpec(shape, lambda j, idx: (0,) * len(shape))
    front = pl.BlockSpec((width // nx + 8, BN), lambda j, idx: (0, jnp.minimum(j, mid - 1)))
    back = pl.BlockSpec((width // ny + 8, BN), lambda j, idx: (0, jnp.maximum(j - mid, 0)))
    outs = pl.pallas_call(
        functools.partial(grad_kernel, groups, steps, nx, ny),
        grid_spec=pltpu.PrefetchScalarGridSpec(
            num_scalar_prefetch=1,
            grid=(steps,),
            in_specs=[
                whole((half, width)),
                whole((half, width)),
                pl.BlockSpec((width, BN), lambda j, idx: (0, idx[0] * steps + j)),
                pl.BlockSpec((rows, BN), lambda j, idx: (0, j)),
                whole(colparts.shape),
                whole(rowparts.shape),
                whole(totals.shape),
            ],
            out_specs=[front] * nx
            + [back] * ny
            + [
                whole((half, width)),
                whole((half, width)),
                pl.BlockSpec((1, BN), lambda j, idx: (0, j)),
            ],
            scratch_shapes=[
                pltpu.VMEM((rows, width), BF16),
                pltpu.VMEM((width, rows), BF16),
                pltpu.VMEM((2 * columns // 128, 128), F32),
                pltpu.VMEM((rows, 128), F32),
                pltpu.VMEM((rows, 128), F32),
                pltpu.VMEM((rows, BN), BF16),
                pltpu.VMEM((width, BN), F32),
                pltpu.VMEM((rows, width), F32),
            ],
        ),
        out_shape=[jax.ShapeDtypeStruct((width // nx + 8, columns // 2), F32)] * nx
        + [jax.ShapeDtypeStruct((width // ny + 8, columns // 2), F32)] * ny
        + [
            jax.ShapeDtypeStruct((half, width), F32),
            jax.ShapeDtypeStruct((half, width), F32),
            jax.ShapeDtypeStruct((1, columns), F32),
        ],
        compiler_params=params(),
    )(idx, own, other, protos, expo, colparts, rowparts, totals)
    return outs[:nx], outs[nx : nx + ny], outs[-3], outs[-2], outs[-1]


def cut_kernel(slot, n, count, part, idx, *refs):
    arrived = refs[:count]
    outs = refs[count : count + n]
    total = refs[count + n]
    value = arrived[0][...]
    for ref in arrived[1:]:
        value = value + ref[...]
    total[...] = value
    own = total.shape[0] - 8
    for s in range(n):
        at = pl.multiple_of(lax.rem(idx[slot] + s, n) * part, part)
        outs[s][:part, :] = total[pl.ds(at, part), :]
        outs[s][part:, :] = total[own:, :]


def cut_pass(idx, arrived, slot, n):
    rows, columns = arrived[0].shape
    part = (rows - 8) // n
    count = len(arrived)
    return pl.pallas_call(
        functools.partial(cut_kernel, slot, n, count, part),
        grid_spec=pltpu.PrefetchScalarGridSpec(
            num_scalar_prefetch=1,
            grid=(columns // BN,),
            in_specs=[pl.BlockSpec((rows, BN), lambda j, idx: (0, j))] * count,
            out_specs=[pl.BlockSpec((part + 8, BN), lambda j, idx: (0, j))] * n,
            scratch_shapes=[pltpu.VMEM((rows, BN), F32)],
        ),
        out_shape=[jax.ShapeDtypeStruct((part + 8, columns), F32)] * n,
        compiler_params=params(),
    )(idx, *arrived)


def proto_kernel(count_a, count_b, part, idx, *refs):
    a_refs = refs[:count_a]
    b_refs = refs[count_a : count_a + count_b]
    protos, winv, mine, theirs = refs[count_a + count_b :]
    columns = a_refs[0].shape[1]
    own = part // 2
    core = idx[0]
    for side, group in enumerate((a_refs, b_refs)):
        value = group[0][...]
        for ref in group[1:]:
            value = value + ref[...]
        span = slice(side * columns, (side + 1) * columns)
        inv = winv[:, span]
        wnorm = protos[:, span].astype(F32) * inv
        grad = (value[:part, :] - wnorm * value[part : part + 1, :]) * inv
        low = grad[:own, :]
        high = grad[own:, :]
        mine[:, span] = jnp.where(core == 0, low, high)
        theirs[:, span] = jnp.where(core == 0, high, low)


def proto_pass(idx, a_parts, b_parts, protos, winv):
    rows, columns = a_parts[0].shape
    part = rows - 8
    total = 2 * columns
    own = part // 2
    whole = lambda shape: pl.BlockSpec(shape, lambda i, idx: (0, 0))
    return pl.pallas_call(
        functools.partial(proto_kernel, len(a_parts), len(b_parts), part),
        grid_spec=pltpu.PrefetchScalarGridSpec(
            num_scalar_prefetch=1,
            grid=(1,),
            in_specs=[whole((rows, columns))] * (len(a_parts) + len(b_parts))
            + [pl.BlockSpec((part, total), lambda i, idx: (idx[4], idx[0])), whole((1, total))],
            out_specs=[whole((own, total))] * 2,
        ),
        out_shape=[jax.ShapeDtypeStruct((own, total), F32)] * 2,
        compiler_params=params(),
    )(idx, *a_parts, *b_parts, protos, winv)


def pack_kernel(nz, crops, masked, per_z, share, patches, mine, came, out):
    total = mine[...] + came[...]
    crop_share = crops // nz
    for z in range(nz):
        out[z, :crop_share, :] = total[z * crop_share : (z + 1) * crop_share, :]
        image = z * share // patches
        start = crops + image * masked
        out[z, crop_share:, :] = total[start : start + per_z * masked, :]


def pack_pass(mine, came, nz, crops, masked, per_z, share, patches):
    width = mine.shape[1]
    out_shape = (nz, crops // nz + per_z * masked, width)
    return pl.pallas_call(
        functools.partial(pack_kernel, nz, crops, masked, per_z, share, patches),
        out_shape=jax.ShapeDtypeStruct(out_shape, F32),
        compiler_params=pltpu.CompilerParams(vmem_limit_bytes=VMEM_LIMIT),
    )(mine, came)


def feature_kernel(nz, crop_share, masked, per_z, share, patches, idx, mask, parts, crops, rows, crop_out, patch_out, total, dense):
    value = parts[0]
    for z in range(1, nz):
        value = value + parts[z]
    total[...] = value
    dense[...] = jnp.zeros_like(dense)
    first_row = idx[3] * share
    first_image = first_row // patches
    offset = first_row - first_image * patches

    def place(m, _):
        image = m // masked
        at = mask[(first_image + image) * masked + m - image * masked] + image * patches - offset

        @pl.when(jnp.logical_and(at >= 0, at < share))
        def _():
            dense[pl.ds(at, 1), :] = total[pl.ds(crop_share + m, 1), :]

        return 0

    lax.fori_loop(0, per_z * masked, place, 0, unroll=4)

    def back(x, fgrad):
        xf = x.astype(F32)
        inv = lax.rsqrt(jnp.sum(xf * xf, axis=-1, keepdims=True) + EPS)
        u = xf * inv
        return (fgrad - u * jnp.sum(u * fgrad, axis=-1, keepdims=True)) * inv

    crop_out[...] = back(crops[...], total[:crop_share, :])
    patch_out[...] = back(rows[...], dense[...])


def feature_pass(idx, mask, parts, crops, patch_rows, nz, masked, per_z, patches):
    width = crops.shape[1]
    crop_share = crops.shape[0] // nz
    share = patch_rows.shape[0] // nz
    return pl.pallas_call(
        functools.partial(feature_kernel, nz, crop_share, masked, per_z, share, patches),
        grid_spec=pltpu.PrefetchScalarGridSpec(
            num_scalar_prefetch=2,
            grid=(1,),
            in_specs=[
                pl.BlockSpec(parts.shape, lambda i, idx, mask: (0, 0, 0)),
                pl.BlockSpec((crop_share, width), lambda i, idx, mask: (idx[3], 0)),
                pl.BlockSpec((share, width), lambda i, idx, mask: (idx[3], 0)),
            ],
            out_specs=[
                pl.BlockSpec((crop_share, width), lambda i, idx, mask: (0, 0)),
                pl.BlockSpec((share, width), lambda i, idx, mask: (0, 0)),
            ],
            scratch_shapes=[pltpu.VMEM(parts.shape[1:], F32), pltpu.VMEM((share, width), F32)],
        ),
        out_shape=[
            jax.ShapeDtypeStruct((crop_share, width), F32),
            jax.ShapeDtypeStruct((share, width), F32),
        ],
        compiler_params=params(),
    )(idx, mask, parts, crops, patch_rows)


def shifted(n, s):
    return [(i, (i + s) % n) for i in range(n)]


def local(
    sizes,
    student_crops,
    teacher_crops,
    student_patches,
    teacher_patches,
    patch_mask,
    student_protos,
    teacher_protos,
):
    nx, ny, nz = sizes
    images, masked = patch_mask.shape
    patches = student_patches.shape[0] // images
    width = student_crops.shape[1]
    crops = student_crops.shape[0]
    half = crops + images * masked
    columns = student_protos.shape[1] // 2
    groups = row_groups(half, crops)
    ix, iy, ic, iz = (lax.axis_index(a) for a in ("x", "y", "c", "z"))
    idx = jnp.stack([ic, ix, iy, iz, ix * ny + iy]).astype(jnp.int32)
    mask_col = patch_mask.reshape(-1, 1)
    swap = [(0, 1), (1, 0)]

    teacher = prep(teacher_crops, teacher_patches, mask_col, images, masked)
    teacher_other = lax.ppermute(teacher, "c", swap)
    student = prep(student_crops, student_patches, mask_col, images, masked)
    student_other = lax.ppermute(student, "c", swap)

    expo, sums = teacher_pass(
        idx, teacher, teacher_other, teacher_protos, groups, columns, nx * ny
    )
    total = None
    totals = None
    for step in range(ITERS):
        colparts = lax.all_to_all(sums, ("x", "y"), 0, 0)
        if step == 0:
            total = denominator_pass(idx, student, student_other, student_protos, columns)
        sums = row_pass(expo, colparts, total if step == 0 else None, half, crops, 2 * nz)
        rowparts = lax.all_to_all(sums, ("c", "z"), 0, 0)
        if step == 0:
            totals = rowparts
        if step < ITERS - 1:
            sums = column_pass(expo, rowparts, groups, nx * ny)

    a_out, b_out, f_mine, f_theirs, winv = grad_pass(
        idx,
        student,
        student_other,
        student_protos,
        expo,
        colparts,
        rowparts,
        totals,
        groups,
        nx,
        ny,
    )
    a_in = [a_out[0]] + [lax.ppermute(a_out[s], "x", shifted(nx, s)) for s in range(1, nx)]
    b_in = [b_out[0]] + [lax.ppermute(b_out[s], "y", shifted(ny, s)) for s in range(1, ny)]
    f_came = lax.ppermute(f_theirs, "c", swap)
    share = student_patches.shape[0] // nz
    per_z = max(1, share // patches)
    packed = pack_pass(f_mine, f_came, nz, crops, masked, per_z, share, patches)
    fparts = lax.all_to_all(packed, "z", 0, 0)
    crop_grad, patch_grad = feature_pass(
        idx,
        patch_mask.reshape(-1),
        fparts,
        student_crops,
        student_patches,
        nz,
        masked,
        per_z,
        patches,
    )
    a_cut = cut_pass(idx, a_in, 2, ny)
    a_in = [a_cut[0]] + [lax.ppermute(a_cut[s], "y", shifted(ny, s)) for s in range(1, ny)]
    b_cut = cut_pass(idx, b_in, 1, nx)
    b_in = [b_cut[0]] + [lax.ppermute(b_cut[s], "x", shifted(nx, s)) for s in range(1, nx)]
    mine, theirs = proto_pass(idx, a_in, b_in, student_protos, winv)
    came = lax.ppermute(theirs, "c", swap)
    proto_grad = jnp.where(
        ic == 0,
        jnp.concatenate([mine, came], axis=1),
        jnp.concatenate([came, mine], axis=1),
    )
    return (proto_grad, crop_grad, patch_grad)


def solution(mesh):
    dp, nz = mesh.devices.shape
    nx = 4 if dp == 32 else 2
    ny = dp // (2 * nx)
    grid = Mesh(mesh.devices.reshape(nx, ny, 2, nz), ("x", "y", "c", "z"))
    rows = ("x", "y", "c")
    in_specs = (
        P(rows, None),
        P(rows, None),
        P(rows, None),
        P(rows, None),
        P(rows, None),
        P(None, "z"),
        P(None, "z"),
    )
    out_specs = (P(rows, "z"), P(rows + ("z",), None), P(rows + ("z",), None))
    return jax.shard_map(
        functools.partial(local, (nx, ny, nz)),
        mesh=grid,
        in_specs=in_specs,
        out_specs=out_specs,
        check_vma=False,
    )
```

time: 755 us -> 217 us (0.29)
  waiting for transfers between devices: 456 us -> 29 us
  blocking collectives: 173 us -> 66.9 us
  Pallas kernels: 0 us -> 75.9 us
  other arithmetic: 68.8 us -> 0.72 us
  matrix products: 33 us -> 0 us
  starting transfers between devices: 0.47 us -> 28.9 us
  between operations: 14.1 us -> 0.84 us
    psum x4 -> x0, waiting for transfers between devices: 357 us -> none  [the longest x3 301 us: balance_apart(): colscale = 1.0 / lax.psum(col_part(rowscale, exponent_matrix), 'dp')]
    psum x4 -> x0, blocking collectives: 173 us -> none  [the longest x1 124 us: local(): coldot = lax.psum(jnp.sum(wslice * shard, axis=0, keepdims=True), 'dp')]
    reduce_scatter x1 -> x0, waiting for transfers between devices: 98.4 us -> none  [local(): lax.psum_scatter(jnp.einsum('rb,rk->bk', student_dino, grad_dino, preferr...]
    pallas_call x0 -> x15, Pallas kernels: none -> 75.9 us  [the longest x3 21.6 us: row_pass(): pl.pallas_call(functools.partial(row_kernel, half // RB, crops // RB, col...]
    all_to_all x0 -> x5, blocking collectives: none -> 66.9 us  [the longest x3 37.9 us: local(): rowparts = lax.all_to_all(sums, ('c', 'z'), 0, 0)]
    reduce_sum x19 -> x0, other arithmetic: 37.6 us -> none  [the longest x6 14.1 us: row_part(): jnp.sum(exponent_matrix.astype(jnp.float32) * colscale[None, :], axis=1)]
    dot_general x8 -> x0, matrix products: 33 us -> none  [the longest x1 8.79 us: local(): jnp.einsum('rb,rk->bk', student_ibot, grad_ibot, preferred_element_type=j...]
    ppermute x0 -> x16, waiting for transfers between devices: none -> 24.8 us  [the longest x3 17.3 us: local(): lax.ppermute(b_out[s], 'y', shifted(ny, s))]
  transfers between devices with their start and end apart: 5 -> 18, of which waited for: 5 -> 7; matrix products, arithmetic and copies ran while one was open for 5% -> 0% of each run, Pallas kernels for 0% -> 10%
where the time goes in v1:
time: 217 us; the launch traced here: 213 us
  Pallas kernels  75.9 us (35%)
  blocking collectives  66.9 us (31%)
  waiting for transfers between devices  29 us (13%)
  starting transfers between devices  28.9 us (13%)
  local copies, waits for them, and re-layouts  11.1 us (5%)
    all_to_all x3, blocking collectives, local(): rowparts = lax.all_to_all(sums, ('c', 'z'), 0, 0)  37.9 us
    all_to_all x2, blocking collectives, local(): colparts = lax.all_to_all(sums, ('x', 'y'), 0, 0)  29 us
    pallas_call x3, Pallas kernels, row_pass(): pl.pallas_call(functools.partial(row_kernel, half // RB, crops // RB, col...  21.6 us
    ppermute x3, waiting for transfers between devices, local(): lax.ppermute(b_out[s], 'y', shifted(ny, s))  17.3 us
    pallas_call x1, Pallas kernels, grad_pass(): pl.pallas_call(functools.partial(grad_kernel, groups, steps, nx, ny), gri...  14.7 us
    pallas_call x2, Pallas kernels, column_pass(): pl.pallas_call(functools.partial(column_kernel, groups), grid=(columns //...  13.7 us
    unnamed x24, local copies, waits for them, and re-layouts  10 us
    pallas_call x1, Pallas kernels, teacher_pass(): pl.pallas_call(functools.partial(teacher_kernel, groups), grid_spec=pltpu...  8.52 us
  transfers between devices with their start and end apart: 18, of which 7 were waited for; matrix products, arithmetic and copies ran while one was open for 0% of the time, Pallas kernels for 10%

profile of v1, /device:TPU:32, one launch (start us, length us, event | category | flops | bytes accessed | tf_op | source)
XLA Modules:
  0.0 213.3 jit_solution(12563988094392878282)
XLA Ops:
  6.7 2.2 %copy-done.2 = bf16[256,8192]{1,0:T(8,128)(2,1)S(1)} copy-done((bf16[256,8192]{1,0:T(8,128)(2,1)S(1)}, bf16[256,8192]{1,0:T(8,128)(2,1)}, u32[]{:S(2)}) %copy-start.2) | copy-done | bytes 4194328
  8.9 8.5 %shard_map.96 = (bf16[1024,4096]{1,0:T(8,128)(2,1)}, f32[16,64,128]{2,1,0:T(8,128)}) custom-call(s32[5]{0:T(128)S(1)} %stack.23.idx, f32[512,256]{1,0:T(8,128)S(1)} %shard_map.95.own, f32[512,256]{1,0:T(8,128)S(1)} %collective-permute-done.1.other, bf16[256,8192]{1,0:T(8,128)(2,1)S(1)} %copy-done.2), custom_call_target="tpu_custom_call" | custom-call | tf_op jit(solution)/shard_map/pallas_call | solution.py:111
  17.5 7.0 %all-to-all-start = ((f32[16,64,128]{2,1,0:T(8,128)}), f32[16,64,128]{2,1,0:T(8,128)S(1)}, u32[]{:S(2)}, u32[]{:S(2)}) async-start(f32[16,64,128]{2,1,0:T(8,128)} %get-tuple-element.29), calls=%async_computation | async-start | bytes 1048576 | tf_op jit(solution)/shard_map/all_to_all | solution.py:595
  24.5 2.2 %copy-done = bf16[256,8192]{1,0:T(8,128)(2,1)S(1)} copy-done((bf16[256,8192]{1,0:T(8,128)(2,1)S(1)}, bf16[256,8192]{1,0:T(8,128)(2,1)}, u32[]{:S(2)}) %copy-start) | copy-done | bytes 4194328
  26.7 5.3 %shard_map.97.refs_0_ = f32[8,128]{1,0:T(8,128)S(1)} custom-call(s32[5]{0:T(128)S(1)} %stack.23.idx, f32[512,256]{1,0:T(8,128)S(1)} %shard_map.94.own, f32[512,256]{1,0:T(8,128)S(1)} %collective-permute-done.other, bf16[256,8192]{1,0:T(8,128)(2,1)S(1)} %copy-done), custom_call_target="tpu_custom_call" | custom-call | tf_op jit(solution)/shard_map/pallas_call | solution.py:164
  32.0 4.1 %all-to-all-done.colparts = f32[16,64,128]{2,1,0:T(8,128)S(1)} async-done(((f32[16,64,128]{2,1,0:T(8,128)}), f32[16,64,128]{2,1,0:T(8,128)S(1)}, u32[]{:S(2)}, u32[]{:S(2)}) %all-to-all-start) | async-done | bytes 524320 | tf_op jit(solution)/shard_map/all_to_all | solution.py:595
  36.2 7.2 %shard_map.98 = f32[16,16,128]{2,1,0:T(8,128)S(1)} custom-call(bf16[1024,4096]{1,0:T(8,128)(2,1)} %get-tuple-element.28.expo, f32[16,64,128]{2,1,0:T(8,128)S(1)} %all-to-all-done.colparts, f32[8,128]{1,0:T(8,128)S(1)} %shard_map.97.refs_0_), custom_call_target="tpu_custom_call" | custom-call | tf_op jit(solution)/shard_map/pallas_call | solution.py:223
  43.4 16.6 %all_to_all.35.rowparts.totals = f32[16,16,128]{2,1,0:T(8,128)S(1)} all-to-all(f32[16,16,128]{2,1,0:T(8,128)S(1)} %shard_map.98), channel_id=1, replica_groups=mesh['x'=4,'y'=4,'c'=2,'z'=8] {'c','z'}, dimensions={0} | all-to-all | bytes 262144 | tf_op jit(solution)/shard_map/all_to_all | solution.py:599
  60.0 6.9 %shard_map.99 = f32[16,64,128]{2,1,0:T(8,128)S(1)} custom-call(bf16[1024,4096]{1,0:T(8,128)(2,1)} %get-tuple-element.28.expo, f32[16,16,128]{2,1,0:T(8,128)S(1)} %all_to_all.35.rowparts.totals), custom_call_target="tpu_custom_call" | custom-call | tf_op jit(solution)/shard_map/pallas_call | solution.py:268
  66.9 14.3 %all_to_all.36.colparts = f32[16,64,128]{2,1,0:T(8,128)S(1)} all-to-all(f32[16,64,128]{2,1,0:T(8,128)S(1)} %shard_map.99), channel_id=1, replica_groups=mesh['x'=4,'y'=4,'c'=2,'z'=8] {'x','y'}, dimensions={0} | all-to-all | bytes 1048576 | tf_op jit(solution)/shard_map/all_to_all | solution.py:595
  81.2 7.2 %shard_map.100 = f32[16,8,128]{2,1,0:T(8,128)S(1)} custom-call(bf16[1024,4096]{1,0:T(8,128)(2,1)} %get-tuple-element.28.expo, f32[16,64,128]{2,1,0:T(8,128)S(1)} %all_to_all.36.colparts), custom_call_target="tpu_custom_call" | custom-call | tf_op jit(solution)/shard_map/pallas_call | solution.py:223
  88.4 10.9 %all_to_all.37.rowparts = f32[16,8,128]{2,1,0:T(8,128)S(1)} all-to-all(f32[16,8,128]{2,1,0:T(8,128)S(1)} %shard_map.100), channel_id=1, replica_groups=mesh['x'=4,'y'=4,'c'=2,'z'=8] {'c','z'}, dimensions={0} | all-to-all | bytes 131072 | tf_op jit(solution)/shard_map/all_to_all | solution.py:599
  99.3 6.9 %shard_map.101 = f32[16,64,128]{2,1,0:T(8,128)S(1)} custom-call(bf16[1024,4096]{1,0:T(8,128)(2,1)} %get-tuple-element.28.expo, f32[16,8,128]{2,1,0:T(8,128)S(1)} %all_to_all.37.rowparts), custom_call_target="tpu_custom_call" | custom-call | tf_op jit(solution)/shard_map/pallas_call | solution.py:268
  106.1 14.7 %all_to_all.38.colparts = f32[16,64,128]{2,1,0:T(8,128)S(1)} all-to-all(f32[16,64,128]{2,1,0:T(8,128)S(1)} %shard_map.101), channel_id=1, replica_groups=mesh['x'=4,'y'=4,'c'=2,'z'=8] {'x','y'}, dimensions={0} | all-to-all | bytes 1048576 | tf_op jit(solution)/shard_map/all_to_all | solution.py:595
  120.9 7.2 %shard_map.102 = f32[16,8,128]{2,1,0:T(8,128)S(1)} custom-call(bf16[1024,4096]{1,0:T(8,128)(2,1)} %get-tuple-element.28.expo, f32[16,64,128]{2,1,0:T(8,128)S(1)} %all_to_all.38.colparts), custom_call_target="tpu_custom_call" | custom-call | tf_op jit(solution)/shard_map/pallas_call | solution.py:223
  128.1 10.4 %all_to_all.39.rowparts = f32[16,8,128]{2,1,0:T(8,128)S(1)} all-to-all(f32[16,8,128]{2,1,0:T(8,128)S(1)} %shard_map.102), channel_id=1, replica_groups=mesh['x'=4,'y'=4,'c'=2,'z'=8] {'c','z'}, dimensions={0} | all-to-all | bytes 131072 | tf_op jit(solution)/shard_map/all_to_all | solution.py:599
  138.5 14.7 %shard_map.103 = (f32[72,2048]{1,0:T(8,128)S(1)}, f32[72,2048]{1,0:T(8,128)}, f32[72,2048]{1,0:T(8,128)}, f32[72,2048]{1,0:T(8,128)}, f32[72,2048]{1,0:T(8,128)S...) custom-call(s32[5]{0:T(128)S(1)} %stack.23.idx, ...), custom_call_target="tpu_custom_call" | custom-call | tf_op jit(solution)/shard_map/pallas_call | solution.py:359
  153.8 1.4 collective-permute-start.8
  155.3 1.1 collective-permute-start.9
  156.7 2.2 %collective-permute-start.3 = (f32[72,2048]{1,0:T(8,128)}, f32[72,2048]{1,0:T(8,128)}, u32[]{:S(2)}, u32[]{:S(2)}) collective-permute-start(f32[72,2048]{1,0:T(8,128)} %get-tuple-element.32), channel_id=1, source_target_pairs={{0,128},{64,192},{128,0},{192,64},{1,129},{65,193},{129,1},{193,65... | collective-permute-start | bytes 1769480 | tf_op jit(solution)/shard_map/ppermute | solution.py:618
  158.9 10.8 %collective-permute-done.10.refs_3_ = f32[72,2048]{1,0:T(8,128)S(1)} collective-permute-done((f32[72,2048]{1,0:T(8,128)}, f32[72,2048]{1,0:T(8,128)S(1)}, u32[]{:S(2)}, u32[]{:S(2)}) %collective-permute-start.10) | collective-permute-done | bytes 589856 | tf_op jit(solution)/shard_map/ppermute | solution.py:619
  172.6 4.6 %all-to-all-start.6 = ((f32[8,112,256]{2,1,0:T(8,128)}), f32[8,112,256]{2,1,0:T(8,128)S(1)}, u32[]{:S(2)}, u32[]{:S(2)}) async-start(f32[8,112,256]{2,1,0:T(8,128)} %shard_map.107), calls=%async_computation.6 | async-start | bytes 1835008 | tf_op jit(solution)/shard_map/all_to_all | solution.py:624
  177.2 6.6 %collective-permute-done.8.refs_1_ = f32[72,2048]{1,0:T(8,128)} collective-permute-done((f32[72,2048]{1,0:T(8,128)}, f32[72,2048]{1,0:T(8,128)}, u32[]{:S(2)}, u32[]{:S(2)}) %collective-permute-start.8) | collective-permute-done | bytes 589856 | tf_op jit(solution)/shard_map/ppermute | solution.py:619
  184.8 2.9 %shard_map.105 = (f32[24,2048]{1,0:T(8,128)S(1)}, f32[24,2048]{1,0:T(8,128)S(1)}, f32[24,2048]{1,0:T(8,128)S(1)}, f32[24,2048]{1,0:T(8,128)S(1)}) custom-call(s32[5]{0:T(128)S(1)} %stack.23.idx, f32[72,2048]{1,0:T(8,128)S(1)} %get-tuple-element.38.refs_0_, f32[72,2048]{1,0:T(8,128)} %collective-permute-done.8.refs_1_, ...), custom_call_target="tpu_custom_call" | custom-call | tf_op jit(solution)/shard_map/pallas_call | solution.py:422
  188.0 2.4 %collective-permute-start.12 = (f32[24,2048]{1,0:T(8,128)S(1)}, f32[24,2048]{1,0:T(8,128)S(1)}, u32[]{:S(2)}, u32[]{:S(2)}) collective-permute-start(f32[24,2048]{1,0:T(8,128)S(1)} %get-tuple-element.44), channel_id=1, source_target_pairs={{0,128},{64,192},{128,0},{192,64},{1,129},{65,193},{129,1},{193,65... | collective-permute-start | bytes 589832 | tf_op jit(solution)/shard_map/ppermute | solution.py:639
  190.4 1.5 collective-permute-start.13
  192.0 2.9 %shard_map.104 = (f32[24,2048]{1,0:T(8,128)S(1)}, f32[24,2048]{1,0:T(8,128)S(1)}, f32[24,2048]{1,0:T(8,128)S(1)}, f32[24,2048]{1,0:T(8,128)S(1)}) custom-call(s32[5]{0:T(128)S(1)} %stack.23.idx, f32[72,2048]{1,0:T(8,128)S(1)} %get-tuple-element.30.refs_0_, f32[72,2048]{1,0:T(8,128)S(1)} %collective-permute-done.2.refs_1_, ...), custom_call_target="tpu_custom_call" | custom-call | tf_op jit(solution)/shard_map/pallas_call | solution.py:422
  194.9 3.8 %collective-permute-start.5 = (f32[24,2048]{1,0:T(8,128)S(1)}, f32[24,2048]{1,0:T(8,128)S(1)}, u32[]{:S(2)}, u32[]{:S(2)}) collective-permute-start(f32[24,2048]{1,0:T(8,128)S(1)} %get-tuple-element.35), channel_id=1, source_target_pairs={{0,16},{16,32},{32,48},{48,0},{1,17},{17,33},{33,49},{49,1},{2,18}... | collective-permute-start | bytes 589832 | tf_op jit(solution)/shard_map/ppermute | solution.py:637
  199.8 1.7 collective-permute-start.7
  201.5 4.6 %collective-permute-done.5.refs_1_ = f32[24,2048]{1,0:T(8,128)S(1)} collective-permute-done((f32[24,2048]{1,0:T(8,128)S(1)}, f32[24,2048]{1,0:T(8,128)S(1)}, u32[]{:S(2)}, u32[]{:S(2)}) %collective-permute-start.5) | collective-permute-done | bytes 196640 | tf_op jit(solution)/shard_map/ppermute | solution.py:637
  207.6 1.2 collective-permute-done.14
  209.6 3.8 %shard_map.108 = (f32[16,256]{1,0:T(8,128)}, f32[128,256]{1,0:T(8,128)}) custom-call(s32[5]{0:T(128)S(1)} %stack.23.idx, s32[384]{0:T(512)S(1)} %reshape.13.mask, f32[8,112,256]{2,1,0:T(8,128)S(1)} %all-to-all-done.6.parts, bf16[128,256]{1,0:T(8,128)(2,1)S(1)} %copy-done.9, bf16[1024,256]{1,0:T(8,128)(2,1)S(1)} %copy-done.4), custom_call_target="tpu_custom_call" | custom-call | tf_op jit(solution)/shard_map/pallas_call | solution.py:533
  (52 shorter events, 14.5 us)
Async XLA Ops:
  1.5 1.0 copy-start.7
  2.5 0.8 copy-start.10
  3.7 3.0 %collective-permute-start.1 = (f32[512,256]{1,0:T(8,128)S(1)}, f32[512,256]{1,0:T(8,128)S(1)}, u32[]{:S(2)}, u32[]{:S(2)}) collective-permute-start(f32[512,256]{1,0:T(8,128)S(1)} %shard_map.95.own), channel_id=1, source_target_pairs={{0,8},{8,0},{1,9},{9,1},{2,10},{10,2},{3,11},{11,3},{4,12},{12,4},... | collective-permute-start | bytes 1572872 | tf_op jit(solution)/shard_map/ppermute | solution.py:585
  3.8 1.0 copy-start.3
  4.9 0.8 copy-start.8
  6.1 18.4 %collective-permute-start = (f32[512,256]{1,0:T(8,128)S(1)}, f32[512,256]{1,0:T(8,128)S(1)}, u32[]{:S(2)}, u32[]{:S(2)}) collective-permute-start(f32[512,256]{1,0:T(8,128)S(1)} %shard_map.94.own), channel_id=1, source_target_pairs={{0,8},{8,0},{1,9},{9,1},{2,10},{10,2},{3,11},{11,3},{4,12},{12,4},... | collective-permute-start | bytes 1572872 | tf_op jit(solution)/shard_map/ppermute | solution.py:587
  6.7 2.2 %copy-start.2 = (bf16[256,8192]{1,0:T(8,128)(2,1)S(1)}, bf16[256,8192]{1,0:T(8,128)(2,1)}, u32[]{:S(2)}) copy-start(bf16[256,8192]{1,0:T(8,128)(2,1)} %protos.3) | copy-start | bytes 12582916
  17.5 18.7 %all-to-all-start = ((f32[16,64,128]{2,1,0:T(8,128)}), f32[16,64,128]{2,1,0:T(8,128)S(1)}, u32[]{:S(2)}, u32[]{:S(2)}) async-start(f32[16,64,128]{2,1,0:T(8,128)} %get-tuple-element.29), calls=%async_computation | async-start | bytes 1048576 | tf_op jit(solution)/shard_map/all_to_all | solution.py:595
  24.5 2.2 %copy-start = (bf16[256,8192]{1,0:T(8,128)(2,1)S(1)}, bf16[256,8192]{1,0:T(8,128)(2,1)}, u32[]{:S(2)}) copy-start(bf16[256,8192]{1,0:T(8,128)(2,1)} %refs_8_.1) | copy-start | bytes 12582916
  153.3 16.4 %collective-permute-start.10 = (f32[72,2048]{1,0:T(8,128)}, f32[72,2048]{1,0:T(8,128)S(1)}, u32[]{:S(2)}, u32[]{:S(2)}) collective-permute-start(f32[72,2048]{1,0:T(8,128)} %get-tuple-element.41), channel_id=1, source_target_pairs={{0,48},{16,0},{32,16},{48,32},{1,49},{17,1},{33,17},{49,33},{2,50}... | collective-permute-start | bytes 1769480 | tf_op jit(solution)/shard_map/ppermute | solution.py:619
  153.8 2.9 %collective-permute-start.15 = (f32[512,256]{1,0:T(8,128)S(1)}, f32[512,256]{1,0:T(8,128)S(1)}, u32[]{:S(2)}, u32[]{:S(2)}) collective-permute-start(f32[512,256]{1,0:T(8,128)S(1)} %get-tuple-element.50), channel_id=1, source_target_pairs={{0,8},{8,0},{1,9},{9,1},{2,10},{10,2},{3,11},{11,3},{4,12},{12,4},... | collective-permute-start | bytes 1572872 | tf_op jit(solution)/shard_map/ppermute | solution.py:620
  153.8 29.9 %collective-permute-start.8 = (f32[72,2048]{1,0:T(8,128)}, f32[72,2048]{1,0:T(8,128)}, u32[]{:S(2)}, u32[]{:S(2)}) collective-permute-start(f32[72,2048]{1,0:T(8,128)} %get-tuple-element.39), channel_id=1, source_target_pairs={{0,16},{16,32},{32,48},{48,0},{1,17},{17,33},{33,49},{49,1},{2,18}... | collective-permute-start | bytes 1769480 | tf_op jit(solution)/shard_map/ppermute | solution.py:619
  155.3 28.5 %collective-permute-start.9 = (f32[72,2048]{1,0:T(8,128)}, f32[72,2048]{1,0:T(8,128)}, u32[]{:S(2)}, u32[]{:S(2)}) collective-permute-start(f32[72,2048]{1,0:T(8,128)} %get-tuple-element.40), channel_id=1, source_target_pairs={{0,32},{16,48},{32,0},{48,16},{1,33},{17,49},{33,1},{49,17},{2,34}... | collective-permute-start | bytes 1769480 | tf_op jit(solution)/shard_map/ppermute | solution.py:619
  156.4 34.0 %collective-permute-start.2 = (f32[72,2048]{1,0:T(8,128)}, f32[72,2048]{1,0:T(8,128)S(1)}, u32[]{:S(2)}, u32[]{:S(2)}) collective-permute-start(f32[72,2048]{1,0:T(8,128)} %get-tuple-element.31), channel_id=1, source_target_pairs={{0,64},{64,128},{128,192},{192,0},{1,65},{65,129},{129,193},{193,1... | collective-permute-start | bytes 1769480 | tf_op jit(solution)/shard_map/ppermute | solution.py:618
  156.7 35.3 %collective-permute-start.3 = (f32[72,2048]{1,0:T(8,128)}, f32[72,2048]{1,0:T(8,128)}, u32[]{:S(2)}, u32[]{:S(2)}) collective-permute-start(f32[72,2048]{1,0:T(8,128)} %get-tuple-element.32), channel_id=1, source_target_pairs={{0,128},{64,192},{128,0},{192,64},{1,129},{65,193},{129,1},{193,65... | collective-permute-start | bytes 1769480 | tf_op jit(solution)/shard_map/ppermute | solution.py:618
  169.7 0.8 copy-start.5
  170.5 21.5 %collective-permute-start.4 = (f32[72,2048]{1,0:T(8,128)}, f32[72,2048]{1,0:T(8,128)}, u32[]{:S(2)}, u32[]{:S(2)}) collective-permute-start(f32[72,2048]{1,0:T(8,128)} %get-tuple-element.33), channel_id=1, source_target_pairs={{0,192},{64,0},{128,64},{192,128},{1,193},{65,1},{129,65},{193,129... | collective-permute-start | bytes 1769480 | tf_op jit(solution)/shard_map/ppermute | solution.py:618
  172.6 36.9 %all-to-all-start.6 = ((f32[8,112,256]{2,1,0:T(8,128)}), f32[8,112,256]{2,1,0:T(8,128)S(1)}, u32[]{:S(2)}, u32[]{:S(2)}) async-start(f32[8,112,256]{2,1,0:T(8,128)} %shard_map.107), calls=%async_computation.6 | async-start | bytes 1835008 | tf_op jit(solution)/shard_map/all_to_all | solution.py:624
  177.2 29.6 %copy-start.1 = (bf16[256,8192]{1,0:T(8,128)(2,1)S(1)}, bf16[256,8192]{1,0:T(8,128)(2,1)}, u32[]{:S(2)}) copy-start(bf16[256,8192]{1,0:T(8,128)(2,1)} %refs_8_.1) | copy-start | bytes 12582916
  183.7 1.1 copy-start.6
  187.7 19.8 %copy-start.11 = (s32[4,96]{1,0:T(4,128)S(1)}, s32[4,96]{1,0:T(4,128)}, u32[]{:S(2)}) copy-start(s32[4,96]{1,0:T(4,128)} %param.11) | copy-start | bytes 4612
  187.7 12.0 %collective-permute-start.11 = (f32[24,2048]{1,0:T(8,128)S(1)}, f32[24,2048]{1,0:T(8,128)S(1)}, u32[]{:S(2)}, u32[]{:S(2)}) collective-permute-start(f32[24,2048]{1,0:T(8,128)S(1)} %get-tuple-element.43), channel_id=1, source_target_pairs={{0,64},{64,128},{128,192},{192,0},{1,65},{65,129},{129,193},{193,1... | collective-permute-start | bytes 589832 | tf_op jit(solution)/shard_map/ppermute | solution.py:639
  188.0 13.5 %collective-permute-start.12 = (f32[24,2048]{1,0:T(8,128)S(1)}, f32[24,2048]{1,0:T(8,128)S(1)}, u32[]{:S(2)}, u32[]{:S(2)}) collective-permute-start(f32[24,2048]{1,0:T(8,128)S(1)} %get-tuple-element.44), channel_id=1, source_target_pairs={{0,128},{64,192},{128,0},{192,64},{1,129},{65,193},{129,1},{193,65... | collective-permute-start | bytes 589832 | tf_op jit(solution)/shard_map/ppermute | solution.py:639
  190.4 11.1 %collective-permute-start.13 = (f32[24,2048]{1,0:T(8,128)S(1)}, f32[24,2048]{1,0:T(8,128)S(1)}, u32[]{:S(2)}, u32[]{:S(2)}) collective-permute-start(f32[24,2048]{1,0:T(8,128)S(1)} %get-tuple-element.45), channel_id=1, source_target_pairs={{0,192},{64,0},{128,64},{192,128},{1,193},{65,1},{129,65},{193,129... | collective-permute-start | bytes 589832 | tf_op jit(solution)/shard_map/ppermute | solution.py:639
  192.0 17.6 %copy-start.4 = (bf16[1024,256]{1,0:T(8,128)(2,1)S(1)}, bf16[1024,256]{1,0:T(8,128)(2,1)}, u32[]{:S(2)}) copy-start(bf16[1024,256]{1,0:T(8,128)(2,1)} %rows.1) | copy-start | bytes 1572868
  192.0 17.6 %copy-start.9 = (bf16[128,256]{1,0:T(8,128)(2,1)S(1)}, bf16[128,256]{1,0:T(8,128)(2,1)}, u32[]{:S(2)}) copy-start(bf16[128,256]{1,0:T(8,128)(2,1)} %crops.5) | copy-start | bytes 196612
  194.9 11.2 %collective-permute-start.5 = (f32[24,2048]{1,0:T(8,128)S(1)}, f32[24,2048]{1,0:T(8,128)S(1)}, u32[]{:S(2)}, u32[]{:S(2)}) collective-permute-start(f32[24,2048]{1,0:T(8,128)S(1)} %get-tuple-element.35), channel_id=1, source_target_pairs={{0,16},{16,32},{32,48},{48,0},{1,17},{17,33},{33,49},{49,1},{2,18}... | collective-permute-start | bytes 589832 | tf_op jit(solution)/shard_map/ppermute | solution.py:637
  198.7 7.4 %collective-permute-start.6 = (f32[24,2048]{1,0:T(8,128)S(1)}, f32[24,2048]{1,0:T(8,128)S(1)}, u32[]{:S(2)}, u32[]{:S(2)}) collective-permute-start(f32[24,2048]{1,0:T(8,128)S(1)} %get-tuple-element.36), channel_id=1, source_target_pairs={{0,32},{16,48},{32,0},{48,16},{1,33},{17,49},{33,1},{49,17},{2,34}... | collective-permute-start | bytes 589832 | tf_op jit(solution)/shard_map/ppermute | solution.py:637
  199.8 7.0 %collective-permute-start.7 = (f32[24,2048]{1,0:T(8,128)S(1)}, f32[24,2048]{1,0:T(8,128)S(1)}, u32[]{:S(2)}, u32[]{:S(2)}) collective-permute-start(f32[24,2048]{1,0:T(8,128)S(1)} %get-tuple-element.37), channel_id=1, source_target_pairs={{0,48},{16,0},{32,16},{48,32},{1,49},{17,1},{33,17},{49,33},{2,50}... | collective-permute-start | bytes 589832 | tf_op jit(solution)/shard_map/ppermute | solution.py:637
  207.4 1.4 collective-permute-start.14

commit v2 on v0

v2 whole, which is shorter than its diff:
```python
import functools

import jax
import jax.numpy as jnp
from jax import lax
from jax.experimental import pallas as pl
from jax.experimental.pallas import tpu as pltpu
from jax.sharding import Mesh, PartitionSpec as P

ITERS = 3
EPS = 1e-06
TEACHER_TEMP = 0.07
STUDENT_TEMP = 0.1
LOSS_SCALE = 256.0
GRAD_SCALE = LOSS_SCALE / STUDENT_TEMP
LOG2E = 1.4426950408889634

BN = 512
F32 = jnp.float32
BF16 = jnp.bfloat16
VMEM_LIMIT = 26 * 1024 * 1024
SMEM = pl.BlockSpec(memory_space=pltpu.SMEM)
VMEM = pl.BlockSpec(memory_space=pltpu.VMEM)


def call(kernel, out_shape, args, scalars=0, scratch=(), flops=0, traffic=0):
    return pl.pallas_call(
        kernel,
        out_shape=out_shape,
        in_specs=[SMEM] * scalars + [VMEM] * (len(args) - scalars),
        scratch_shapes=list(scratch),
        compiler_params=pltpu.CompilerParams(vmem_limit_bytes=VMEM_LIMIT),
        cost_estimate=pl.CostEstimate(flops=flops, bytes_accessed=traffic, transcendentals=0),
    )(*args)


def array(shape, dtype=F32):
    return jax.ShapeDtypeStruct(shape, dtype)


def unit(x):
    xf = x.astype(F32)
    return xf * lax.rsqrt(jnp.sum(xf * xf, axis=-1, keepdims=True) + EPS)


def unit_cols(w):
    wf = w.astype(F32)
    inv = lax.rsqrt(jnp.sum(wf * wf, axis=0, keepdims=True) + EPS)
    return wf * inv, inv


def prep_kernel(crops, patch_rows, mask, out):
    images, masked = mask.shape
    patches = patch_rows.shape[0] // images
    count = crops.shape[0]
    out[:count, :] = unit(crops[...])
    for i in range(images):
        place = lax.broadcasted_iota(jnp.int32, (patches, masked), 0)
        chosen = (place == mask[i : i + 1, :]).astype(F32).astype(BF16)
        rows = lax.dot_general(
            chosen,
            patch_rows[i * patches : (i + 1) * patches, :],
            (((0,), (0,)), ((), ())),
            preferred_element_type=F32,
        )
        out[count + i * masked : count + (i + 1) * masked, :] = unit(rows)


def prep(crops, patch_rows, mask):
    count = crops.shape[0] + mask.size
    return call(prep_kernel, array((count, crops.shape[1])), [crops, patch_rows, mask])


def place_rows(core, crops, own, other, dest):
    half = own.shape[0]
    rest = half - crops
    for side, ref in ((core, own), (1 - core, other)):
        at = pl.multiple_of(side * crops, crops)
        dest[pl.ds(at, crops), :] = ref[:crops, :].astype(dest.dtype)
        at = pl.multiple_of(2 * crops + side * rest, 128)
        dest[pl.ds(at, rest), :] = ref[crops:, :].astype(dest.dtype)


def row_blocks(start, stop):
    return [(a, min(a + 256, stop)) for a in range(start, stop, 256)]


def proto_block(core, step, protos):
    columns = protos.shape[1] // 2
    at = pl.multiple_of(core * columns + step * BN, BN)
    return unit_cols(protos[:, pl.ds(at, BN)])


def put_columns(step, heads, out):
    copies = out.shape[0]
    per_head = out.shape[1] // 2
    for head in range(2):
        for t in range(BN // 128):
            piece = heads[head][:, 128 * t : 128 * (t + 1)]
            out[:, pl.ds(head * per_head + step * (BN // 128) + t, 1), :] = jnp.broadcast_to(
                piece[None], (copies, 1, 128)
            )


def get_columns(step, head, lines):
    base = head * (lines.shape[0] // 2) + step * (BN // 128)
    return jnp.concatenate([lines[pl.ds(base + t, 1), :] for t in range(BN // 128)], axis=1)


def line_up(values):
    return jnp.concatenate([values[t : t + 1, :] for t in range(values.shape[0])], axis=1)


def teacher_kernel(crops, idx, own, other, protos, expo, sums, feats):
    place_rows(idx[0], crops, own, other, feats)
    rows, columns = expo.shape

    def step(j, _):
        w = proto_block(idx[0], j, protos)[0].astype(BF16)
        at = pl.multiple_of(j * BN, BN)
        heads = []
        for first, last in ((0, 2 * crops), (2 * crops, rows)):
            part = jnp.zeros((1, BN), F32)
            for start, stop in row_blocks(first, last):
                score = jnp.dot(feats[start:stop, :], w, preferred_element_type=F32)
                e = jnp.exp2(score * (LOG2E / TEACHER_TEMP)).astype(BF16)
                expo[start:stop, pl.ds(at, BN)] = e
                part = part + jnp.sum(e.astype(F32), axis=0, keepdims=True)
            heads.append(part)
        put_columns(j, heads, sums)
        return 0

    lax.fori_loop(0, columns // BN, step, 0)


def teacher_pass(idx, own, other, protos, crops, copies):
    half, width = own.shape
    columns = protos.shape[1] // 2
    return call(
        functools.partial(teacher_kernel, crops),
        [array((2 * half, columns), BF16), array((copies, 2 * columns // 128, 128))],
        [idx, own, other, protos],
        scalars=1,
        scratch=[pltpu.VMEM((2 * half, width), BF16)],
        flops=4 * half * width * columns,
        traffic=4 * half * columns,
    )


def student_kernel(crops, idx, own, other, protos, expo, total, mix, turned, feats, acc):
    place_rows(idx[0], crops, own, other, feats)
    turned[...] = jnp.transpose(feats[...].astype(F32)).astype(BF16)
    acc[...] = jnp.zeros_like(acc)
    mix[...] = jnp.zeros_like(mix)
    rows, columns = expo.shape

    def step(j, _):
        w = proto_block(idx[0], j, protos)[0].astype(BF16)
        at = pl.multiple_of(j * BN, BN)
        for start, stop in row_blocks(0, rows):
            score = jnp.dot(feats[start:stop, :], w, preferred_element_type=F32)
            p = jnp.exp2(score * (LOG2E / STUDENT_TEMP))
            part = p[:, :128]
            for t in range(1, BN // 128):
                part = part + p[:, 128 * t : 128 * (t + 1)]
            acc[start:stop, :] += part
            p = p.astype(BF16)
            expo[start:stop, pl.ds(at, BN)] = p
            mix[start:stop, :] += lax.dot_general(
                p, w, (((1,), (1,)), ((), ())), preferred_element_type=F32
            )
        return 0

    lax.fori_loop(0, columns // BN, step, 0)
    for t in range(rows // 128):
        block = jnp.transpose(acc[128 * t : 128 * (t + 1), :])
        total[t : t + 1, :] = jnp.sum(block, axis=0, keepdims=True)


def student_pass(idx, own, other, protos, crops):
    half, width = own.shape
    columns = protos.shape[1] // 2
    rows = 2 * half
    return call(
        functools.partial(student_kernel, crops),
        [
            array((rows, columns), BF16),
            array((rows // 128, 128)),
            array((rows, width)),
            array((width, rows), BF16),
        ],
        [idx, own, other, protos],
        scalars=1,
        scratch=[pltpu.VMEM((rows, width), BF16), pltpu.VMEM((rows, 128), F32)],
        flops=4 * rows * width * columns,
        traffic=2 * rows * columns,
    )


def row_kernel(crops, extra, expo, colparts, *refs):
    if extra:
        total, out, colscale = refs
    else:
        out, colscale = refs
    copies = out.shape[0]
    rows, columns = expo.shape
    per_head = columns // 128
    colscale[...] = 1.0 / jnp.sum(colparts[...], axis=0)
    if extra:
        count = total.shape[0]
        out[:, count:, :] = jnp.broadcast_to(total[...][None], (copies, count, 128))

    def block(i, _):
        head = jnp.where(i < 2 * crops // 128, 0, 1)
        at = pl.multiple_of(i * 128, 128)

        def chunk(k, acc):
            e = expo[pl.ds(at, 128), pl.ds(pl.multiple_of(k * 128, 128), 128)].astype(F32)
            return acc + e * colscale[pl.ds(head * per_head + k, 1), :]

        acc = lax.fori_loop(0, per_head, chunk, jnp.zeros((128, 128), F32), unroll=8)
        sums = jnp.sum(jnp.transpose(acc), axis=0, keepdims=True)
        out[:, pl.ds(i, 1), :] = jnp.broadcast_to(sums[None], (copies, 1, 128))
        return 0

    lax.fori_loop(0, rows // 128, block, 0)


def row_pass(expo, colparts, total, crops, copies):
    rows, columns = expo.shape
    extra = total is not None
    return call(
        functools.partial(row_kernel, crops, extra),
        array((copies, rows // 128 * (2 if extra else 1), 128)),
        [expo, colparts] + ([total] if extra else []),
        scratch=[pltpu.VMEM((2 * columns // 128, 128), F32)],
        flops=2 * rows * columns,
        traffic=2 * rows * columns,
    )


def split3(v):
    high = v.astype(BF16)
    rest = v - high.astype(F32)
    middle = rest.astype(BF16)
    low = (rest - middle.astype(F32)).astype(BF16)
    pad = jnp.zeros((13, v.shape[1]), F32)
    parts = [high.astype(F32), middle.astype(F32), low.astype(F32), pad]
    return jnp.concatenate(parts, axis=0).astype(BF16)


def column_kernel(crops, expo, rowparts, out):
    rows, columns = expo.shape
    scale = line_up(1.0 / jnp.sum(rowparts[:, : rows // 128, :], axis=0))
    spans = [(0, 2 * crops), (2 * crops, rows)]
    lefts = [split3(scale[:, first:last]) for first, last in spans]
    for j in range(columns // BN):
        heads = []
        for left, (first, last) in zip(lefts, spans):
            sums = jnp.dot(
                left, expo[first:last, j * BN : (j + 1) * BN], preferred_element_type=F32
            )
            heads.append(sums[0:1, :] + sums[1:2, :] + sums[2:3, :])
        put_columns(j, heads, out)


def column_pass(expo, rowparts, crops, copies):
    rows, columns = expo.shape
    return call(
        functools.partial(column_kernel, crops),
        array((copies, 2 * columns // 128, 128)),
        [expo, rowparts],
        flops=2 * rows * columns,
        traffic=2 * rows * columns,
    )


def prob_kernel(turned, student_expo, totals, out):
    rows, columns = student_expo.shape
    sub = rows // 128
    scale = line_up(GRAD_SCALE / jnp.sum(totals[:, sub : 2 * sub, :], axis=0))
    left = (turned[...].astype(F32) * scale).astype(BF16)
    for j in range(columns // BN):
        span = slice(j * BN, (j + 1) * BN)
        out[:, span] = jnp.dot(left, student_expo[:, span], preferred_element_type=F32)


def prob_pass(turned, student_expo, totals):
    width = turned.shape[0]
    rows, columns = student_expo.shape
    return call(
        prob_kernel,
        array((width, columns)),
        [turned, student_expo, totals],
        flops=2 * rows * columns * width,
        traffic=2 * rows * columns,
    )


def weight_kernel(crops, idx, turned, expo, prob, protos, colparts, rowparts, out, winv_out, scales, left):
    rows, columns = expo.shape
    copies = out.shape[0]
    width = turned.shape[0]
    part = width // copies
    scales[...] = GRAD_SCALE / jnp.sum(colparts[...], axis=0)
    scale = line_up(1.0 / jnp.sum(rowparts[:, : rows // 128, :], axis=0))
    left[...] = (turned[...].astype(F32) * scale).astype(BF16)
    spans = [(0, 2 * crops), (2 * crops, rows)]
    tail = columns // 128 * part

    def step(j, _):
        at = pl.multiple_of(j * BN, BN)
        wsum = prob[:, pl.ds(at, BN)]
        for head, (first, last) in enumerate(spans):
            target = jnp.dot(
                left[:, first:last], expo[first:last, pl.ds(at, BN)], preferred_element_type=F32
            )
            wsum = wsum - target * get_columns(j, head, scales)
        wnorm, winv = proto_block(idx[0], j, protos)
        winv_out[:, pl.ds(at, BN)] = winv
        coldot = jnp.sum(wnorm * wsum, axis=0, keepdims=True)
        for t in range(BN // 128):
            lanes = slice(128 * t, 128 * (t + 1))
            row = pl.multiple_of((j * (BN // 128) + t) * part, part)
            for d in range(copies):
                out[d, pl.ds(row, part), :] = wsum[d * part : (d + 1) * part, lanes]
            out[:, pl.ds(tail + j * (BN // 128) + t, 1), :] = jnp.broadcast_to(
                coldot[:, lanes][None], (copies, 1, 128)
            )
        return 0

    lax.fori_loop(0, columns // BN, step, 0)


def weight_pass(idx, turned, expo, prob, protos, colparts, rowparts, crops, copies):
    width, rows = turned.shape
    columns = expo.shape[1]
    lines = columns // 128 * (width // copies + 1)
    return call(
        functools.partial(weight_kernel, crops),
        [array((copies, lines, 128)), array((1, columns))],
        [idx, turned, expo, prob, protos, colparts, rowparts],
        scalars=1,
        scratch=[
            pltpu.VMEM((2 * columns // 128, 128), F32),
            pltpu.VMEM((width, rows), BF16),
        ],
        flops=2 * rows * columns * width,
        traffic=2 * rows * columns,
    )


def proto_kernel(idx, parts, protos, winv, mine, theirs):
    columns = winv.shape[1]
    copies = parts.shape[0]
    part = protos.shape[0] // copies
    own = part // 2
    core = idx[0]
    tail = columns // 128 * part
    row = pl.multiple_of(idx[2] * part, part)
    for t in range(columns // 128):
        lanes = slice(128 * t, 128 * (t + 1))
        wsum = jnp.sum(parts[:, t * part : (t + 1) * part, :], axis=0)
        coldot = jnp.sum(parts[:, tail + t : tail + t + 1, :], axis=0)
        inv = winv[:, lanes]
        at = pl.multiple_of(core * columns + 128 * t, 128)
        wnorm = protos[pl.ds(row, part), pl.ds(at, 128)].astype(F32) * inv
        grad = (wsum - wnorm * coldot) * inv
        low = grad[:own, :]
        high = grad[own:, :]
        mine[:, lanes] = jnp.where(core == 0, low, high)
        theirs[:, lanes] = jnp.where(core == 0, high, low)


def proto_pass(idx, parts, protos, winv):
    own = protos.shape[0] // parts.shape[0] // 2
    columns = winv.shape[1]
    return call(
        proto_kernel,
        [array((own, columns)), array((own, columns))],
        [idx, parts, protos, winv],
        scalars=1,
    )


def target_kernel(crops, idx, expo, protos, colparts, out, scales):
    rows, columns = expo.shape
    scales[...] = 1.0 / jnp.sum(colparts[...], axis=0)
    out[...] = jnp.zeros_like(out)

    def step(j, _):
        wnorm = proto_block(idx[0], j, protos)[0]
        at = pl.multiple_of(j * BN, BN)
        for head, (first, last) in enumerate(((0, 2 * crops), (2 * crops, rows))):
            w = (wnorm * get_columns(j, head, scales)).astype(BF16)
            out[first:last, :] += lax.dot_general(
                expo[first:last, pl.ds(at, BN)],
                w,
                (((1,), (1,)), ((), ())),
                preferred_element_type=F32,
            )
        return 0

    lax.fori_loop(0, columns // BN, step, 0)


def target_pass(idx, expo, protos, colparts, crops):
    rows, columns = expo.shape
    width = protos.shape[0]
    return call(
        functools.partial(target_kernel, crops),
        array((rows, width)),
        [idx, expo, protos, colparts],
        scalars=1,
        scratch=[pltpu.VMEM((2 * columns // 128, 128), F32)],
        flops=2 * rows * columns * width,
        traffic=2 * rows * columns,
    )


def spread_row(line):
    return jnp.transpose(jnp.broadcast_to(line, (128, 128)))


def combine_kernel(crops, idx, mix, target, totals, rowparts, mine, theirs, buf):
    rows, width = mix.shape
    sub = rows // 128
    prob = GRAD_SCALE / jnp.sum(totals[:, sub : 2 * sub, :], axis=0)
    row = GRAD_SCALE / jnp.sum(rowparts[:, :sub, :], axis=0)
    for t in range(sub):
        span = slice(128 * t, 128 * (t + 1))
        p = jnp.concatenate([spread_row(prob[t : t + 1, :])] * (width // 128), axis=1)
        r = jnp.concatenate([spread_row(row[t : t + 1, :])] * (width // 128), axis=1)
        buf[span, :] = mix[span, :] * p - target[span, :] * r
    rest = rows // 2 - crops
    for side, ref in ((idx[0], mine), (1 - idx[0], theirs)):
        ref[:crops, :] = buf[pl.ds(pl.multiple_of(side * crops, crops), crops), :]
        ref[crops:, :] = buf[pl.ds(pl.multiple_of(2 * crops + side * rest, 128), rest), :]


def combine_pass(idx, mix, target, totals, rowparts, crops):
    rows, width = mix.shape
    return call(
        functools.partial(combine_kernel, crops),
        [array((rows // 2, width)), array((rows // 2, width))],
        [idx, mix, target, totals, rowparts],
        scalars=1,
        scratch=[pltpu.VMEM((rows, width), F32)],
    )


def pack_kernel(nz, crops, mine, came, out):
    half = mine.shape[0]
    chunk = half // nz
    share = crops // nz
    rest = chunk - share
    for z in range(nz):
        for src, dst, size in ((z * share, z * chunk, share), (crops + z * rest, z * chunk + share, rest)):
            out[dst : dst + size, :] = mine[src : src + size, :] + came[src : src + size, :]


def pack_pass(mine, came, nz, crops):
    return call(functools.partial(pack_kernel, nz, crops), array(mine.shape), [mine, came])


def feature_kernel(pair, patches, idx, mask, *refs):
    if pair:
        own, other, crops, rows, crop_out, patch_out, masked_rows, dense = refs
    else:
        own, crops, rows, crop_out, patch_out, masked_rows, dense = refs
    z = idx[1]
    masked = mask.shape[1]
    crop_share = crop_out.shape[0]
    share = patch_out.shape[0]
    rest = own.shape[0] - crop_share
    if pair:
        odd = lax.rem(z, 2)
        masked_rows[pl.ds(pl.multiple_of(odd * rest, 8), rest), :] = own[crop_share:, :]
        masked_rows[pl.ds(pl.multiple_of((1 - odd) * rest, 8), rest), :] = other[crop_share:, :]
    else:
        masked_rows[...] = own[crop_share:, :]
    dense[...] = jnp.zeros_like(dense)
    first_row = z * share
    first_image = first_row // patches
    offset = first_row - first_image * patches
    for image in range(masked_rows.shape[0] // masked):

        def place(m, _):
            at = mask[first_image + image, m] + image * patches - offset

            @pl.when(jnp.logical_and(at >= 0, at < share))
            def _():
                dense[pl.ds(at, 1), :] = masked_rows[pl.ds(image * masked + m, 1), :]

            return 0

        lax.fori_loop(0, masked, place, 0, unroll=4)

    def back(x, fgrad):
        xf = x.astype(F32)
        inv = lax.rsqrt(jnp.sum(xf * xf, axis=-1, keepdims=True) + EPS)
        u = xf * inv
        return (fgrad - u * jnp.sum(u * fgrad, axis=-1, keepdims=True)) * inv

    crop_at = pl.multiple_of(z * crop_share, 16)
    patch_at = pl.multiple_of(z * share, 128)
    crop_out[...] = back(crops[pl.ds(crop_at, crop_share), :], own[:crop_share, :])
    patch_out[...] = back(rows[pl.ds(patch_at, share), :], dense[...])


def feature_pass(idx, mask, pieces, crops, patch_rows, nz, patches):
    width = crops.shape[1]
    crop_share = crops.shape[0] // nz
    share = patch_rows.shape[0] // nz
    count = len(pieces) * (pieces[0].shape[0] - crop_share)
    return call(
        functools.partial(feature_kernel, len(pieces) == 2, patches),
        [array((crop_share, width)), array((share, width))],
        [idx, mask, *pieces, crops, patch_rows],
        scalars=2,
        scratch=[pltpu.VMEM((count, width), F32), pltpu.VMEM((share, width), F32)],
    )


def local(
    sizes,
    student_crops,
    teacher_crops,
    student_patches,
    teacher_patches,
    patch_mask,
    student_protos,
    teacher_protos,
):
    nx, ny, nz = sizes
    images, masked = patch_mask.shape
    patches = student_patches.shape[0] // images
    crops = student_crops.shape[0]
    ix, iy, ic, iz = (lax.axis_index(a) for a in ("x", "y", "c", "z"))
    idx = jnp.stack([ic, iz, ix * ny + iy]).astype(jnp.int32)
    swap = [(0, 1), (1, 0)]

    teacher = prep(teacher_crops, teacher_patches, patch_mask)
    teacher_other = lax.ppermute(teacher, "c", swap)
    student = prep(student_crops, student_patches, patch_mask)
    student_other = lax.ppermute(student, "c", swap)

    expo, sums = teacher_pass(idx, teacher, teacher_other, teacher_protos, crops, nx * ny)
    for step in range(ITERS):
        colparts = lax.all_to_all(sums, ("x", "y"), 0, 0)
        if step == 0:
            student_expo, total, mix, turned = student_pass(
                idx, student, student_other, student_protos, crops
            )
        sums = row_pass(expo, colparts, total if step == 0 else None, crops, 2 * nz)
        rowparts = lax.all_to_all(sums, ("c", "z"), 0, 0)
        if step == 0:
            totals = rowparts
        if step < ITERS - 1:
            sums = column_pass(expo, rowparts, crops, nx * ny)

    prob = prob_pass(turned, student_expo, totals)
    target = target_pass(idx, expo, student_protos, colparts, crops)
    outgoing, winv = weight_pass(
        idx, turned, expo, prob, student_protos, colparts, rowparts, crops, nx * ny
    )
    parts = lax.all_to_all(outgoing, ("x", "y"), 0, 0)
    f_mine, f_theirs = combine_pass(idx, mix, target, totals, rowparts, crops)
    f_came = lax.ppermute(f_theirs, "c", swap)
    packed = pack_pass(f_mine, f_came, nz, crops)
    own = lax.psum_scatter(packed, "z", scatter_dimension=0, tiled=True)
    pieces = [own]
    if student_patches.shape[0] // nz < patches:
        pieces.append(lax.ppermute(own, "z", [(i, i ^ 1) for i in range(nz)]))
    crop_grad, patch_grad = feature_pass(
        idx, patch_mask, pieces, student_crops, student_patches, nz, patches
    )
    mine, theirs = proto_pass(idx, parts, student_protos, winv)
    came = lax.ppermute(theirs, "c", swap)
    proto_grad = jnp.where(
        ic == 0,
        jnp.concatenate([mine, came], axis=1),
        jnp.concatenate([came, mine], axis=1),
    )
    return (proto_grad, crop_grad, patch_grad)


def solution(mesh):
    dp, nz = mesh.devices.shape
    nx = 4 if dp == 32 else 2
    ny = dp // (2 * nx)
    grid = Mesh(mesh.devices.reshape(nx, ny, 2, nz), ("x", "y", "c", "z"))
    rows = ("x", "y", "c")
    in_specs = (
        P(rows, None),
        P(rows, None),
        P(rows, None),
        P(rows, None),
        P(rows, None),
        P(None, "z"),
        P(None, "z"),
    )
    out_specs = (P(rows, "z"), P(rows + ("z",), None), P(rows + ("z",), None))
    return jax.shard_map(
        functools.partial(local, (nx, ny, nz)),
        mesh=grid,
        in_specs=in_specs,
        out_specs=out_specs,
        check_vma=False,
    )
```

time: 755 us -> 243 us (0.32)
  the two profiles are of different devices: /device:TPU:32 before, /device:TPU:28 now
where the time goes in v2:
time: 243 us; the launch traced here: 242 us
  blocking collectives  57 us (23%)
  waiting for transfers between devices  56.6 us (23%)
  Pallas kernels  49.5 us (20%)
  local copies, waits for them, and re-layouts  42.5 us (17%)
  starting transfers between devices  21.8 us (9%)
  between operations  14.3 us (6%)
    all_to_all x1, waiting for transfers between devices, local(): parts = lax.all_to_all(outgoing, ('x', 'y'), 0, 0)  51.7 us
    pallas_call x16, Pallas kernels, call(): pl.pallas_call(kernel, out_shape=out_shape, in_specs=[SMEM] * scalars + [...  49.5 us
    unnamed x48, local copies, waits for them, and re-layouts  42.5 us
    all_to_all x2, blocking collectives, local(): rowparts = lax.all_to_all(sums, ('c', 'z'), 0, 0)  28.5 us
    all_to_all x2, blocking collectives, local(): colparts = lax.all_to_all(sums, ('x', 'y'), 0, 0)  28.5 us
    all_to_all x1, starting transfers between devices, local(): parts = lax.all_to_all(outgoing, ('x', 'y'), 0, 0)  8.5 us
    all_to_all x1, starting transfers between devices, local(): colparts = lax.all_to_all(sums, ('x', 'y'), 0, 0)  7.11 us
  transfers between devices with their start and end apart: 9, of which 4 were waited for; matrix products, arithmetic and copies ran while one was open for 0% of the time, Pallas kernels for 13%

profile of v2, /device:TPU:28, one launch (start us, length us, event | category | flops | bytes accessed | tf_op | source)
XLA Modules:
  0.0 242.4 jit_solution(2428325184195638795)
XLA Ops:
  13.1 2.2 copy-done.23
  15.3 6.9 %shard_map.97 = (bf16[1024,4096]{1,0:T(8,128)(2,1)S(1)}, f32[16,64,128]{2,1,0:T(8,128)}) custom-call(s32[3]{0:T(128)S(1)} %pad_add_fusion.idx, f32[512,256]{1,0:T(8,128)S(1)} %shard_map.96.own, f32[512,256]{1,0:T(8,128)S(1)} %collective-permute-done.1.other, bf16[256,8192]{1,0:T(8,128)(2,1)S(1)} %copy-done.23), custom_call_target="tpu_custom_call" | custom-call | flops 2147483648 | bytes 8388608 | tf_op jit(solution)/shard_map/pallas_call | solution.py:27
  22.2 3.3 %copy-done = bf16[1024,4096]{1,0:T(8,128)(2,1)} copy-done((bf16[1024,4096]{1,0:T(8,128)(2,1)}, bf16[1024,4096]{1,0:T(8,128)(2,1)S(1)}, u32[]{:S(2)}) %copy-start) | copy-done | bytes 8388632
  25.5 7.1 %all-to-all-start = ((f32[16,64,128]{2,1,0:T(8,128)}), f32[16,64,128]{2,1,0:T(8,128)S(1)}, u32[]{:S(2)}, u32[]{:S(2)}) async-start(f32[16,64,128]{2,1,0:T(8,128)} %get-tuple-element.20), calls=%async_computation | async-start | bytes 1048576 | tf_op jit(solution)/shard_map/all_to_all | solution.py:550
  32.6 2.2 copy-done.5
  34.8 8.9 %shard_map.95 = (bf16[1024,4096]{1,0:T(8,128)(2,1)S(1)}, f32[8,128]{1,0:T(8,128)S(1)}, f32[1024,256]{1,0:T(8,128)S(1)}, bf16[256,1024]{1,0:T(8,128)(2,1)S(1)}) custom-call(s32[3]{0:T(128)S(1)} %pad_add_fusion.idx, f32[512,256]{1,0:T(8,128)S(1)} %shard_map.94.own, f32[512,256]{1,0:T(8,128)S(1)} %collective-permute-done.other, bf16[256,8192]{1,0:T(8,128)(2,1)S(1)} %copy-done.5), custom_call_target="tpu_custom_call" | custom-call | flops 4294967296 | bytes 8388608 | tf_op jit(solution)/shard_map/pallas_call | solution.py:27
  43.7 3.2 %copy-done.11 = bf16[1024,4096]{1,0:T(8,128)(2,1)} copy-done((bf16[1024,4096]{1,0:T(8,128)(2,1)}, bf16[1024,4096]{1,0:T(8,128)(2,1)S(1)}, u32[]{:S(2)}) %copy-start.11) | copy-done | bytes 8388632
  47.0 3.4 %copy-done.1 = bf16[1024,4096]{1,0:T(8,128)(2,1)S(1)} copy-done((bf16[1024,4096]{1,0:T(8,128)(2,1)S(1)}, bf16[1024,4096]{1,0:T(8,128)(2,1)}, u32[]{:S(2)}) %copy-start.1) | copy-done | bytes 8388632
  50.3 3.3 %shard_map.98 = f32[16,16,128]{2,1,0:T(8,128)S(1)} custom-call(bf16[1024,4096]{1,0:T(8,128)(2,1)S(1)} %copy-done.1, f32[16,64,128]{2,1,0:T(8,128)S(1)} %all-to-all-done.colparts, f32[8,128]{1,0:T(8,128)S(1)} %get-tuple-element.21.refs_0_), custom_call_target="tpu_custom_call" | custom-call | flops 8388608 | bytes 8388608 | tf_op jit(solution)/shard_map/pallas_call | solution.py:27
  53.6 16.8 %all_to_all.35.totals.rowparts = f32[16,16,128]{2,1,0:T(8,128)S(1)} all-to-all(f32[16,16,128]{2,1,0:T(8,128)S(1)} %shard_map.98), channel_id=1, replica_groups=mesh['x'=4,'y'=4,'c'=2,'z'=8] {'c','z'}, dimensions={0} | all-to-all | bytes 262144 | tf_op jit(solution)/shard_map/all_to_all | solution.py:556
  71.8 13.9 %all_to_all.36.colparts = f32[16,64,128]{2,1,0:T(8,128)S(1)} all-to-all(f32[16,64,128]{2,1,0:T(8,128)S(1)} %shard_map.100), channel_id=1, replica_groups=mesh['x'=4,'y'=4,'c'=2,'z'=8] {'x','y'}, dimensions={0} | all-to-all | bytes 1048576 | tf_op jit(solution)/shard_map/all_to_all | solution.py:550
  85.8 3.3 %shard_map.101 = f32[16,8,128]{2,1,0:T(8,128)S(1)} custom-call(bf16[1024,4096]{1,0:T(8,128)(2,1)S(1)} %copy-done.2, f32[16,64,128]{2,1,0:T(8,128)S(1)} %all_to_all.36.colparts), custom_call_target="tpu_custom_call" | custom-call | flops 8388608 | bytes 8388608 | tf_op jit(solution)/shard_map/pallas_call | solution.py:27
  89.0 11.7 %all_to_all.37.rowparts = f32[16,8,128]{2,1,0:T(8,128)S(1)} all-to-all(f32[16,8,128]{2,1,0:T(8,128)S(1)} %shard_map.101), channel_id=1, replica_groups=mesh['x'=4,'y'=4,'c'=2,'z'=8] {'c','z'}, dimensions={0} | all-to-all | bytes 131072 | tf_op jit(solution)/shard_map/all_to_all | solution.py:556
  102.1 14.5 %all_to_all.38.colparts = f32[16,64,128]{2,1,0:T(8,128)S(1)} all-to-all(f32[16,64,128]{2,1,0:T(8,128)S(1)} %shard_map.102), channel_id=1, replica_groups=mesh['x'=4,'y'=4,'c'=2,'z'=8] {'x','y'}, dimensions={0} | all-to-all | bytes 1048576 | tf_op jit(solution)/shard_map/all_to_all | solution.py:550
  116.6 3.9 %shard_map.103 = f32[16,8,128]{2,1,0:T(8,128)} custom-call(bf16[1024,4096]{1,0:T(8,128)(2,1)S(1)} %copy-done.2, f32[16,64,128]{2,1,0:T(8,128)S(1)} %all_to_all.38.colparts), custom_call_target="tpu_custom_call" | custom-call | flops 8388608 | bytes 8388608 | tf_op jit(solution)/shard_map/pallas_call | solution.py:27
  120.5 3.5 %all-to-all-start.5 = ((f32[16,8,128]{2,1,0:T(8,128)}), f32[16,8,128]{2,1,0:T(8,128)S(1)}, u32[]{:S(2)}, u32[]{:S(2)}) async-start(f32[16,8,128]{2,1,0:T(8,128)} %shard_map.103), calls=%async_computation.5 | async-start | bytes 131072 | tf_op jit(solution)/shard_map/all_to_all | solution.py:556
  124.0 3.4 %copy-done.12 = bf16[1024,4096]{1,0:T(8,128)(2,1)S(1)} copy-done((bf16[1024,4096]{1,0:T(8,128)(2,1)S(1)}, bf16[1024,4096]{1,0:T(8,128)(2,1)}, u32[]{:S(2)}) %copy-start.12) | copy-done | bytes 8388632
  127.4 2.3 shard_map.99.prob
  129.8 2.0 copy-done.9
  131.9 3.4 %copy-done.3 = bf16[1024,4096]{1,0:T(8,128)(2,1)S(1)} copy-done((bf16[1024,4096]{1,0:T(8,128)(2,1)S(1)}, bf16[1024,4096]{1,0:T(8,128)(2,1)}, u32[]{:S(2)}) %copy-start.3) | copy-done | bytes 8388632
  135.3 2.2 copy-done.6
  137.5 2.2 copy-done.10
  139.7 5.3 %shard_map.104 = (f32[16,544,128]{2,1,0:T(8,128)S(1)}, f32[1,4096]{1,0:T(1,128)S(1)}) custom-call(s32[3]{0:T(128)S(1)} %pad_add_fusion.idx, bf16[256,1024]{1,0:T(8,128)(2,1)S(1)} %get-tuple-element.17.turned, bf16[1024,4096]{1,0:T(8,128)(2,1)S(1)} %copy-done.3, f32[256,4096]{1,0:T(8,128)S(1)} %copy-done.10, bf16[256,8192]{1,0:T(8,128)(2,1)S(1)} %copy-done.6, ...), custom_call_target="tpu_custom_call" | custom-call | flops 2147483648 | bytes 8388608 | tf_op jit(solution)/shard_map/pallas_call | solution.py:27
  146.9 8.5 %all-to-all-start.6 = ((f32[16,544,128]{2,1,0:T(8,128)}), f32[16,544,128]{2,1,0:T(8,128)}, u32[]{:S(2)}, u32[]{:S(2)}) async-start(f32[16,544,128]{2,1,0:T(8,128)} %copy-done.13), calls=%async_computation.6 | async-start | bytes 8912896 | tf_op jit(solution)/shard_map/all_to_all | solution.py:567
  155.5 3.4 %copy-done.4 = bf16[1024,4096]{1,0:T(8,128)(2,1)S(1)} copy-done((bf16[1024,4096]{1,0:T(8,128)(2,1)S(1)}, bf16[1024,4096]{1,0:T(8,128)(2,1)}, u32[]{:S(2)}) %copy-start.4) | copy-done | bytes 8388632
  158.9 2.2 copy-done.7
  161.0 5.1 %shard_map.106.target = f32[1024,256]{1,0:T(8,128)S(1)} custom-call(s32[3]{0:T(128)S(1)} %pad_add_fusion.idx, bf16[1024,4096]{1,0:T(8,128)(2,1)S(1)} %copy-done.4, bf16[256,8192]{1,0:T(8,128)(2,1)S(1)} %copy-done.7, f32[16,64,128]{2,1,0:T(8,128)S(1)} %all_to_all.38.colparts), custom_call_target="tpu_custom_call" | custom-call | flops 2147483648 | bytes 8388608 | tf_op jit(solution)/shard_map/pallas_call | solution.py:27
  170.0 51.7 %all-to-all-done.6.parts = f32[16,544,128]{2,1,0:T(8,128)} async-done(((f32[16,544,128]{2,1,0:T(8,128)}), f32[16,544,128]{2,1,0:T(8,128)}, u32[]{:S(2)}, u32[]{:S(2)}) %all-to-all-start.6) | async-done | bytes 4456480 | tf_op jit(solution)/shard_map/all_to_all | solution.py:567
  221.6 2.2 copy-done.8
  223.8 2.6 %shard_map.105 = (f32[8,4096]{1,0:T(8,128)S(1)}, f32[8,4096]{1,0:T(8,128)S(1)}) custom-call(s32[3]{0:T(128)S(1)} %pad_add_fusion.idx, f32[16,544,128]{2,1,0:T(8,128)} %all-to-all-done.6.parts, bf16[256,8192]{1,0:T(8,128)(2,1)S(1)} %copy-done.8, f32[1,4096]{1,0:T(1,128)S(1)} %get-tuple-element.23.winv), custom_call_target="tpu_custom_call" | custom-call | tf_op jit(solution)/shard_map/pallas_call | solution.py:27
  228.4 2.9 %collective-permute-done.4.refs_1_ = f32[64,256]{1,0:T(8,128)S(1)} collective-permute-done((f32[64,256]{1,0:T(8,128)}, f32[64,256]{1,0:T(8,128)S(1)}, u32[]{:S(2)}, u32[]{:S(2)}) %collective-permute-start.4) | collective-permute-done | bytes 65568 | tf_op jit(solution)/shard_map/ppermute | solution.py:574
  232.1 2.7 %shard_map.109 = (f32[16,256]{1,0:T(8,128)}, f32[128,256]{1,0:T(8,128)}) custom-call(s32[3]{0:T(128)S(1)} %pad_add_fusion.idx, s32[4,96]{1,0:T(4,128)S(1)} %copy-done.22, f32[64,256]{1,0:T(8,128)S(1)} %copy-done.20, f32[64,256]{1,0:T(8,128)S(1)} %collective-permute-done.4.refs_1_, bf16[128,256]{1,0:T(8,128)(2,1)S(1)} %copy-done.18, ...), custom_call_target="tpu_custom_call" | custom-call | tf_op jit(solution)/shard_map/pallas_call | solution.py:27
  (57 shorter events, 18.1 us)
Async XLA Ops:
  7.2 1.0 copy-start.16
  8.2 0.8 copy-start.19
  10.1 3.0 %collective-permute-start.1 = (f32[512,256]{1,0:T(8,128)S(1)}, f32[512,256]{1,0:T(8,128)S(1)}, u32[]{:S(2)}, u32[]{:S(2)}) collective-permute-start(f32[512,256]{1,0:T(8,128)S(1)} %shard_map.96.own), channel_id=1, source_target_pairs={{0,8},{8,0},{1,9},{9,1},{2,10},{10,2},{3,11},{11,3},{4,12},{12,4},... | collective-permute-start | bytes 1572872 | tf_op jit(solution)/shard_map/ppermute | solution.py:544
  10.2 1.0 copy-start.14
  11.2 0.8 copy-start.17
  12.4 20.2 %collective-permute-start = (f32[512,256]{1,0:T(8,128)S(1)}, f32[512,256]{1,0:T(8,128)S(1)}, u32[]{:S(2)}, u32[]{:S(2)}) collective-permute-start(f32[512,256]{1,0:T(8,128)S(1)} %shard_map.94.own), channel_id=1, source_target_pairs={{0,8},{8,0},{1,9},{9,1},{2,10},{10,2},{3,11},{11,3},{4,12},{12,4},... | collective-permute-start | bytes 1572872 | tf_op jit(solution)/shard_map/ppermute | solution.py:546
  13.1 2.2 copy-start.23
  22.2 3.3 %copy-start = (bf16[1024,4096]{1,0:T(8,128)(2,1)}, bf16[1024,4096]{1,0:T(8,128)(2,1)S(1)}, u32[]{:S(2)}) copy-start(bf16[1024,4096]{1,0:T(8,128)(2,1)S(1)} %get-tuple-element.18.expo) | copy-start | bytes 25165828
  25.5 21.5 %all-to-all-start = ((f32[16,64,128]{2,1,0:T(8,128)}), f32[16,64,128]{2,1,0:T(8,128)S(1)}, u32[]{:S(2)}, u32[]{:S(2)}) async-start(f32[16,64,128]{2,1,0:T(8,128)} %get-tuple-element.20), calls=%async_computation | async-start | bytes 1048576 | tf_op jit(solution)/shard_map/all_to_all | solution.py:550
  32.6 2.2 copy-start.5
  43.7 3.3 %copy-start.11 = (bf16[1024,4096]{1,0:T(8,128)(2,1)}, bf16[1024,4096]{1,0:T(8,128)(2,1)S(1)}, u32[]{:S(2)}) copy-start(bf16[1024,4096]{1,0:T(8,128)(2,1)S(1)} %get-tuple-element.19.student_expo) | copy-start | bytes 25165828
  47.0 3.4 %copy-start.1 = (bf16[1024,4096]{1,0:T(8,128)(2,1)S(1)}, bf16[1024,4096]{1,0:T(8,128)(2,1)}, u32[]{:S(2)}) copy-start(bf16[1024,4096]{1,0:T(8,128)(2,1)} %copy-done) | copy-start | bytes 25165828
  50.3 20.1 %copy-start.2 = (bf16[1024,4096]{1,0:T(8,128)(2,1)S(1)}, bf16[1024,4096]{1,0:T(8,128)(2,1)}, u32[]{:S(2)}) copy-start(bf16[1024,4096]{1,0:T(8,128)(2,1)} %copy-done) | copy-start | bytes 25165828
  120.5 11.4 %all-to-all-start.5 = ((f32[16,8,128]{2,1,0:T(8,128)}), f32[16,8,128]{2,1,0:T(8,128)S(1)}, u32[]{:S(2)}, u32[]{:S(2)}) async-start(f32[16,8,128]{2,1,0:T(8,128)} %shard_map.103), calls=%async_computation.5 | async-start | bytes 131072 | tf_op jit(solution)/shard_map/all_to_all | solution.py:556
  124.0 3.4 %copy-start.12 = (bf16[1024,4096]{1,0:T(8,128)(2,1)S(1)}, bf16[1024,4096]{1,0:T(8,128)(2,1)}, u32[]{:S(2)}) copy-start(bf16[1024,4096]{1,0:T(8,128)(2,1)} %copy-done.11) | copy-start | bytes 25165828
  129.7 2.0 copy-start.9
  131.9 3.4 %copy-start.3 = (bf16[1024,4096]{1,0:T(8,128)(2,1)S(1)}, bf16[1024,4096]{1,0:T(8,128)(2,1)}, u32[]{:S(2)}) copy-start(bf16[1024,4096]{1,0:T(8,128)(2,1)} %copy-done) | copy-start | bytes 25165828
  135.3 2.2 copy-start.6
  137.5 2.2 copy-start.10
  144.9 2.0 copy-start.13
  146.9 74.7 %all-to-all-start.6 = ((f32[16,544,128]{2,1,0:T(8,128)}), f32[16,544,128]{2,1,0:T(8,128)}, u32[]{:S(2)}, u32[]{:S(2)}) async-start(f32[16,544,128]{2,1,0:T(8,128)} %copy-done.13), calls=%async_computation.6 | async-start | bytes 8912896 | tf_op jit(solution)/shard_map/all_to_all | solution.py:567
  155.4 71.1 %reduce-scatter.2.cloned.1.call-start = ((), (), s32[]{:S(2)}) async-start(), calls=%async_computation.8 | async-start | bytes 589824 | tf_op jit(solution)/shard_map/reduce_scatter | solution.py:571
  155.5 3.4 %copy-start.4 = (bf16[1024,4096]{1,0:T(8,128)(2,1)S(1)}, bf16[1024,4096]{1,0:T(8,128)(2,1)}, u32[]{:S(2)}) copy-start(bf16[1024,4096]{1,0:T(8,128)(2,1)} %copy-done) | copy-start | bytes 25165828
  158.9 2.2 copy-start.7
  167.1 2.0 collective-permute-start.3
  169.9 61.3 %copy-start.15 = (bf16[1024,256]{1,0:T(8,128)(2,1)S(1)}, bf16[1024,256]{1,0:T(8,128)(2,1)}, u32[]{:S(2)}) copy-start(bf16[1024,256]{1,0:T(8,128)(2,1)} %refs_3_.1) | copy-start | bytes 1572868
  221.6 2.2 copy-start.8
  223.8 7.5 %copy-start.18 = (bf16[128,256]{1,0:T(8,128)(2,1)S(1)}, bf16[128,256]{1,0:T(8,128)(2,1)}, u32[]{:S(2)}) copy-start(bf16[128,256]{1,0:T(8,128)(2,1)} %refs_2_.1) | copy-start | bytes 196612
  223.8 7.5 %copy-start.22 = (s32[4,96]{1,0:T(4,128)S(1)}, s32[4,96]{1,0:T(4,128)}, u32[]{:S(2)}) copy-start(s32[4,96]{1,0:T(4,128)} %mask.5) | copy-start | bytes 4612
  226.5 8.4 %collective-permute-start.2 = (f32[8,4096]{1,0:T(8,128)S(1)}, f32[8,4096]{1,0:T(8,128)S(1)}, u32[]{:S(2)}, u32[]{:S(2)}) collective-permute-start(f32[8,4096]{1,0:T(8,128)S(1)} %get-tuple-element.25), channel_id=1, source_target_pairs={{0,8},{8,0},{1,9},{9,1},{2,10},{10,2},{3,11},{11,3},{4,12},{12,4},... | collective-permute-start | bytes 393224 | tf_op jit(solution)/shard_map/ppermute | solution.py:579
  226.6 4.7 %collective-permute-start.4 = (f32[64,256]{1,0:T(8,128)}, f32[64,256]{1,0:T(8,128)S(1)}, u32[]{:S(2)}, u32[]{:S(2)}) collective-permute-start(f32[64,256]{1,0:T(8,128)} %reduce-scatter.2.cloned.1.call-done.refs_0_), channel_id=1, source_target_pairs={{0,1},{1,0},{2,3},{3,2},{4,5},{5,4},{6,7},{7,6},{8,9},{9,8},{10,11... | collective-permute-start | bytes 196616 | tf_op jit(solution)/shard_map/ppermute | solution.py:574
  231.3 0.8 copy-start.20
  (1 other events, 0.7 us)
Sparse Core Ops, SparseCore 0:
  170.1 38.4 reduce-scatter.1

commit v3 on v2

v3 whole, which is shorter than its diff:
```python
import functools

import jax
import jax.numpy as jnp
from jax import lax
from jax.experimental import pallas as pl
from jax.experimental.pallas import tpu as pltpu
from jax.sharding import Mesh, PartitionSpec as P

ITERS = 3
EPS = 1e-06
TEACHER_TEMP = 0.07
STUDENT_TEMP = 0.1
LOSS_SCALE = 256.0
GRAD_SCALE = LOSS_SCALE / STUDENT_TEMP
LOG2E = 1.4426950408889634

BN = 512
F32 = jnp.float32
BF16 = jnp.bfloat16
VMEM_LIMIT = 16 * 1024 * 1024
SMEM = pl.BlockSpec(memory_space=pltpu.SMEM)
VMEM = pl.BlockSpec(memory_space=pltpu.VMEM)
HBM = pl.BlockSpec(memory_space=pltpu.HBM)


def call(kernel, out_shape, args, specs="", scratch=(), flops=0, traffic=0):
    spaces = {"s": SMEM, "v": VMEM, "h": HBM}
    return pl.pallas_call(
        kernel,
        out_shape=out_shape,
        in_specs=[spaces[letter] for letter in specs],
        scratch_shapes=list(scratch),
        compiler_params=pltpu.CompilerParams(vmem_limit_bytes=VMEM_LIMIT),
        cost_estimate=pl.CostEstimate(flops=flops, bytes_accessed=traffic, transcendentals=0),
    )(*args)


def array(shape, dtype=F32):
    return jax.ShapeDtypeStruct(shape, dtype)


def stream(source, buf, sem, steps, body):
    def copy(j, slot):
        return pltpu.make_async_copy(source(j), buf.at[slot], sem.at[slot])

    copy(0, 0).start()

    def step(j, _):
        slot = lax.rem(j, 2)

        @pl.when(j + 1 < steps)
        def _():
            copy(j + 1, 1 - slot).start()

        copy(j, slot).wait()
        body(j, buf.at[slot])
        return 0

    lax.fori_loop(0, steps, step, 0)


def unit(x):
    xf = x.astype(F32)
    return xf * lax.rsqrt(jnp.sum(xf * xf, axis=-1, keepdims=True) + EPS)


def unit_cols(w):
    wf = w.astype(F32)
    inv = lax.rsqrt(jnp.sum(wf * wf, axis=0, keepdims=True) + EPS)
    return wf * inv, inv


def prep_kernel(tcrops, tpatch, scrops, spatch, mask, out, tc, tp, sc, sp, sem):
    images, masked = mask.shape
    patches = tp.shape[0] // images
    count = tc.shape[0]
    half = out.shape[0] // 2
    copies = [
        pltpu.make_async_copy(src, dst, sem.at[i])
        for i, (src, dst) in enumerate(((tcrops, tc), (tpatch, tp), (scrops, sc), (spatch, sp)))
    ]
    for copy in copies:
        copy.start()
    for side, (crops, patch_rows) in enumerate(((tc, tp), (sc, sp))):
        copies[2 * side].wait()
        copies[2 * side + 1].wait()
        base = side * half
        out[base : base + count, :] = unit(crops[...])
        for i in range(images):
            place = lax.broadcasted_iota(jnp.int32, (patches, masked), 0)
            chosen = (place == mask[i : i + 1, :]).astype(F32).astype(BF16)
            rows = lax.dot_general(
                chosen,
                patch_rows[i * patches : (i + 1) * patches, :],
                (((0,), (0,)), ((), ())),
                preferred_element_type=F32,
            )
            at = base + count + i * masked
            out[at : at + masked, :] = unit(rows)


def prep(tcrops, tpatch, scrops, spatch, mask):
    half = tcrops.shape[0] + mask.size
    return call(
        prep_kernel,
        array((2 * half, tcrops.shape[1])),
        [tcrops, tpatch, scrops, spatch, mask],
        "hhhhv",
        scratch=[pltpu.VMEM(a.shape, BF16) for a in (tcrops, tpatch, scrops, spatch)]
        + [pltpu.SemaphoreType.DMA((4,))],
    )


def place_rows(core, crops, base, half, own, other, dest):
    rest = half - crops
    for side, ref in ((core, own), (1 - core, other)):
        at = pl.multiple_of(side * crops, crops)
        dest[pl.ds(at, crops), :] = ref[base : base + crops, :].astype(dest.dtype)
        at = pl.multiple_of(2 * crops + side * rest, 128)
        dest[pl.ds(at, rest), :] = ref[base + crops : base + half, :].astype(dest.dtype)


def row_blocks(start, stop):
    return [(a, min(a + 256, stop)) for a in range(start, stop, 256)]


def proto_source(core, protos):
    columns = protos.shape[1] // 2
    return lambda j: protos.at[:, pl.ds(pl.multiple_of(core * columns + j * BN, BN), BN)]


def proto_scratch(width):
    return [pltpu.VMEM((2, width, BN), BF16), pltpu.SemaphoreType.DMA((2,))]


def put_columns(step, heads, out):
    copies = out.shape[0]
    per_head = out.shape[1] // 2
    for head in range(2):
        for t in range(BN // 128):
            piece = heads[head][:, 128 * t : 128 * (t + 1)]
            out[:, pl.ds(head * per_head + step * (BN // 128) + t, 1), :] = jnp.broadcast_to(
                piece[None], (copies, 1, 128)
            )


def get_columns(step, head, lines):
    base = head * (lines.shape[0] // 2) + step * (BN // 128)
    return jnp.concatenate([lines[pl.ds(base + t, 1), :] for t in range(BN // 128)], axis=1)


def line_up(values):
    return jnp.concatenate([values[t : t + 1, :] for t in range(values.shape[0])], axis=1)


def teacher_kernel(crops, idx, own, other, protos, expo, sums, feats, buf, sem):
    rows, columns = expo.shape
    place_rows(idx[0], crops, 0, rows // 2, own, other, feats)

    def step(j, block):
        w = unit_cols(block[...])[0].astype(BF16)
        at = pl.multiple_of(j * BN, BN)
        heads = []
        for first, last in ((0, 2 * crops), (2 * crops, rows)):
            part = jnp.zeros((1, BN), F32)
            for start, stop in row_blocks(first, last):
                score = jnp.dot(feats[start:stop, :], w, preferred_element_type=F32)
                e = jnp.exp2(score * (LOG2E / TEACHER_TEMP)).astype(BF16)
                expo[start:stop, pl.ds(at, BN)] = e
                part = part + jnp.sum(e.astype(F32), axis=0, keepdims=True)
            heads.append(part)
        put_columns(j, heads, sums)

    stream(proto_source(idx[0], protos), buf, sem, columns // BN, step)


def teacher_pass(idx, own, other, protos, crops, copies):
    rows, width = own.shape
    columns = protos.shape[1] // 2
    return call(
        functools.partial(teacher_kernel, crops),
        [array((rows, columns), BF16), array((copies, 2 * columns // 128, 128))],
        [idx, own, other, protos],
        "svvh",
        scratch=[pltpu.VMEM((rows, width), BF16)] + proto_scratch(width),
        flops=2 * rows * width * columns,
        traffic=2 * rows * columns,
    )


def student_kernel(crops, idx, own, other, protos, total, mix, feats, acc, buf, sem):
    rows = feats.shape[0]
    place_rows(idx[0], crops, rows // 2, rows // 2, own, other, feats)
    acc[...] = jnp.zeros_like(acc)
    mix[...] = jnp.zeros_like(mix)

    def step(j, block):
        w = unit_cols(block[...])[0].astype(BF16)
        for start, stop in row_blocks(0, rows):
            score = jnp.dot(feats[start:stop, :], w, preferred_element_type=F32)
            p = jnp.exp2(score * (LOG2E / STUDENT_TEMP))
            part = p[:, :128]
            for t in range(1, BN // 128):
                part = part + p[:, 128 * t : 128 * (t + 1)]
            acc[start:stop, :] += part
            mix[start:stop, :] += lax.dot_general(
                p.astype(BF16), w, (((1,), (1,)), ((), ())), preferred_element_type=F32
            )

    stream(proto_source(idx[0], protos), buf, sem, protos.shape[1] // 2 // BN, step)
    for t in range(rows // 128):
        block = jnp.transpose(acc[128 * t : 128 * (t + 1), :])
        total[t : t + 1, :] = jnp.sum(block, axis=0, keepdims=True)


def student_pass(idx, own, other, protos, crops):
    rows, width = own.shape
    columns = protos.shape[1] // 2
    return call(
        functools.partial(student_kernel, crops),
        [array((rows // 128, 128)), array((rows, width))],
        [idx, own, other, protos],
        "svvh",
        scratch=[pltpu.VMEM((rows, width), BF16), pltpu.VMEM((rows, 128), F32)]
        + proto_scratch(width),
        flops=4 * rows * width * columns,
        traffic=2 * width * columns,
    )


def sum_rows(crops, expo, colscale, out):
    copies = out.shape[0]
    rows, columns = expo.shape
    per_head = columns // 128

    def block(i, _):
        head = jnp.where(i < 2 * crops // 128, 0, 1)
        at = pl.multiple_of(i * 128, 128)

        def chunk(k, acc):
            e = expo[pl.ds(at, 128), pl.ds(pl.multiple_of(k * 128, 128), 128)].astype(F32)
            return acc + e * colscale[pl.ds(head * per_head + k, 1), :]

        acc = lax.fori_loop(0, per_head, chunk, jnp.zeros((128, 128), F32), unroll=8)
        sums = jnp.sum(jnp.transpose(acc), axis=0, keepdims=True)
        out[:, pl.ds(i, 1), :] = jnp.broadcast_to(sums[None], (copies, 1, 128))
        return 0

    lax.fori_loop(0, rows // 128, block, 0)


def row_kernel(crops, extra, expo, colparts, *refs):
    if extra:
        total, out, colscale = refs
        count = total.shape[0]
        out[:, count:, :] = jnp.broadcast_to(total[...][None], (out.shape[0], count, 128))
    else:
        out, colscale = refs
    colscale[...] = 1.0 / jnp.sum(colparts[...], axis=0)
    sum_rows(crops, expo, colscale, out)


def row_pass(expo, colparts, total, crops, copies):
    rows, columns = expo.shape
    extra = total is not None
    return call(
        functools.partial(row_kernel, crops, extra),
        array((copies, rows // 128 * (2 if extra else 1), 128)),
        [expo, colparts] + ([total] if extra else []),
        "vvv" if extra else "vv",
        scratch=[pltpu.VMEM((2 * columns // 128, 128), F32)],
        flops=2 * rows * columns,
        traffic=2 * rows * columns,
    )


def last_row_kernel(crops, idx, expo, colparts, protos, out, target, colscale, buf, sem):
    rows, columns = expo.shape
    colscale[...] = 1.0 / jnp.sum(colparts[...], axis=0)
    target[...] = jnp.zeros_like(target)

    def step(j, block):
        wnorm = unit_cols(block[...])[0]
        at = pl.multiple_of(j * BN, BN)
        for head, (first, last) in enumerate(((0, 2 * crops), (2 * crops, rows))):
            w = (wnorm * get_columns(j, head, colscale)).astype(BF16)
            target[first:last, :] += lax.dot_general(
                expo[first:last, pl.ds(at, BN)],
                w,
                (((1,), (1,)), ((), ())),
                preferred_element_type=F32,
            )

    stream(proto_source(idx[0], protos), buf, sem, columns // BN, step)
    sum_rows(crops, expo, colscale, out)


def last_row_pass(idx, expo, colparts, protos, crops, copies):
    rows, columns = expo.shape
    width = protos.shape[0]
    return call(
        functools.partial(last_row_kernel, crops),
        [array((copies, rows // 128, 128)), array((rows, width))],
        [idx, expo, colparts, protos],
        "svvh",
        scratch=[pltpu.VMEM((2 * columns // 128, 128), F32)] + proto_scratch(width),
        flops=2 * rows * columns * width,
        traffic=2 * rows * columns,
    )


def split3(v):
    high = v.astype(BF16)
    rest = v - high.astype(F32)
    middle = rest.astype(BF16)
    low = (rest - middle.astype(F32)).astype(BF16)
    pad = jnp.zeros((13, v.shape[1]), F32)
    parts = [high.astype(F32), middle.astype(F32), low.astype(F32), pad]
    return jnp.concatenate(parts, axis=0).astype(BF16)


def column_kernel(crops, expo, rowparts, out):
    rows, columns = expo.shape
    scale = line_up(1.0 / jnp.sum(rowparts[:, : rows // 128, :], axis=0))
    spans = [(0, 2 * crops), (2 * crops, rows)]
    lefts = [split3(scale[:, first:last]) for first, last in spans]
    for j in range(columns // BN):
        heads = []
        for left, (first, last) in zip(lefts, spans):
            sums = jnp.dot(
                left, expo[first:last, j * BN : (j + 1) * BN], preferred_element_type=F32
            )
            heads.append(sums[0:1, :] + sums[1:2, :] + sums[2:3, :])
        put_columns(j, heads, out)


def column_pass(expo, rowparts, crops, copies):
    rows, columns = expo.shape
    return call(
        functools.partial(column_kernel, crops),
        array((copies, 2 * columns // 128, 128)),
        [expo, rowparts],
        "vv",
        flops=2 * rows * columns,
        traffic=2 * rows * columns,
    )


def part_source(idx, ny, protos):
    columns = protos.shape[1] // 2
    part = columns // ny
    at = pl.multiple_of(idx[0] * columns + idx[3] * part, 128)
    return protos.at[:, pl.ds(at, part)]


def stream_rows(ny, base, half, own, other, buf, sem, body):
    def copy(step, slot):
        ref = own if step < ny else other
        return pltpu.make_async_copy(
            ref.at[step % ny, pl.ds(base, half), :], buf.at[slot], sem.at[slot]
        )

    copy(0, 0).start()
    for step in range(2 * ny):
        if step + 1 < 2 * ny:
            copy(step + 1, (step + 1) % 2).start()
        copy(step, step % 2).wait()
        body(step // ny, step % ny, buf.at[step % 2])


def wide_teacher_kernel(ny, crops, idx, own, other, protos, expo_d, expo_i, w, wbuf, buf, sem, wsem):
    half = buf.shape[1]
    rest = half - crops
    fetch = pltpu.make_async_copy(part_source(idx, ny, protos), wbuf, wsem)
    fetch.start()
    fetch.wait()
    w[...] = unit_cols(wbuf[...])[0].astype(BF16)

    def body(side, y, ref):
        place = 2 * y + jnp.where(idx[0] == side, 0, 1)
        feats = ref[...].astype(BF16)
        for start in range(0, half, 128):
            score = jnp.dot(feats[start : start + 128, :], w[...], preferred_element_type=F32)
            e = jnp.exp2(score * (LOG2E / TEACHER_TEMP)).astype(BF16)
            if start < crops:
                expo_d[pl.ds(pl.multiple_of(place * crops + start, 128), 128), :] = e
            else:
                at = pl.multiple_of(place * rest + start - crops, 128)
                expo_i[pl.ds(at, 128), :] = e

    stream_rows(ny, 0, half, own, other, buf, sem, body)


def wide_teacher_pass(idx, own, other, protos, crops):
    ny, rows, width = own.shape
    half = rows // 2
    part = protos.shape[1] // 2 // ny
    return call(
        functools.partial(wide_teacher_kernel, ny, crops),
        [array((2 * ny * crops, part), BF16), array((2 * ny * (half - crops), part), BF16)],
        [idx, own, other, protos],
        "shhh",
        scratch=[
            pltpu.VMEM((width, part), BF16),
            pltpu.VMEM((width, part), BF16),
            pltpu.VMEM((2, half, width), F32),
            pltpu.SemaphoreType.DMA((2,)),
            pltpu.SemaphoreType.DMA,
        ],
        flops=2 * 2 * ny * half * width * part,
        traffic=8 * ny * half * width,
    )


def wide_student_kernel(ny, crops, idx, own, other, protos, *refs):
    totals = refs[:ny]
    out, wnorm_out, turned_d, turned_i, w, wbuf, scale, left, expo, buf, sem, wsem = refs[ny:]
    half = buf.shape[1]
    rest = half - crops
    sub = totals[0].shape[0]
    fetch = pltpu.make_async_copy(part_source(idx, ny, protos), wbuf, wsem)
    fetch.start()
    for s in range(ny):
        y = lax.rem(idx[3] + ny - s, ny)
        scale[pl.ds(pl.multiple_of(y * sub, sub), sub), :] = GRAD_SCALE / totals[s][...]
    fetch.wait()
    wnorm_out[...] = unit_cols(wbuf[...])[0]
    w[...] = wnorm_out[...].astype(BF16)
    out[...] = jnp.zeros_like(out)

    def body(side, y, ref):
        core = jnp.where(idx[0] == side, 0, 1)
        place = 2 * y + core
        feats = ref[...].astype(BF16)
        turned = jnp.transpose(feats.astype(F32))
        turned_d[:, pl.ds(pl.multiple_of(place * crops, 128), crops)] = turned[:, :crops].astype(BF16)
        turned_i[:, pl.ds(pl.multiple_of(place * rest, 128), rest)] = turned[:, crops:].astype(BF16)
        lines = [scale[pl.ds(y * sub + core * (crops // 128) + t, 1), :] for t in range(crops // 128)]
        first = y * sub + 2 * crops // 128 + core * (rest // 128)
        lines += [scale[pl.ds(first + t, 1), :] for t in range(rest // 128)]
        left[...] = (turned * jnp.concatenate(lines, axis=1)).astype(BF16)
        for start in range(0, half, 128):
            score = jnp.dot(feats[start : start + 128, :], w[...], preferred_element_type=F32)
            expo[start : start + 128, :] = jnp.exp2(score * (LOG2E / STUDENT_TEMP)).astype(BF16)
        out[...] += jnp.dot(left[...], expo[...], preferred_element_type=F32)

    stream_rows(ny, half, half, own, other, buf, sem, body)


def wide_student_pass(idx, own, other, protos, totals, crops):
    ny, rows, width = own.shape
    half = rows // 2
    part = protos.shape[1] // 2 // ny
    return call(
        functools.partial(wide_student_kernel, ny, crops),
        [
            array((width, part)),
            array((width, part)),
            array((width, 2 * ny * crops), BF16),
            array((width, 2 * ny * (half - crops)), BF16),
        ],
        [idx, own, other, protos, *totals],
        "shhh" + "v" * ny,
        scratch=[
            pltpu.VMEM((width, part), BF16),
            pltpu.VMEM((width, part), BF16),
            pltpu.VMEM((ny * rows // 128, 128), F32),
            pltpu.VMEM((width, half), BF16),
            pltpu.VMEM((half, part), BF16),
            pltpu.VMEM((2, half, width), F32),
            pltpu.SemaphoreType.DMA((2,)),
            pltpu.SemaphoreType.DMA,
        ],
        flops=4 * 2 * ny * half * width * part,
        traffic=8 * ny * half * width,
    )


def weight_kernel(ny, crops, idx, prob, wnorm, turned_d, turned_i, expo_d, expo_i, colparts, rowparts, out, left_d, left_i, scales, rowscale):
    copies, _, _ = out.shape
    width, part = prob.shape
    own = width // copies
    group = rowparts.shape[0] // ny
    sub = rowparts.shape[1]
    scales[...] = GRAD_SCALE / jnp.sum(colparts[...], axis=0)
    for y in range(ny):
        rowscale[y * sub : (y + 1) * sub, :] = 1.0 / jnp.sum(
            rowparts[y * group : (y + 1) * group], axis=0
        )
    cd = crops // 128
    ci = sub // 2 - cd
    lines_d, lines_i = [], []
    for y in range(ny):
        for core in range(2):
            for t in range(cd):
                at = y * sub + core * cd + t
                lines_d.append(rowscale[at : at + 1, :])
            for t in range(ci):
                at = y * sub + 2 * cd + core * ci + t
                lines_i.append(rowscale[at : at + 1, :])
    left_d[...] = (turned_d[...].astype(F32) * jnp.concatenate(lines_d, axis=1)).astype(BF16)
    left_i[...] = (turned_i[...].astype(F32) * jnp.concatenate(lines_i, axis=1)).astype(BF16)
    per_head = scales.shape[0] // 2
    first = idx[3] * (part // 128)
    for at in range(0, part, BN):
        span = slice(at, at + BN)
        wsum = prob[:, span]
        for head, (left, expo) in enumerate(((left_d, expo_d), (left_i, expo_i))):
            target = jnp.dot(left[...], expo[:, span], preferred_element_type=F32)
            base = head * per_head + first + at // 128
            line = [scales[pl.ds(base + t, 1), :] for t in range(BN // 128)]
            wsum = wsum - target * jnp.concatenate(line, axis=1)
        coldot = jnp.sum(wnorm[:, span] * wsum, axis=0, keepdims=True)
        for t in range(BN // 128):
            lanes = slice(128 * t, 128 * (t + 1))
            row = at // 128 + t
            for d in range(copies):
                out[d, row * own : (row + 1) * own, :] = wsum[d * own : (d + 1) * own, lanes]
            tail = part // 128 * own + row
            out[:, tail : tail + 1, :] = jnp.broadcast_to(
                coldot[:, lanes][None], (copies, 1, 128)
            )


def weight_pass(idx, prob, wnorm, turned, expo, colparts, rowparts, crops, ny, copies):
    width, part = prob.shape
    lines = part // 128 * (width // copies + 1)
    rows = turned[0].shape[1] + turned[1].shape[1]
    return call(
        functools.partial(weight_kernel, ny, crops),
        array((copies, lines, 128)),
        [idx, prob, wnorm, *turned, *expo, colparts, rowparts],
        "svvvvvvvv",
        scratch=[
            pltpu.VMEM(turned[0].shape, BF16),
            pltpu.VMEM(turned[1].shape, BF16),
            pltpu.VMEM(colparts.shape[1:], F32),
            pltpu.VMEM((ny * rowparts.shape[1], 128), F32),
        ],
        flops=2 * rows * width * part,
        traffic=2 * rows * part,
    )


def norm_kernel(protos, out):
    out[...] = unit_cols(protos[...])[1]


def norm_pass(protos):
    width, columns = protos.shape
    step = columns // 8
    return pl.pallas_call(
        norm_kernel,
        grid=(8,),
        in_specs=[pl.BlockSpec((width, step), lambda j: (0, j))],
        out_specs=pl.BlockSpec((1, step), lambda j: (0, j)),
        out_shape=array((1, columns)),
        compiler_params=pltpu.CompilerParams(vmem_limit_bytes=VMEM_LIMIT),
        cost_estimate=pl.CostEstimate(
            flops=3 * width * columns, bytes_accessed=2 * width * columns, transcendentals=0
        ),
    )(protos)


def proto_kernel(nx, ny, idx, parts, protos, winv, out, rows, sem):
    own, columns = out.shape
    copies = parts.shape[0]
    part = columns // (2 * ny)
    tail = part // 128 * own
    at = pl.multiple_of(idx[2] * (2 * own), 2 * own)
    fetch = pltpu.make_async_copy(protos.at[pl.ds(at, 2 * own), :], rows, sem)
    fetch.start()
    fetch.wait()
    for y in range(ny):
        for core in range(2):
            for t in range(part // 128):
                first = core * (columns // 2) + y * part + 128 * t
                lanes = slice(first, first + 128)
                wsum = jnp.zeros((own, 128), F32)
                coldot = jnp.zeros((1, 128), F32)
                for x in range(nx):
                    source = (x * ny + y) * 2 + core
                    wsum = wsum + parts[source, t * own : (t + 1) * own, :]
                    coldot = coldot + parts[source, tail + t : tail + t + 1, :]
                inv = winv[:, lanes]
                both = rows[:, lanes].astype(F32)
                wnorm = jnp.where(idx[0] == 0, both[:own, :], both[own:, :]) * inv
                out[:, lanes] = (wsum - wnorm * coldot) * inv


def proto_pass(idx, parts, protos, winv, nx, ny):
    width, columns = protos.shape
    own = width // parts.shape[0]
    return call(
        functools.partial(proto_kernel, nx, ny),
        array((own, columns)),
        [idx, parts, protos, winv],
        "svhv",
        scratch=[pltpu.VMEM((2 * own, columns), BF16), pltpu.SemaphoreType.DMA],
    )


def spread_row(line):
    return jnp.transpose(jnp.broadcast_to(line, (128, 128)))


def scaled_kernel(crops, idx, mix, totals, mine, theirs, buf):
    rows, width = mix.shape
    prob = GRAD_SCALE / totals[...]
    for t in range(rows // 128):
        span = slice(128 * t, 128 * (t + 1))
        p = jnp.concatenate([spread_row(prob[t : t + 1, :])] * (width // 128), axis=1)
        buf[span, :] = mix[span, :] * p
    part_rows(crops, idx, buf, mine, theirs)


def plain_kernel(crops, idx, mix, mine, theirs):
    part_rows(crops, idx, mix, mine, theirs)


def part_rows(crops, idx, buf, mine, theirs):
    rest = mine.shape[0] - crops
    for side, ref in ((idx[0], mine), (1 - idx[0], theirs)):
        ref[:crops, :] = buf[pl.ds(pl.multiple_of(side * crops, crops), crops), :]
        ref[crops:, :] = buf[pl.ds(pl.multiple_of(2 * crops + side * rest, 128), rest), :]


def part_pass(idx, mix, totals, crops):
    rows, width = mix.shape
    shapes = [array((rows // 2, width)), array((rows // 2, width))]
    if totals is None:
        return call(functools.partial(plain_kernel, crops), shapes, [idx, mix], "sv")
    return call(
        functools.partial(scaled_kernel, crops),
        shapes,
        [idx, mix, totals],
        "svv",
        scratch=[pltpu.VMEM((rows, width), F32)],
    )


def pack_kernel(nz, crops, mine, came, out):
    half = mine.shape[0]
    chunk = half // nz
    share = crops // nz
    rest = chunk - share
    for z in range(nz):
        for src, dst, size in ((z * share, z * chunk, share), (crops + z * rest, z * chunk + share, rest)):
            out[dst : dst + size, :] = mine[src : src + size, :] + came[src : src + size, :]


def pack_pass(mine, came, nz, crops):
    return call(functools.partial(pack_kernel, nz, crops), array(mine.shape), [mine, came], "vv")


def feature_kernel(nz, ny, crops, pair, patches, idx, mask, rowparts, *refs):
    count = 4 if pair else 2
    pieces = refs[:count]
    all_crops, all_rows, crop_out, patch_out, masked_rows, dense, scale, crop_rows = refs[count:]
    z = idx[1]
    masked = mask.shape[1]
    crop_share = crop_out.shape[0]
    share = patch_out.shape[0]
    crop_at = pl.multiple_of(z * crop_share, 16)
    patch_at = pl.multiple_of(z * share, 128)
    rest = pieces[0].shape[0] - crop_share
    sub = rowparts.shape[1]
    group = rowparts.shape[0] // ny
    cd = crops // 128
    ci = sub // 2 - cd
    sums = jnp.sum(rowparts[pl.ds(idx[3] * group, group), :, :], axis=0)
    row = GRAD_SCALE / sums
    low = idx[0] == 0
    for t in range(cd + ci):
        a, b = (t, cd + t) if t < cd else (cd + t, cd + ci + t)
        line = jnp.where(low, row[a : a + 1, :], row[b : b + 1, :])
        scale[128 * t : 128 * (t + 1), :] = spread_row(line)
    wide = pieces[0].shape[1] // 128

    def fgrad(prob, target, at, size):
        r = scale[pl.ds(pl.multiple_of(at, 16), size), :]
        return prob - target * jnp.concatenate([r] * wide, axis=1)

    crop_rows[...] = fgrad(
        pieces[0][:crop_share, :], pieces[1][:crop_share, :], z * crop_share, crop_share
    )
    spots = ((z, 0),) if not pair else ((z, 0), (z + 1 - 2 * lax.rem(z, 2), 2))
    for place, which in spots:
        value = fgrad(
            pieces[which][crop_share:, :], pieces[which + 1][crop_share:, :], crops + place * rest, rest
        )
        at = pl.multiple_of(lax.rem(place, 2) * rest, 8) if pair else 0
        masked_rows[pl.ds(at, rest), :] = value
    dense[...] = jnp.zeros_like(dense)
    first_row = z * share
    first_image = first_row // patches
    offset = first_row - first_image * patches
    for image in range(masked_rows.shape[0] // masked):

        def put(m, _):
            at = mask[first_image + image, m] + image * patches - offset

            @pl.when(jnp.logical_and(at >= 0, at < share))
            def _():
                dense[pl.ds(at, 1), :] = masked_rows[pl.ds(image * masked + m, 1), :]

            return 0

        lax.fori_loop(0, masked, put, 0, unroll=4)

    def back(x, d):
        xf = x.astype(F32)
        inv = lax.rsqrt(jnp.sum(xf * xf, axis=-1, keepdims=True) + EPS)
        u = xf * inv
        return (d - u * jnp.sum(u * d, axis=-1, keepdims=True)) * inv

    crop_out[...] = back(all_crops[pl.ds(crop_at, crop_share), :], crop_rows[...])
    patch_out[...] = back(all_rows[pl.ds(patch_at, share), :], dense[...])


def feature_pass(idx, mask, rowparts, pieces, all_crops, all_rows, nz, ny, patches):
    crops, width = all_crops.shape
    crop_share = crops // nz
    share = all_rows.shape[0] // nz
    pair = len(pieces) == 4
    count = len(pieces) // 2 * (pieces[0].shape[0] - crop_share)
    half = rowparts.shape[1] // 2 * 128
    return call(
        functools.partial(feature_kernel, nz, ny, crops, pair, patches),
        [array((crop_share, width)), array((share, width))],
        [idx, mask, rowparts, *pieces, all_crops, all_rows],
        "ssv" + "v" * len(pieces) + "vv",
        scratch=[
            pltpu.VMEM((count, width), F32),
            pltpu.VMEM((share, width), F32),
            pltpu.VMEM((half, 128), F32),
            pltpu.VMEM((crop_share, width), F32),
        ],
    )


def shifted(n, s):
    return [(i, (i + s) % n) for i in range(n)]


def local(
    sizes,
    student_crops,
    teacher_crops,
    student_patches,
    teacher_patches,
    patch_mask,
    student_protos,
    teacher_protos,
):
    nx, ny, nz = sizes
    images, masked = patch_mask.shape
    patches = student_patches.shape[0] // images
    crops = student_crops.shape[0]
    ix, iy, ic, iz = (lax.axis_index(a) for a in ("x", "y", "c", "z"))
    idx = jnp.stack([ic, iz, ix * ny + iy, iy]).astype(jnp.int32)
    swap = [(0, 1), (1, 0)]

    own = prep(teacher_crops, teacher_patches, student_crops, student_patches, patch_mask)
    other = lax.ppermute(own, "c", swap)
    all_own = lax.all_gather(own, "y")
    all_other = lax.ppermute(all_own, "c", swap)

    expo, sums = teacher_pass(idx, own, other, teacher_protos, crops, nx * ny)
    sub = 2 * (crops + images * masked) // 128
    for step in range(ITERS):
        colparts = lax.all_to_all(sums, ("x", "y"), 0, 0)
        if step == 0:
            total, mix = student_pass(idx, own, other, student_protos, crops)
        if step < ITERS - 1:
            sums = row_pass(expo, colparts, total if step == 0 else None, crops, 2 * nz)
            rowparts = lax.all_to_all(sums, ("c", "z"), 0, 0)
            if step == 0:
                totals = jnp.sum(rowparts[:, sub:, :], axis=0)
            sums = column_pass(expo, rowparts, crops, nx * ny)
        else:
            sums, target = last_row_pass(
                idx, expo, colparts, student_protos, crops, 2 * nz * ny
            )
            rowparts = lax.all_to_all(sums, ("y", "c", "z"), 0, 0)

    all_totals = [totals] + [lax.ppermute(totals, "y", shifted(ny, s)) for s in range(1, ny)]
    wide_expo = wide_teacher_pass(idx, all_own, all_other, teacher_protos, crops)
    prob, wnorm, *turned = wide_student_pass(
        idx, all_own, all_other, student_protos, all_totals, crops
    )
    winv = norm_pass(student_protos)
    outgoing = weight_pass(
        idx, prob, wnorm, turned, wide_expo, colparts, rowparts, crops, ny, nx * ny * 2
    )
    parts = lax.all_to_all(outgoing, ("x", "y", "c"), 0, 0)
    proto_grad = proto_pass(idx, parts, student_protos, winv, nx, ny)

    reduced = []
    for value, scale in ((mix, totals), (target, None)):
        mine, theirs = part_pass(idx, value, scale, crops)
        packed = pack_pass(mine, lax.ppermute(theirs, "c", swap), nz, crops)
        reduced.append(lax.psum_scatter(packed, "z", scatter_dimension=0, tiled=True))
    pieces = list(reduced)
    if student_patches.shape[0] // nz < patches:
        pair = [(i, i ^ 1) for i in range(nz)]
        pieces += [lax.ppermute(r, "z", pair) for r in reduced]
    crop_grad, patch_grad = feature_pass(
        idx, patch_mask, rowparts, pieces, student_crops, student_patches, nz, ny, patches
    )
    return (proto_grad, crop_grad, patch_grad)


def solution(mesh):
    dp, nz = mesh.devices.shape
    nx = 4 if dp == 32 else 2
    ny = dp // (2 * nx)
    grid = Mesh(mesh.devices.reshape(nx, ny, 2, nz), ("x", "y", "c", "z"))
    rows = ("x", "y", "c")
    in_specs = (
        P(rows, None),
        P(rows, None),
        P(rows, None),
        P(rows, None),
        P(rows, None),
        P(None, "z"),
        P(None, "z"),
    )
    out_specs = (P(rows, "z"), P(rows + ("z",), None), P(rows + ("z",), None))
    return jax.shard_map(
        functools.partial(local, (nx, ny, nz)),
        mesh=grid,
        in_specs=in_specs,
        out_specs=out_specs,
        check_vma=False,
    )
```

time: 243 us -> 309 us (1.27)
  the two profiles are of different devices: /device:TPU:28 before, /device:TPU:32 now
where the time goes in v3:
time: 309 us; the launch traced here: 306 us
  waiting for transfers between devices  110 us (36%)
  Pallas kernels  66 us (21%)
  local copies, waits for them, and re-layouts  47.5 us (15%)
  blocking collectives  33.4 us (11%)
  starting transfers between devices  32.9 us (11%)
  between operations  15.8 us (5%)
    pallas_call x17, Pallas kernels, call(): pl.pallas_call(kernel, out_shape=out_shape, in_specs=[spaces[letter] for...  65.3 us
    all_gather x1, waiting for transfers between devices, local(): all_own = lax.all_gather(own, 'y')  53.6 us
    unnamed x66, local copies, waits for them, and re-layouts  47.5 us
    reduce_scatter x2, waiting for transfers between devices, local(): lax.psum_scatter(packed, 'z', scatter_dimension=0, tiled=True)  37.4 us
    all_to_all x1, blocking collectives, local(): colparts = lax.all_to_all(sums, ('x', 'y'), 0, 0)  17.9 us
    all_to_all x1, blocking collectives, local(): rowparts = lax.all_to_all(sums, ('c', 'z'), 0, 0)  15.5 us
    all_to_all x2, starting transfers between devices, local(): colparts = lax.all_to_all(sums, ('x', 'y'), 0, 0)  9.44 us
    ppermute x1, waiting for transfers between devices, local(): other = lax.ppermute(own, 'c', swap)  7.91 us
  transfers between devices with their start and end apart: 17, of which 7 were waited for; matrix products, arithmetic and copies ran while one was open for 0% of the time, Pallas kernels for 21%

profile of v3, /device:TPU:32, one launch (start us, length us, event | category | flops | bytes accessed | tf_op | source)
XLA Modules:
  0.0 305.8 jit_solution(3292486368787681060)
XLA Ops:
  14.5 53.6 %all-gather.3.cloned.1.call-done = f32[4096,256]{1,0:T(8,128)} async-done(((f32[1024,256]{1,0:T(8,128)}), f32[4096,256]{1,0:T(8,128)}) %all-gather.3.cloned.1.call-update) | async-done | bytes 4194320 | tf_op jit(solution)/shard_map/all_gather | solution.py:767
  68.6 7.9 %collective-permute-done.1.other = f32[1024,256]{1,0:T(8,128)S(1)} collective-permute-done((f32[1024,256]{1,0:T(8,128)}, f32[1024,256]{1,0:T(8,128)S(1)}, u32[]{:S(2)}, u32[]{:S(2)}) %collective-permute-start.1) | collective-permute-done | bytes 1048608 | tf_op jit(solution)/shard_map/ppermute | solution.py:766
  78.7 7.8 %shard_map.95 = (bf16[1024,4096]{1,0:T(8,128)(2,1)S(1)}, f32[16,64,128]{2,1,0:T(8,128)}) custom-call(s32[4]{0:T(128)S(1)} %pad_add_fusion.idx, f32[1024,256]{1,0:T(8,128)} %shard_map.94.own, f32[1024,256]{1,0:T(8,128)S(1)} %collective-permute-done.1.other, bf16[256,8192]{1,0:T(8,128)(2,1)S(1)} %copy-done.11), custom_call_target="tpu_custom_call" | custom-call | flops 2147483648 | bytes 8388608 | tf_op jit(solution)/shard_map/pallas_call | solution.py:29
  86.5 3.3 %copy-done = bf16[1024,4096]{1,0:T(8,128)(2,1)} copy-done((bf16[1024,4096]{1,0:T(8,128)(2,1)}, bf16[1024,4096]{1,0:T(8,128)(2,1)S(1)}, u32[]{:S(2)}) %copy-start) | copy-done | bytes 8388632
  89.8 5.9 %all-to-all-start = ((f32[16,64,128]{2,1,0:T(8,128)}), f32[16,64,128]{2,1,0:T(8,128)S(1)}, u32[]{:S(2)}, u32[]{:S(2)}) async-start(f32[16,64,128]{2,1,0:T(8,128)} %get-tuple-element.22), calls=%async_computation | async-start | bytes 1048576 | tf_op jit(solution)/shard_map/all_to_all | solution.py:773
  97.9 9.6 %shard_map.96 = (f32[8,128]{1,0:T(8,128)S(1)}, f32[1024,256]{1,0:T(8,128)S(1)}) custom-call(s32[4]{0:T(128)S(1)} %pad_add_fusion.idx, f32[1024,256]{1,0:T(8,128)} %shard_map.94.own, f32[1024,256]{1,0:T(8,128)S(1)} %collective-permute-done.1.other, bf16[256,8192]{1,0:T(8,128)(2,1)S(1)} %copy-done.4), custom_call_target="tpu_custom_call" | custom-call | flops 4294967296 | bytes 2097152 | tf_op jit(solution)/shard_map/pallas_call | solution.py:29
  107.7 3.4 %copy-done.1 = bf16[1024,4096]{1,0:T(8,128)(2,1)S(1)} copy-done((bf16[1024,4096]{1,0:T(8,128)(2,1)S(1)}, bf16[1024,4096]{1,0:T(8,128)(2,1)}, u32[]{:S(2)}) %copy-start.1) | copy-done | bytes 8388632
  111.1 3.3 %shard_map.97 = f32[16,16,128]{2,1,0:T(8,128)S(1)} custom-call(bf16[1024,4096]{1,0:T(8,128)(2,1)S(1)} %copy-done.1, f32[16,64,128]{2,1,0:T(8,128)S(1)} %all-to-all-done.colparts, f32[8,128]{1,0:T(8,128)S(1)} %get-tuple-element.23.refs_0_), custom_call_target="tpu_custom_call" | custom-call | flops 8388608 | bytes 8388608 | tf_op jit(solution)/shard_map/pallas_call | solution.py:29
  114.4 15.5 %all_to_all.35.rowparts = f32[16,16,128]{2,1,0:T(8,128)S(1)} all-to-all(f32[16,16,128]{2,1,0:T(8,128)S(1)} %shard_map.97), channel_id=1, replica_groups=mesh['x'=4,'y'=4,'c'=2,'z'=8] {'c','z'}, dimensions={0} | all-to-all | bytes 262144 | tf_op jit(solution)/shard_map/all_to_all | solution.py:778
  131.3 17.9 %all_to_all.36.colparts = f32[16,64,128]{2,1,0:T(8,128)S(1)} all-to-all(f32[16,64,128]{2,1,0:T(8,128)S(1)} %shard_map.100), channel_id=1, replica_groups=mesh['x'=4,'y'=4,'c'=2,'z'=8] {'x','y'}, dimensions={0} | all-to-all | bytes 1048576 | tf_op jit(solution)/shard_map/all_to_all | solution.py:773
  149.2 3.9 %shard_map.101 = f32[16,8,128]{2,1,0:T(8,128)} custom-call(bf16[1024,4096]{1,0:T(8,128)(2,1)S(1)} %copy-done.1, f32[16,64,128]{2,1,0:T(8,128)S(1)} %all_to_all.36.colparts), custom_call_target="tpu_custom_call" | custom-call | flops 8388608 | bytes 8388608 | tf_op jit(solution)/shard_map/pallas_call | solution.py:29
  153.0 4.1 %all-to-all-start.3 = ((f32[16,8,128]{2,1,0:T(8,128)}), f32[16,8,128]{2,1,0:T(8,128)S(1)}, u32[]{:S(2)}, u32[]{:S(2)}) async-start(f32[16,8,128]{2,1,0:T(8,128)} %shard_map.101), calls=%async_computation.3 | async-start | bytes 131072 | tf_op jit(solution)/shard_map/all_to_all | solution.py:778
  158.2 5.9 %all-to-all-done.3.rowparts = f32[16,8,128]{2,1,0:T(8,128)S(1)} async-done(((f32[16,8,128]{2,1,0:T(8,128)}), f32[16,8,128]{2,1,0:T(8,128)S(1)}, u32[]{:S(2)}, u32[]{:S(2)}) %all-to-all-start.3) | async-done | bytes 65568 | tf_op jit(solution)/shard_map/all_to_all | solution.py:778
  164.1 3.4 %copy-done.2 = bf16[1024,4096]{1,0:T(8,128)(2,1)S(1)} copy-done((bf16[1024,4096]{1,0:T(8,128)(2,1)S(1)}, bf16[1024,4096]{1,0:T(8,128)(2,1)}, u32[]{:S(2)}) %copy-start.2) | copy-done | bytes 8388632
  167.5 2.2 shard_map.102
  169.7 3.6 %all-to-all-start.4 = ((f32[16,64,128]{2,1,0:T(8,128)}), f32[16,64,128]{2,1,0:T(8,128)S(1)}, u32[]{:S(2)}, u32[]{:S(2)}) async-start(f32[16,64,128]{2,1,0:T(8,128)} %shard_map.102), calls=%async_computation.4 | async-start | bytes 1048576 | tf_op jit(solution)/shard_map/all_to_all | solution.py:773
  176.2 2.7 collective-permute-start.3
  180.3 4.7 %all-to-all-done.4.colparts = f32[16,64,128]{2,1,0:T(8,128)S(1)} async-done(((f32[16,64,128]{2,1,0:T(8,128)}), f32[16,64,128]{2,1,0:T(8,128)S(1)}, u32[]{:S(2)}, u32[]{:S(2)}) %all-to-all-start.4) | async-done | bytes 524320 | tf_op jit(solution)/shard_map/all_to_all | solution.py:773
  185.0 3.4 %copy-done.3 = bf16[1024,4096]{1,0:T(8,128)(2,1)S(1)} copy-done((bf16[1024,4096]{1,0:T(8,128)(2,1)S(1)}, bf16[1024,4096]{1,0:T(8,128)(2,1)}, u32[]{:S(2)}) %copy-start.3) | copy-done | bytes 8388632
  188.4 2.2 copy-done.5
  190.6 9.3 %shard_map.103 = (f32[64,8,128]{2,1,0:T(8,128)}, f32[1024,256]{1,0:T(8,128)S(1)}) custom-call(s32[4]{0:T(128)S(1)} %pad_add_fusion.idx, bf16[1024,4096]{1,0:T(8,128)(2,1)S(1)} %copy-done.3, f32[16,64,128]{2,1,0:T(8,128)S(1)} %all-to-all-done.4.colparts, bf16[256,8192]{1,0:T(8,128)(2,1)S(1)} %copy-done.5), custom_call_target="tpu_custom_call" | custom-call | flops 2147483648 | bytes 8388608 | tf_op jit(solution)/shard_map/pallas_call | solution.py:29
  202.1 4.8 %all-to-all-start.5 = ((f32[64,8,128]{2,1,0:T(8,128)}), f32[64,8,128]{2,1,0:T(8,128)S(1)}, u32[]{:S(2)}, u32[]{:S(2)}) async-start(f32[64,8,128]{2,1,0:T(8,128)} %get-tuple-element.30), calls=%async_computation.5 | async-start | bytes 524288 | tf_op jit(solution)/shard_map/all_to_all | solution.py:786
  209.2 2.2 copy-done.13
  211.4 7.1 %shard_map.98 = (f32[256,1024]{1,0:T(8,128)S(1)}, f32[256,1024]{1,0:T(8,128)S(1)}, bf16[256,1024]{1,0:T(8,128)(2,1)S(1)}, bf16[256,3072]{1,0:T(8,128)(2,1)S(1)}) custom-call(s32[4]{0:T(128)S(1)} %pad_add_fusion.idx, f32[4,1024,256]{2,1,0:T(8,128)S(1)} %bitcast.6, f32[4,1024,256]{2,1,0:T(8,128)} %collective-permute-done.other, ...), custom_call_target="tpu_custom_call" | custom-call | flops 4294967296 | bytes 4194304 | tf_op jit(solution)/shard_map/pallas_call | solution.py:29
  221.7 5.5 %shard_map.99 = (bf16[1024,1024]{1,0:T(8,128)(2,1)S(1)}, bf16[3072,1024]{1,0:T(8,128)(2,1)S(1)}) custom-call(s32[4]{0:T(128)S(1)} %pad_add_fusion.idx, f32[4,1024,256]{2,1,0:T(8,128)S(1)} %bitcast.7, f32[4,1024,256]{2,1,0:T(8,128)} %collective-permute-done.other, bf16[256,8192]{1,0:T(8,128)(2,1)S(1)} %copy-done.12), custom_call_target="tpu_custom_call" | custom-call | flops 2147483648 | bytes 4194304 | tf_op jit(solution)/shard_map/pallas_call | solution.py:29
  227.2 2.6 copy-done.9
  229.8 2.8 copy-done.10
  236.5 4.0 %shard_map.104 = f32[32,72,128]{2,1,0:T(8,128)} custom-call(s32[4]{0:T(128)S(1)} %pad_add_fusion.idx, f32[256,1024]{1,0:T(8,128)S(1)} %copy-done.20, f32[256,1024]{1,0:T(8,128)S(1)} %copy-done.22, bf16[256,1024]{1,0:T(8,128)(2,1)S(1)} %get-tuple-element.26.turned_d, bf16[256,3072]{1,0:T(8,128)(2,1)S(1)} %copy-done.18, ...), custom_call_target="tpu_custom_call" | custom-call | flops 2147483648 | bytes 8388608 | tf_op jit(solution)/shard_map/pallas_call | solution.py:29
  240.5 5.8 %all-to-all-start.6 = ((f32[32,72,128]{2,1,0:T(8,128)}), f32[32,72,128]{2,1,0:T(8,128)S(1)}, u32[]{:S(2)}, u32[]{:S(2)}) async-start(f32[32,72,128]{2,1,0:T(8,128)} %shard_map.104), calls=%async_computation.6 | async-start | bytes 2359296 | tf_op jit(solution)/shard_map/all_to_all | solution.py:797
  250.0 37.4 %reduce-scatter.5.cloned.1.call-done.refs_1_ = f32[64,256]{1,0:T(8,128)} async-done(((f32[512,256]{1,0:T(8,128)}), f32[64,256]{1,0:T(8,128)}) %reduce-scatter.5.cloned.1.call-update) | async-done | bytes 65552 | tf_op jit(solution)/shard_map/reduce_scatter | solution.py:804
  291.9 2.9 shard_map.111
  294.8 2.2 copy-done.8
  (93 shorter events, 39.3 us)
Async XLA Ops:
  8.0 60.1 %all-gather.3.cloned.1.call-start = ((), (), s32[]{:S(2)}) async-start(), calls=%async_computation.11 | async-start | bytes 5242880 | tf_op jit(solution)/shard_map/all_gather | solution.py:767
  68.1 138.9 %collective-permute-start = (f32[4,1024,256]{2,1,0:T(8,128)}, f32[4,1024,256]{2,1,0:T(8,128)}, u32[]{:S(2)}, u32[]{:S(2)}) collective-permute-start(f32[4,1024,256]{2,1,0:T(8,128)} %bitcast.5), channel_id=1, source_target_pairs={{0,8},{8,0},{1,9},{9,1},{2,10},{10,2},{3,11},{11,3},{4,12},{12,4},... | collective-permute-start | bytes 12582920 | tf_op jit(solution)/shard_map/ppermute | solution.py:768
  68.1 8.5 %collective-permute-start.1 = (f32[1024,256]{1,0:T(8,128)}, f32[1024,256]{1,0:T(8,128)S(1)}, u32[]{:S(2)}, u32[]{:S(2)}) collective-permute-start(f32[1024,256]{1,0:T(8,128)} %shard_map.94.own), channel_id=1, source_target_pairs={{0,8},{8,0},{1,9},{9,1},{2,10},{10,2},{3,11},{11,3},{4,12},{12,4},... | collective-permute-start | bytes 3145736 | tf_op jit(solution)/shard_map/ppermute | solution.py:766
  86.5 3.3 %copy-start = (bf16[1024,4096]{1,0:T(8,128)(2,1)}, bf16[1024,4096]{1,0:T(8,128)(2,1)S(1)}, u32[]{:S(2)}) copy-start(bf16[1024,4096]{1,0:T(8,128)(2,1)S(1)} %get-tuple-element.21.expo) | copy-start | bytes 25165828
  89.8 17.9 %all-to-all-start = ((f32[16,64,128]{2,1,0:T(8,128)}), f32[16,64,128]{2,1,0:T(8,128)S(1)}, u32[]{:S(2)}, u32[]{:S(2)}) async-start(f32[16,64,128]{2,1,0:T(8,128)} %get-tuple-element.22), calls=%async_computation | async-start | bytes 1048576 | tf_op jit(solution)/shard_map/all_to_all | solution.py:773
  95.7 2.2 copy-start.4
  107.7 3.4 %copy-start.1 = (bf16[1024,4096]{1,0:T(8,128)(2,1)S(1)}, bf16[1024,4096]{1,0:T(8,128)(2,1)}, u32[]{:S(2)}) copy-start(bf16[1024,4096]{1,0:T(8,128)(2,1)} %copy-done) | copy-start | bytes 25165828
  153.0 11.1 %all-to-all-start.3 = ((f32[16,8,128]{2,1,0:T(8,128)}), f32[16,8,128]{2,1,0:T(8,128)S(1)}, u32[]{:S(2)}, u32[]{:S(2)}) async-start(f32[16,8,128]{2,1,0:T(8,128)} %shard_map.101), calls=%async_computation.3 | async-start | bytes 131072 | tf_op jit(solution)/shard_map/all_to_all | solution.py:778
  158.0 15.4 %collective-permute-start.5 = (f32[512,256]{1,0:T(8,128)S(1)}, f32[512,256]{1,0:T(8,128)S(1)}, u32[]{:S(2)}, u32[]{:S(2)}) collective-permute-start(f32[512,256]{1,0:T(8,128)S(1)} %get-tuple-element.33), channel_id=1, source_target_pairs={{0,8},{8,0},{1,9},{9,1},{2,10},{10,2},{3,11},{11,3},{4,12},{12,4},... | collective-permute-start | bytes 1572872 | tf_op jit(solution)/shard_map/ppermute | solution.py:803
  164.1 3.4 %copy-start.2 = (bf16[1024,4096]{1,0:T(8,128)(2,1)S(1)}, bf16[1024,4096]{1,0:T(8,128)(2,1)}, u32[]{:S(2)}) copy-start(bf16[1024,4096]{1,0:T(8,128)(2,1)} %copy-done) | copy-start | bytes 25165828
  169.7 15.3 %all-to-all-start.4 = ((f32[16,64,128]{2,1,0:T(8,128)}), f32[16,64,128]{2,1,0:T(8,128)S(1)}, u32[]{:S(2)}, u32[]{:S(2)}) async-start(f32[16,64,128]{2,1,0:T(8,128)} %shard_map.102), calls=%async_computation.4 | async-start | bytes 1048576 | tf_op jit(solution)/shard_map/all_to_all | solution.py:773
  173.3 76.1 %reduce-scatter.3.cloned.1.call-start = ((), (), s32[]{:S(2)}) async-start(), calls=%async_computation.9 | async-start | bytes 589824 | tf_op jit(solution)/shard_map/reduce_scatter | solution.py:804
  174.2 32.7 %collective-permute-start.2 = (f32[8,128]{1,0:T(8,128)S(1)}, f32[8,128]{1,0:T(8,128)S(1)}, u32[]{:S(2)}, u32[]{:S(2)}) collective-permute-start(f32[8,128]{1,0:T(8,128)S(1)} %slice_reduce_fusion.refs_0_.totals), channel_id=1, source_target_pairs={{0,16},{16,32},{32,48},{48,0},{1,17},{17,33},{33,49},{49,1},{2,18}... | collective-permute-start | bytes 12296 | tf_op jit(solution)/shard_map/ppermute | solution.py:788
  176.2 30.8 %collective-permute-start.3 = (f32[8,128]{1,0:T(8,128)S(1)}, f32[8,128]{1,0:T(8,128)S(1)}, u32[]{:S(2)}, u32[]{:S(2)}) collective-permute-start(f32[8,128]{1,0:T(8,128)S(1)} %slice_reduce_fusion.refs_0_.totals), channel_id=1, source_target_pairs={{0,32},{16,48},{32,0},{48,16},{1,33},{17,49},{33,1},{49,17},{2,34}... | collective-permute-start | bytes 12296 | tf_op jit(solution)/shard_map/ppermute | solution.py:788
  178.8 28.1 %collective-permute-start.4 = (f32[8,128]{1,0:T(8,128)S(1)}, f32[8,128]{1,0:T(8,128)S(1)}, u32[]{:S(2)}, u32[]{:S(2)}) collective-permute-start(f32[8,128]{1,0:T(8,128)S(1)} %slice_reduce_fusion.refs_0_.totals), channel_id=1, source_target_pairs={{0,48},{16,0},{32,16},{48,32},{1,49},{17,1},{33,17},{49,33},{2,50}... | collective-permute-start | bytes 12296 | tf_op jit(solution)/shard_map/ppermute | solution.py:788
  185.0 3.4 %copy-start.3 = (bf16[1024,4096]{1,0:T(8,128)(2,1)S(1)}, bf16[1024,4096]{1,0:T(8,128)(2,1)}, u32[]{:S(2)}) copy-start(bf16[1024,4096]{1,0:T(8,128)(2,1)} %copy-done) | copy-start | bytes 25165828
  188.4 2.2 copy-start.5
  202.1 44.2 %collective-permute-start.6 = (f32[512,256]{1,0:T(8,128)}, f32[512,256]{1,0:T(8,128)}, u32[]{:S(2)}, u32[]{:S(2)}) collective-permute-start(f32[512,256]{1,0:T(8,128)} %get-tuple-element.36), channel_id=1, source_target_pairs={{0,8},{8,0},{1,9},{9,1},{2,10},{10,2},{3,11},{11,3},{4,12},{12,4},... | collective-permute-start | bytes 1572872 | tf_op jit(solution)/shard_map/ppermute | solution.py:803
  202.1 27.7 %all-to-all-start.5 = ((f32[64,8,128]{2,1,0:T(8,128)}), f32[64,8,128]{2,1,0:T(8,128)S(1)}, u32[]{:S(2)}, u32[]{:S(2)}) async-start(f32[64,8,128]{2,1,0:T(8,128)} %get-tuple-element.30), calls=%async_computation.5 | async-start | bytes 524288 | tf_op jit(solution)/shard_map/all_to_all | solution.py:786
  207.0 2.2 copy-start.6
  209.2 2.2 copy-start.13
  211.4 10.3 %copy-start.12 = (bf16[256,8192]{1,0:T(8,128)(2,1)S(1)}, bf16[256,8192]{1,0:T(8,128)(2,1)}, u32[]{:S(2)}) copy-start(bf16[256,8192]{1,0:T(8,128)(2,1)} %protos.10) | copy-start | bytes 12582916
  211.4 10.3 %copy-start.14 = (f32[4096,256]{1,0:T(8,128)S(1)}, f32[4096,256]{1,0:T(8,128)}, u32[]{:S(2)}) copy-start(f32[4096,256]{1,0:T(8,128)} %all-gather.3.cloned.1.call-done) | copy-start | bytes 12582916
  227.2 2.6 copy-start.9
  229.8 2.8 copy-start.10
  240.5 51.4 %copy-start.16 = (bf16[1024,256]{1,0:T(8,128)(2,1)S(1)}, bf16[1024,256]{1,0:T(8,128)(2,1)}, u32[]{:S(2)}) copy-start(bf16[1024,256]{1,0:T(8,128)(2,1)} %refs_5_.1) | copy-start | bytes 1572868
  240.5 51.4 %copy-start.27 = (bf16[128,256]{1,0:T(8,128)(2,1)S(1)}, bf16[128,256]{1,0:T(8,128)(2,1)}, u32[]{:S(2)}) copy-start(bf16[128,256]{1,0:T(8,128)(2,1)} %refs_4_.1) | copy-start | bytes 196612
  240.5 51.4 %copy-start.32 = (s32[4,96]{1,0:T(4,128)S(1)}, s32[4,96]{1,0:T(4,128)}, u32[]{:S(2)}) copy-start(s32[4,96]{1,0:T(4,128)} %mask.3) | copy-start | bytes 4612
  240.5 54.3 %all-to-all-start.6 = ((f32[32,72,128]{2,1,0:T(8,128)}), f32[32,72,128]{2,1,0:T(8,128)S(1)}, u32[]{:S(2)}, u32[]{:S(2)}) async-start(f32[32,72,128]{2,1,0:T(8,128)} %shard_map.104), calls=%async_computation.6 | async-start | bytes 2359296 | tf_op jit(solution)/shard_map/all_to_all | solution.py:797
  246.3 41.1 %reduce-scatter.5.cloned.1.call-start = ((), (), s32[]{:S(2)}) async-start(), calls=%async_computation.10 | async-start | bytes 589824 | tf_op jit(solution)/shard_map/reduce_scatter | solution.py:804
  249.4 42.2 %collective-permute-start.7 = (f32[64,256]{1,0:T(8,128)}, f32[64,256]{1,0:T(8,128)S(1)}, u32[]{:S(2)}, u32[]{:S(2)}) collective-permute-start(f32[64,256]{1,0:T(8,128)} %reduce-scatter.3.cloned.1.call-done.refs_0_), channel_id=1, source_target_pairs={{0,1},{1,0},{2,3},{3,2},{4,5},{5,4},{6,7},{7,6},{8,9},{9,8},{10,11... | collective-permute-start | bytes 196616 | tf_op jit(solution)/shard_map/ppermute | solution.py:808
  287.4 4.5 %collective-permute-start.8 = (f32[64,256]{1,0:T(8,128)}, f32[64,256]{1,0:T(8,128)S(1)}, u32[]{:S(2)}, u32[]{:S(2)}) collective-permute-start(f32[64,256]{1,0:T(8,128)} %reduce-scatter.5.cloned.1.call-done.refs_1_), channel_id=1, source_target_pairs={{0,1},{1,0},{2,3},{3,2},{4,5},{5,4},{6,7},{7,6},{8,9},{9,8},{10,11... | collective-permute-start | bytes 196616 | tf_op jit(solution)/shard_map/ppermute | solution.py:808
  (18 other events, 22.1 us)
Sparse Core Ops, SparseCore 0:
  14.6 53.4 all-gather.2
Sparse Core Ops, SparseCore 1:
  176.3 34.2 reduce-scatter.2
  249.5 37.9 reduce-scatter.4

commit v4 on v3

--- a/solution.py
+++ b/solution.py
@@ -18,17 +18,22 @@
 BN = 512
 F32 = jnp.float32
 BF16 = jnp.bfloat16
-VMEM_LIMIT = 16 * 1024 * 1024
+VMEM_LIMIT = 58 * 1024 * 1024
 SMEM = pl.BlockSpec(memory_space=pltpu.SMEM)
 VMEM = pl.BlockSpec(memory_space=pltpu.VMEM)
 HBM = pl.BlockSpec(memory_space=pltpu.HBM)
 
 
-def call(kernel, out_shape, args, specs="", scratch=(), flops=0, traffic=0):
+def call(kernel, out_shape, args, specs, outs="", scratch=(), flops=0, traffic=0):
     spaces = {"s": SMEM, "v": VMEM, "h": HBM}
+    if not isinstance(out_shape, list):
+        out_specs = VMEM
+    else:
+        out_specs = [spaces[letter] for letter in outs or "v" * len(out_shape)]
     return pl.pallas_call(
         kernel,
         out_shape=out_shape,
+        out_specs=out_specs,
         in_specs=[spaces[letter] for letter in specs],
         scratch_shapes=list(scratch),
         compiler_params=pltpu.CompilerParams(vmem_limit_bytes=VMEM_LIMIT),
@@ -154,25 +159,38 @@
     return jnp.concatenate([values[t : t + 1, :] for t in range(values.shape[0])], axis=1)
 
 
-def teacher_kernel(crops, idx, own, other, protos, expo, sums, feats, buf, sem):
+def teacher_kernel(crops, idx, own, other, protos, expo, sums, feats, out, osem, buf, sem):
     rows, columns = expo.shape
     place_rows(idx[0], crops, 0, rows // 2, own, other, feats)
+    steps = columns // BN
+
+    def leave(j, slot):
+        at = pl.multiple_of(j * BN, BN)
+        return pltpu.make_async_copy(out.at[slot], expo.at[:, pl.ds(at, BN)], osem.at[slot])
 
     def step(j, block):
         w = unit_cols(block[...])[0].astype(BF16)
-        at = pl.multiple_of(j * BN, BN)
+        slot = lax.rem(j, 2)
+
+        @pl.when(j >= 2)
+        def _():
+            leave(j - 2, slot).wait()
+
         heads = []
         for first, last in ((0, 2 * crops), (2 * crops, rows)):
             part = jnp.zeros((1, BN), F32)
             for start, stop in row_blocks(first, last):
                 score = jnp.dot(feats[start:stop, :], w, preferred_element_type=F32)
                 e = jnp.exp2(score * (LOG2E / TEACHER_TEMP)).astype(BF16)
-                expo[start:stop, pl.ds(at, BN)] = e
+                out[slot, start:stop, :] = e
                 part = part + jnp.sum(e.astype(F32), axis=0, keepdims=True)
             heads.append(part)
+        leave(j, slot).start()
         put_columns(j, heads, sums)
 
-    stream(proto_source(idx[0], protos), buf, sem, columns // BN, step)
+    stream(proto_source(idx[0], protos), buf, sem, steps, step)
+    for j in (steps - 2, steps - 1):
+        leave(j, j % 2).wait()
 
 
 def teacher_pass(idx, own, other, protos, crops, copies):
@@ -183,7 +201,13 @@
         [array((rows, columns), BF16), array((copies, 2 * columns // 128, 128))],
         [idx, own, other, protos],
         "svvh",
-        scratch=[pltpu.VMEM((rows, width), BF16)] + proto_scratch(width),
+        "hv",
+        scratch=[
+            pltpu.VMEM((rows, width), BF16),
+            pltpu.VMEM((2, rows, BN), BF16),
+            pltpu.SemaphoreType.DMA((2,)),
+        ]
+        + proto_scratch(width),
         flops=2 * rows * width * columns,
         traffic=2 * rows * columns,
     )
@@ -229,14 +253,37 @@
     )
 
 
-def sum_rows(crops, expo, colscale, out):
+def row_copies(source, dest, sems):
+    return [
+        pltpu.make_async_copy(
+            source.at[pl.ds(128 * i, 128), :], dest.at[pl.ds(128 * i, 128), :], sems.at[i]
+        )
+        for i in range(source.shape[0] // 128)
+    ]
+
+
+def column_copies(source, dest, sems):
+    return [
+        pltpu.make_async_copy(
+            source.at[:, pl.ds(BN * j, BN)], dest.at[:, pl.ds(BN * j, BN)], sems.at[j]
+        )
+        for j in range(source.shape[1] // BN)
+    ]
+
+
+def expo_scratch(expo, blocks):
+    return [pltpu.VMEM(expo.shape, BF16), pltpu.SemaphoreType.DMA((blocks,))]
+
+
+def sum_rows(crops, expo, copies_in, colscale, out):
     copies = out.shape[0]
     rows, columns = expo.shape
     per_head = columns // 128
 
-    def block(i, _):
-        head = jnp.where(i < 2 * crops // 128, 0, 1)
-        at = pl.multiple_of(i * 128, 128)
+    for i in range(rows // 128):
+        copies_in[i].wait()
+        head = 0 if i < 2 * crops // 128 else 1
+        at = 128 * i
 
         def chunk(k, acc):
             e = expo[pl.ds(at, 128), pl.ds(pl.multiple_of(k * 128, 128), 128)].astype(F32)
@@ -244,21 +291,20 @@
 
         acc = lax.fori_loop(0, per_head, chunk, jnp.zeros((128, 128), F32), unroll=8)
         sums = jnp.sum(jnp.transpose(acc), axis=0, keepdims=True)
-        out[:, pl.ds(i, 1), :] = jnp.broadcast_to(sums[None], (copies, 1, 128))
-        return 0
-
-    lax.fori_loop(0, rows // 128, block, 0)
+        out[:, i : i + 1, :] = jnp.broadcast_to(sums[None], (copies, 1, 128))
 
 
 def row_kernel(crops, extra, expo, colparts, *refs):
+    out, colscale, buf, sems = refs[-4:]
+    copies_in = row_copies(expo, buf, sems)
+    for copy in copies_in:
+        copy.start()
     if extra:
-        total, out, colscale = refs
+        total = refs[0]
         count = total.shape[0]
         out[:, count:, :] = jnp.broadcast_to(total[...][None], (out.shape[0], count, 128))
-    else:
-        out, colscale = refs
     colscale[...] = 1.0 / jnp.sum(colparts[...], axis=0)
-    sum_rows(crops, expo, colscale, out)
+    sum_rows(crops, buf, copies_in, colscale, out)
 
 
 def row_pass(expo, colparts, total, crops, copies):
@@ -268,43 +314,52 @@
         functools.partial(row_kernel, crops, extra),
         array((copies, rows // 128 * (2 if extra else 1), 128)),
         [expo, colparts] + ([total] if extra else []),
-        "vvv" if extra else "vv",
-        scratch=[pltpu.VMEM((2 * columns // 128, 128), F32)],
+        "hvv" if extra else "hv",
+        scratch=[pltpu.VMEM((2 * columns // 128, 128), F32)] + expo_scratch(expo, rows // 128),
         flops=2 * rows * columns,
         traffic=2 * rows * columns,
     )
 
 
-def last_row_kernel(crops, idx, expo, colparts, protos, out, target, colscale, buf, sem):
+def target_kernel(crops, idx, expo, colparts, protos, mine, theirs, target, colscale, ebuf, esem, buf, sem):
     rows, columns = expo.shape
+    steps = columns // BN
+    copies_in = column_copies(expo, ebuf, esem)
+    for copy in copies_in:
+        copy.start()
     colscale[...] = 1.0 / jnp.sum(colparts[...], axis=0)
     target[...] = jnp.zeros_like(target)
 
     def step(j, block):
         wnorm = unit_cols(block[...])[0]
         at = pl.multiple_of(j * BN, BN)
+        pltpu.make_async_copy(
+            expo.at[:, pl.ds(at, BN)], ebuf.at[:, pl.ds(at, BN)], esem.at[j]
+        ).wait()
         for head, (first, last) in enumerate(((0, 2 * crops), (2 * crops, rows))):
             w = (wnorm * get_columns(j, head, colscale)).astype(BF16)
             target[first:last, :] += lax.dot_general(
-                expo[first:last, pl.ds(at, BN)],
+                ebuf[first:last, pl.ds(at, BN)],
                 w,
                 (((1,), (1,)), ((), ())),
                 preferred_element_type=F32,
             )
 
-    stream(proto_source(idx[0], protos), buf, sem, columns // BN, step)
-    sum_rows(crops, expo, colscale, out)
-
-
-def last_row_pass(idx, expo, colparts, protos, crops, copies):
+    stream(proto_source(idx[0], protos), buf, sem, steps, step)
+    part_rows(crops, idx, target, mine, theirs)
+
+
+def target_pass(idx, expo, colparts, protos, crops):
     rows, columns = expo.shape
     width = protos.shape[0]
     return call(
-        functools.partial(last_row_kernel, crops),
-        [array((copies, rows // 128, 128)), array((rows, width))],
+        functools.partial(target_kernel, crops),
+        [array((rows // 2, width)), array((rows // 2, width))],
         [idx, expo, colparts, protos],
-        "svvh",
-        scratch=[pltpu.VMEM((2 * columns // 128, 128), F32)] + proto_scratch(width),
+        "shvh",
+        scratch=[pltpu.VMEM((rows, width), F32), pltpu.VMEM((2 * columns // 128, 128), F32)]
+        + expo_scratch(expo, columns // BN)
+        + proto_scratch(width),
         flops=2 * rows * columns * width,
         traffic=2 * rows * columns,
     )
@@ -320,16 +375,20 @@
     return jnp.concatenate(parts, axis=0).astype(BF16)
 
 
-def column_kernel(crops, expo, rowparts, out):
+def column_kernel(crops, expo, rowparts, out, buf, sems):
     rows, columns = expo.shape
+    copies_in = column_copies(expo, buf, sems)
+    for copy in copies_in:
+        copy.start()
     scale = line_up(1.0 / jnp.sum(rowparts[:, : rows // 128, :], axis=0))
     spans = [(0, 2 * crops), (2 * crops, rows)]
     lefts = [split3(scale[:, first:last]) for first, last in spans]
     for j in range(columns // BN):
+        copies_in[j].wait()
         heads = []
         for left, (first, last) in zip(lefts, spans):
             sums = jnp.dot(
-                left, expo[first:last, j * BN : (j + 1) * BN], preferred_element_type=F32
+                left, buf[first:last, j * BN : (j + 1) * BN], preferred_element_type=F32
             )
             heads.append(sums[0:1, :] + sums[1:2, :] + sums[2:3, :])
         put_columns(j, heads, out)
@@ -341,7 +400,8 @@
         functools.partial(column_kernel, crops),
         array((copies, 2 * columns // 128, 128)),
         [expo, rowparts],
-        "vv",
+        "hv",
+        scratch=expo_scratch(expo, columns // BN),
         flops=2 * rows * columns,
         traffic=2 * rows * columns,
     )
@@ -369,27 +429,44 @@
         body(step // ny, step % ny, buf.at[step % 2])
 
 
-def wide_teacher_kernel(ny, crops, idx, own, other, protos, expo_d, expo_i, w, wbuf, buf, sem, wsem):
+def wide_teacher_kernel(ny, crops, idx, own, other, protos, expo_d, expo_i, w, wbuf, out, osem, buf, sem, wsem):
     half = buf.shape[1]
     rest = half - crops
     fetch = pltpu.make_async_copy(part_source(idx, ny, protos), wbuf, wsem)
     fetch.start()
     fetch.wait()
     w[...] = unit_cols(wbuf[...])[0].astype(BF16)
+    leaving = []
 
     def body(side, y, ref):
         place = 2 * y + jnp.where(idx[0] == side, 0, 1)
+        slot = len(leaving) % 2
+        if len(leaving) >= 2:
+            for copy in leaving[-2]:
+                copy.wait()
         feats = ref[...].astype(BF16)
         for start in range(0, half, 128):
             score = jnp.dot(feats[start : start + 128, :], w[...], preferred_element_type=F32)
             e = jnp.exp2(score * (LOG2E / TEACHER_TEMP)).astype(BF16)
-            if start < crops:
-                expo_d[pl.ds(pl.multiple_of(place * crops + start, 128), 128), :] = e
-            else:
-                at = pl.multiple_of(place * rest + start - crops, 128)
-                expo_i[pl.ds(at, 128), :] = e
+            out[slot, start : start + 128, :] = e
+        at_d = pl.multiple_of(place * crops, 128)
+        at_i = pl.multiple_of(place * rest, 128)
+        copies = (
+            pltpu.make_async_copy(
+                out.at[slot, pl.ds(0, crops), :], expo_d.at[pl.ds(at_d, crops), :], osem.at[slot, 0]
+            ),
+            pltpu.make_async_copy(
+                out.at[slot, pl.ds(crops, rest), :], expo_i.at[pl.ds(at_i, rest), :], osem.at[slot, 1]
+            ),
+        )
+        for copy in copies:
+            copy.start()
+        leaving.append(copies)
 
     stream_rows(ny, 0, half, own, other, buf, sem, body)
+    for copies in leaving[-2:]:
+        for copy in copies:
+            copy.wait()
 
 
 def wide_teacher_pass(idx, own, other, protos, crops):
@@ -401,9 +478,12 @@
         [array((2 * ny * crops, part), BF16), array((2 * ny * (half - crops), part), BF16)],
         [idx, own, other, protos],
         "shhh",
+        "hh",
         scratch=[
             pltpu.VMEM((width, part), BF16),
             pltpu.VMEM((width, part), BF16),
+            pltpu.VMEM((2, half, part), BF16),
+            pltpu.SemaphoreType.DMA((2, 2)),
             pltpu.VMEM((2, half, width), F32),
             pltpu.SemaphoreType.DMA((2,)),
             pltpu.SemaphoreType.DMA,
@@ -477,10 +557,15 @@
     )
 
 
-def weight_kernel(ny, crops, idx, prob, wnorm, turned_d, turned_i, expo_d, expo_i, colparts, rowparts, out, left_d, left_i, scales, rowscale):
+def weight_kernel(ny, crops, idx, prob, wnorm, turned_d, turned_i, expo_d, expo_i, colparts, rowparts, out, left_d, left_i, scales, rowscale, buf_d, buf_i, sems_d, sems_i):
     copies, _, _ = out.shape
     width, part = prob.shape
     own = width // copies
+    copies_d = column_copies(expo_d, buf_d, sems_d)
+    copies_i = column_copies(expo_i, buf_i, sems_i)
+    for pair in zip(copies_d, copies_i):
+        for copy in pair:
+            copy.start()
     group = rowparts.shape[0] // ny
     sub = rowparts.shape[1]
     scales[...] = GRAD_SCALE / jnp.sum(colparts[...], axis=0)
@@ -506,7 +591,9 @@
     for at in range(0, part, BN):
         span = slice(at, at + BN)
         wsum = prob[:, span]
-        for head, (left, expo) in enumerate(((left_d, expo_d), (left_i, expo_i))):
+        copies_d[at // BN].wait()
+        copies_i[at // BN].wait()
+        for head, (left, expo) in enumerate(((left_d, buf_d), (left_i, buf_i))):
             target = jnp.dot(left[...], expo[:, span], preferred_element_type=F32)
             base = head * per_head + first + at // 128
             line = [scales[pl.ds(base + t, 1), :] for t in range(BN // 128)]
@@ -531,12 +618,16 @@
         functools.partial(weight_kernel, ny, crops),
         array((copies, lines, 128)),
         [idx, prob, wnorm, *turned, *expo, colparts, rowparts],
-        "svvvvvvvv",
+        "svvvvhhvv",
         scratch=[
             pltpu.VMEM(turned[0].shape, BF16),
             pltpu.VMEM(turned[1].shape, BF16),
             pltpu.VMEM(colparts.shape[1:], F32),
             pltpu.VMEM((ny * rowparts.shape[1], 128), F32),
+            pltpu.VMEM(expo[0].shape, BF16),
+            pltpu.VMEM(expo[1].shape, BF16),
+            pltpu.SemaphoreType.DMA((part // BN,)),
+            pltpu.SemaphoreType.DMA((part // BN,)),
         ],
         flops=2 * rows * width * part,
         traffic=2 * rows * part,
@@ -615,10 +706,6 @@
     part_rows(crops, idx, buf, mine, theirs)
 
 
-def plain_kernel(crops, idx, mix, mine, theirs):
-    part_rows(crops, idx, mix, mine, theirs)
-
-
 def part_rows(crops, idx, buf, mine, theirs):
     rest = mine.shape[0] - crops
     for side, ref in ((idx[0], mine), (1 - idx[0], theirs)):
@@ -628,19 +715,16 @@
 
 def part_pass(idx, mix, totals, crops):
     rows, width = mix.shape
-    shapes = [array((rows // 2, width)), array((rows // 2, width))]
-    if totals is None:
-        return call(functools.partial(plain_kernel, crops), shapes, [idx, mix], "sv")
     return call(
         functools.partial(scaled_kernel, crops),
-        shapes,
+        [array((rows // 2, width)), array((rows // 2, width))],
         [idx, mix, totals],
         "svv",
         scratch=[pltpu.VMEM((rows, width), F32)],
     )
 
 
-def pack_kernel(nz, crops, mine, came, out):
+def pack_rows(nz, crops, mine, came, out):
     half = mine.shape[0]
     chunk = half // nz
     share = crops // nz
@@ -650,48 +734,117 @@
             out[dst : dst + size, :] = mine[src : src + size, :] + came[src : src + size, :]
 
 
-def pack_pass(mine, came, nz, crops):
-    return call(functools.partial(pack_kernel, nz, crops), array(mine.shape), [mine, came], "vv")
-
-
-def feature_kernel(nz, ny, crops, pair, patches, idx, mask, rowparts, *refs):
-    count = 4 if pair else 2
-    pieces = refs[:count]
-    all_crops, all_rows, crop_out, patch_out, masked_rows, dense, scale, crop_rows = refs[count:]
-    z = idx[1]
-    masked = mask.shape[1]
-    crop_share = crop_out.shape[0]
-    share = patch_out.shape[0]
-    crop_at = pl.multiple_of(z * crop_share, 16)
-    patch_at = pl.multiple_of(z * share, 128)
-    rest = pieces[0].shape[0] - crop_share
+def halve(idx, bit, total, keep, send):
+    size = total.shape[0] // 2
+    side = lax.rem(idx[1] // bit, 2)
+    keep[...] = total[pl.ds(pl.multiple_of(side * size, 64), size), :]
+    send[...] = total[pl.ds(pl.multiple_of((1 - side) * size, 64), size), :]
+
+
+def pack_half_kernel(nz, crops, idx, mine, came, keep, send, total):
+    pack_rows(nz, crops, mine, came, total)
+    halve(idx, nz // 2, total, keep, send)
+
+
+def pack_half_pass(idx, mine, came, nz, crops):
+    rows, width = mine.shape
+    return call(
+        functools.partial(pack_half_kernel, nz, crops),
+        [array((rows // 2, width)), array((rows // 2, width))],
+        [idx, mine, came],
+        "svv",
+        scratch=[pltpu.VMEM((rows, width), F32)],
+    )
+
+
+def fold_kernel(bit, idx, mine, came, keep, send, total):
+    total[...] = mine[...] + came[...]
+    halve(idx, bit, total, keep, send)
+
+
+def fold_pass(idx, mine, came, bit):
+    rows, width = mine.shape
+    return call(
+        functools.partial(fold_kernel, bit),
+        [array((rows // 2, width)), array((rows // 2, width))],
+        [idx, mine, came],
+        "svv",
+        scratch=[pltpu.VMEM((rows, width), F32)],
+    )
+
+
+def add_kernel(mine, came, out):
+    out[...] = mine[...] + came[...]
+
+
+def add_pass(mine, came):
+    return call(add_kernel, array(mine.shape), [mine, came], "vv")
+
+
+def mix_kernel(nz, ny, crops, bit, idx, rowparts, target, target_came, prob, prob_came, *refs):
+    scale = refs[-1]
+    total = refs[-2]
     sub = rowparts.shape[1]
     group = rowparts.shape[0] // ny
     cd = crops // 128
     ci = sub // 2 - cd
-    sums = jnp.sum(rowparts[pl.ds(idx[3] * group, group), :, :], axis=0)
-    row = GRAD_SCALE / sums
+    row = GRAD_SCALE / jnp.sum(rowparts[pl.ds(idx[3] * group, group), :, :], axis=0)
     low = idx[0] == 0
     for t in range(cd + ci):
         a, b = (t, cd + t) if t < cd else (cd + t, cd + ci + t)
         line = jnp.where(low, row[a : a + 1, :], row[b : b + 1, :])
         scale[128 * t : 128 * (t + 1), :] = spread_row(line)
-    wide = pieces[0].shape[1] // 128
-
-    def fgrad(prob, target, at, size):
-        r = scale[pl.ds(pl.multiple_of(at, 16), size), :]
-        return prob - target * jnp.concatenate([r] * wide, axis=1)
-
-    crop_rows[...] = fgrad(
-        pieces[0][:crop_share, :], pieces[1][:crop_share, :], z * crop_share, crop_share
-    )
-    spots = ((z, 0),) if not pair else ((z, 0), (z + 1 - 2 * lax.rem(z, 2), 2))
-    for place, which in spots:
-        value = fgrad(
-            pieces[which][crop_share:, :], pieces[which + 1][crop_share:, :], crops + place * rest, rest
-        )
-        at = pl.multiple_of(lax.rem(place, 2) * rest, 8) if pair else 0
-        masked_rows[pl.ds(at, rest), :] = value
+    rows, width = target.shape
+    here = nz // 2
+    chunk = rows // here
+    share = crops // nz
+    rest = chunk - share
+    first = idx[1] // here * here
+    for k in range(here):
+        z = first + k
+        for at, src, size in ((0, z * share, share), (share, crops + z * rest, rest)):
+            r = scale[pl.ds(pl.multiple_of(src, 16), size), :]
+            span = slice(k * chunk + at, k * chunk + at + size)
+            value = target[span, :] + target_came[span, :]
+            total[span, :] = (
+                prob[span, :]
+                + prob_came[span, :]
+                - value * jnp.concatenate([r] * (width // 128), axis=1)
+            )
+    if bit:
+        halve(idx, bit, total, refs[0], refs[1])
+
+
+def mix_pass(idx, rowparts, target, target_came, prob, prob_came, nz, ny, crops, bit):
+    rows, width = target.shape
+    half = rowparts.shape[1] // 2 * 128
+    shapes = [array((rows // 2, width))] * 2 if bit else array((rows, width))
+    return call(
+        functools.partial(mix_kernel, nz, ny, crops, bit),
+        shapes,
+        [idx, rowparts, target, target_came, prob, prob_came],
+        "svvvvv",
+        scratch=([pltpu.VMEM((rows, width), F32)] if bit else []) + [pltpu.VMEM((half, 128), F32)],
+    )
+
+
+def feature_kernel(pair, patches, idx, mask, *refs):
+    pieces = refs[: 2 if pair else 1]
+    all_crops, all_rows, crop_out, patch_out, masked_rows, dense, total = refs[len(pieces) :]
+    z = idx[1]
+    masked = mask.shape[1]
+    crop_share = crop_out.shape[0]
+    share = patch_out.shape[0]
+    total[...] = pieces[0][...] + pieces[1][...] if pair else pieces[0][...]
+    chunk = total.shape[0] // len(pieces)
+    rest = chunk - crop_share
+    for side in range(len(pieces)):
+        masked_rows[side * rest : (side + 1) * rest, :] = total[
+            side * chunk + crop_share : (side + 1) * chunk, :
+        ]
+    crop_at = pl.multiple_of(z * crop_share, 16)
+    patch_at = pl.multiple_of(z * share, 128)
+    start = pl.multiple_of(lax.rem(z, len(pieces)) * chunk, 16)
     dense[...] = jnp.zeros_like(dense)
     first_row = z * share
     first_image = first_row // patches
@@ -715,29 +868,30 @@
         u = xf * inv
         return (d - u * jnp.sum(u * d, axis=-1, keepdims=True)) * inv
 
-    crop_out[...] = back(all_crops[pl.ds(crop_at, crop_share), :], crop_rows[...])
+    crop_out[...] = back(all_crops[pl.ds(crop_at, crop_share), :], total[pl.ds(start, crop_share), :])
     patch_out[...] = back(all_rows[pl.ds(patch_at, share), :], dense[...])
 
 
-def feature_pass(idx, mask, rowparts, pieces, all_crops, all_rows, nz, ny, patches):
+def feature_pass(idx, mask, pieces, all_crops, all_rows, nz, patches):
     crops, width = all_crops.shape
     crop_share = crops // nz
     share = all_rows.shape[0] // nz
-    pair = len(pieces) == 4
-    count = len(pieces) // 2 * (pieces[0].shape[0] - crop_share)
-    half = rowparts.shape[1] // 2 * 128
-    return call(
-        functools.partial(feature_kernel, nz, ny, crops, pair, patches),
+    rows = pieces[0].shape[0]
+    return call(
+        functools.partial(feature_kernel, len(pieces) == 2, patches),
         [array((crop_share, width)), array((share, width))],
-        [idx, mask, rowparts, *pieces, all_crops, all_rows],
-        "ssv" + "v" * len(pieces) + "vv",
+        [idx, mask, *pieces, all_crops, all_rows],
+        "ss" + "v" * len(pieces) + "vv",
         scratch=[
-            pltpu.VMEM((count, width), F32),
+            pltpu.VMEM((rows - len(pieces) * crop_share, width), F32),
             pltpu.VMEM((share, width), F32),
-            pltpu.VMEM((half, 128), F32),
-            pltpu.VMEM((crop_share, width), F32),
+            pltpu.VMEM((rows, width), F32),
         ],
     )
+
+
+def tie(*values):
+    return lax.optimization_barrier(values)
 
 
 def shifted(n, s):
@@ -765,49 +919,74 @@
     own = prep(teacher_crops, teacher_patches, student_crops, student_patches, patch_mask)
     other = lax.ppermute(own, "c", swap)
     all_own = lax.all_gather(own, "y")
-    all_other = lax.ppermute(all_own, "c", swap)
-
     expo, sums = teacher_pass(idx, own, other, teacher_protos, crops, nx * ny)
     sub = 2 * (crops + images * masked) // 128
-    for step in range(ITERS):
-        colparts = lax.all_to_all(sums, ("x", "y"), 0, 0)
-        if step == 0:
-            total, mix = student_pass(idx, own, other, student_protos, crops)
-        if step < ITERS - 1:
-            sums = row_pass(expo, colparts, total if step == 0 else None, crops, 2 * nz)
-            rowparts = lax.all_to_all(sums, ("c", "z"), 0, 0)
-            if step == 0:
-                totals = jnp.sum(rowparts[:, sub:, :], axis=0)
-            sums = column_pass(expo, rowparts, crops, nx * ny)
-        else:
-            sums, target = last_row_pass(
-                idx, expo, colparts, student_protos, crops, 2 * nz * ny
-            )
-            rowparts = lax.all_to_all(sums, ("y", "c", "z"), 0, 0)
-
+
+    pair = student_patches.shape[0] // nz < patches
+
+    def across(value, bit):
+        return lax.ppermute(value, "z", [(i, i ^ bit) for i in range(nz)])
+
+    colparts = lax.all_to_all(sums, ("x", "y"), 0, 0)
+    total, mix = student_pass(idx, own, other, student_protos, crops)
+    winv = norm_pass(student_protos)
+    colparts, winv = tie(colparts, winv)
+    sums = row_pass(expo, colparts, total, crops, 2 * nz)
+    rowparts = lax.all_to_all(sums, ("c", "z"), 0, 0)
+    totals = jnp.sum(rowparts[:, sub:, :], axis=0)
+    sums = column_pass(expo, rowparts, crops, nx * ny)
+
+    colparts = lax.all_to_all(sums, ("x", "y"), 0, 0)
+    totals, _ = tie(totals, sums)
     all_totals = [totals] + [lax.ppermute(totals, "y", shifted(ny, s)) for s in range(1, ny)]
+    mine, theirs = part_pass(idx, mix, totals, crops)
+    p_keep, p_send = pack_half_pass(idx, mine, lax.ppermute(theirs, "c", swap), nz, crops)
+    colparts, p_send, *all_totals = tie(colparts, p_send, *all_totals)
+    p_came = across(p_send, nz // 2)
+    sums = row_pass(expo, colparts, None, crops, 2 * nz)
+    all_own, sums = tie(all_own, sums)
+    all_other = lax.ppermute(all_own, "c", swap)
+    rowparts = lax.all_to_all(sums, ("c", "z"), 0, 0)
+    sums = column_pass(expo, rowparts, crops, nx * ny)
+
+    colparts = lax.all_to_all(sums, ("x", "y"), 0, 0)
+    all_own, all_other, _ = tie(all_own, all_other, sums)
     wide_expo = wide_teacher_pass(idx, all_own, all_other, teacher_protos, crops)
+    colparts, p_came, *wide_expo = tie(colparts, p_came, *wide_expo)
+    target_mine, target_theirs = target_pass(idx, expo, colparts, student_protos, crops)
+    colparts, target_theirs = tie(colparts, target_theirs)
+    sums = row_pass(expo, colparts, None, crops, 2 * nz * ny)
+    target_came = lax.ppermute(target_theirs, "c", swap)
+    keep, send = pack_half_pass(idx, target_mine, target_came, nz, crops)
+    sums, send = tie(sums, send)
+    rowparts = lax.all_to_all(sums, ("y", "c", "z"), 0, 0)
+    came = across(send, nz // 2)
+    all_own, all_other, _ = tie(all_own, all_other, sums)
     prob, wnorm, *turned = wide_student_pass(
         idx, all_own, all_other, student_protos, all_totals, crops
     )
-    winv = norm_pass(student_protos)
+    prob, came = tie(prob, came)
     outgoing = weight_pass(
         idx, prob, wnorm, turned, wide_expo, colparts, rowparts, crops, ny, nx * ny * 2
     )
     parts = lax.all_to_all(outgoing, ("x", "y", "c"), 0, 0)
     proto_grad = proto_pass(idx, parts, student_protos, winv, nx, ny)
-
-    reduced = []
-    for value, scale in ((mix, totals), (target, None)):
-        mine, theirs = part_pass(idx, value, scale, crops)
-        packed = pack_pass(mine, lax.ppermute(theirs, "c", swap), nz, crops)
-        reduced.append(lax.psum_scatter(packed, "z", scatter_dimension=0, tiled=True))
-    pieces = list(reduced)
-    if student_patches.shape[0] // nz < patches:
-        pair = [(i, i ^ 1) for i in range(nz)]
-        pieces += [lax.ppermute(r, "z", pair) for r in reduced]
+    bits = [nz >> k for k in range(2, nz.bit_length()) if nz >> k > (1 if pair else 0)]
+    total = mix_pass(
+        idx, rowparts, keep, came, p_keep, p_came, nz, ny, crops, bits[0] if bits else 0
+    )
+    for i, bit in enumerate(bits):
+        keep, send = total
+        came = across(send, bit)
+        if i + 1 < len(bits):
+            total = fold_pass(idx, keep, came, bits[i + 1])
+        else:
+            total = add_pass(keep, came)
+    pieces = [total]
+    if pair:
+        pieces.append(across(total, 1))
     crop_grad, patch_grad = feature_pass(
-        idx, patch_mask, rowparts, pieces, student_crops, student_patches, nz, ny, patches
+        idx, patch_mask, pieces, student_crops, student_patches, nz, patches
     )
     return (proto_grad, crop_grad, patch_grad)
 

time: 309 us -> 253 us (0.82)
  waiting for transfers between devices: 110 us -> 31.7 us
  Pallas kernels: 66 us -> 118 us
  local copies, waits for them, and re-layouts: 47.5 us -> 8.21 us
  starting transfers between devices: 32.9 us -> 47.4 us
  blocking collectives: 33.4 us -> 28.3 us
    all_gather x1, waiting for transfers between devices: 53.6 us -> 0.02 us  [local(): all_own = lax.all_gather(own, 'y')]
    pallas_call x17 -> x19, Pallas kernels: 65.3 us -> 112 us  [call(): pl.pallas_call(kernel, out_shape=out_shape, out_specs=out_specs, in_specs...]
    unnamed x66 -> x34, local copies, waits for them, and re-layouts: 47.5 us -> 8.21 us
    reduce_scatter x2 -> x0, waiting for transfers between devices: 37.4 us -> none  [local(): lax.psum_scatter(packed, 'z', scatter_dimension=0, tiled=True)]
    ppermute x4 -> x6, waiting for transfers between devices: 0.3 us -> 25.1 us  [the longest x4 25.1 us: across(): return lax.ppermute(value, 'z', [(i, i ^ bit) for i in range(nz)])]
    all_to_all x1 -> x0, blocking collectives: 17.9 us -> none  [local(): colparts = lax.all_to_all(sums, ('x', 'y'), 0, 0)]
    all_to_all x1 -> x2, blocking collectives: 15.5 us -> 28.3 us  [local(): rowparts = lax.all_to_all(sums, ('c', 'z'), 0, 0)]
    ppermute x4 -> x6, starting transfers between devices: 2.08 us -> 10.5 us  [the longest x4 10.4 us: across(): return lax.ppermute(value, 'z', [(i, i ^ bit) for i in range(nz)])]
  transfers between devices with their start and end apart: 17 -> 17, of which waited for: 7 -> 8; matrix products, arithmetic and copies ran while one was open for 0% -> 1% of each run, Pallas kernels for 21% -> 36%
where the time goes in v4:
time: 253 us; the launch traced here: 249 us
  Pallas kernels  118 us (47%)
  starting transfers between devices  47.4 us (19%)
  waiting for transfers between devices  31.7 us (13%)
  blocking collectives  28.3 us (11%)
  between operations  14.3 us (6%)
  local copies, waits for them, and re-layouts  8.21 us (3%)
    pallas_call x19, Pallas kernels, call(): pl.pallas_call(kernel, out_shape=out_shape, out_specs=out_specs, in_specs...  112 us
    all_to_all x2, blocking collectives, local(): rowparts = lax.all_to_all(sums, ('c', 'z'), 0, 0)  28.3 us
    ppermute x4, waiting for transfers between devices, across(): return lax.ppermute(value, 'z', [(i, i ^ bit) for i in range(nz)])  25.1 us
    all_to_all x3, starting transfers between devices, local(): colparts = lax.all_to_all(sums, ('x', 'y'), 0, 0)  17.8 us
    ppermute x4, starting transfers between devices, across(): return lax.ppermute(value, 'z', [(i, i ^ bit) for i in range(nz)])  10.4 us
    unnamed x34, local copies, waits for them, and re-layouts  8.21 us
    all_to_all x1, starting transfers between devices, local(): parts = lax.all_to_all(outgoing, ('x', 'y', 'c'), 0, 0)  7.26 us
    all_to_all x1, starting transfers between devices, local(): rowparts = lax.all_to_all(sums, ('y', 'c', 'z'), 0, 0)  6.7 us
  transfers between devices with their start and end apart: 17, of which 8 were waited for; matrix products, arithmetic and copies ran while one was open for 1% of the time, Pallas kernels for 36%

profile of v4, /device:TPU:32, one launch (start us, length us, event | category | flops | bytes accessed | tf_op | source)
XLA Modules:
  0.0 248.8 jit_solution(3294399178562914864)
XLA Ops:
  7.2 3.5 %shard_map.94.own = f32[1024,256]{1,0:T(8,128)} custom-call(bf16[128,256]{1,0:T(8,128)(2,1)} %tcrops.1, bf16[1024,256]{1,0:T(8,128)(2,1)} %tpatch.1, bf16[128,256]{1,0:T(8,128)(2,1)} %refs_2_.1, bf16[1024,256]{1,0:T(8,128)(2,1)} %refs_3_.1, s32[4,96]{1,0:T(4,128)} %mask.3), custom_call_target="tpu_custom_call" | custom-call | tf_op jit(solution)/shard_map/pallas_call | solution.py:33
  14.7 11.3 %shard_map.95 = (bf16[1024,4096]{1,0:T(8,128)(2,1)}, f32[16,64,128]{2,1,0:T(8,128)}) custom-call(s32[4]{0:T(128)} %pad_add_fusion.idx, f32[1024,256]{1,0:T(8,128)} %shard_map.94.own, f32[1024,256]{1,0:T(8,128)} %copy-done.12, bf16[256,8192]{1,0:T(8,128)(2,1)} %protos.10), custom_call_target="tpu_custom_call" | custom-call | flops 2147483648 | bytes 8388608 | tf_op jit(solution)/shard_map/pallas_call | solution.py:33
  26.0 7.0 %all-to-all-start = ((f32[16,64,128]{2,1,0:T(8,128)}), f32[16,64,128]{2,1,0:T(8,128)S(1)}, u32[]{:S(2)}, u32[]{:S(2)}) async-start(f32[16,64,128]{2,1,0:T(8,128)} %get-tuple-element.51), calls=%async_computation | async-start | bytes 1048576 | tf_op jit(solution)/shard_map/all_to_all | solution.py:930
  33.1 5.7 %shard_map.96.winv = f32[1,8192]{1,0:T(1,128)} custom-call(bf16[256,8192]{1,0:T(8,128)(2,1)} %protos.13), custom_call_target="tpu_custom_call" | custom-call | flops 6291456 | bytes 4194304 | tf_op jit(solution)/shard_map/pallas_call | solution.py:644
  38.8 11.4 %shard_map.97 = (f32[8,128]{1,0:T(8,128)}, f32[1024,256]{1,0:T(8,128)}) custom-call(s32[4]{0:T(128)} %pad_add_fusion.idx, f32[1024,256]{1,0:T(8,128)} %shard_map.94.own, f32[1024,256]{1,0:T(8,128)} %copy-done.12, bf16[256,8192]{1,0:T(8,128)(2,1)} %protos.13), custom_call_target="tpu_custom_call" | custom-call | flops 4294967296 | bytes 2097152 | tf_op jit(solution)/shard_map/pallas_call | solution.py:33
  51.0 6.2 %shard_map.98 = f32[16,16,128]{2,1,0:T(8,128)} custom-call(bf16[1024,4096]{1,0:T(8,128)(2,1)} %get-tuple-element.50.expo, f32[16,64,128]{2,1,0:T(8,128)} %copy-done.4, f32[8,128]{1,0:T(8,128)} %get-tuple-element.53.refs_0_), custom_call_target="tpu_custom_call" | custom-call | flops 8388608 | bytes 8388608 | tf_op jit(solution)/shard_map/pallas_call | solution.py:33
  57.2 16.9 %all_to_all.35.rowparts = f32[16,16,128]{2,1,0:T(8,128)} all-to-all(f32[16,16,128]{2,1,0:T(8,128)} %shard_map.98), channel_id=1, replica_groups=mesh['x'=4,'y'=4,'c'=2,'z'=8] {'c','z'}, dimensions={0} | all-to-all | bytes 262144 | tf_op jit(solution)/shard_map/all_to_all | solution.py:935
  74.1 5.6 %shard_map.99 = f32[16,64,128]{2,1,0:T(8,128)} custom-call(bf16[1024,4096]{1,0:T(8,128)(2,1)} %get-tuple-element.50.expo, f32[16,16,128]{2,1,0:T(8,128)} %all_to_all.35.rowparts), custom_call_target="tpu_custom_call" | custom-call | flops 8388608 | bytes 8388608 | tf_op jit(solution)/shard_map/pallas_call | solution.py:33
  80.3 2.5 %shard_map.100 = (f32[512,256]{1,0:T(8,128)}, f32[512,256]{1,0:T(8,128)}) custom-call(s32[4]{0:T(128)} %pad_add_fusion.idx, f32[1024,256]{1,0:T(8,128)} %get-tuple-element.54.mix, f32[8,128]{1,0:T(8,128)} %slice_reduce_fusion.totals.refs_0_), custom_call_target="tpu_custom_call" | custom-call | tf_op jit(solution)/shard_map/pallas_call | solution.py:33
  82.8 7.2 %all-to-all-start.2 = ((f32[16,64,128]{2,1,0:T(8,128)}), f32[16,64,128]{2,1,0:T(8,128)S(1)}, u32[]{:S(2)}, u32[]{:S(2)}) async-start(f32[16,64,128]{2,1,0:T(8,128)} %shard_map.99), calls=%async_computation.2 | async-start | bytes 1048576 | tf_op jit(solution)/shard_map/all_to_all | solution.py:939
  90.0 3.1 %collective-permute-start.4 = (f32[8,128]{1,0:T(8,128)}, f32[8,128]{1,0:T(8,128)S(1)}, u32[]{:S(2)}, u32[]{:S(2)}) collective-permute-start(f32[8,128]{1,0:T(8,128)} %slice_reduce_fusion.totals.refs_0_), channel_id=1, source_target_pairs={{0,48},{16,0},{32,16},{48,32},{1,49},{17,1},{33,17},{49,33},{2,50}... | collective-permute-start | bytes 12296 | tf_op jit(solution)/shard_map/ppermute | solution.py:941
  99.5 2.6 %all-to-all-done.2.colparts = f32[16,64,128]{2,1,0:T(8,128)S(1)} async-done(((f32[16,64,128]{2,1,0:T(8,128)}), f32[16,64,128]{2,1,0:T(8,128)S(1)}, u32[]{:S(2)}, u32[]{:S(2)}) %all-to-all-start.2) | async-done | bytes 524320 | tf_op jit(solution)/shard_map/all_to_all | solution.py:939
  103.0 6.2 %shard_map.102 = f32[16,8,128]{2,1,0:T(8,128)} custom-call(bf16[1024,4096]{1,0:T(8,128)(2,1)} %get-tuple-element.50.expo, f32[16,64,128]{2,1,0:T(8,128)} %copy-done.3), custom_call_target="tpu_custom_call" | custom-call | flops 8388608 | bytes 8388608 | tf_op jit(solution)/shard_map/pallas_call | solution.py:33
  109.3 11.4 %all_to_all.36.rowparts = f32[16,8,128]{2,1,0:T(8,128)} all-to-all(f32[16,8,128]{2,1,0:T(8,128)} %shard_map.102), channel_id=1, replica_groups=mesh['x'=4,'y'=4,'c'=2,'z'=8] {'c','z'}, dimensions={0} | all-to-all | bytes 131072 | tf_op jit(solution)/shard_map/all_to_all | solution.py:949
  120.7 5.5 %shard_map.103 = f32[16,64,128]{2,1,0:T(8,128)} custom-call(bf16[1024,4096]{1,0:T(8,128)(2,1)} %get-tuple-element.50.expo, f32[16,8,128]{2,1,0:T(8,128)} %all_to_all.36.rowparts), custom_call_target="tpu_custom_call" | custom-call | flops 8388608 | bytes 8388608 | tf_op jit(solution)/shard_map/pallas_call | solution.py:33
  126.2 3.6 %all-to-all-start.4 = ((f32[16,64,128]{2,1,0:T(8,128)}), f32[16,64,128]{2,1,0:T(8,128)S(1)}, u32[]{:S(2)}, u32[]{:S(2)}) async-start(f32[16,64,128]{2,1,0:T(8,128)} %shard_map.103), calls=%async_computation.4 | async-start | bytes 1048576 | tf_op jit(solution)/shard_map/all_to_all | solution.py:952
  131.3 9.2 %shard_map.104 = (bf16[1024,1024]{1,0:T(8,128)(2,1)}, bf16[3072,1024]{1,0:T(8,128)(2,1)}) custom-call(s32[4]{0:T(128)} %pad_add_fusion.idx, f32[4,1024,256]{2,1,0:T(8,128)} %bitcast.6, f32[4,1024,256]{2,1,0:T(8,128)} %collective-permute-done.5.other, bf16[256,8192]{1,0:T(8,128)(2,1)} %protos.10), custom_call_target="tpu_custom_call" | custom-call | flops 2147483648 | bytes 4194304 | tf_op jit(solution)/shard_map/pallas_call | solution.py:33
  140.5 6.9 %collective-permute-done.6.prob_came = f32[256,256]{1,0:T(8,128)S(1)} collective-permute-done((f32[256,256]{1,0:T(8,128)S(1)}, f32[256,256]{1,0:T(8,128)S(1)}, u32[]{:S(2)}, u32[]{:S(2)}) %collective-permute-start.6) | collective-permute-done | bytes 262176 | tf_op jit(solution)/shard_map/ppermute | solution.py:928
  148.2 11.4 %shard_map.105 = (f32[512,256]{1,0:T(8,128)}, f32[512,256]{1,0:T(8,128)}) custom-call(s32[4]{0:T(128)} %pad_add_fusion.idx, bf16[1024,4096]{1,0:T(8,128)(2,1)} %get-tuple-element.50.expo, f32[16,64,128]{2,1,0:T(8,128)} %copy-done, bf16[256,8192]{1,0:T(8,128)(2,1)} %protos.13), custom_call_target="tpu_custom_call" | custom-call | flops 2147483648 | bytes 8388608 | tf_op jit(solution)/shard_map/pallas_call | solution.py:33
  159.7 6.3 %shard_map.106 = f32[64,8,128]{2,1,0:T(8,128)} custom-call(bf16[1024,4096]{1,0:T(8,128)(2,1)} %get-tuple-element.50.expo, f32[16,64,128]{2,1,0:T(8,128)} %copy-done), custom_call_target="tpu_custom_call" | custom-call | flops 8388608 | bytes 8388608 | tf_op jit(solution)/shard_map/pallas_call | solution.py:33
  169.0 6.7 %all-to-all-start.5 = ((f32[64,8,128]{2,1,0:T(8,128)}), f32[64,8,128]{2,1,0:T(8,128)S(1)}, u32[]{:S(2)}, u32[]{:S(2)}) async-start(f32[64,8,128]{2,1,0:T(8,128)} %shard_map.106), calls=%async_computation.5 | async-start | bytes 524288 | tf_op jit(solution)/shard_map/all_to_all | solution.py:962
  175.7 4.8 %collective-permute-start.8 = (f32[256,256]{1,0:T(8,128)}, f32[256,256]{1,0:T(8,128)S(1)}, u32[]{:S(2)}, u32[]{:S(2)}) collective-permute-start(f32[256,256]{1,0:T(8,128)} %get-tuple-element.81), channel_id=1, source_target_pairs={{0,4},{1,5},{2,6},{3,7},{4,0},{5,1},{6,2},{7,3},{8,12},{9,13},{10,... | collective-permute-start | bytes 786440 | tf_op jit(solution)/shard_map/ppermute | solution.py:928
  180.5 9.9 %shard_map.108 = (f32[256,1024]{1,0:T(8,128)}, f32[256,1024]{1,0:T(8,128)}, bf16[256,1024]{1,0:T(8,128)(2,1)}, bf16[256,3072]{1,0:T(8,128)(2,1)}) custom-call(s32[4]{0:T(128)} %pad_add_fusion.idx, f32[4,1024,256]{2,1,0:T(8,128)} %bitcast.7, f32[4,1024,256]{2,1,0:T(8,128)} %collective-permute-done.5.other, bf16[256,8192]{1,0:T(8,128)(2,1)} %protos.13, ...), custom_call_target="tpu_custom_call" | custom-call | flops 4294967296 | bytes 4194304 | tf_op jit(solution)/shard_map/pallas_call | solution.py:33
  190.5 7.4 %collective-permute-done.8.target_came = f32[256,256]{1,0:T(8,128)S(1)} collective-permute-done((f32[256,256]{1,0:T(8,128)}, f32[256,256]{1,0:T(8,128)S(1)}, u32[]{:S(2)}, u32[]{:S(2)}) %collective-permute-start.8) | collective-permute-done | bytes 262176 | tf_op jit(solution)/shard_map/ppermute | solution.py:928
  198.7 8.3 %shard_map.109 = f32[32,72,128]{2,1,0:T(8,128)} custom-call(s32[4]{0:T(128)} %pad_add_fusion.idx, f32[256,1024]{1,0:T(8,128)} %get-tuple-element.82.prob, f32[256,1024]{1,0:T(8,128)} %get-tuple-element.83.wnorm, bf16[256,1024]{1,0:T(8,128)(2,1)} %get-tuple-element.84.turned_d, bf16[256,3072]{1,0:T(8,128)(2,1)} %get-tuple-element.85.turned_i, ...), custom_call_target="tpu_custom_call" | custom-call | flops 2147483648 | bytes 8388608 | tf_op jit(solution)/shard_map/pallas_call | solution.py:33
  207.0 7.3 %all-to-all-start.6 = ((f32[32,72,128]{2,1,0:T(8,128)}), f32[32,72,128]{2,1,0:T(8,128)S(1)}, u32[]{:S(2)}, u32[]{:S(2)}) async-start(f32[32,72,128]{2,1,0:T(8,128)} %shard_map.109), calls=%async_computation.6 | async-start | bytes 2359296 | tf_op jit(solution)/shard_map/all_to_all | solution.py:972
  214.3 2.2 shard_map.111
  216.5 6.9 %collective-permute-done.9.came = f32[128,256]{1,0:T(8,128)S(1)} collective-permute-done((f32[128,256]{1,0:T(8,128)}, f32[128,256]{1,0:T(8,128)S(1)}, u32[]{:S(2)}, u32[]{:S(2)}) %collective-permute-start.9) | collective-permute-done | bytes 131104 | tf_op jit(solution)/shard_map/ppermute | solution.py:928
  225.7 4.2 %collective-permute-start.10 = (f32[128,256]{1,0:T(8,128)}, f32[128,256]{1,0:T(8,128)S(1)}, u32[]{:S(2)}, u32[]{:S(2)}) collective-permute-start(f32[128,256]{1,0:T(8,128)} %shard_map.112.refs_0_), channel_id=1, source_target_pairs={{0,1},{1,0},{2,3},{3,2},{4,5},{5,4},{6,7},{7,6},{8,9},{9,8},{10,11... | collective-permute-start | bytes 393224 | tf_op jit(solution)/shard_map/ppermute | solution.py:928
  229.9 3.9 %collective-permute-done.10.refs_1_ = f32[128,256]{1,0:T(8,128)S(1)} collective-permute-done((f32[128,256]{1,0:T(8,128)}, f32[128,256]{1,0:T(8,128)S(1)}, u32[]{:S(2)}, u32[]{:S(2)}) %collective-permute-start.10) | collective-permute-done | bytes 131104 | tf_op jit(solution)/shard_map/ppermute | solution.py:928
  234.4 3.4 %shard_map.113 = (f32[16,256]{1,0:T(8,128)}, f32[128,256]{1,0:T(8,128)}) custom-call(s32[4]{0:T(128)} %pad_add_fusion.idx, s32[4,96]{1,0:T(4,128)} %mask.3, f32[128,256]{1,0:T(8,128)} %shard_map.112.refs_0_, f32[128,256]{1,0:T(8,128)} %copy-done.11, bf16[128,256]{1,0:T(8,128)(2,1)} %refs_2_.1, bf16[1024,256]{1,0:T(8,128)(2,1)} %refs_3_.1), custom_call_target="tpu_custom_call" | custom-call | tf_op jit(solution)/shard_map/pallas_call | solution.py:33
  238.8 3.1 %shard_map.110 = f32[8,8192]{1,0:T(8,128)} custom-call(s32[4]{0:T(128)} %pad_add_fusion.idx, f32[32,72,128]{2,1,0:T(8,128)} %copy-done.1, bf16[256,8192]{1,0:T(8,128)(2,1)} %protos.13, f32[1,8192]{1,0:T(1,128)} %shard_map.96.winv), custom_call_target="tpu_custom_call" | custom-call | tf_op jit(solution)/shard_map/pallas_call | solution.py:33
  (61 shorter events, 22.8 us)
Async XLA Ops:
  7.2 102.0 %all-gather.3.cloned.1.call-start = ((), (), s32[]{:S(2)}) async-start(), calls=%async_computation.7 | async-start | bytes 5242880 | tf_op jit(solution)/shard_map/all_gather | solution.py:921
  10.7 3.0 %collective-permute-start = (f32[1024,256]{1,0:T(8,128)}, f32[1024,256]{1,0:T(8,128)S(1)}, u32[]{:S(2)}, u32[]{:S(2)}) collective-permute-start(f32[1024,256]{1,0:T(8,128)} %shard_map.94.own), channel_id=1, source_target_pairs={{0,8},{8,0},{1,9},{9,1},{2,10},{10,2},{3,11},{11,3},{4,12},{12,4},... | collective-permute-start | bytes 3145736 | tf_op jit(solution)/shard_map/ppermute | solution.py:920
  13.7 1.0 copy-start.12
  26.0 24.2 %all-to-all-start = ((f32[16,64,128]{2,1,0:T(8,128)}), f32[16,64,128]{2,1,0:T(8,128)S(1)}, u32[]{:S(2)}, u32[]{:S(2)}) async-start(f32[16,64,128]{2,1,0:T(8,128)} %get-tuple-element.51), calls=%async_computation | async-start | bytes 1048576 | tf_op jit(solution)/shard_map/all_to_all | solution.py:930
  50.2 0.8 copy-start.4
  74.1 5.6 %copy-start.5 = (f32[16,16,128]{2,1,0:T(8,128)S(1)}, f32[16,16,128]{2,1,0:T(8,128)}, u32[]{:S(2)}) copy-start(f32[16,16,128]{2,1,0:T(8,128)} %all_to_all.35.rowparts) | copy-start | bytes 393220
  82.8 12.1 %collective-permute-start.1 = (f32[512,256]{1,0:T(8,128)}, f32[512,256]{1,0:T(8,128)S(1)}, u32[]{:S(2)}, u32[]{:S(2)}) collective-permute-start(f32[512,256]{1,0:T(8,128)} %get-tuple-element.57), channel_id=1, source_target_pairs={{0,8},{8,0},{1,9},{9,1},{2,10},{10,2},{3,11},{11,3},{4,12},{12,4},... | collective-permute-start | bytes 1572872 | tf_op jit(solution)/shard_map/ppermute | solution.py:943
  82.8 19.4 %all-to-all-start.2 = ((f32[16,64,128]{2,1,0:T(8,128)}), f32[16,64,128]{2,1,0:T(8,128)S(1)}, u32[]{:S(2)}, u32[]{:S(2)}) async-start(f32[16,64,128]{2,1,0:T(8,128)} %shard_map.99), calls=%async_computation.2 | async-start | bytes 1048576 | tf_op jit(solution)/shard_map/all_to_all | solution.py:939
  90.0 7.8 %collective-permute-start.4 = (f32[8,128]{1,0:T(8,128)}, f32[8,128]{1,0:T(8,128)S(1)}, u32[]{:S(2)}, u32[]{:S(2)}) collective-permute-start(f32[8,128]{1,0:T(8,128)} %slice_reduce_fusion.totals.refs_0_), channel_id=1, source_target_pairs={{0,48},{16,0},{32,16},{48,32},{1,49},{17,1},{33,17},{49,33},{2,50}... | collective-permute-start | bytes 12296 | tf_op jit(solution)/shard_map/ppermute | solution.py:941
  93.2 5.5 %collective-permute-start.3 = (f32[8,128]{1,0:T(8,128)}, f32[8,128]{1,0:T(8,128)S(1)}, u32[]{:S(2)}, u32[]{:S(2)}) collective-permute-start(f32[8,128]{1,0:T(8,128)} %slice_reduce_fusion.totals.refs_0_), channel_id=1, source_target_pairs={{0,32},{16,48},{32,0},{48,16},{1,33},{17,49},{33,1},{49,17},{2,34}... | collective-permute-start | bytes 12296 | tf_op jit(solution)/shard_map/ppermute | solution.py:941
  94.0 5.5 %collective-permute-start.2 = (f32[8,128]{1,0:T(8,128)}, f32[8,128]{1,0:T(8,128)S(1)}, u32[]{:S(2)}, u32[]{:S(2)}) collective-permute-start(f32[8,128]{1,0:T(8,128)} %slice_reduce_fusion.totals.refs_0_), channel_id=1, source_target_pairs={{0,16},{16,32},{32,48},{48,0},{1,17},{17,33},{33,49},{49,1},{2,18}... | collective-permute-start | bytes 12296 | tf_op jit(solution)/shard_map/ppermute | solution.py:941
  94.9 0.8 copy-start.6
  97.8 42.7 %copy-start.14 = (f32[8,128]{1,0:T(8,128)}, f32[8,128]{1,0:T(8,128)S(1)}, u32[]{:S(2)}) copy-start(f32[8,128]{1,0:T(8,128)S(1)} %collective-permute-done.4.refs_3_) | copy-start | bytes 12292
  98.6 41.9 %copy-start.15 = (f32[8,128]{1,0:T(8,128)}, f32[8,128]{1,0:T(8,128)S(1)}, u32[]{:S(2)}) copy-start(f32[8,128]{1,0:T(8,128)S(1)} %collective-permute-done.3.refs_2_) | copy-start | bytes 12292
  99.5 41.0 %copy-start.16 = (f32[8,128]{1,0:T(8,128)}, f32[8,128]{1,0:T(8,128)S(1)}, u32[]{:S(2)}) copy-start(f32[8,128]{1,0:T(8,128)S(1)} %collective-permute-done.2.refs_1_) | copy-start | bytes 12292
  102.2 0.8 copy-start.3
  109.2 22.1 %collective-permute-start.5 = (f32[4,1024,256]{2,1,0:T(8,128)}, f32[4,1024,256]{2,1,0:T(8,128)}, u32[]{:S(2)}, u32[]{:S(2)}) collective-permute-start(f32[4,1024,256]{2,1,0:T(8,128)} %bitcast.5), channel_id=1, source_target_pairs={{0,8},{8,0},{1,9},{9,1},{2,10},{10,2},{3,11},{11,3},{4,12},{12,4},... | collective-permute-start | bytes 12582920 | tf_op jit(solution)/shard_map/ppermute | solution.py:948
  120.7 9.1 %copy-start.13 = (f32[256,256]{1,0:T(8,128)S(1)}, f32[256,256]{1,0:T(8,128)}, u32[]{:S(2)}) copy-start(f32[256,256]{1,0:T(8,128)} %get-tuple-element.64) | copy-start | bytes 786436
  126.2 21.2 %all-to-all-start.4 = ((f32[16,64,128]{2,1,0:T(8,128)}), f32[16,64,128]{2,1,0:T(8,128)S(1)}, u32[]{:S(2)}, u32[]{:S(2)}) async-start(f32[16,64,128]{2,1,0:T(8,128)} %shard_map.103), calls=%async_computation.4 | async-start | bytes 1048576 | tf_op jit(solution)/shard_map/all_to_all | solution.py:952
  129.8 17.6 %collective-permute-start.6 = (f32[256,256]{1,0:T(8,128)S(1)}, f32[256,256]{1,0:T(8,128)S(1)}, u32[]{:S(2)}, u32[]{:S(2)}) collective-permute-start(f32[256,256]{1,0:T(8,128)S(1)} %copy-done.13), channel_id=1, source_target_pairs={{0,4},{1,5},{2,6},{3,7},{4,0},{5,1},{6,2},{7,3},{8,12},{9,13},{10,... | collective-permute-start | bytes 786440 | tf_op jit(solution)/shard_map/ppermute | solution.py:928
  147.4 43.1 %copy-start.8 = (f32[256,256]{1,0:T(8,128)}, f32[256,256]{1,0:T(8,128)S(1)}, u32[]{:S(2)}) copy-start(f32[256,256]{1,0:T(8,128)S(1)} %collective-permute-done.6.prob_came) | copy-start | bytes 786436
  147.4 0.9 copy-start
  159.6 6.5 %collective-permute-start.7 = (f32[512,256]{1,0:T(8,128)}, f32[512,256]{1,0:T(8,128)S(1)}, u32[]{:S(2)}, u32[]{:S(2)}) collective-permute-start(f32[512,256]{1,0:T(8,128)} %get-tuple-element.71), channel_id=1, source_target_pairs={{0,8},{8,0},{1,9},{9,1},{2,10},{10,2},{3,11},{11,3},{4,12},{12,4},... | collective-permute-start | bytes 1572872 | tf_op jit(solution)/shard_map/ppermute | solution.py:959
  166.1 0.8 copy-start.7
  169.0 28.9 %all-to-all-start.5 = ((f32[64,8,128]{2,1,0:T(8,128)}), f32[64,8,128]{2,1,0:T(8,128)S(1)}, u32[]{:S(2)}, u32[]{:S(2)}) async-start(f32[64,8,128]{2,1,0:T(8,128)} %shard_map.106), calls=%async_computation.5 | async-start | bytes 524288 | tf_op jit(solution)/shard_map/all_to_all | solution.py:962
  175.7 22.2 %collective-permute-start.8 = (f32[256,256]{1,0:T(8,128)}, f32[256,256]{1,0:T(8,128)S(1)}, u32[]{:S(2)}, u32[]{:S(2)}) collective-permute-start(f32[256,256]{1,0:T(8,128)} %get-tuple-element.81), channel_id=1, source_target_pairs={{0,4},{1,5},{2,6},{3,7},{4,0},{5,1},{6,2},{7,3},{8,12},{9,13},{10,... | collective-permute-start | bytes 786440 | tf_op jit(solution)/shard_map/ppermute | solution.py:928
  197.9 16.4 %copy-start.9 = (f32[256,256]{1,0:T(8,128)}, f32[256,256]{1,0:T(8,128)S(1)}, u32[]{:S(2)}) copy-start(f32[256,256]{1,0:T(8,128)S(1)} %collective-permute-done.8.target_came) | copy-start | bytes 786436
  197.9 0.8 copy-start.2
  207.0 30.8 %all-to-all-start.6 = ((f32[32,72,128]{2,1,0:T(8,128)}), f32[32,72,128]{2,1,0:T(8,128)S(1)}, u32[]{:S(2)}, u32[]{:S(2)}) async-start(f32[32,72,128]{2,1,0:T(8,128)} %shard_map.109), calls=%async_computation.6 | async-start | bytes 2359296 | tf_op jit(solution)/shard_map/all_to_all | solution.py:972
  216.5 6.9 %collective-permute-start.9 = (f32[128,256]{1,0:T(8,128)}, f32[128,256]{1,0:T(8,128)S(1)}, u32[]{:S(2)}, u32[]{:S(2)}) collective-permute-start(f32[128,256]{1,0:T(8,128)} %get-tuple-element.94), channel_id=1, source_target_pairs={{0,2},{1,3},{2,0},{3,1},{4,6},{5,7},{6,4},{7,5},{8,10},{9,11},{10,... | collective-permute-start | bytes 393224 | tf_op jit(solution)/shard_map/ppermute | solution.py:928
  225.7 8.0 %collective-permute-start.10 = (f32[128,256]{1,0:T(8,128)}, f32[128,256]{1,0:T(8,128)S(1)}, u32[]{:S(2)}, u32[]{:S(2)}) collective-permute-start(f32[128,256]{1,0:T(8,128)} %shard_map.112.refs_0_), channel_id=1, source_target_pairs={{0,1},{1,0},{2,3},{3,2},{4,5},{5,4},{6,7},{7,6},{8,9},{9,8},{10,11... | collective-permute-start | bytes 393224 | tf_op jit(solution)/shard_map/ppermute | solution.py:928
  237.8 1.0 copy-start.1
  (2 other events, 1.3 us)
Sparse Core Ops, SparseCore 0:
  10.8 59.0 all-gather.2

commit v5 on v4

--- a/solution.py
+++ b/solution.py
@@ -18,7 +18,7 @@
 BN = 512
 F32 = jnp.float32
 BF16 = jnp.bfloat16
-VMEM_LIMIT = 58 * 1024 * 1024
+VMEM_LIMIT = 52 * 1024 * 1024
 SMEM = pl.BlockSpec(memory_space=pltpu.SMEM)
 VMEM = pl.BlockSpec(memory_space=pltpu.VMEM)
 HBM = pl.BlockSpec(memory_space=pltpu.HBM)
@@ -130,13 +130,13 @@
     return [(a, min(a + 256, stop)) for a in range(start, stop, 256)]
 
 
-def proto_source(core, protos):
+def proto_source(core, protos, size=BN):
     columns = protos.shape[1] // 2
-    return lambda j: protos.at[:, pl.ds(pl.multiple_of(core * columns + j * BN, BN), BN)]
-
-
-def proto_scratch(width):
-    return [pltpu.VMEM((2, width, BN), BF16), pltpu.SemaphoreType.DMA((2,))]
+    return lambda j: protos.at[:, pl.ds(pl.multiple_of(core * columns + j * size, size), size)]
+
+
+def proto_scratch(width, size=BN):
+    return [pltpu.VMEM((2, width, size), BF16), pltpu.SemaphoreType.DMA((2,))]
 
 
 def put_columns(step, heads, out):
@@ -181,9 +181,9 @@
             part = jnp.zeros((1, BN), F32)
             for start, stop in row_blocks(first, last):
                 score = jnp.dot(feats[start:stop, :], w, preferred_element_type=F32)
-                e = jnp.exp2(score * (LOG2E / TEACHER_TEMP)).astype(BF16)
-                out[slot, start:stop, :] = e
-                part = part + jnp.sum(e.astype(F32), axis=0, keepdims=True)
+                e = jnp.exp2(score * (LOG2E / TEACHER_TEMP))
+                out[slot, start:stop, :] = e.astype(BF16)
+                part = part + jnp.sum(e, axis=0, keepdims=True)
             heads.append(part)
         leave(j, slot).start()
         put_columns(j, heads, sums)
@@ -215,6 +215,7 @@
 
 def student_kernel(crops, idx, own, other, protos, total, mix, feats, acc, buf, sem):
     rows = feats.shape[0]
+    size = buf.shape[2]
     place_rows(idx[0], crops, rows // 2, rows // 2, own, other, feats)
     acc[...] = jnp.zeros_like(acc)
     mix[...] = jnp.zeros_like(mix)
@@ -225,14 +226,14 @@
             score = jnp.dot(feats[start:stop, :], w, preferred_element_type=F32)
             p = jnp.exp2(score * (LOG2E / STUDENT_TEMP))
             part = p[:, :128]
-            for t in range(1, BN // 128):
+            for t in range(1, size // 128):
                 part = part + p[:, 128 * t : 128 * (t + 1)]
             acc[start:stop, :] += part
             mix[start:stop, :] += lax.dot_general(
                 p.astype(BF16), w, (((1,), (1,)), ((), ())), preferred_element_type=F32
             )
 
-    stream(proto_source(idx[0], protos), buf, sem, protos.shape[1] // 2 // BN, step)
+    stream(proto_source(idx[0], protos, size), buf, sem, protos.shape[1] // 2 // size, step)
     for t in range(rows // 128):
         block = jnp.transpose(acc[128 * t : 128 * (t + 1), :])
         total[t : t + 1, :] = jnp.sum(block, axis=0, keepdims=True)
@@ -247,7 +248,7 @@
         [idx, own, other, protos],
         "svvh",
         scratch=[pltpu.VMEM((rows, width), BF16), pltpu.VMEM((rows, 128), F32)]
-        + proto_scratch(width),
+        + proto_scratch(width, 2 * BN),
         flops=4 * rows * width * columns,
         traffic=2 * width * columns,
     )
@@ -557,15 +558,23 @@
     )
 
 
-def weight_kernel(ny, crops, idx, prob, wnorm, turned_d, turned_i, expo_d, expo_i, colparts, rowparts, out, left_d, left_i, scales, rowscale, buf_d, buf_i, sems_d, sems_i):
+def weight_kernel(ny, crops, idx, prob, wnorm, turned_d, turned_i, expo_d, expo_i, colparts, rowparts, out, left_d, left_i, scales, rowscale, buf_d, buf_i, sems_d, sems_i, targets):
     copies, _, _ = out.shape
     width, part = prob.shape
     own = width // copies
-    copies_d = column_copies(expo_d, buf_d, sems_d)
-    copies_i = column_copies(expo_i, buf_i, sems_i)
-    for pair in zip(copies_d, copies_i):
-        for copy in pair:
-            copy.start()
+    streams = []
+    for expo, buf, sems in ((expo_d, buf_d, sems_d), (expo_i, buf_i, sems_i)):
+        size = buf.shape[0] // sems.shape[0]
+        streams.append(
+            [
+                pltpu.make_async_copy(
+                    expo.at[pl.ds(i * size, size), :], buf.at[pl.ds(i * size, size), :], sems.at[i]
+                )
+                for i in range(sems.shape[0])
+            ]
+        )
+    for copy in streams[0] + streams[1]:
+        copy.start()
     group = rowparts.shape[0] // ny
     sub = rowparts.shape[1]
     scales[...] = GRAD_SCALE / jnp.sum(colparts[...], axis=0)
@@ -588,16 +597,23 @@
     left_i[...] = (turned_i[...].astype(F32) * jnp.concatenate(lines_i, axis=1)).astype(BF16)
     per_head = scales.shape[0] // 2
     first = idx[3] * (part // 128)
+    for head, (left, buf) in enumerate(((left_d, buf_d), (left_i, buf_i))):
+        size = buf.shape[0] // len(streams[head])
+        for i, copy in enumerate(streams[head]):
+            copy.wait()
+            span = slice(i * size, (i + 1) * size)
+            value = jnp.dot(left[:, span], buf[span, :], preferred_element_type=F32)
+            if i == 0:
+                targets[head] = value
+            else:
+                targets[head] += value
     for at in range(0, part, BN):
         span = slice(at, at + BN)
         wsum = prob[:, span]
-        copies_d[at // BN].wait()
-        copies_i[at // BN].wait()
-        for head, (left, expo) in enumerate(((left_d, buf_d), (left_i, buf_i))):
-            target = jnp.dot(left[...], expo[:, span], preferred_element_type=F32)
+        for head in range(2):
             base = head * per_head + first + at // 128
             line = [scales[pl.ds(base + t, 1), :] for t in range(BN // 128)]
-            wsum = wsum - target * jnp.concatenate(line, axis=1)
+            wsum = wsum - targets[head, :, span] * jnp.concatenate(line, axis=1)
         coldot = jnp.sum(wnorm[:, span] * wsum, axis=0, keepdims=True)
         for t in range(BN // 128):
             lanes = slice(128 * t, 128 * (t + 1))
@@ -626,8 +642,9 @@
             pltpu.VMEM((ny * rowparts.shape[1], 128), F32),
             pltpu.VMEM(expo[0].shape, BF16),
             pltpu.VMEM(expo[1].shape, BF16),
-            pltpu.SemaphoreType.DMA((part // BN,)),
-            pltpu.SemaphoreType.DMA((part // BN,)),
+            pltpu.SemaphoreType.DMA((expo[0].shape[0] // 512,)),
+            pltpu.SemaphoreType.DMA((expo[1].shape[0] // 512,)),
+            pltpu.VMEM((2, width, part), F32),
         ],
         flops=2 * rows * width * part,
         traffic=2 * rows * part,
@@ -771,14 +788,6 @@
         "svv",
         scratch=[pltpu.VMEM((rows, width), F32)],
     )
-
-
-def add_kernel(mine, came, out):
-    out[...] = mine[...] + came[...]
-
-
-def add_pass(mine, came):
-    return call(add_kernel, array(mine.shape), [mine, came], "vv")
 
 
 def mix_kernel(nz, ny, crops, bit, idx, rowparts, target, target_came, prob, prob_came, *refs):
@@ -828,23 +837,26 @@
     )
 
 
-def feature_kernel(pair, patches, idx, mask, *refs):
-    pieces = refs[: 2 if pair else 1]
-    all_crops, all_rows, crop_out, patch_out, masked_rows, dense, total = refs[len(pieces) :]
+def feature_kernel(count, chunks, patches, idx, mask, *refs):
+    pieces = refs[:count]
+    all_crops, all_rows, crop_out, patch_out, masked_rows, dense, total = refs[count:]
     z = idx[1]
     masked = mask.shape[1]
     crop_share = crop_out.shape[0]
     share = patch_out.shape[0]
-    total[...] = pieces[0][...] + pieces[1][...] if pair else pieces[0][...]
-    chunk = total.shape[0] // len(pieces)
+    value = pieces[0][...]
+    for piece in pieces[1:]:
+        value = value + piece[...]
+    total[...] = value
+    chunk = total.shape[0] // chunks
     rest = chunk - crop_share
-    for side in range(len(pieces)):
+    for side in range(chunks):
         masked_rows[side * rest : (side + 1) * rest, :] = total[
             side * chunk + crop_share : (side + 1) * chunk, :
         ]
     crop_at = pl.multiple_of(z * crop_share, 16)
     patch_at = pl.multiple_of(z * share, 128)
-    start = pl.multiple_of(lax.rem(z, len(pieces)) * chunk, 16)
+    start = pl.multiple_of(lax.rem(z, chunks) * chunk, 16)
     dense[...] = jnp.zeros_like(dense)
     first_row = z * share
     first_image = first_row // patches
@@ -872,18 +884,18 @@
     patch_out[...] = back(all_rows[pl.ds(patch_at, share), :], dense[...])
 
 
-def feature_pass(idx, mask, pieces, all_crops, all_rows, nz, patches):
+def feature_pass(idx, mask, pieces, all_crops, all_rows, nz, patches, pair):
     crops, width = all_crops.shape
     crop_share = crops // nz
     share = all_rows.shape[0] // nz
     rows = pieces[0].shape[0]
     return call(
-        functools.partial(feature_kernel, len(pieces) == 2, patches),
+        functools.partial(feature_kernel, len(pieces), 2 if pair else 1, patches),
         [array((crop_share, width)), array((share, width))],
         [idx, mask, *pieces, all_crops, all_rows],
         "ss" + "v" * len(pieces) + "vv",
         scratch=[
-            pltpu.VMEM((rows - len(pieces) * crop_share, width), F32),
+            pltpu.VMEM((rows - (2 if pair else 1) * crop_share, width), F32),
             pltpu.VMEM((share, width), F32),
             pltpu.VMEM((rows, width), F32),
         ],
@@ -929,10 +941,11 @@
 
     colparts = lax.all_to_all(sums, ("x", "y"), 0, 0)
     total, mix = student_pass(idx, own, other, student_protos, crops)
-    winv = norm_pass(student_protos)
-    colparts, winv = tie(colparts, winv)
     sums = row_pass(expo, colparts, total, crops, 2 * nz)
     rowparts = lax.all_to_all(sums, ("c", "z"), 0, 0)
+    later_protos, _ = tie(student_protos, sums)
+    winv = norm_pass(later_protos)
+    rowparts, winv = tie(rowparts, winv)
     totals = jnp.sum(rowparts[:, sub:, :], axis=0)
     sums = column_pass(expo, rowparts, crops, nx * ny)
 
@@ -975,18 +988,19 @@
     total = mix_pass(
         idx, rowparts, keep, came, p_keep, p_came, nz, ny, crops, bits[0] if bits else 0
     )
+    pieces = [total]
     for i, bit in enumerate(bits):
         keep, send = total
-        came = across(send, bit)
-        if i + 1 < len(bits):
-            total = fold_pass(idx, keep, came, bits[i + 1])
-        else:
-            total = add_pass(keep, came)
-    pieces = [total]
-    if pair:
+        last = i + 1 == len(bits)
+        pieces = [keep, across(send, bit)]
+        if last and pair:
+            pieces += [across(keep, 1), across(send, bit ^ 1)]
+        elif not last:
+            total = fold_pass(idx, *pieces, bits[i + 1])
+    if pair and not bits:
         pieces.append(across(total, 1))
     crop_grad, patch_grad = feature_pass(
-        idx, patch_mask, pieces, student_crops, student_patches, nz, patches
+        idx, patch_mask, pieces, student_crops, student_patches, nz, patches, pair
     )
     return (proto_grad, crop_grad, patch_grad)
 

time: 253 us -> 228 us (0.901)
  Pallas kernels: 118 us -> 96.2 us
  blocking collectives: 28.3 us -> 10.6 us
  waiting for transfers between devices: 31.7 us -> 39.4 us
  starting transfers between devices: 47.4 us -> 54.3 us
    pallas_call x19 -> x18, Pallas kernels: 112 us -> 91.5 us  [call(): pl.pallas_call(kernel, out_shape=out_shape, out_specs=out_specs, in_specs...]
    all_to_all x2 -> x1, blocking collectives: 28.3 us -> 10.6 us  [local(): rowparts = lax.all_to_all(sums, ('c', 'z'), 0, 0)]
    all_to_all x0 -> x1, starting transfers between devices: none -> 8.6 us  [local(): rowparts = lax.all_to_all(sums, ('c', 'z'), 0, 0)]
    all_to_all x0 -> x1, waiting for transfers between devices: none -> 3.54 us  [local(): rowparts = lax.all_to_all(sums, ('c', 'z'), 0, 0)]
    ppermute x4 -> x5, waiting for transfers between devices: 25.1 us -> 22.9 us  [across(): return lax.ppermute(value, 'z', [(i, i ^ bit) for i in range(nz)])]
    unnamed x34 -> x24, local copies, waits for them, and re-layouts: 8.21 us -> 8.58 us
    ppermute x4 -> x5, starting transfers between devices: 10.4 us -> 10.8 us  [across(): return lax.ppermute(value, 'z', [(i, i ^ bit) for i in range(nz)])]
  transfers between devices with their start and end apart: 17 -> 19, of which waited for: 8 -> 11; matrix products, arithmetic and copies ran while one was open for 1% -> 0% of each run, Pallas kernels for 36% -> 32%
where the time goes in v5:
time: 228 us; the launch traced here: 223 us
  Pallas kernels  96.2 us (42%)
  starting transfers between devices  54.3 us (24%)
  waiting for transfers between devices  39.4 us (17%)
  between operations  14.3 us (6%)
  blocking collectives  10.6 us (5%)
  local copies, waits for them, and re-layouts  8.58 us (4%)
    pallas_call x18, Pallas kernels, call(): pl.pallas_call(kernel, out_shape=out_shape, out_specs=out_specs, in_specs...  91.5 us
    ppermute x5, waiting for transfers between devices, across(): return lax.ppermute(value, 'z', [(i, i ^ bit) for i in range(nz)])  22.9 us
    all_to_all x3, starting transfers between devices, local(): colparts = lax.all_to_all(sums, ('x', 'y'), 0, 0)  15.8 us
    ppermute x5, starting transfers between devices, across(): return lax.ppermute(value, 'z', [(i, i ^ bit) for i in range(nz)])  10.8 us
    all_to_all x1, blocking collectives, local(): rowparts = lax.all_to_all(sums, ('c', 'z'), 0, 0)  10.6 us
    all_to_all x1, starting transfers between devices, local(): rowparts = lax.all_to_all(sums, ('c', 'z'), 0, 0)  8.6 us
    unnamed x24, local copies, waits for them, and re-layouts  8.58 us
    all_to_all x1, starting transfers between devices, local(): parts = lax.all_to_all(outgoing, ('x', 'y', 'c'), 0, 0)  7.26 us
  transfers between devices with their start and end apart: 19, of which 11 were waited for; matrix products, arithmetic and copies ran while one was open for 0% of the time, Pallas kernels for 32%

profile of v5, /device:TPU:32, one launch (start us, length us, event | category | flops | bytes accessed | tf_op | source)
XLA Modules:
  0.0 223.4 jit_solution(6990120998367117368)
XLA Ops:
  13.8 2.8 %collective-permute-done.other = f32[1024,256]{1,0:T(8,128)S(1)} collective-permute-done((f32[1024,256]{1,0:T(8,128)}, f32[1024,256]{1,0:T(8,128)S(1)}, u32[]{:S(2)}, u32[]{:S(2)}) %collective-permute-start) | collective-permute-done | bytes 1048608 | tf_op jit(solution)/shard_map/ppermute | solution.py:932
  18.8 10.5 %shard_map.95 = (bf16[1024,4096]{1,0:T(8,128)(2,1)}, f32[16,64,128]{2,1,0:T(8,128)}) custom-call(s32[4]{0:T(128)S(1)} %pad_add_fusion.idx, f32[1024,256]{1,0:T(8,128)S(1)} %copy-done, f32[1024,256]{1,0:T(8,128)} %copy-done.11, bf16[256,8192]{1,0:T(8,128)(2,1)} %protos.9), custom_call_target="tpu_custom_call" | custom-call | flops 2147483648 | bytes 8388608 | tf_op jit(solution)/shard_map/pallas_call | solution.py:33
  29.3 7.0 %all-to-all-start = ((f32[16,64,128]{2,1,0:T(8,128)}), f32[16,64,128]{2,1,0:T(8,128)S(1)}, u32[]{:S(2)}, u32[]{:S(2)}) async-start(f32[16,64,128]{2,1,0:T(8,128)} %get-tuple-element.52), calls=%async_computation | async-start | bytes 1048576 | tf_op jit(solution)/shard_map/all_to_all | solution.py:942
  36.3 8.8 %shard_map.96 = (f32[8,128]{1,0:T(8,128)S(1)}, f32[1024,256]{1,0:T(8,128)S(1)}) custom-call(s32[4]{0:T(128)S(1)} %pad_add_fusion.idx, f32[1024,256]{1,0:T(8,128)} %shard_map.94.own, f32[1024,256]{1,0:T(8,128)} %copy-done.11, bf16[256,8192]{1,0:T(8,128)(2,1)} %protos.12), custom_call_target="tpu_custom_call" | custom-call | flops 4294967296 | bytes 2097152 | tf_op jit(solution)/shard_map/pallas_call | solution.py:33
  48.2 5.2 %shard_map.97 = f32[16,16,128]{2,1,0:T(8,128)} custom-call(bf16[1024,4096]{1,0:T(8,128)(2,1)} %get-tuple-element.51.expo, f32[16,64,128]{2,1,0:T(8,128)S(1)} %all-to-all-done.colparts, f32[8,128]{1,0:T(8,128)S(1)} %get-tuple-element.53.refs_0_), custom_call_target="tpu_custom_call" | custom-call | flops 8388608 | bytes 8388608 | tf_op jit(solution)/shard_map/pallas_call | solution.py:33
  53.3 8.6 %all-to-all-start.1 = ((f32[16,16,128]{2,1,0:T(8,128)}), f32[16,16,128]{2,1,0:T(8,128)S(1)}, u32[]{:S(2)}, u32[]{:S(2)}) async-start(f32[16,16,128]{2,1,0:T(8,128)} %shard_map.97), calls=%async_computation.1 | async-start | bytes 262144 | tf_op jit(solution)/shard_map/all_to_all | solution.py:945
  61.9 4.7 %shard_map.98.winv = f32[1,8192]{1,0:T(1,128)S(1)} custom-call(bf16[256,8192]{1,0:T(8,128)(2,1)} %protos.12), custom_call_target="tpu_custom_call" | custom-call | flops 6291456 | bytes 4194304 | tf_op jit(solution)/shard_map/pallas_call | solution.py:661
  66.6 3.5 %all-to-all-done.1.rowparts = f32[16,16,128]{2,1,0:T(8,128)S(1)} async-done(((f32[16,16,128]{2,1,0:T(8,128)}), f32[16,16,128]{2,1,0:T(8,128)S(1)}, u32[]{:S(2)}, u32[]{:S(2)}) %all-to-all-start.1) | async-done | bytes 131104 | tf_op jit(solution)/shard_map/all_to_all | solution.py:945
  70.2 4.6 %shard_map.99 = f32[16,64,128]{2,1,0:T(8,128)} custom-call(bf16[1024,4096]{1,0:T(8,128)(2,1)} %get-tuple-element.51.expo, f32[16,16,128]{2,1,0:T(8,128)S(1)} %all-to-all-done.1.rowparts), custom_call_target="tpu_custom_call" | custom-call | flops 8388608 | bytes 8388608 | tf_op jit(solution)/shard_map/pallas_call | solution.py:33
  76.4 5.1 %all-to-all-start.2 = ((f32[16,64,128]{2,1,0:T(8,128)}), f32[16,64,128]{2,1,0:T(8,128)S(1)}, u32[]{:S(2)}, u32[]{:S(2)}) async-start(f32[16,64,128]{2,1,0:T(8,128)} %shard_map.99), calls=%async_computation.2 | async-start | bytes 1048576 | tf_op jit(solution)/shard_map/all_to_all | solution.py:952
  81.5 3.1 %collective-permute-start.4 = (f32[8,128]{1,0:T(8,128)S(1)}, f32[8,128]{1,0:T(8,128)S(1)}, u32[]{:S(2)}, u32[]{:S(2)}) collective-permute-start(f32[8,128]{1,0:T(8,128)S(1)} %slice_reduce_fusion.totals.refs_0_), channel_id=1, source_target_pairs={{0,48},{16,0},{32,16},{48,32},{1,49},{17,1},{33,17},{49,33},{2,50}... | collective-permute-start | bytes 12296 | tf_op jit(solution)/shard_map/ppermute | solution.py:954
  87.0 2.8 %collective-permute-done.3.refs_2_ = f32[8,128]{1,0:T(8,128)S(1)} collective-permute-done((f32[8,128]{1,0:T(8,128)S(1)}, f32[8,128]{1,0:T(8,128)S(1)}, u32[]{:S(2)}, u32[]{:S(2)}) %collective-permute-start.3) | collective-permute-done | bytes 4128 | tf_op jit(solution)/shard_map/ppermute | solution.py:954
  91.1 2.6 %all-to-all-done.2.colparts = f32[16,64,128]{2,1,0:T(8,128)S(1)} async-done(((f32[16,64,128]{2,1,0:T(8,128)}), f32[16,64,128]{2,1,0:T(8,128)S(1)}, u32[]{:S(2)}, u32[]{:S(2)}) %all-to-all-start.2) | async-done | bytes 524320 | tf_op jit(solution)/shard_map/all_to_all | solution.py:952
  93.7 4.5 %shard_map.102 = f32[16,8,128]{2,1,0:T(8,128)S(1)} custom-call(bf16[1024,4096]{1,0:T(8,128)(2,1)} %get-tuple-element.51.expo, f32[16,64,128]{2,1,0:T(8,128)S(1)} %all-to-all-done.2.colparts), custom_call_target="tpu_custom_call" | custom-call | flops 8388608 | bytes 8388608 | tf_op jit(solution)/shard_map/pallas_call | solution.py:33
  98.3 10.6 %all_to_all.35.rowparts = f32[16,8,128]{2,1,0:T(8,128)S(1)} all-to-all(f32[16,8,128]{2,1,0:T(8,128)S(1)} %shard_map.102), channel_id=1, replica_groups=mesh['x'=4,'y'=4,'c'=2,'z'=8] {'c','z'}, dimensions={0} | all-to-all | bytes 131072 | tf_op jit(solution)/shard_map/all_to_all | solution.py:962
  108.9 4.6 %shard_map.103 = f32[16,64,128]{2,1,0:T(8,128)} custom-call(bf16[1024,4096]{1,0:T(8,128)(2,1)} %get-tuple-element.51.expo, f32[16,8,128]{2,1,0:T(8,128)S(1)} %all_to_all.35.rowparts), custom_call_target="tpu_custom_call" | custom-call | flops 8388608 | bytes 8388608 | tf_op jit(solution)/shard_map/pallas_call | solution.py:33
  113.5 3.6 %all-to-all-start.4 = ((f32[16,64,128]{2,1,0:T(8,128)}), f32[16,64,128]{2,1,0:T(8,128)S(1)}, u32[]{:S(2)}, u32[]{:S(2)}) async-start(f32[16,64,128]{2,1,0:T(8,128)} %shard_map.103), calls=%async_computation.4 | async-start | bytes 1048576 | tf_op jit(solution)/shard_map/all_to_all | solution.py:965
  118.6 9.0 %shard_map.104 = (bf16[1024,1024]{1,0:T(8,128)(2,1)}, bf16[3072,1024]{1,0:T(8,128)(2,1)}) custom-call(s32[4]{0:T(128)S(1)} %pad_add_fusion.idx, f32[4,1024,256]{2,1,0:T(8,128)} %bitcast.6, f32[4,1024,256]{2,1,0:T(8,128)} %collective-permute-done.5.other, bf16[256,8192]{1,0:T(8,128)(2,1)} %protos.9), custom_call_target="tpu_custom_call" | custom-call | flops 2147483648 | bytes 4194304 | tf_op jit(solution)/shard_map/pallas_call | solution.py:33
  127.7 7.1 %collective-permute-done.6.prob_came = f32[256,256]{1,0:T(8,128)S(1)} collective-permute-done((f32[256,256]{1,0:T(8,128)S(1)}, f32[256,256]{1,0:T(8,128)S(1)}, u32[]{:S(2)}, u32[]{:S(2)}) %collective-permute-start.6) | collective-permute-done | bytes 262176 | tf_op jit(solution)/shard_map/ppermute | solution.py:940
  134.7 9.9 %shard_map.105 = (f32[512,256]{1,0:T(8,128)S(1)}, f32[512,256]{1,0:T(8,128)S(1)}) custom-call(s32[4]{0:T(128)S(1)} %pad_add_fusion.idx, bf16[1024,4096]{1,0:T(8,128)(2,1)} %get-tuple-element.51.expo, f32[16,64,128]{2,1,0:T(8,128)S(1)} %all-to-all-done.4.colparts, bf16[256,8192]{1,0:T(8,128)(2,1)} %protos.12), custom_call_target="tpu_custom_call" | custom-call | flops 2147483648 | bytes 8388608 | tf_op jit(solution)/shard_map/pallas_call | solution.py:33
  144.8 5.3 %shard_map.106 = f32[64,8,128]{2,1,0:T(8,128)} custom-call(bf16[1024,4096]{1,0:T(8,128)(2,1)} %get-tuple-element.51.expo, f32[16,64,128]{2,1,0:T(8,128)S(1)} %all-to-all-done.4.colparts), custom_call_target="tpu_custom_call" | custom-call | flops 8388608 | bytes 8388608 | tf_op jit(solution)/shard_map/pallas_call | solution.py:33
  150.7 6.7 %all-to-all-start.5 = ((f32[64,8,128]{2,1,0:T(8,128)}), f32[64,8,128]{2,1,0:T(8,128)S(1)}, u32[]{:S(2)}, u32[]{:S(2)}) async-start(f32[64,8,128]{2,1,0:T(8,128)} %shard_map.106), calls=%async_computation.5 | async-start | bytes 524288 | tf_op jit(solution)/shard_map/all_to_all | solution.py:975
  157.4 4.8 %collective-permute-start.8 = (f32[256,256]{1,0:T(8,128)S(1)}, f32[256,256]{1,0:T(8,128)S(1)}, u32[]{:S(2)}, u32[]{:S(2)}) collective-permute-start(f32[256,256]{1,0:T(8,128)S(1)} %get-tuple-element.83), channel_id=1, source_target_pairs={{0,4},{1,5},{2,6},{3,7},{4,0},{5,1},{6,2},{7,3},{8,12},{9,13},{10,... | collective-permute-start | bytes 786440 | tf_op jit(solution)/shard_map/ppermute | solution.py:940
  162.2 9.5 %shard_map.108 = (f32[256,1024]{1,0:T(8,128)S(1)}, f32[256,1024]{1,0:T(8,128)}, bf16[256,1024]{1,0:T(8,128)(2,1)S(1)}, bf16[256,3072]{1,0:T(8,128)(2,1)}) custom-call(s32[4]{0:T(128)S(1)} %pad_add_fusion.idx, f32[4,1024,256]{2,1,0:T(8,128)} %bitcast.7, f32[4,1024,256]{2,1,0:T(8,128)} %collective-permute-done.5.other, bf16[256,8192]{1,0:T(8,128)(2,1)} %protos.12, ...), custom_call_target="tpu_custom_call" | custom-call | flops 4294967296 | bytes 4194304 | tf_op jit(solution)/shard_map/pallas_call | solution.py:33
  172.7 6.8 %collective-permute-done.8.target_came = f32[256,256]{1,0:T(8,128)S(1)} collective-permute-done((f32[256,256]{1,0:T(8,128)S(1)}, f32[256,256]{1,0:T(8,128)S(1)}, u32[]{:S(2)}, u32[]{:S(2)}) %collective-permute-start.8) | collective-permute-done | bytes 262176 | tf_op jit(solution)/shard_map/ppermute | solution.py:940
  179.6 9.0 %shard_map.109 = f32[32,72,128]{2,1,0:T(8,128)} custom-call(s32[4]{0:T(128)S(1)} %pad_add_fusion.idx, f32[256,1024]{1,0:T(8,128)} %copy-done.3, f32[256,1024]{1,0:T(8,128)} %get-tuple-element.85.wnorm, bf16[256,1024]{1,0:T(8,128)(2,1)S(1)} %get-tuple-element.86.turned_d, bf16[256,3072]{1,0:T(8,128)(2,1)} %get-tuple-element.87.turned_i, ...), custom_call_target="tpu_custom_call" | custom-call | flops 2147483648 | bytes 8388608 | tf_op jit(solution)/shard_map/pallas_call | solution.py:33
  188.6 7.3 %all-to-all-start.6 = ((f32[32,72,128]{2,1,0:T(8,128)}), f32[32,72,128]{2,1,0:T(8,128)S(1)}, u32[]{:S(2)}, u32[]{:S(2)}) async-start(f32[32,72,128]{2,1,0:T(8,128)} %shard_map.109), calls=%async_computation.6 | async-start | bytes 2359296 | tf_op jit(solution)/shard_map/all_to_all | solution.py:985
  198.2 2.9 %collective-permute-start.9 = (f32[128,256]{1,0:T(8,128)S(1)}, f32[128,256]{1,0:T(8,128)S(1)}, u32[]{:S(2)}, u32[]{:S(2)}) collective-permute-start(f32[128,256]{1,0:T(8,128)S(1)} %get-tuple-element.96), channel_id=1, source_target_pairs={{0,2},{1,3},{2,0},{3,1},{4,6},{5,7},{6,4},{7,5},{8,10},{9,11},{10,... | collective-permute-start | bytes 393224 | tf_op jit(solution)/shard_map/ppermute | solution.py:940
  201.1 2.6 %collective-permute-done.10.refs_2_ = f32[128,256]{1,0:T(8,128)S(1)} collective-permute-done((f32[128,256]{1,0:T(8,128)S(1)}, f32[128,256]{1,0:T(8,128)S(1)}, u32[]{:S(2)}, u32[]{:S(2)}) %collective-permute-start.10) | collective-permute-done | bytes 131104 | tf_op jit(solution)/shard_map/ppermute | solution.py:940
  203.7 6.5 %collective-permute-done.11.refs_3_ = f32[128,256]{1,0:T(8,128)S(1)} collective-permute-done((f32[128,256]{1,0:T(8,128)S(1)}, f32[128,256]{1,0:T(8,128)S(1)}, u32[]{:S(2)}, u32[]{:S(2)}) %collective-permute-start.11) | collective-permute-done | bytes 131104 | tf_op jit(solution)/shard_map/ppermute | solution.py:940
  210.2 2.7 %shard_map.112 = (f32[16,256]{1,0:T(8,128)}, f32[128,256]{1,0:T(8,128)}) custom-call(s32[4]{0:T(128)S(1)} %pad_add_fusion.idx, s32[4,96]{1,0:T(4,128)S(1)} %copy-done.10, f32[128,256]{1,0:T(8,128)S(1)} %get-tuple-element.95.refs_0_, f32[128,256]{1,0:T(8,128)S(1)} %collective-permute-done.9.refs_1_, f32[128,256]{1,0:T(8,128)S(1)} %collective-permute-done.10.refs_2_, ...), custom_call_target="tpu_custom_call" | custom-call | tf_op jit(solution)/shard_map/pallas_call | solution.py:33
  214.2 2.3 %shard_map.110 = f32[8,8192]{1,0:T(8,128)} custom-call(s32[4]{0:T(128)S(1)} %pad_add_fusion.idx, f32[32,72,128]{2,1,0:T(8,128)S(1)} %all-to-all-done.6.parts, bf16[256,8192]{1,0:T(8,128)(2,1)} %protos.12, f32[1,8192]{1,0:T(1,128)S(1)} %shard_map.98.winv), custom_call_target="tpu_custom_call" | custom-call | tf_op jit(solution)/shard_map/pallas_call | solution.py:33
  (53 shorter events, 24.2 us)
Async XLA Ops:
  7.2 91.0 %all-gather.3.cloned.1.call-start = ((), (), s32[]{:S(2)}) async-start(), calls=%async_computation.7 | async-start | bytes 5242880 | tf_op jit(solution)/shard_map/all_gather | solution.py:933
  7.2 1.0 copy-start.1
  8.3 1.0 copy-start.5
  9.3 0.8 copy-start.6
  10.1 0.8 copy-start.8
  11.0 0.7 copy-start.9
  13.6 3.0 %collective-permute-start = (f32[1024,256]{1,0:T(8,128)}, f32[1024,256]{1,0:T(8,128)S(1)}, u32[]{:S(2)}, u32[]{:S(2)}) collective-permute-start(f32[1024,256]{1,0:T(8,128)} %shard_map.94.own), channel_id=1, source_target_pairs={{0,8},{8,0},{1,9},{9,1},{2,10},{10,2},{3,11},{11,3},{4,12},{12,4},... | collective-permute-start | bytes 3145736 | tf_op jit(solution)/shard_map/ppermute | solution.py:932
  16.6 1.0 copy-start.11
  17.5 1.2 copy-start
  29.3 18.9 %all-to-all-start = ((f32[16,64,128]{2,1,0:T(8,128)}), f32[16,64,128]{2,1,0:T(8,128)S(1)}, u32[]{:S(2)}, u32[]{:S(2)}) async-start(f32[16,64,128]{2,1,0:T(8,128)} %get-tuple-element.52), calls=%async_computation | async-start | bytes 1048576 | tf_op jit(solution)/shard_map/all_to_all | solution.py:942
  45.1 1.0 copy-start.4
  53.3 16.8 %all-to-all-start.1 = ((f32[16,16,128]{2,1,0:T(8,128)}), f32[16,16,128]{2,1,0:T(8,128)S(1)}, u32[]{:S(2)}, u32[]{:S(2)}) async-start(f32[16,16,128]{2,1,0:T(8,128)} %shard_map.97), calls=%async_computation.1 | async-start | bytes 262144 | tf_op jit(solution)/shard_map/all_to_all | solution.py:945
  76.3 10.1 %collective-permute-start.1 = (f32[512,256]{1,0:T(8,128)S(1)}, f32[512,256]{1,0:T(8,128)S(1)}, u32[]{:S(2)}, u32[]{:S(2)}) collective-permute-start(f32[512,256]{1,0:T(8,128)S(1)} %get-tuple-element.59), channel_id=1, source_target_pairs={{0,8},{8,0},{1,9},{9,1},{2,10},{10,2},{3,11},{11,3},{4,12},{12,4},... | collective-permute-start | bytes 1572872 | tf_op jit(solution)/shard_map/ppermute | solution.py:956
  76.4 17.3 %all-to-all-start.2 = ((f32[16,64,128]{2,1,0:T(8,128)}), f32[16,64,128]{2,1,0:T(8,128)S(1)}, u32[]{:S(2)}, u32[]{:S(2)}) async-start(f32[16,64,128]{2,1,0:T(8,128)} %shard_map.99), calls=%async_computation.2 | async-start | bytes 1048576 | tf_op jit(solution)/shard_map/all_to_all | solution.py:952
  81.5 5.5 %collective-permute-start.4 = (f32[8,128]{1,0:T(8,128)S(1)}, f32[8,128]{1,0:T(8,128)S(1)}, u32[]{:S(2)}, u32[]{:S(2)}) collective-permute-start(f32[8,128]{1,0:T(8,128)S(1)} %slice_reduce_fusion.totals.refs_0_), channel_id=1, source_target_pairs={{0,48},{16,0},{32,16},{48,32},{1,49},{17,1},{33,17},{49,33},{2,50}... | collective-permute-start | bytes 12296 | tf_op jit(solution)/shard_map/ppermute | solution.py:954
  84.7 5.1 %collective-permute-start.3 = (f32[8,128]{1,0:T(8,128)S(1)}, f32[8,128]{1,0:T(8,128)S(1)}, u32[]{:S(2)}, u32[]{:S(2)}) collective-permute-start(f32[8,128]{1,0:T(8,128)S(1)} %slice_reduce_fusion.totals.refs_0_), channel_id=1, source_target_pairs={{0,32},{16,48},{32,0},{48,16},{1,33},{17,49},{33,1},{49,17},{2,34}... | collective-permute-start | bytes 12296 | tf_op jit(solution)/shard_map/ppermute | solution.py:954
  85.6 5.6 %collective-permute-start.2 = (f32[8,128]{1,0:T(8,128)S(1)}, f32[8,128]{1,0:T(8,128)S(1)}, u32[]{:S(2)}, u32[]{:S(2)}) collective-permute-start(f32[8,128]{1,0:T(8,128)S(1)} %slice_reduce_fusion.totals.refs_0_), channel_id=1, source_target_pairs={{0,16},{16,32},{32,48},{48,0},{1,17},{17,33},{33,49},{49,1},{2,18}... | collective-permute-start | bytes 12296 | tf_op jit(solution)/shard_map/ppermute | solution.py:954
  98.2 20.4 %collective-permute-start.5 = (f32[4,1024,256]{2,1,0:T(8,128)}, f32[4,1024,256]{2,1,0:T(8,128)}, u32[]{:S(2)}, u32[]{:S(2)}) collective-permute-start(f32[4,1024,256]{2,1,0:T(8,128)} %bitcast.5), channel_id=1, source_target_pairs={{0,8},{8,0},{1,9},{9,1},{2,10},{10,2},{3,11},{11,3},{4,12},{12,4},... | collective-permute-start | bytes 12582920 | tf_op jit(solution)/shard_map/ppermute | solution.py:961
  113.5 21.2 %all-to-all-start.4 = ((f32[16,64,128]{2,1,0:T(8,128)}), f32[16,64,128]{2,1,0:T(8,128)S(1)}, u32[]{:S(2)}, u32[]{:S(2)}) async-start(f32[16,64,128]{2,1,0:T(8,128)} %shard_map.103), calls=%async_computation.4 | async-start | bytes 1048576 | tf_op jit(solution)/shard_map/all_to_all | solution.py:965
  117.1 17.6 %collective-permute-start.6 = (f32[256,256]{1,0:T(8,128)S(1)}, f32[256,256]{1,0:T(8,128)S(1)}, u32[]{:S(2)}, u32[]{:S(2)}) collective-permute-start(f32[256,256]{1,0:T(8,128)S(1)} %get-tuple-element.66), channel_id=1, source_target_pairs={{0,4},{1,5},{2,6},{3,7},{4,0},{5,1},{6,2},{7,3},{8,12},{9,13},{10,... | collective-permute-start | bytes 786440 | tf_op jit(solution)/shard_map/ppermute | solution.py:940
  144.7 5.4 %collective-permute-start.7 = (f32[512,256]{1,0:T(8,128)S(1)}, f32[512,256]{1,0:T(8,128)S(1)}, u32[]{:S(2)}, u32[]{:S(2)}) collective-permute-start(f32[512,256]{1,0:T(8,128)S(1)} %get-tuple-element.73), channel_id=1, source_target_pairs={{0,8},{8,0},{1,9},{9,1},{2,10},{10,2},{3,11},{11,3},{4,12},{12,4},... | collective-permute-start | bytes 1572872 | tf_op jit(solution)/shard_map/ppermute | solution.py:972
  150.7 28.8 %all-to-all-start.5 = ((f32[64,8,128]{2,1,0:T(8,128)}), f32[64,8,128]{2,1,0:T(8,128)S(1)}, u32[]{:S(2)}, u32[]{:S(2)}) async-start(f32[64,8,128]{2,1,0:T(8,128)} %shard_map.106), calls=%async_computation.5 | async-start | bytes 524288 | tf_op jit(solution)/shard_map/all_to_all | solution.py:975
  157.4 22.2 %collective-permute-start.8 = (f32[256,256]{1,0:T(8,128)S(1)}, f32[256,256]{1,0:T(8,128)S(1)}, u32[]{:S(2)}, u32[]{:S(2)}) collective-permute-start(f32[256,256]{1,0:T(8,128)S(1)} %get-tuple-element.83), channel_id=1, source_target_pairs={{0,4},{1,5},{2,6},{3,7},{4,0},{5,1},{6,2},{7,3},{8,12},{9,13},{10,... | collective-permute-start | bytes 786440 | tf_op jit(solution)/shard_map/ppermute | solution.py:940
  171.7 1.0 copy-start.3
  179.6 30.6 %copy-start.2 = (bf16[1024,256]{1,0:T(8,128)(2,1)S(1)}, bf16[1024,256]{1,0:T(8,128)(2,1)}, u32[]{:S(2)}) copy-start(bf16[1024,256]{1,0:T(8,128)(2,1)} %refs_5_.1) | copy-start | bytes 1572868
  179.6 30.6 %copy-start.7 = (bf16[128,256]{1,0:T(8,128)(2,1)S(1)}, bf16[128,256]{1,0:T(8,128)(2,1)}, u32[]{:S(2)}) copy-start(bf16[128,256]{1,0:T(8,128)(2,1)} %refs_4_.1) | copy-start | bytes 196612
  179.6 30.6 %copy-start.10 = (s32[4,96]{1,0:T(4,128)S(1)}, s32[4,96]{1,0:T(4,128)}, u32[]{:S(2)}) copy-start(s32[4,96]{1,0:T(4,128)} %mask.3) | copy-start | bytes 4612
  188.6 25.6 %all-to-all-start.6 = ((f32[32,72,128]{2,1,0:T(8,128)}), f32[32,72,128]{2,1,0:T(8,128)S(1)}, u32[]{:S(2)}, u32[]{:S(2)}) async-start(f32[32,72,128]{2,1,0:T(8,128)} %shard_map.109), calls=%async_computation.6 | async-start | bytes 2359296 | tf_op jit(solution)/shard_map/all_to_all | solution.py:985
  196.7 7.1 %collective-permute-start.10 = (f32[128,256]{1,0:T(8,128)S(1)}, f32[128,256]{1,0:T(8,128)S(1)}, u32[]{:S(2)}, u32[]{:S(2)}) collective-permute-start(f32[128,256]{1,0:T(8,128)S(1)} %get-tuple-element.95.refs_0_), channel_id=1, source_target_pairs={{0,1},{1,0},{2,3},{3,2},{4,5},{5,4},{6,7},{7,6},{8,9},{9,8},{10,11... | collective-permute-start | bytes 393224 | tf_op jit(solution)/shard_map/ppermute | solution.py:940
  198.2 12.0 %collective-permute-start.11 = (f32[128,256]{1,0:T(8,128)S(1)}, f32[128,256]{1,0:T(8,128)S(1)}, u32[]{:S(2)}, u32[]{:S(2)}) collective-permute-start(f32[128,256]{1,0:T(8,128)S(1)} %get-tuple-element.96), channel_id=1, source_target_pairs={{0,3},{1,2},{2,1},{3,0},{4,7},{5,6},{6,5},{7,4},{8,11},{9,10},{10,... | collective-permute-start | bytes 393224 | tf_op jit(solution)/shard_map/ppermute | solution.py:940
  198.2 12.0 %collective-permute-start.9 = (f32[128,256]{1,0:T(8,128)S(1)}, f32[128,256]{1,0:T(8,128)S(1)}, u32[]{:S(2)}, u32[]{:S(2)}) collective-permute-start(f32[128,256]{1,0:T(8,128)S(1)} %get-tuple-element.96), channel_id=1, source_target_pairs={{0,2},{1,3},{2,0},{3,1},{4,6},{5,7},{6,4},{7,5},{8,10},{9,11},{10,... | collective-permute-start | bytes 393224 | tf_op jit(solution)/shard_map/ppermute | solution.py:940
Sparse Core Ops, SparseCore 0:
  13.7 59.0 all-gather.2

commit v6 on v5

--- a/solution.py
+++ b/solution.py
@@ -46,20 +46,15 @@
 
 
 def stream(source, buf, sem, steps, body):
-    def copy(j, slot):
-        return pltpu.make_async_copy(source(j), buf.at[slot], sem.at[slot])
-
-    copy(0, 0).start()
+    def copy(j):
+        return pltpu.make_async_copy(source(j), buf.at[j], sem.at[j])
+
+    for j in range(steps):
+        copy(j).start()
 
     def step(j, _):
-        slot = lax.rem(j, 2)
-
-        @pl.when(j + 1 < steps)
-        def _():
-            copy(j + 1, 1 - slot).start()
-
-        copy(j, slot).wait()
-        body(j, buf.at[slot])
+        copy(j).wait()
+        body(j, buf.at[j])
         return 0
 
     lax.fori_loop(0, steps, step, 0)
@@ -135,8 +130,9 @@
     return lambda j: protos.at[:, pl.ds(pl.multiple_of(core * columns + j * size, size), size)]
 
 
-def proto_scratch(width, size=BN):
-    return [pltpu.VMEM((2, width, size), BF16), pltpu.SemaphoreType.DMA((2,))]
+def proto_scratch(width, columns, size=BN):
+    steps = columns // size
+    return [pltpu.VMEM((steps, width, size), BF16), pltpu.SemaphoreType.DMA((steps,))]
 
 
 def put_columns(step, heads, out):
@@ -170,11 +166,11 @@
 
     def step(j, block):
         w = unit_cols(block[...])[0].astype(BF16)
-        slot = lax.rem(j, 2)
-
-        @pl.when(j >= 2)
+        slot = lax.rem(j, 4)
+
+        @pl.when(j >= 4)
         def _():
-            leave(j - 2, slot).wait()
+            leave(j - 4, slot).wait()
 
         heads = []
         for first, last in ((0, 2 * crops), (2 * crops, rows)):
@@ -189,8 +185,8 @@
         put_columns(j, heads, sums)
 
     stream(proto_source(idx[0], protos), buf, sem, steps, step)
-    for j in (steps - 2, steps - 1):
-        leave(j, j % 2).wait()
+    for j in range(max(steps - 4, 0), steps):
+        leave(j, j % 4).wait()
 
 
 def teacher_pass(idx, own, other, protos, crops, copies):
@@ -204,10 +200,10 @@
         "hv",
         scratch=[
             pltpu.VMEM((rows, width), BF16),
-            pltpu.VMEM((2, rows, BN), BF16),
-            pltpu.SemaphoreType.DMA((2,)),
+            pltpu.VMEM((4, rows, BN), BF16),
+            pltpu.SemaphoreType.DMA((4,)),
         ]
-        + proto_scratch(width),
+        + proto_scratch(width, columns),
         flops=2 * rows * width * columns,
         traffic=2 * rows * columns,
     )
@@ -248,7 +244,7 @@
         [idx, own, other, protos],
         "svvh",
         scratch=[pltpu.VMEM((rows, width), BF16), pltpu.VMEM((rows, 128), F32)]
-        + proto_scratch(width, 2 * BN),
+        + proto_scratch(width, columns, 2 * BN),
         flops=4 * rows * width * columns,
         traffic=2 * width * columns,
     )
@@ -360,7 +356,7 @@
         "shvh",
         scratch=[pltpu.VMEM((rows, width), F32), pltpu.VMEM((2 * columns // 128, 128), F32)]
         + expo_scratch(expo, columns // BN)
-        + proto_scratch(width),
+        + proto_scratch(width, columns),
         flops=2 * rows * columns * width,
         traffic=2 * rows * columns,
     )
@@ -415,35 +411,36 @@
     return protos.at[:, pl.ds(at, part)]
 
 
-def stream_rows(ny, base, half, own, other, buf, sem, body):
-    def copy(step, slot):
-        ref = own if step < ny else other
-        return pltpu.make_async_copy(
-            ref.at[step % ny, pl.ds(base, half), :], buf.at[slot], sem.at[slot]
-        )
-
-    copy(0, 0).start()
-    for step in range(2 * ny):
-        if step + 1 < 2 * ny:
-            copy(step + 1, (step + 1) % 2).start()
-        copy(step, step % 2).wait()
-        body(step // ny, step % ny, buf.at[step % 2])
-
-
-def wide_teacher_kernel(ny, crops, idx, own, other, protos, expo_d, expo_i, w, wbuf, out, osem, buf, sem, wsem):
+def stream_rows(ny, here, base, half, refs, buf, sem, ready, body):
+    copies = [
+        pltpu.make_async_copy(ref.at[pl.ds(base, half), :], buf.at[i], sem.at[i])
+        for i, ref in enumerate(refs)
+    ]
+    for copy in copies:
+        copy.start()
+    ready()
+    for i, copy in enumerate(copies):
+        copy.wait()
+        body(i // ny, lax.rem(here + ny - i % ny, ny), buf.at[i])
+
+
+def wide_teacher_kernel(ny, crops, idx, protos, *refs):
+    expo_d, expo_i, w, wbuf, out, osem, buf, sem, wsem = refs[2 * ny :]
     half = buf.shape[1]
     rest = half - crops
     fetch = pltpu.make_async_copy(part_source(idx, ny, protos), wbuf, wsem)
     fetch.start()
-    fetch.wait()
-    w[...] = unit_cols(wbuf[...])[0].astype(BF16)
     leaving = []
+
+    def ready():
+        fetch.wait()
+        w[...] = unit_cols(wbuf[...])[0].astype(BF16)
 
     def body(side, y, ref):
         place = 2 * y + jnp.where(idx[0] == side, 0, 1)
-        slot = len(leaving) % 2
-        if len(leaving) >= 2:
-            for copy in leaving[-2]:
+        slot = len(leaving) % 4
+        if len(leaving) >= 4:
+            for copy in leaving[-4]:
                 copy.wait()
         feats = ref[...].astype(BF16)
         for start in range(0, half, 128):
@@ -464,29 +461,30 @@
             copy.start()
         leaving.append(copies)
 
-    stream_rows(ny, 0, half, own, other, buf, sem, body)
-    for copies in leaving[-2:]:
+    stream_rows(ny, idx[3], 0, half, refs[: 2 * ny], buf, sem, ready, body)
+    for copies in leaving[-4:]:
         for copy in copies:
             copy.wait()
 
 
-def wide_teacher_pass(idx, own, other, protos, crops):
-    ny, rows, width = own.shape
+def wide_teacher_pass(idx, gathered, protos, crops):
+    ny = len(gathered) // 2
+    rows, width = gathered[0].shape
     half = rows // 2
     part = protos.shape[1] // 2 // ny
     return call(
         functools.partial(wide_teacher_kernel, ny, crops),
         [array((2 * ny * crops, part), BF16), array((2 * ny * (half - crops), part), BF16)],
-        [idx, own, other, protos],
-        "shhh",
+        [idx, protos, *gathered],
+        "sh" + "h" * len(gathered),
         "hh",
         scratch=[
             pltpu.VMEM((width, part), BF16),
             pltpu.VMEM((width, part), BF16),
-            pltpu.VMEM((2, half, part), BF16),
-            pltpu.SemaphoreType.DMA((2, 2)),
-            pltpu.VMEM((2, half, width), F32),
-            pltpu.SemaphoreType.DMA((2,)),
+            pltpu.VMEM((4, half, part), BF16),
+            pltpu.SemaphoreType.DMA((4, 2)),
+            pltpu.VMEM((2 * ny, half, width), F32),
+            pltpu.SemaphoreType.DMA((2 * ny,)),
             pltpu.SemaphoreType.DMA,
         ],
         flops=2 * 2 * ny * half * width * part,
@@ -494,7 +492,9 @@
     )
 
 
-def wide_student_kernel(ny, crops, idx, own, other, protos, *refs):
+def wide_student_kernel(ny, crops, idx, protos, *refs):
+    gathered = refs[: 2 * ny]
+    refs = refs[2 * ny :]
     totals = refs[:ny]
     out, wnorm_out, turned_d, turned_i, w, wbuf, scale, left, expo, buf, sem, wsem = refs[ny:]
     half = buf.shape[1]
@@ -505,10 +505,12 @@
     for s in range(ny):
         y = lax.rem(idx[3] + ny - s, ny)
         scale[pl.ds(pl.multiple_of(y * sub, sub), sub), :] = GRAD_SCALE / totals[s][...]
-    fetch.wait()
-    wnorm_out[...] = unit_cols(wbuf[...])[0]
-    w[...] = wnorm_out[...].astype(BF16)
     out[...] = jnp.zeros_like(out)
+
+    def ready():
+        fetch.wait()
+        wnorm_out[...] = unit_cols(wbuf[...])[0]
+        w[...] = wnorm_out[...].astype(BF16)
 
     def body(side, y, ref):
         core = jnp.where(idx[0] == side, 0, 1)
@@ -526,11 +528,12 @@
             expo[start : start + 128, :] = jnp.exp2(score * (LOG2E / STUDENT_TEMP)).astype(BF16)
         out[...] += jnp.dot(left[...], expo[...], preferred_element_type=F32)
 
-    stream_rows(ny, half, half, own, other, buf, sem, body)
-
-
-def wide_student_pass(idx, own, other, protos, totals, crops):
-    ny, rows, width = own.shape
+    stream_rows(ny, idx[3], half, half, gathered, buf, sem, ready, body)
+
+
+def wide_student_pass(idx, gathered, protos, totals, crops):
+    ny = len(gathered) // 2
+    rows, width = gathered[0].shape
     half = rows // 2
     part = protos.shape[1] // 2 // ny
     return call(
@@ -541,16 +544,16 @@
             array((width, 2 * ny * crops), BF16),
             array((width, 2 * ny * (half - crops)), BF16),
         ],
-        [idx, own, other, protos, *totals],
-        "shhh" + "v" * ny,
+        [idx, protos, *gathered, *totals],
+        "sh" + "h" * len(gathered) + "v" * ny,
         scratch=[
             pltpu.VMEM((width, part), BF16),
             pltpu.VMEM((width, part), BF16),
             pltpu.VMEM((ny * rows // 128, 128), F32),
             pltpu.VMEM((width, half), BF16),
             pltpu.VMEM((half, part), BF16),
-            pltpu.VMEM((2, half, width), F32),
-            pltpu.SemaphoreType.DMA((2,)),
+            pltpu.VMEM((2 * ny, half, width), F32),
+            pltpu.SemaphoreType.DMA((2 * ny,)),
             pltpu.SemaphoreType.DMA,
         ],
         flops=4 * 2 * ny * half * width * part,
@@ -558,7 +561,15 @@
     )
 
 
-def weight_kernel(ny, crops, idx, prob, wnorm, turned_d, turned_i, expo_d, expo_i, colparts, rowparts, out, left_d, left_i, scales, rowscale, buf_d, buf_i, sems_d, sems_i, targets):
+def weight_kernel(ny, crops, idx, prob_in, wnorm_in, turned_d_in, turned_i_in, expo_d, expo_i, colparts, rowparts, out, left_d, left_i, scales, rowscale, buf_d, buf_i, sems_d, sems_i, targets, prob, wnorm, turned_d, turned_i, sem):
+    loads = [
+        pltpu.make_async_copy(src, dst, sem.at[i])
+        for i, (src, dst) in enumerate(
+            ((turned_d_in, turned_d), (turned_i_in, turned_i), (prob_in, prob), (wnorm_in, wnorm))
+        )
+    ]
+    for copy in loads[:2]:
+        copy.start()
     copies, _, _ = out.shape
     width, part = prob.shape
     own = width // copies
@@ -573,7 +584,7 @@
                 for i in range(sems.shape[0])
             ]
         )
-    for copy in streams[0] + streams[1]:
+    for copy in streams[0] + streams[1] + loads[2:]:
         copy.start()
     group = rowparts.shape[0] // ny
     sub = rowparts.shape[1]
@@ -593,6 +604,8 @@
             for t in range(ci):
                 at = y * sub + 2 * cd + core * ci + t
                 lines_i.append(rowscale[at : at + 1, :])
+    loads[0].wait()
+    loads[1].wait()
     left_d[...] = (turned_d[...].astype(F32) * jnp.concatenate(lines_d, axis=1)).astype(BF16)
     left_i[...] = (turned_i[...].astype(F32) * jnp.concatenate(lines_i, axis=1)).astype(BF16)
     per_head = scales.shape[0] // 2
@@ -607,6 +620,8 @@
                 targets[head] = value
             else:
                 targets[head] += value
+    loads[2].wait()
+    loads[3].wait()
     for at in range(0, part, BN):
         span = slice(at, at + BN)
         wsum = prob[:, span]
@@ -634,7 +649,7 @@
         functools.partial(weight_kernel, ny, crops),
         array((copies, lines, 128)),
         [idx, prob, wnorm, *turned, *expo, colparts, rowparts],
-        "svvvvhhvv",
+        "shhhhhhvv",
         scratch=[
             pltpu.VMEM(turned[0].shape, BF16),
             pltpu.VMEM(turned[1].shape, BF16),
@@ -645,30 +660,44 @@
             pltpu.SemaphoreType.DMA((expo[0].shape[0] // 512,)),
             pltpu.SemaphoreType.DMA((expo[1].shape[0] // 512,)),
             pltpu.VMEM((2, width, part), F32),
+            pltpu.VMEM((width, part), F32),
+            pltpu.VMEM((width, part), F32),
+            pltpu.VMEM(turned[0].shape, BF16),
+            pltpu.VMEM(turned[1].shape, BF16),
+            pltpu.SemaphoreType.DMA((4,)),
         ],
         flops=2 * rows * width * part,
         traffic=2 * rows * part,
     )
 
 
-def norm_kernel(protos, out):
-    out[...] = unit_cols(protos[...])[1]
+def norm_kernel(protos, out, buf, sem):
+    blocks, size, _ = buf.shape
+    copies = [
+        pltpu.make_async_copy(protos.at[pl.ds(i * size, size), :], buf.at[i], sem.at[i])
+        for i in range(blocks)
+    ]
+    for copy in copies:
+        copy.start()
+    for i, copy in enumerate(copies):
+        copy.wait()
+        w = buf[i].astype(F32)
+        part = jnp.sum(w * w, axis=0, keepdims=True)
+        out[...] = part if i == 0 else out[...] + part
+    out[...] = lax.rsqrt(out[...] + EPS)
 
 
 def norm_pass(protos):
     width, columns = protos.shape
-    step = columns // 8
-    return pl.pallas_call(
+    return call(
         norm_kernel,
-        grid=(8,),
-        in_specs=[pl.BlockSpec((width, step), lambda j: (0, j))],
-        out_specs=pl.BlockSpec((1, step), lambda j: (0, j)),
-        out_shape=array((1, columns)),
-        compiler_params=pltpu.CompilerParams(vmem_limit_bytes=VMEM_LIMIT),
-        cost_estimate=pl.CostEstimate(
-            flops=3 * width * columns, bytes_accessed=2 * width * columns, transcendentals=0
-        ),
-    )(protos)
+        array((1, columns)),
+        [protos],
+        "h",
+        scratch=[pltpu.VMEM((8, width // 8, columns), BF16), pltpu.SemaphoreType.DMA((8,))],
+        flops=3 * width * columns,
+        traffic=2 * width * columns,
+    )
 
 
 def proto_kernel(nx, ny, idx, parts, protos, winv, out, rows, sem):
@@ -930,7 +959,9 @@
 
     own = prep(teacher_crops, teacher_patches, student_crops, student_patches, patch_mask)
     other = lax.ppermute(own, "c", swap)
-    all_own = lax.all_gather(own, "y")
+    up, down = shifted(ny, 1), shifted(ny, ny - 1)
+    from_up = lax.ppermute(own, "y", up)
+    from_down = lax.ppermute(own, "y", down) if ny > 2 else None
     expo, sums = teacher_pass(idx, own, other, teacher_protos, crops, nx * ny)
     sub = 2 * (crops + images * masked) // 128
 
@@ -945,7 +976,12 @@
     rowparts = lax.all_to_all(sums, ("c", "z"), 0, 0)
     later_protos, _ = tie(student_protos, sums)
     winv = norm_pass(later_protos)
-    rowparts, winv = tie(rowparts, winv)
+    rowparts, winv, from_up, from_down = tie(rowparts, winv, from_up, from_down)
+    ring = [own, from_up]
+    while len(ring) < ny - 1:
+        ring.append(lax.ppermute(ring[-1], "y", up))
+    if ny > 2:
+        ring.append(from_down)
     totals = jnp.sum(rowparts[:, sub:, :], axis=0)
     sums = column_pass(expo, rowparts, crops, nx * ny)
 
@@ -957,14 +993,14 @@
     colparts, p_send, *all_totals = tie(colparts, p_send, *all_totals)
     p_came = across(p_send, nz // 2)
     sums = row_pass(expo, colparts, None, crops, 2 * nz)
-    all_own, sums = tie(all_own, sums)
-    all_other = lax.ppermute(all_own, "c", swap)
+    sums, *ring = tie(sums, *ring)
+    gathered = ring + [other] + [lax.ppermute(rows, "c", swap) for rows in ring[1:]]
     rowparts = lax.all_to_all(sums, ("c", "z"), 0, 0)
     sums = column_pass(expo, rowparts, crops, nx * ny)
 
     colparts = lax.all_to_all(sums, ("x", "y"), 0, 0)
-    all_own, all_other, _ = tie(all_own, all_other, sums)
-    wide_expo = wide_teacher_pass(idx, all_own, all_other, teacher_protos, crops)
+    *gathered, _ = tie(*gathered, sums)
+    wide_expo = wide_teacher_pass(idx, gathered, teacher_protos, crops)
     colparts, p_came, *wide_expo = tie(colparts, p_came, *wide_expo)
     target_mine, target_theirs = target_pass(idx, expo, colparts, student_protos, crops)
     colparts, target_theirs = tie(colparts, target_theirs)
@@ -974,10 +1010,8 @@
     sums, send = tie(sums, send)
     rowparts = lax.all_to_all(sums, ("y", "c", "z"), 0, 0)
     came = across(send, nz // 2)
-    all_own, all_other, _ = tie(all_own, all_other, sums)
-    prob, wnorm, *turned = wide_student_pass(
-        idx, all_own, all_other, student_protos, all_totals, crops
-    )
+    *gathered, _ = tie(*gathered, sums)
+    prob, wnorm, *turned = wide_student_pass(idx, gathered, student_protos, all_totals, crops)
     prob, came = tie(prob, came)
     outgoing = weight_pass(
         idx, prob, wnorm, turned, wide_expo, colparts, rowparts, crops, ny, nx * ny * 2

time: 228 us -> 220 us (0.965)
  between operations: 14.3 us -> 1.14 us
  Pallas kernels: 96.2 us -> 85.9 us
  waiting for transfers between devices: 39.4 us -> 49.4 us
  starting transfers between devices: 54.3 us -> 60.7 us
    ppermute x3, waiting for transfers between devices: 4.08 us -> 12.7 us  [local(): lax.ppermute(totals, 'y', shifted(ny, s))]
    pallas_call x18 -> x19, Pallas kernels: 91.5 us -> 85.9 us  [call(): pl.pallas_call(kernel, out_shape=out_shape, out_specs=out_specs, in_specs...]
    pallas_call x1 -> x0, Pallas kernels: 4.67 us -> none  [norm_pass(): pl.pallas_call(norm_kernel, grid=(8,), in_specs=[pl.BlockSpec((width, ste...]
    ppermute x1 -> x6, starting transfers between devices: 0.09 us -> 3.78 us  [the longest x1 3.09 us: local(): from_down = lax.ppermute(own, 'y', down) if ny > 2 else None]
    all_to_all x3, starting transfers between devices: 15.8 us -> 18.6 us  [local(): colparts = lax.all_to_all(sums, ('x', 'y'), 0, 0)]
    ppermute x1, waiting for transfers between devices: 2.77 us -> 0.01 us  [local(): other = lax.ppermute(own, 'c', swap)]
    all_to_all x1, waiting for transfers between devices: 3.54 us -> 5.85 us  [local(): rowparts = lax.all_to_all(sums, ('c', 'z'), 0, 0)]
    unnamed x24 -> x26, local copies, waits for them, and re-layouts: 8.58 us -> 8.61 us
  transfers between devices with their start and end apart: 19 -> 23, of which waited for: 11 -> 9; matrix products, arithmetic and copies ran while one was open for 0% -> 0% of each run, Pallas kernels for 32% -> 30%
where the time goes in v6:
time: 220 us; the launch traced here: 217 us
  Pallas kernels  85.9 us (39%)
  starting transfers between devices  60.7 us (28%)
  waiting for transfers between devices  49.4 us (22%)
  blocking collectives  10.9 us (5%)
  local copies, waits for them, and re-layouts  8.61 us (4%)
    pallas_call x19, Pallas kernels, call(): pl.pallas_call(kernel, out_shape=out_shape, out_specs=out_specs, in_specs...  85.9 us
    ppermute x5, waiting for transfers between devices, across(): return lax.ppermute(value, 'z', [(i, i ^ bit) for i in range(nz)])  25.2 us
    all_to_all x3, starting transfers between devices, local(): colparts = lax.all_to_all(sums, ('x', 'y'), 0, 0)  18.6 us
    ppermute x3, waiting for transfers between devices, local(): lax.ppermute(totals, 'y', shifted(ny, s))  12.7 us
    all_to_all x1, blocking collectives, local(): rowparts = lax.all_to_all(sums, ('c', 'z'), 0, 0)  10.9 us
    ppermute x5, starting transfers between devices, across(): return lax.ppermute(value, 'z', [(i, i ^ bit) for i in range(nz)])  10.6 us
    unnamed x26, local copies, waits for them, and re-layouts  8.61 us
    all_to_all x1, starting transfers between devices, local(): rowparts = lax.all_to_all(sums, ('c', 'z'), 0, 0)  8.6 us
  transfers between devices with their start and end apart: 23, of which 9 were waited for; matrix products, arithmetic and copies ran while one was open for 0% of the time, Pallas kernels for 30%

profile of v6, /device:TPU:32, one launch (start us, length us, event | category | flops | bytes accessed | tf_op | source)
XLA Modules:
  0.0 216.7 jit_solution(7103497298843969594)
XLA Ops:
  7.1 3.1 %collective-permute-start.2 = (f32[1024,256]{1,0:T(8,128)}, f32[1024,256]{1,0:T(8,128)}, u32[]{:S(2)}, u32[]{:S(2)}) collective-permute-start(f32[1024,256]{1,0:T(8,128)} %shard_map.94.own.refs_0_), channel_id=1, source_target_pairs={{0,48},{16,0},{32,16},{48,32},{1,49},{17,1},{33,17},{49,33},{2,50}... | collective-permute-start | bytes 3145736 | tf_op jit(solution)/shard_map/ppermute | solution.py:964
  12.5 8.9 %shard_map.95 = (bf16[1024,4096]{1,0:T(8,128)(2,1)}, f32[16,64,128]{2,1,0:T(8,128)}) custom-call(s32[4]{0:T(128)S(1)} %pad_add_fusion.idx, f32[1024,256]{1,0:T(8,128)S(1)} %copy-done, f32[1024,256]{1,0:T(8,128)} %copy-done.12, bf16[256,8192]{1,0:T(8,128)(2,1)} %protos.9), custom_call_target="tpu_custom_call" | custom-call | flops 2147483648 | bytes 8388608 | tf_op jit(solution)/shard_map/pallas_call | solution.py:33
  21.4 7.1 %all-to-all-start = ((f32[16,64,128]{2,1,0:T(8,128)}), f32[16,64,128]{2,1,0:T(8,128)S(1)}, u32[]{:S(2)}, u32[]{:S(2)}) async-start(f32[16,64,128]{2,1,0:T(8,128)} %get-tuple-element.69), calls=%async_computation | async-start | bytes 1048576 | tf_op jit(solution)/shard_map/all_to_all | solution.py:973
  28.5 8.7 %shard_map.96 = (f32[8,128]{1,0:T(8,128)S(1)}, f32[1024,256]{1,0:T(8,128)S(1)}) custom-call(s32[4]{0:T(128)S(1)} %pad_add_fusion.idx, f32[1024,256]{1,0:T(8,128)} %shard_map.94.own.refs_0_, f32[1024,256]{1,0:T(8,128)} %copy-done.12, bf16[256,8192]{1,0:T(8,128)(2,1)} %protos.12), custom_call_target="tpu_custom_call" | custom-call | flops 4294967296 | bytes 2097152 | tf_op jit(solution)/shard_map/pallas_call | solution.py:33
  38.2 4.3 %all-to-all-done.colparts = f32[16,64,128]{2,1,0:T(8,128)S(1)} async-done(((f32[16,64,128]{2,1,0:T(8,128)}), f32[16,64,128]{2,1,0:T(8,128)S(1)}, u32[]{:S(2)}, u32[]{:S(2)}) %all-to-all-start) | async-done | bytes 524320 | tf_op jit(solution)/shard_map/all_to_all | solution.py:973
  42.5 5.1 %shard_map.97 = f32[16,16,128]{2,1,0:T(8,128)} custom-call(bf16[1024,4096]{1,0:T(8,128)(2,1)} %get-tuple-element.68.expo, f32[16,64,128]{2,1,0:T(8,128)S(1)} %all-to-all-done.colparts, f32[8,128]{1,0:T(8,128)S(1)} %get-tuple-element.70.refs_0_), custom_call_target="tpu_custom_call" | custom-call | flops 8388608 | bytes 8388608 | tf_op jit(solution)/shard_map/pallas_call | solution.py:33
  47.6 8.6 %all-to-all-start.1 = ((f32[16,16,128]{2,1,0:T(8,128)}), f32[16,16,128]{2,1,0:T(8,128)S(1)}, u32[]{:S(2)}, u32[]{:S(2)}) async-start(f32[16,16,128]{2,1,0:T(8,128)} %shard_map.97), calls=%async_computation.1 | async-start | bytes 262144 | tf_op jit(solution)/shard_map/all_to_all | solution.py:976
  56.2 2.3 %shard_map.98.winv = f32[1,8192]{1,0:T(1,128)S(1)} custom-call(bf16[256,8192]{1,0:T(8,128)(2,1)} %protos.12), custom_call_target="tpu_custom_call" | custom-call | flops 6291456 | bytes 4194304 | tf_op jit(solution)/shard_map/pallas_call | solution.py:33
  58.6 5.8 %all-to-all-done.1.rowparts = f32[16,16,128]{2,1,0:T(8,128)S(1)} async-done(((f32[16,16,128]{2,1,0:T(8,128)}), f32[16,16,128]{2,1,0:T(8,128)S(1)}, u32[]{:S(2)}, u32[]{:S(2)}) %all-to-all-start.1) | async-done | bytes 131104 | tf_op jit(solution)/shard_map/all_to_all | solution.py:976
  64.5 4.6 %shard_map.99 = f32[16,64,128]{2,1,0:T(8,128)} custom-call(bf16[1024,4096]{1,0:T(8,128)(2,1)} %get-tuple-element.68.expo, f32[16,16,128]{2,1,0:T(8,128)S(1)} %all-to-all-done.1.rowparts), custom_call_target="tpu_custom_call" | custom-call | flops 8388608 | bytes 8388608 | tf_op jit(solution)/shard_map/pallas_call | solution.py:33
  70.7 7.1 %all-to-all-start.2 = ((f32[16,64,128]{2,1,0:T(8,128)}), f32[16,64,128]{2,1,0:T(8,128)S(1)}, u32[]{:S(2)}, u32[]{:S(2)}) async-start(f32[16,64,128]{2,1,0:T(8,128)} %shard_map.99), calls=%async_computation.2 | async-start | bytes 1048576 | tf_op jit(solution)/shard_map/all_to_all | solution.py:988
  77.8 3.1 %collective-permute-start.6 = (f32[8,128]{1,0:T(8,128)S(1)}, f32[8,128]{1,0:T(8,128)S(1)}, u32[]{:S(2)}, u32[]{:S(2)}) collective-permute-start(f32[8,128]{1,0:T(8,128)S(1)} %slice_reduce_fusion.totals.refs_8_), channel_id=1, source_target_pairs={{0,48},{16,0},{32,16},{48,32},{1,49},{17,1},{33,17},{49,33},{2,50}... | collective-permute-start | bytes 12296 | tf_op jit(solution)/shard_map/ppermute | solution.py:990
  83.3 11.2 %collective-permute-done.5.refs_10_ = f32[8,128]{1,0:T(8,128)S(1)} collective-permute-done((f32[8,128]{1,0:T(8,128)S(1)}, f32[8,128]{1,0:T(8,128)S(1)}, u32[]{:S(2)}, u32[]{:S(2)}) %collective-permute-start.5) | collective-permute-done | bytes 4128 | tf_op jit(solution)/shard_map/ppermute | solution.py:990
  96.1 4.5 %shard_map.102 = f32[16,8,128]{2,1,0:T(8,128)S(1)} custom-call(bf16[1024,4096]{1,0:T(8,128)(2,1)} %get-tuple-element.68.expo, f32[16,64,128]{2,1,0:T(8,128)S(1)} %all-to-all-done.2.colparts), custom_call_target="tpu_custom_call" | custom-call | flops 8388608 | bytes 8388608 | tf_op jit(solution)/shard_map/pallas_call | solution.py:33
  101.3 10.9 %all_to_all.35.rowparts = f32[16,8,128]{2,1,0:T(8,128)S(1)} all-to-all(f32[16,8,128]{2,1,0:T(8,128)S(1)} %shard_map.102), channel_id=1, replica_groups=mesh['x'=4,'y'=4,'c'=2,'z'=8] {'c','z'}, dimensions={0} | all-to-all | bytes 131072 | tf_op jit(solution)/shard_map/all_to_all | solution.py:998
  112.2 4.7 %shard_map.103 = f32[16,64,128]{2,1,0:T(8,128)} custom-call(bf16[1024,4096]{1,0:T(8,128)(2,1)} %get-tuple-element.68.expo, f32[16,8,128]{2,1,0:T(8,128)S(1)} %all_to_all.35.rowparts), custom_call_target="tpu_custom_call" | custom-call | flops 8388608 | bytes 8388608 | tf_op jit(solution)/shard_map/pallas_call | solution.py:33
  116.9 4.4 %all-to-all-start.4 = ((f32[16,64,128]{2,1,0:T(8,128)}), f32[16,64,128]{2,1,0:T(8,128)S(1)}, u32[]{:S(2)}, u32[]{:S(2)}) async-start(f32[16,64,128]{2,1,0:T(8,128)} %shard_map.103), calls=%async_computation.4 | async-start | bytes 1048576 | tf_op jit(solution)/shard_map/all_to_all | solution.py:1001
  122.9 6.5 %shard_map.104 = (bf16[1024,1024]{1,0:T(8,128)(2,1)}, bf16[3072,1024]{1,0:T(8,128)(2,1)}) custom-call(s32[4]{0:T(128)S(1)} %pad_add_fusion.idx, bf16[256,8192]{1,0:T(8,128)(2,1)} %protos.9, f32[1024,256]{1,0:T(8,128)S(1)} %copy-done.1, f32[1024,256]{1,0:T(8,128)} %collective-permute-done.1.refs_1_, f32[1024,256]{1,0:T(8,128)} %collective-permute-done.7.refs_2_, ...), custom_call_target="tpu_custom_call" | custom-call | flops 2147483648 | bytes 4194304 | tf_op jit(solution)/shard_map/pallas_call | solution.py:33
  129.4 9.3 %collective-permute-done.11.prob_came = f32[256,256]{1,0:T(8,128)S(1)} collective-permute-done((f32[256,256]{1,0:T(8,128)S(1)}, f32[256,256]{1,0:T(8,128)S(1)}, u32[]{:S(2)}, u32[]{:S(2)}) %collective-permute-start.11) | collective-permute-done | bytes 262176 | tf_op jit(solution)/shard_map/ppermute | solution.py:971
  138.7 6.6 %shard_map.105 = (f32[512,256]{1,0:T(8,128)S(1)}, f32[512,256]{1,0:T(8,128)S(1)}) custom-call(s32[4]{0:T(128)S(1)} %pad_add_fusion.idx, bf16[1024,4096]{1,0:T(8,128)(2,1)} %get-tuple-element.68.expo, f32[16,64,128]{2,1,0:T(8,128)S(1)} %all-to-all-done.4.colparts, bf16[256,8192]{1,0:T(8,128)(2,1)} %protos.12), custom_call_target="tpu_custom_call" | custom-call | flops 2147483648 | bytes 8388608 | tf_op jit(solution)/shard_map/pallas_call | solution.py:33
  145.3 5.3 %shard_map.106 = f32[64,8,128]{2,1,0:T(8,128)} custom-call(bf16[1024,4096]{1,0:T(8,128)(2,1)} %get-tuple-element.68.expo, f32[16,64,128]{2,1,0:T(8,128)S(1)} %all-to-all-done.4.colparts), custom_call_target="tpu_custom_call" | custom-call | flops 8388608 | bytes 8388608 | tf_op jit(solution)/shard_map/pallas_call | solution.py:33
  151.3 6.8 %all-to-all-start.5 = ((f32[64,8,128]{2,1,0:T(8,128)}), f32[64,8,128]{2,1,0:T(8,128)S(1)}, u32[]{:S(2)}, u32[]{:S(2)}) async-start(f32[64,8,128]{2,1,0:T(8,128)} %shard_map.106), calls=%async_computation.5 | async-start | bytes 524288 | tf_op jit(solution)/shard_map/all_to_all | solution.py:1011
  158.1 4.6 %collective-permute-start.13 = (f32[256,256]{1,0:T(8,128)S(1)}, f32[256,256]{1,0:T(8,128)S(1)}, u32[]{:S(2)}, u32[]{:S(2)}) collective-permute-start(f32[256,256]{1,0:T(8,128)S(1)} %get-tuple-element.117), channel_id=1, source_target_pairs={{0,4},{1,5},{2,6},{3,7},{4,0},{5,1},{6,2},{7,3},{8,12},{9,13},{10,... | collective-permute-start | bytes 786440 | tf_op jit(solution)/shard_map/ppermute | solution.py:971
  162.6 9.7 %shard_map.108 = (f32[256,1024]{1,0:T(8,128)S(1)}, f32[256,1024]{1,0:T(8,128)}, bf16[256,1024]{1,0:T(8,128)(2,1)S(1)}, bf16[256,3072]{1,0:T(8,128)(2,1)}) custom-call(s32[4]{0:T(128)S(1)} %pad_add_fusion.idx, bf16[256,8192]{1,0:T(8,128)(2,1)} %protos.12, f32[1024,256]{1,0:T(8,128)} %shard_map.94.own.refs_0_, f32[1024,256]{1,0:T(8,128)} %collective-permute-done.1.refs_1_, ...), custom_call_target="tpu_custom_call" | custom-call | flops 4294967296 | bytes 4194304 | tf_op jit(solution)/shard_map/pallas_call | solution.py:33
  173.3 6.9 %collective-permute-done.13.target_came = f32[256,256]{1,0:T(8,128)S(1)} collective-permute-done((f32[256,256]{1,0:T(8,128)S(1)}, f32[256,256]{1,0:T(8,128)S(1)}, u32[]{:S(2)}, u32[]{:S(2)}) %collective-permute-start.13) | collective-permute-done | bytes 262176 | tf_op jit(solution)/shard_map/ppermute | solution.py:971
  180.3 8.4 %shard_map.109 = f32[32,72,128]{2,1,0:T(8,128)} custom-call(s32[4]{0:T(128)S(1)} %pad_add_fusion.idx, f32[256,1024]{1,0:T(8,128)} %copy-done.4, f32[256,1024]{1,0:T(8,128)} %get-tuple-element.119.wnorm_in, bf16[256,1024]{1,0:T(8,128)(2,1)S(1)} %get-tuple-element.120.turned_d_in, bf16[256,3072]{1,0:T(8,128)(2,1)} %get-tuple-element.121.turned_i_in, ...), custom_call_target="tpu_custom_call" | custom-call | flops 2147483648 | bytes 8388608 | tf_op jit(solution)/shard_map/pallas_call | solution.py:33
  188.6 7.2 %all-to-all-start.6 = ((f32[32,72,128]{2,1,0:T(8,128)}), f32[32,72,128]{2,1,0:T(8,128)S(1)}, u32[]{:S(2)}, u32[]{:S(2)}) async-start(f32[32,72,128]{2,1,0:T(8,128)} %shard_map.109), calls=%async_computation.6 | async-start | bytes 2359296 | tf_op jit(solution)/shard_map/all_to_all | solution.py:1019
  198.2 2.9 %collective-permute-start.14 = (f32[128,256]{1,0:T(8,128)S(1)}, f32[128,256]{1,0:T(8,128)S(1)}, u32[]{:S(2)}, u32[]{:S(2)}) collective-permute-start(f32[128,256]{1,0:T(8,128)S(1)} %get-tuple-element.130), channel_id=1, source_target_pairs={{0,2},{1,3},{2,0},{3,1},{4,6},{5,7},{6,4},{7,5},{8,10},{9,11},{10,... | collective-permute-start | bytes 393224 | tf_op jit(solution)/shard_map/ppermute | solution.py:971
  201.1 2.6 %collective-permute-done.15.refs_2_ = f32[128,256]{1,0:T(8,128)S(1)} collective-permute-done((f32[128,256]{1,0:T(8,128)S(1)}, f32[128,256]{1,0:T(8,128)S(1)}, u32[]{:S(2)}, u32[]{:S(2)}) %collective-permute-start.15) | collective-permute-done | bytes 131104 | tf_op jit(solution)/shard_map/ppermute | solution.py:971
  203.7 6.4 %collective-permute-done.16.refs_3_ = f32[128,256]{1,0:T(8,128)S(1)} collective-permute-done((f32[128,256]{1,0:T(8,128)S(1)}, f32[128,256]{1,0:T(8,128)S(1)}, u32[]{:S(2)}, u32[]{:S(2)}) %collective-permute-start.16) | collective-permute-done | bytes 131104 | tf_op jit(solution)/shard_map/ppermute | solution.py:971
  210.2 2.7 %shard_map.112 = (f32[16,256]{1,0:T(8,128)}, f32[128,256]{1,0:T(8,128)}) custom-call(s32[4]{0:T(128)S(1)} %pad_add_fusion.idx, s32[4,96]{1,0:T(4,128)S(1)} %copy-done.11, f32[128,256]{1,0:T(8,128)S(1)} %get-tuple-element.129.refs_0_, f32[128,256]{1,0:T(8,128)S(1)} %collective-permute-done.14.refs_1_, f32[128,256]{1,0:T(8,128)S(1)} %collective-permute-done.15.refs_2_, ...), custom_call_target="tpu_custom_call" | custom-call | tf_op jit(solution)/shard_map/pallas_call | solution.py:33
  214.2 2.3 %shard_map.110 = f32[8,8192]{1,0:T(8,128)} custom-call(s32[4]{0:T(128)S(1)} %pad_add_fusion.idx, f32[32,72,128]{2,1,0:T(8,128)S(1)} %all-to-all-done.6.parts, bf16[256,8192]{1,0:T(8,128)(2,1)} %protos.12, f32[1,8192]{1,0:T(1,128)S(1)} %shard_map.98.winv), custom_call_target="tpu_custom_call" | custom-call | tf_op jit(solution)/shard_map/pallas_call | solution.py:33
  (62 shorter events, 22.9 us)
Async XLA Ops:
  0.6 1.0 copy-start.2
  1.7 1.0 copy-start.6
  7.0 3.3 %collective-permute-start = (f32[1024,256]{1,0:T(8,128)}, f32[1024,256]{1,0:T(8,128)S(1)}, u32[]{:S(2)}, u32[]{:S(2)}) collective-permute-start(f32[1024,256]{1,0:T(8,128)} %shard_map.94.own.refs_0_), channel_id=1, source_target_pairs={{0,8},{8,0},{1,9},{9,1},{2,10},{10,2},{3,11},{11,3},{4,12},{12,4},... | collective-permute-start | bytes 3145736 | tf_op jit(solution)/shard_map/ppermute | solution.py:961
  7.1 51.4 %collective-permute-start.2 = (f32[1024,256]{1,0:T(8,128)}, f32[1024,256]{1,0:T(8,128)}, u32[]{:S(2)}, u32[]{:S(2)}) collective-permute-start(f32[1024,256]{1,0:T(8,128)} %shard_map.94.own.refs_0_), channel_id=1, source_target_pairs={{0,48},{16,0},{32,16},{48,32},{1,49},{17,1},{33,17},{49,33},{2,50}... | collective-permute-start | bytes 3145736 | tf_op jit(solution)/shard_map/ppermute | solution.py:964
  10.2 48.4 %collective-permute-start.1 = (f32[1024,256]{1,0:T(8,128)}, f32[1024,256]{1,0:T(8,128)}, u32[]{:S(2)}, u32[]{:S(2)}) collective-permute-start(f32[1024,256]{1,0:T(8,128)} %shard_map.94.own.refs_0_), channel_id=1, source_target_pairs={{0,16},{16,32},{32,48},{48,0},{1,17},{17,33},{33,49},{49,1},{2,18}... | collective-permute-start | bytes 3145736 | tf_op jit(solution)/shard_map/ppermute | solution.py:963
  10.3 1.0 copy-start.12
  11.3 1.2 copy-start
  21.4 21.1 %all-to-all-start = ((f32[16,64,128]{2,1,0:T(8,128)}), f32[16,64,128]{2,1,0:T(8,128)S(1)}, u32[]{:S(2)}, u32[]{:S(2)}) async-start(f32[16,64,128]{2,1,0:T(8,128)} %get-tuple-element.69), calls=%async_computation | async-start | bytes 1048576 | tf_op jit(solution)/shard_map/all_to_all | solution.py:973
  47.6 16.8 %all-to-all-start.1 = ((f32[16,16,128]{2,1,0:T(8,128)}), f32[16,16,128]{2,1,0:T(8,128)S(1)}, u32[]{:S(2)}, u32[]{:S(2)}) async-start(f32[16,16,128]{2,1,0:T(8,128)} %shard_map.97), calls=%async_computation.1 | async-start | bytes 262144 | tf_op jit(solution)/shard_map/all_to_all | solution.py:976
  64.5 36.1 %collective-permute-start.7 = (f32[1024,256]{1,0:T(8,128)}, f32[1024,256]{1,0:T(8,128)}, u32[]{:S(2)}, u32[]{:S(2)}) collective-permute-start(f32[1024,256]{1,0:T(8,128)} %collective-permute-done.1.refs_1_), channel_id=1, source_target_pairs={{0,16},{16,32},{32,48},{48,0},{1,17},{17,33},{33,49},{49,1},{2,18}... | collective-permute-start | bytes 3145736 | tf_op jit(solution)/shard_map/ppermute | solution.py:982
  70.6 12.1 %collective-permute-start.3 = (f32[512,256]{1,0:T(8,128)S(1)}, f32[512,256]{1,0:T(8,128)S(1)}, u32[]{:S(2)}, u32[]{:S(2)}) collective-permute-start(f32[512,256]{1,0:T(8,128)S(1)} %get-tuple-element.76), channel_id=1, source_target_pairs={{0,8},{8,0},{1,9},{9,1},{2,10},{10,2},{3,11},{11,3},{4,12},{12,4},... | collective-permute-start | bytes 1572872 | tf_op jit(solution)/shard_map/ppermute | solution.py:992
  70.7 25.4 %all-to-all-start.2 = ((f32[16,64,128]{2,1,0:T(8,128)}), f32[16,64,128]{2,1,0:T(8,128)S(1)}, u32[]{:S(2)}, u32[]{:S(2)}) async-start(f32[16,64,128]{2,1,0:T(8,128)} %shard_map.99), calls=%async_computation.2 | async-start | bytes 1048576 | tf_op jit(solution)/shard_map/all_to_all | solution.py:988
  77.8 5.5 %collective-permute-start.6 = (f32[8,128]{1,0:T(8,128)S(1)}, f32[8,128]{1,0:T(8,128)S(1)}, u32[]{:S(2)}, u32[]{:S(2)}) collective-permute-start(f32[8,128]{1,0:T(8,128)S(1)} %slice_reduce_fusion.totals.refs_8_), channel_id=1, source_target_pairs={{0,48},{16,0},{32,16},{48,32},{1,49},{17,1},{33,17},{49,33},{2,50}... | collective-permute-start | bytes 12296 | tf_op jit(solution)/shard_map/ppermute | solution.py:990
  81.0 13.6 %collective-permute-start.5 = (f32[8,128]{1,0:T(8,128)S(1)}, f32[8,128]{1,0:T(8,128)S(1)}, u32[]{:S(2)}, u32[]{:S(2)}) collective-permute-start(f32[8,128]{1,0:T(8,128)S(1)} %slice_reduce_fusion.totals.refs_8_), channel_id=1, source_target_pairs={{0,32},{16,48},{32,0},{48,16},{1,33},{17,49},{33,1},{49,17},{2,34}... | collective-permute-start | bytes 12296 | tf_op jit(solution)/shard_map/ppermute | solution.py:990
  81.8 14.2 %collective-permute-start.4 = (f32[8,128]{1,0:T(8,128)S(1)}, f32[8,128]{1,0:T(8,128)S(1)}, u32[]{:S(2)}, u32[]{:S(2)}) collective-permute-start(f32[8,128]{1,0:T(8,128)S(1)} %slice_reduce_fusion.totals.refs_8_), channel_id=1, source_target_pairs={{0,16},{16,32},{32,48},{48,0},{1,17},{17,33},{33,49},{49,1},{2,18}... | collective-permute-start | bytes 12296 | tf_op jit(solution)/shard_map/ppermute | solution.py:990
  100.6 22.3 %collective-permute-start.8 = (f32[1024,256]{1,0:T(8,128)}, f32[1024,256]{1,0:T(8,128)}, u32[]{:S(2)}, u32[]{:S(2)}) collective-permute-start(f32[1024,256]{1,0:T(8,128)} %collective-permute-done.1.refs_1_), channel_id=1, source_target_pairs={{0,8},{8,0},{1,9},{9,1},{2,10},{10,2},{3,11},{11,3},{4,12},{12,4},... | collective-permute-start | bytes 3145736 | tf_op jit(solution)/shard_map/ppermute | solution.py:997
  100.7 22.2 %collective-permute-start.9 = (f32[1024,256]{1,0:T(8,128)}, f32[1024,256]{1,0:T(8,128)}, u32[]{:S(2)}, u32[]{:S(2)}) collective-permute-start(f32[1024,256]{1,0:T(8,128)} %collective-permute-done.7.refs_2_), channel_id=1, source_target_pairs={{0,8},{8,0},{1,9},{9,1},{2,10},{10,2},{3,11},{11,3},{4,12},{12,4},... | collective-permute-start | bytes 3145736 | tf_op jit(solution)/shard_map/ppermute | solution.py:997
  101.2 21.7 %collective-permute-start.10 = (f32[1024,256]{1,0:T(8,128)}, f32[1024,256]{1,0:T(8,128)}, u32[]{:S(2)}, u32[]{:S(2)}) collective-permute-start(f32[1024,256]{1,0:T(8,128)} %collective-permute-done.2.refs_3_), channel_id=1, source_target_pairs={{0,8},{8,0},{1,9},{9,1},{2,10},{10,2},{3,11},{11,3},{4,12},{12,4},... | collective-permute-start | bytes 3145736 | tf_op jit(solution)/shard_map/ppermute | solution.py:997
  112.2 10.7 %copy-start.1 = (f32[1024,256]{1,0:T(8,128)S(1)}, f32[1024,256]{1,0:T(8,128)}, u32[]{:S(2)}) copy-start(f32[1024,256]{1,0:T(8,128)} %shard_map.94.own.refs_0_) | copy-start | bytes 3145732
  116.9 21.8 %all-to-all-start.4 = ((f32[16,64,128]{2,1,0:T(8,128)}), f32[16,64,128]{2,1,0:T(8,128)S(1)}, u32[]{:S(2)}, u32[]{:S(2)}) async-start(f32[16,64,128]{2,1,0:T(8,128)} %shard_map.103), calls=%async_computation.4 | async-start | bytes 1048576 | tf_op jit(solution)/shard_map/all_to_all | solution.py:1001
  121.3 17.3 %collective-permute-start.11 = (f32[256,256]{1,0:T(8,128)S(1)}, f32[256,256]{1,0:T(8,128)S(1)}, u32[]{:S(2)}, u32[]{:S(2)}) collective-permute-start(f32[256,256]{1,0:T(8,128)S(1)} %get-tuple-element.94), channel_id=1, source_target_pairs={{0,4},{1,5},{2,6},{3,7},{4,0},{5,1},{6,2},{7,3},{8,12},{9,13},{10,... | collective-permute-start | bytes 786440 | tf_op jit(solution)/shard_map/ppermute | solution.py:971
  145.2 5.4 %collective-permute-start.12 = (f32[512,256]{1,0:T(8,128)S(1)}, f32[512,256]{1,0:T(8,128)S(1)}, u32[]{:S(2)}, u32[]{:S(2)}) collective-permute-start(f32[512,256]{1,0:T(8,128)S(1)} %get-tuple-element.101), channel_id=1, source_target_pairs={{0,8},{8,0},{1,9},{9,1},{2,10},{10,2},{3,11},{11,3},{4,12},{12,4},... | collective-permute-start | bytes 1572872 | tf_op jit(solution)/shard_map/ppermute | solution.py:1008
  151.3 29.0 %all-to-all-start.5 = ((f32[64,8,128]{2,1,0:T(8,128)}), f32[64,8,128]{2,1,0:T(8,128)S(1)}, u32[]{:S(2)}, u32[]{:S(2)}) async-start(f32[64,8,128]{2,1,0:T(8,128)} %shard_map.106), calls=%async_computation.5 | async-start | bytes 524288 | tf_op jit(solution)/shard_map/all_to_all | solution.py:1011
  158.1 22.2 %collective-permute-start.13 = (f32[256,256]{1,0:T(8,128)S(1)}, f32[256,256]{1,0:T(8,128)S(1)}, u32[]{:S(2)}, u32[]{:S(2)}) collective-permute-start(f32[256,256]{1,0:T(8,128)S(1)} %get-tuple-element.117), channel_id=1, source_target_pairs={{0,4},{1,5},{2,6},{3,7},{4,0},{5,1},{6,2},{7,3},{8,12},{9,13},{10,... | collective-permute-start | bytes 786440 | tf_op jit(solution)/shard_map/ppermute | solution.py:971
  172.3 1.0 copy-start.4
  180.3 29.9 %copy-start.3 = (bf16[1024,256]{1,0:T(8,128)(2,1)S(1)}, bf16[1024,256]{1,0:T(8,128)(2,1)}, u32[]{:S(2)}) copy-start(bf16[1024,256]{1,0:T(8,128)(2,1)} %refs_5_.1) | copy-start | bytes 1572868
  180.3 29.9 %copy-start.8 = (bf16[128,256]{1,0:T(8,128)(2,1)S(1)}, bf16[128,256]{1,0:T(8,128)(2,1)}, u32[]{:S(2)}) copy-start(bf16[128,256]{1,0:T(8,128)(2,1)} %refs_4_.1) | copy-start | bytes 196612
  180.3 29.9 %copy-start.11 = (s32[4,96]{1,0:T(4,128)S(1)}, s32[4,96]{1,0:T(4,128)}, u32[]{:S(2)}) copy-start(s32[4,96]{1,0:T(4,128)} %mask.3) | copy-start | bytes 4612
  188.6 25.6 %all-to-all-start.6 = ((f32[32,72,128]{2,1,0:T(8,128)}), f32[32,72,128]{2,1,0:T(8,128)S(1)}, u32[]{:S(2)}, u32[]{:S(2)}) async-start(f32[32,72,128]{2,1,0:T(8,128)} %shard_map.109), calls=%async_computation.6 | async-start | bytes 2359296 | tf_op jit(solution)/shard_map/all_to_all | solution.py:1019
  196.6 7.1 %collective-permute-start.15 = (f32[128,256]{1,0:T(8,128)S(1)}, f32[128,256]{1,0:T(8,128)S(1)}, u32[]{:S(2)}, u32[]{:S(2)}) collective-permute-start(f32[128,256]{1,0:T(8,128)S(1)} %get-tuple-element.129.refs_0_), channel_id=1, source_target_pairs={{0,1},{1,0},{2,3},{3,2},{4,5},{5,4},{6,7},{7,6},{8,9},{9,8},{10,11... | collective-permute-start | bytes 393224 | tf_op jit(solution)/shard_map/ppermute | solution.py:971
  198.2 12.0 %collective-permute-start.16 = (f32[128,256]{1,0:T(8,128)S(1)}, f32[128,256]{1,0:T(8,128)S(1)}, u32[]{:S(2)}, u32[]{:S(2)}) collective-permute-start(f32[128,256]{1,0:T(8,128)S(1)} %get-tuple-element.130), channel_id=1, source_target_pairs={{0,3},{1,2},{2,1},{3,0},{4,7},{5,6},{6,5},{7,4},{8,11},{9,10},{10,... | collective-permute-start | bytes 393224 | tf_op jit(solution)/shard_map/ppermute | solution.py:971
  198.2 12.0 %collective-permute-start.14 = (f32[128,256]{1,0:T(8,128)S(1)}, f32[128,256]{1,0:T(8,128)S(1)}, u32[]{:S(2)}, u32[]{:S(2)}) collective-permute-start(f32[128,256]{1,0:T(8,128)S(1)} %get-tuple-element.130), channel_id=1, source_target_pairs={{0,2},{1,3},{2,0},{3,1},{4,6},{5,7},{6,4},{7,5},{8,10},{9,11},{10,... | collective-permute-start | bytes 393224 | tf_op jit(solution)/shard_map/ppermute | solution.py:971
  (4 other events, 3.3 us)

commit v7 on v6

--- a/solution.py
+++ b/solution.py
@@ -443,10 +443,9 @@
             for copy in leaving[-4]:
                 copy.wait()
         feats = ref[...].astype(BF16)
-        for start in range(0, half, 128):
-            score = jnp.dot(feats[start : start + 128, :], w[...], preferred_element_type=F32)
-            e = jnp.exp2(score * (LOG2E / TEACHER_TEMP)).astype(BF16)
-            out[slot, start : start + 128, :] = e
+        for start, stop in row_blocks(0, half):
+            score = jnp.dot(feats[start:stop, :], w[...], preferred_element_type=F32)
+            out[slot, start:stop, :] = jnp.exp2(score * (LOG2E / TEACHER_TEMP)).astype(BF16)
         at_d = pl.multiple_of(place * crops, 128)
         at_i = pl.multiple_of(place * rest, 128)
         copies = (
@@ -523,9 +522,9 @@
         first = y * sub + 2 * crops // 128 + core * (rest // 128)
         lines += [scale[pl.ds(first + t, 1), :] for t in range(rest // 128)]
         left[...] = (turned * jnp.concatenate(lines, axis=1)).astype(BF16)
-        for start in range(0, half, 128):
-            score = jnp.dot(feats[start : start + 128, :], w[...], preferred_element_type=F32)
-            expo[start : start + 128, :] = jnp.exp2(score * (LOG2E / STUDENT_TEMP)).astype(BF16)
+        for start, stop in row_blocks(0, half):
+            score = jnp.dot(feats[start:stop, :], w[...], preferred_element_type=F32)
+            expo[start:stop, :] = jnp.exp2(score * (LOG2E / STUDENT_TEMP)).astype(BF16)
         out[...] += jnp.dot(left[...], expo[...], preferred_element_type=F32)
 
     stream_rows(ny, idx[3], half, half, gathered, buf, sem, ready, body)
@@ -972,16 +971,17 @@
 
     colparts = lax.all_to_all(sums, ("x", "y"), 0, 0)
     total, mix = student_pass(idx, own, other, student_protos, crops)
-    sums = row_pass(expo, colparts, total, crops, 2 * nz)
-    rowparts = lax.all_to_all(sums, ("c", "z"), 0, 0)
-    later_protos, _ = tie(student_protos, sums)
-    winv = norm_pass(later_protos)
-    rowparts, winv, from_up, from_down = tie(rowparts, winv, from_up, from_down)
+    colparts, total, from_up, from_down = tie(colparts, total, from_up, from_down)
     ring = [own, from_up]
     while len(ring) < ny - 1:
         ring.append(lax.ppermute(ring[-1], "y", up))
     if ny > 2:
         ring.append(from_down)
+    sums = row_pass(expo, colparts, total, crops, 2 * nz)
+    rowparts = lax.all_to_all(sums, ("c", "z"), 0, 0)
+    later_protos, _ = tie(student_protos, sums)
+    winv = norm_pass(later_protos)
+    rowparts, winv = tie(rowparts, winv)
     totals = jnp.sum(rowparts[:, sub:, :], axis=0)
     sums = column_pass(expo, rowparts, crops, nx * ny)
 
@@ -990,18 +990,21 @@
     all_totals = [totals] + [lax.ppermute(totals, "y", shifted(ny, s)) for s in range(1, ny)]
     mine, theirs = part_pass(idx, mix, totals, crops)
     p_keep, p_send = pack_half_pass(idx, mine, lax.ppermute(theirs, "c", swap), nz, crops)
-    colparts, p_send, *all_totals = tie(colparts, p_send, *all_totals)
+    colparts, p_send = tie(colparts, p_send)
     p_came = across(p_send, nz // 2)
     sums = row_pass(expo, colparts, None, crops, 2 * nz)
     sums, *ring = tie(sums, *ring)
     gathered = ring + [other] + [lax.ppermute(rows, "c", swap) for rows in ring[1:]]
     rowparts = lax.all_to_all(sums, ("c", "z"), 0, 0)
+    rowparts, p_came = tie(rowparts, p_came)
     sums = column_pass(expo, rowparts, crops, nx * ny)
 
     colparts = lax.all_to_all(sums, ("x", "y"), 0, 0)
     *gathered, _ = tie(*gathered, sums)
     wide_expo = wide_teacher_pass(idx, gathered, teacher_protos, crops)
-    colparts, p_came, *wide_expo = tie(colparts, p_came, *wide_expo)
+    wide_expo, all_totals = list(wide_expo), list(all_totals)
+    colparts, *both = tie(colparts, *wide_expo, *all_totals)
+    wide_expo, all_totals = both[:2], both[2:]
     target_mine, target_theirs = target_pass(idx, expo, colparts, student_protos, crops)
     colparts, target_theirs = tie(colparts, target_theirs)
     sums = row_pass(expo, colparts, None, crops, 2 * nz * ny)

time: 220 us -> 217 us (0.986)
  blocking collectives: 10.9 us -> 0 us
  starting transfers between devices: 60.7 us -> 65.2 us
    ppermute x3, waiting for transfers between devices: 12.7 us -> 0.01 us  [local(): lax.ppermute(totals, 'y', shifted(ny, s))]
    all_to_all x1 -> x0, blocking collectives: 10.9 us -> none  [local(): rowparts = lax.all_to_all(sums, ('c', 'z'), 0, 0)]
    all_to_all x3, waiting for transfers between devices: 4.3 us -> 12.2 us  [local(): colparts = lax.all_to_all(sums, ('x', 'y'), 0, 0)]
    all_to_all x1 -> x2, starting transfers between devices: 8.6 us -> 15 us  [local(): rowparts = lax.all_to_all(sums, ('c', 'z'), 0, 0)]
    ppermute x1, waiting for transfers between devices: 0.01 us -> 3.41 us  [local(): from_up = lax.ppermute(own, 'y', up)]
    ppermute x5, waiting for transfers between devices: 25.2 us -> 27.5 us  [across(): return lax.ppermute(value, 'z', [(i, i ^ bit) for i in range(nz)])]
    unnamed x26 -> x30, local copies, waits for them, and re-layouts: 8.61 us -> 10 us
    all_to_all x1 -> x2, waiting for transfers between devices: 5.85 us -> 5.76 us  [local(): rowparts = lax.all_to_all(sums, ('c', 'z'), 0, 0)]
  transfers between devices with their start and end apart: 23 -> 24, of which waited for: 9 -> 12; matrix products, arithmetic and copies ran while one was open for 0% -> 0% of each run, Pallas kernels for 30% -> 31%
where the time goes in v7:
time: 217 us; the launch traced here: 212 us
  Pallas kernels  86 us (40%)
  starting transfers between devices  65.2 us (30%)
  waiting for transfers between devices  50 us (23%)
  local copies, waits for them, and re-layouts  10 us (5%)
    pallas_call x19, Pallas kernels, call(): pl.pallas_call(kernel, out_shape=out_shape, out_specs=out_specs, in_specs...  86 us
    ppermute x5, waiting for transfers between devices, across(): return lax.ppermute(value, 'z', [(i, i ^ bit) for i in range(nz)])  27.5 us
    all_to_all x3, starting transfers between devices, local(): colparts = lax.all_to_all(sums, ('x', 'y'), 0, 0)  17.8 us
    all_to_all x2, starting transfers between devices, local(): rowparts = lax.all_to_all(sums, ('c', 'z'), 0, 0)  15 us
    all_to_all x3, waiting for transfers between devices, local(): colparts = lax.all_to_all(sums, ('x', 'y'), 0, 0)  12.2 us
    ppermute x5, starting transfers between devices, across(): return lax.ppermute(value, 'z', [(i, i ^ bit) for i in range(nz)])  10.4 us
    unnamed x30, local copies, waits for them, and re-layouts  10 us
    all_to_all x1, starting transfers between devices, local(): parts = lax.all_to_all(outgoing, ('x', 'y', 'c'), 0, 0)  7.24 us
  transfers between devices with their start and end apart: 24, of which 12 were waited for; matrix products, arithmetic and copies ran while one was open for 0% of the time, Pallas kernels for 31%

profile of v7, /device:TPU:32, one launch (start us, length us, event | category | flops | bytes accessed | tf_op | source)
XLA Modules:
  0.0 212.4 jit_solution(116800833765791525)
XLA Ops:
  7.1 3.1 %collective-permute-start.2 = (f32[1024,256]{1,0:T(8,128)}, f32[1024,256]{1,0:T(8,128)}, u32[]{:S(2)}, u32[]{:S(2)}) collective-permute-start(f32[1024,256]{1,0:T(8,128)} %shard_map.94.own.refs_0_), channel_id=1, source_target_pairs={{0,48},{16,0},{32,16},{48,32},{1,49},{17,1},{33,17},{49,33},{2,50}... | collective-permute-start | bytes 3145736 | tf_op jit(solution)/shard_map/ppermute | solution.py:963
  12.5 8.9 %shard_map.95 = (bf16[1024,4096]{1,0:T(8,128)(2,1)}, f32[16,64,128]{2,1,0:T(8,128)}) custom-call(s32[4]{0:T(128)S(1)} %pad_add_fusion.idx, f32[1024,256]{1,0:T(8,128)S(1)} %copy-done, f32[1024,256]{1,0:T(8,128)} %copy-done.14, bf16[256,8192]{1,0:T(8,128)(2,1)} %protos.9), custom_call_target="tpu_custom_call" | custom-call | flops 2147483648 | bytes 8388608 | tf_op jit(solution)/shard_map/pallas_call | solution.py:33
  21.4 7.1 %all-to-all-start = ((f32[16,64,128]{2,1,0:T(8,128)}), f32[16,64,128]{2,1,0:T(8,128)S(1)}, u32[]{:S(2)}, u32[]{:S(2)}) async-start(f32[16,64,128]{2,1,0:T(8,128)} %get-tuple-element.72), calls=%async_computation | async-start | bytes 1048576 | tf_op jit(solution)/shard_map/all_to_all | solution.py:972
  28.5 8.7 %shard_map.96 = (f32[8,128]{1,0:T(8,128)S(1)}, f32[1024,256]{1,0:T(8,128)S(1)}) custom-call(s32[4]{0:T(128)S(1)} %pad_add_fusion.idx, f32[1024,256]{1,0:T(8,128)} %shard_map.94.own.refs_0_, f32[1024,256]{1,0:T(8,128)} %copy-done.14, bf16[256,8192]{1,0:T(8,128)(2,1)} %protos.12), custom_call_target="tpu_custom_call" | custom-call | flops 4294967296 | bytes 2097152 | tf_op jit(solution)/shard_map/pallas_call | solution.py:33
  38.8 3.4 %collective-permute-done.1.refs_1_ = f32[1024,256]{1,0:T(8,128)} collective-permute-done((f32[1024,256]{1,0:T(8,128)}, f32[1024,256]{1,0:T(8,128)}, u32[]{:S(2)}, u32[]{:S(2)}) %collective-permute-start.1) | collective-permute-done | bytes 1048608 | tf_op jit(solution)/shard_map/ppermute | solution.py:962
  42.5 5.1 %shard_map.97 = f32[16,16,128]{2,1,0:T(8,128)} custom-call(bf16[1024,4096]{1,0:T(8,128)(2,1)} %get-tuple-element.71.expo, f32[16,64,128]{2,1,0:T(8,128)S(1)} %all-to-all-done.colparts, f32[8,128]{1,0:T(8,128)S(1)} %get-tuple-element.75.refs_0_), custom_call_target="tpu_custom_call" | custom-call | flops 8388608 | bytes 8388608 | tf_op jit(solution)/shard_map/pallas_call | solution.py:33
  47.6 8.6 %all-to-all-start.1 = ((f32[16,16,128]{2,1,0:T(8,128)}), f32[16,16,128]{2,1,0:T(8,128)S(1)}, u32[]{:S(2)}, u32[]{:S(2)}) async-start(f32[16,16,128]{2,1,0:T(8,128)} %shard_map.97), calls=%async_computation.1 | async-start | bytes 262144 | tf_op jit(solution)/shard_map/all_to_all | solution.py:981
  56.2 2.3 %shard_map.98.winv = f32[1,8192]{1,0:T(1,128)S(1)} custom-call(bf16[256,8192]{1,0:T(8,128)(2,1)} %protos.12), custom_call_target="tpu_custom_call" | custom-call | flops 6291456 | bytes 4194304 | tf_op jit(solution)/shard_map/pallas_call | solution.py:33
  59.2 5.3 %all-to-all-done.1.rowparts = f32[16,16,128]{2,1,0:T(8,128)S(1)} async-done(((f32[16,16,128]{2,1,0:T(8,128)}), f32[16,16,128]{2,1,0:T(8,128)S(1)}, u32[]{:S(2)}, u32[]{:S(2)}) %all-to-all-start.1) | async-done | bytes 131104 | tf_op jit(solution)/shard_map/all_to_all | solution.py:981
  64.5 4.6 %shard_map.99 = f32[16,64,128]{2,1,0:T(8,128)} custom-call(bf16[1024,4096]{1,0:T(8,128)(2,1)} %get-tuple-element.71.expo, f32[16,16,128]{2,1,0:T(8,128)S(1)} %all-to-all-done.1.rowparts), custom_call_target="tpu_custom_call" | custom-call | flops 8388608 | bytes 8388608 | tf_op jit(solution)/shard_map/pallas_call | solution.py:33
  70.7 7.1 %all-to-all-start.2 = ((f32[16,64,128]{2,1,0:T(8,128)}), f32[16,64,128]{2,1,0:T(8,128)S(1)}, u32[]{:S(2)}, u32[]{:S(2)}) async-start(f32[16,64,128]{2,1,0:T(8,128)} %shard_map.99), calls=%async_computation.2 | async-start | bytes 1048576 | tf_op jit(solution)/shard_map/all_to_all | solution.py:988
  78.5 11.5 %all-to-all-done.2.colparts = f32[16,64,128]{2,1,0:T(8,128)S(1)} async-done(((f32[16,64,128]{2,1,0:T(8,128)}), f32[16,64,128]{2,1,0:T(8,128)S(1)}, u32[]{:S(2)}, u32[]{:S(2)}) %all-to-all-start.2) | async-done | bytes 524320 | tf_op jit(solution)/shard_map/all_to_all | solution.py:988
  90.0 5.1 %shard_map.102 = f32[16,8,128]{2,1,0:T(8,128)} custom-call(bf16[1024,4096]{1,0:T(8,128)(2,1)} %get-tuple-element.71.expo, f32[16,64,128]{2,1,0:T(8,128)S(1)} %all-to-all-done.2.colparts), custom_call_target="tpu_custom_call" | custom-call | flops 8388608 | bytes 8388608 | tf_op jit(solution)/shard_map/pallas_call | solution.py:33
  97.4 6.4 %all-to-all-start.3 = ((f32[16,8,128]{2,1,0:T(8,128)}), f32[16,8,128]{2,1,0:T(8,128)S(1)}, u32[]{:S(2)}, u32[]{:S(2)}) async-start(f32[16,8,128]{2,1,0:T(8,128)} %shard_map.102), calls=%async_computation.3 | async-start | bytes 131072 | tf_op jit(solution)/shard_map/all_to_all | solution.py:998
  103.8 11.2 %collective-permute-done.8.prob_came = f32[256,256]{1,0:T(8,128)S(1)} collective-permute-done((f32[256,256]{1,0:T(8,128)S(1)}, f32[256,256]{1,0:T(8,128)S(1)}, u32[]{:S(2)}, u32[]{:S(2)}) %collective-permute-start.8) | collective-permute-done | bytes 262176 | tf_op jit(solution)/shard_map/ppermute | solution.py:970
  115.4 4.6 %shard_map.103 = f32[16,64,128]{2,1,0:T(8,128)} custom-call(bf16[1024,4096]{1,0:T(8,128)(2,1)} %get-tuple-element.71.expo, f32[16,8,128]{2,1,0:T(8,128)S(1)} %all-to-all-done.3.rowparts), custom_call_target="tpu_custom_call" | custom-call | flops 8388608 | bytes 8388608 | tf_op jit(solution)/shard_map/pallas_call | solution.py:33
  120.0 3.6 %all-to-all-start.4 = ((f32[16,64,128]{2,1,0:T(8,128)}), f32[16,64,128]{2,1,0:T(8,128)S(1)}, u32[]{:S(2)}, u32[]{:S(2)}) async-start(f32[16,64,128]{2,1,0:T(8,128)} %shard_map.103), calls=%async_computation.4 | async-start | bytes 1048576 | tf_op jit(solution)/shard_map/all_to_all | solution.py:1002
  123.6 3.0 %collective-permute-start.11 = (f32[8,128]{1,0:T(8,128)S(1)}, f32[8,128]{1,0:T(8,128)S(1)}, u32[]{:S(2)}, u32[]{:S(2)}) collective-permute-start(f32[8,128]{1,0:T(8,128)S(1)} %slice_reduce_fusion.totals.refs_8_), channel_id=1, source_target_pairs={{0,48},{16,0},{32,16},{48,32},{1,49},{17,1},{33,17},{49,33},{2,50}... | collective-permute-start | bytes 12296 | tf_op jit(solution)/shard_map/ppermute | solution.py:990
  128.4 6.4 %shard_map.104 = (bf16[1024,1024]{1,0:T(8,128)(2,1)}, bf16[3072,1024]{1,0:T(8,128)(2,1)}) custom-call(s32[4]{0:T(128)S(1)} %pad_add_fusion.idx, bf16[256,8192]{1,0:T(8,128)(2,1)} %protos.9, f32[1024,256]{1,0:T(8,128)S(1)} %copy-done.1, f32[1024,256]{1,0:T(8,128)} %collective-permute-done.1.refs_1_, f32[1024,256]{1,0:T(8,128)} %collective-permute-done.4.refs_2_, ...), custom_call_target="tpu_custom_call" | custom-call | flops 2147483648 | bytes 4194304 | tf_op jit(solution)/shard_map/pallas_call | solution.py:33
  135.4 6.6 %shard_map.105 = (f32[512,256]{1,0:T(8,128)S(1)}, f32[512,256]{1,0:T(8,128)S(1)}) custom-call(s32[4]{0:T(128)S(1)} %pad_add_fusion.idx, bf16[1024,4096]{1,0:T(8,128)(2,1)} %get-tuple-element.71.expo, f32[16,64,128]{2,1,0:T(8,128)S(1)} %all-to-all-done.4.colparts, bf16[256,8192]{1,0:T(8,128)(2,1)} %protos.12), custom_call_target="tpu_custom_call" | custom-call | flops 2147483648 | bytes 8388608 | tf_op jit(solution)/shard_map/pallas_call | solution.py:33
  142.0 5.3 %shard_map.106 = f32[64,8,128]{2,1,0:T(8,128)} custom-call(bf16[1024,4096]{1,0:T(8,128)(2,1)} %get-tuple-element.71.expo, f32[16,64,128]{2,1,0:T(8,128)S(1)} %all-to-all-done.4.colparts), custom_call_target="tpu_custom_call" | custom-call | flops 8388608 | bytes 8388608 | tf_op jit(solution)/shard_map/pallas_call | solution.py:33
  148.0 5.7 %all-to-all-start.5 = ((f32[64,8,128]{2,1,0:T(8,128)}), f32[64,8,128]{2,1,0:T(8,128)S(1)}, u32[]{:S(2)}, u32[]{:S(2)}) async-start(f32[64,8,128]{2,1,0:T(8,128)} %shard_map.106), calls=%async_computation.5 | async-start | bytes 524288 | tf_op jit(solution)/shard_map/all_to_all | solution.py:1014
  153.7 4.6 %collective-permute-start.13 = (f32[256,256]{1,0:T(8,128)S(1)}, f32[256,256]{1,0:T(8,128)S(1)}, u32[]{:S(2)}, u32[]{:S(2)}) collective-permute-start(f32[256,256]{1,0:T(8,128)S(1)} %get-tuple-element.123), channel_id=1, source_target_pairs={{0,4},{1,5},{2,6},{3,7},{4,0},{5,1},{6,2},{7,3},{8,12},{9,13},{10,... | collective-permute-start | bytes 786440 | tf_op jit(solution)/shard_map/ppermute | solution.py:970
  158.3 9.3 %shard_map.108 = (f32[256,1024]{1,0:T(8,128)S(1)}, f32[256,1024]{1,0:T(8,128)}, bf16[256,1024]{1,0:T(8,128)(2,1)S(1)}, bf16[256,3072]{1,0:T(8,128)(2,1)}) custom-call(s32[4]{0:T(128)S(1)} %pad_add_fusion.idx, bf16[256,8192]{1,0:T(8,128)(2,1)} %protos.12, f32[1024,256]{1,0:T(8,128)} %shard_map.94.own.refs_0_, f32[1024,256]{1,0:T(8,128)} %collective-permute-done.1.refs_1_, ...), custom_call_target="tpu_custom_call" | custom-call | flops 4294967296 | bytes 4194304 | tf_op jit(solution)/shard_map/pallas_call | solution.py:33
  168.6 7.3 %collective-permute-done.13.target_came = f32[256,256]{1,0:T(8,128)S(1)} collective-permute-done((f32[256,256]{1,0:T(8,128)S(1)}, f32[256,256]{1,0:T(8,128)S(1)}, u32[]{:S(2)}, u32[]{:S(2)}) %collective-permute-start.13) | collective-permute-done | bytes 262176 | tf_op jit(solution)/shard_map/ppermute | solution.py:970
  175.9 8.4 %shard_map.109 = f32[32,72,128]{2,1,0:T(8,128)} custom-call(s32[4]{0:T(128)S(1)} %pad_add_fusion.idx, f32[256,1024]{1,0:T(8,128)} %copy-done.4, f32[256,1024]{1,0:T(8,128)} %get-tuple-element.125.wnorm_in, bf16[256,1024]{1,0:T(8,128)(2,1)S(1)} %get-tuple-element.126.turned_d_in, bf16[256,3072]{1,0:T(8,128)(2,1)} %get-tuple-element.127.turned_i_in, ...), custom_call_target="tpu_custom_call" | custom-call | flops 2147483648 | bytes 8388608 | tf_op jit(solution)/shard_map/pallas_call | solution.py:33
  184.3 7.2 %all-to-all-start.6 = ((f32[32,72,128]{2,1,0:T(8,128)}), f32[32,72,128]{2,1,0:T(8,128)S(1)}, u32[]{:S(2)}, u32[]{:S(2)}) async-start(f32[32,72,128]{2,1,0:T(8,128)} %shard_map.109), calls=%async_computation.6 | async-start | bytes 2359296 | tf_op jit(solution)/shard_map/all_to_all | solution.py:1022
  193.9 2.9 %collective-permute-start.14 = (f32[128,256]{1,0:T(8,128)S(1)}, f32[128,256]{1,0:T(8,128)S(1)}, u32[]{:S(2)}, u32[]{:S(2)}) collective-permute-start(f32[128,256]{1,0:T(8,128)S(1)} %get-tuple-element.136), channel_id=1, source_target_pairs={{0,2},{1,3},{2,0},{3,1},{4,6},{5,7},{6,4},{7,5},{8,10},{9,11},{10,... | collective-permute-start | bytes 393224 | tf_op jit(solution)/shard_map/ppermute | solution.py:970
  196.8 2.6 %collective-permute-done.15.refs_2_ = f32[128,256]{1,0:T(8,128)S(1)} collective-permute-done((f32[128,256]{1,0:T(8,128)S(1)}, f32[128,256]{1,0:T(8,128)S(1)}, u32[]{:S(2)}, u32[]{:S(2)}) %collective-permute-start.15) | collective-permute-done | bytes 131104 | tf_op jit(solution)/shard_map/ppermute | solution.py:970
  199.4 6.4 %collective-permute-done.16.refs_3_ = f32[128,256]{1,0:T(8,128)S(1)} collective-permute-done((f32[128,256]{1,0:T(8,128)S(1)}, f32[128,256]{1,0:T(8,128)S(1)}, u32[]{:S(2)}, u32[]{:S(2)}) %collective-permute-start.16) | collective-permute-done | bytes 131104 | tf_op jit(solution)/shard_map/ppermute | solution.py:970
  206.7 2.7 %shard_map.112 = (f32[16,256]{1,0:T(8,128)}, f32[128,256]{1,0:T(8,128)}) custom-call(s32[4]{0:T(128)S(1)} %pad_add_fusion.idx, s32[4,96]{1,0:T(4,128)S(1)} %copy-done.13, f32[128,256]{1,0:T(8,128)S(1)} %get-tuple-element.135.refs_0_, f32[128,256]{1,0:T(8,128)S(1)} %collective-permute-done.14.refs_1_, f32[128,256]{1,0:T(8,128)S(1)} %collective-permute-done.15.refs_2_, ...), custom_call_target="tpu_custom_call" | custom-call | tf_op jit(solution)/shard_map/pallas_call | solution.py:33
  209.9 2.3 %shard_map.110 = f32[8,8192]{1,0:T(8,128)} custom-call(s32[4]{0:T(128)S(1)} %pad_add_fusion.idx, f32[32,72,128]{2,1,0:T(8,128)S(1)} %all-to-all-done.6.parts, bf16[256,8192]{1,0:T(8,128)(2,1)} %protos.12, f32[1,8192]{1,0:T(1,128)S(1)} %copy-done.10), custom_call_target="tpu_custom_call" | custom-call | tf_op jit(solution)/shard_map/pallas_call | solution.py:33
  (67 shorter events, 23.8 us)
Async XLA Ops:
  0.6 1.0 copy-start.2
  1.7 1.0 copy-start.6
  7.0 3.3 %collective-permute-start = (f32[1024,256]{1,0:T(8,128)}, f32[1024,256]{1,0:T(8,128)S(1)}, u32[]{:S(2)}, u32[]{:S(2)}) collective-permute-start(f32[1024,256]{1,0:T(8,128)} %shard_map.94.own.refs_0_), channel_id=1, source_target_pairs={{0,8},{8,0},{1,9},{9,1},{2,10},{10,2},{3,11},{11,3},{4,12},{12,4},... | collective-permute-start | bytes 3145736 | tf_op jit(solution)/shard_map/ppermute | solution.py:960
  7.1 31.7 %collective-permute-start.2 = (f32[1024,256]{1,0:T(8,128)}, f32[1024,256]{1,0:T(8,128)}, u32[]{:S(2)}, u32[]{:S(2)}) collective-permute-start(f32[1024,256]{1,0:T(8,128)} %shard_map.94.own.refs_0_), channel_id=1, source_target_pairs={{0,48},{16,0},{32,16},{48,32},{1,49},{17,1},{33,17},{49,33},{2,50}... | collective-permute-start | bytes 3145736 | tf_op jit(solution)/shard_map/ppermute | solution.py:963
  10.2 32.0 %collective-permute-start.1 = (f32[1024,256]{1,0:T(8,128)}, f32[1024,256]{1,0:T(8,128)}, u32[]{:S(2)}, u32[]{:S(2)}) collective-permute-start(f32[1024,256]{1,0:T(8,128)} %shard_map.94.own.refs_0_), channel_id=1, source_target_pairs={{0,16},{16,32},{32,48},{48,0},{1,17},{17,33},{33,49},{49,1},{2,18}... | collective-permute-start | bytes 3145736 | tf_op jit(solution)/shard_map/ppermute | solution.py:962
  11.3 1.2 copy-start
  21.4 21.1 %all-to-all-start = ((f32[16,64,128]{2,1,0:T(8,128)}), f32[16,64,128]{2,1,0:T(8,128)S(1)}, u32[]{:S(2)}, u32[]{:S(2)}) async-start(f32[16,64,128]{2,1,0:T(8,128)} %get-tuple-element.72), calls=%async_computation | async-start | bytes 1048576 | tf_op jit(solution)/shard_map/all_to_all | solution.py:972
  42.5 52.6 %collective-permute-start.4 = (f32[1024,256]{1,0:T(8,128)}, f32[1024,256]{1,0:T(8,128)}, u32[]{:S(2)}, u32[]{:S(2)}) collective-permute-start(f32[1024,256]{1,0:T(8,128)} %collective-permute-done.1.refs_1_), channel_id=1, source_target_pairs={{0,16},{16,32},{32,48},{48,0},{1,17},{17,33},{33,49},{49,1},{2,18}... | collective-permute-start | bytes 3145736 | tf_op jit(solution)/shard_map/ppermute | solution.py:977
  47.6 16.8 %all-to-all-start.1 = ((f32[16,16,128]{2,1,0:T(8,128)}), f32[16,16,128]{2,1,0:T(8,128)S(1)}, u32[]{:S(2)}, u32[]{:S(2)}) async-start(f32[16,16,128]{2,1,0:T(8,128)} %shard_map.97), calls=%async_computation.1 | async-start | bytes 262144 | tf_op jit(solution)/shard_map/all_to_all | solution.py:981
  70.6 7.2 %collective-permute-start.3 = (f32[512,256]{1,0:T(8,128)S(1)}, f32[512,256]{1,0:T(8,128)S(1)}, u32[]{:S(2)}, u32[]{:S(2)}) collective-permute-start(f32[512,256]{1,0:T(8,128)S(1)} %get-tuple-element.81), channel_id=1, source_target_pairs={{0,8},{8,0},{1,9},{9,1},{2,10},{10,2},{3,11},{11,3},{4,12},{12,4},... | collective-permute-start | bytes 1572872 | tf_op jit(solution)/shard_map/ppermute | solution.py:992
  70.7 19.2 %all-to-all-start.2 = ((f32[16,64,128]{2,1,0:T(8,128)}), f32[16,64,128]{2,1,0:T(8,128)S(1)}, u32[]{:S(2)}, u32[]{:S(2)}) async-start(f32[16,64,128]{2,1,0:T(8,128)} %shard_map.99), calls=%async_computation.2 | async-start | bytes 1048576 | tf_op jit(solution)/shard_map/all_to_all | solution.py:988
  95.1 32.4 %collective-permute-start.5 = (f32[1024,256]{1,0:T(8,128)}, f32[1024,256]{1,0:T(8,128)}, u32[]{:S(2)}, u32[]{:S(2)}) collective-permute-start(f32[1024,256]{1,0:T(8,128)} %collective-permute-done.1.refs_1_), channel_id=1, source_target_pairs={{0,8},{8,0},{1,9},{9,1},{2,10},{10,2},{3,11},{11,3},{4,12},{12,4},... | collective-permute-start | bytes 3145736 | tf_op jit(solution)/shard_map/ppermute | solution.py:997
  95.4 33.0 %collective-permute-start.6 = (f32[1024,256]{1,0:T(8,128)}, f32[1024,256]{1,0:T(8,128)}, u32[]{:S(2)}, u32[]{:S(2)}) collective-permute-start(f32[1024,256]{1,0:T(8,128)} %collective-permute-done.4.refs_2_), channel_id=1, source_target_pairs={{0,8},{8,0},{1,9},{9,1},{2,10},{10,2},{3,11},{11,3},{4,12},{12,4},... | collective-permute-start | bytes 3145736 | tf_op jit(solution)/shard_map/ppermute | solution.py:997
  95.9 32.5 %collective-permute-start.7 = (f32[1024,256]{1,0:T(8,128)}, f32[1024,256]{1,0:T(8,128)}, u32[]{:S(2)}, u32[]{:S(2)}) collective-permute-start(f32[1024,256]{1,0:T(8,128)} %collective-permute-done.2.refs_3_), channel_id=1, source_target_pairs={{0,8},{8,0},{1,9},{9,1},{2,10},{10,2},{3,11},{11,3},{4,12},{12,4},... | collective-permute-start | bytes 3145736 | tf_op jit(solution)/shard_map/ppermute | solution.py:997
  96.0 18.9 %collective-permute-start.8 = (f32[256,256]{1,0:T(8,128)S(1)}, f32[256,256]{1,0:T(8,128)S(1)}, u32[]{:S(2)}, u32[]{:S(2)}) collective-permute-start(f32[256,256]{1,0:T(8,128)S(1)} %get-tuple-element.91), channel_id=1, source_target_pairs={{0,4},{1,5},{2,6},{3,7},{4,0},{5,1},{6,2},{7,3},{8,12},{9,13},{10,... | collective-permute-start | bytes 786440 | tf_op jit(solution)/shard_map/ppermute | solution.py:970
  97.4 18.1 %all-to-all-start.3 = ((f32[16,8,128]{2,1,0:T(8,128)}), f32[16,8,128]{2,1,0:T(8,128)S(1)}, u32[]{:S(2)}, u32[]{:S(2)}) async-start(f32[16,8,128]{2,1,0:T(8,128)} %shard_map.102), calls=%async_computation.3 | async-start | bytes 131072 | tf_op jit(solution)/shard_map/all_to_all | solution.py:998
  103.8 24.6 %copy-start.1 = (f32[1024,256]{1,0:T(8,128)S(1)}, f32[1024,256]{1,0:T(8,128)}, u32[]{:S(2)}) copy-start(f32[1024,256]{1,0:T(8,128)} %shard_map.94.own.refs_0_) | copy-start | bytes 3145732
  120.0 15.3 %all-to-all-start.4 = ((f32[16,64,128]{2,1,0:T(8,128)}), f32[16,64,128]{2,1,0:T(8,128)S(1)}, u32[]{:S(2)}, u32[]{:S(2)}) async-start(f32[16,64,128]{2,1,0:T(8,128)} %shard_map.103), calls=%async_computation.4 | async-start | bytes 1048576 | tf_op jit(solution)/shard_map/all_to_all | solution.py:1002
  123.6 11.2 %collective-permute-start.11 = (f32[8,128]{1,0:T(8,128)S(1)}, f32[8,128]{1,0:T(8,128)S(1)}, u32[]{:S(2)}, u32[]{:S(2)}) collective-permute-start(f32[8,128]{1,0:T(8,128)S(1)} %slice_reduce_fusion.totals.refs_8_), channel_id=1, source_target_pairs={{0,48},{16,0},{32,16},{48,32},{1,49},{17,1},{33,17},{49,33},{2,50}... | collective-permute-start | bytes 12296 | tf_op jit(solution)/shard_map/ppermute | solution.py:990
  126.7 8.2 %collective-permute-start.10 = (f32[8,128]{1,0:T(8,128)S(1)}, f32[8,128]{1,0:T(8,128)S(1)}, u32[]{:S(2)}, u32[]{:S(2)}) collective-permute-start(f32[8,128]{1,0:T(8,128)S(1)} %slice_reduce_fusion.totals.refs_8_), channel_id=1, source_target_pairs={{0,32},{16,48},{32,0},{48,16},{1,33},{17,49},{33,1},{49,17},{2,34}... | collective-permute-start | bytes 12296 | tf_op jit(solution)/shard_map/ppermute | solution.py:990
  127.5 7.3 %collective-permute-start.9 = (f32[8,128]{1,0:T(8,128)S(1)}, f32[8,128]{1,0:T(8,128)S(1)}, u32[]{:S(2)}, u32[]{:S(2)}) collective-permute-start(f32[8,128]{1,0:T(8,128)S(1)} %slice_reduce_fusion.totals.refs_8_), channel_id=1, source_target_pairs={{0,16},{16,32},{32,48},{48,0},{1,17},{17,33},{33,49},{49,1},{2,18}... | collective-permute-start | bytes 12296 | tf_op jit(solution)/shard_map/ppermute | solution.py:990
  141.9 5.4 %collective-permute-start.12 = (f32[512,256]{1,0:T(8,128)S(1)}, f32[512,256]{1,0:T(8,128)S(1)}, u32[]{:S(2)}, u32[]{:S(2)}) collective-permute-start(f32[512,256]{1,0:T(8,128)S(1)} %get-tuple-element.107), channel_id=1, source_target_pairs={{0,8},{8,0},{1,9},{9,1},{2,10},{10,2},{3,11},{11,3},{4,12},{12,4},... | collective-permute-start | bytes 1572872 | tf_op jit(solution)/shard_map/ppermute | solution.py:1011
  148.0 27.9 %all-to-all-start.5 = ((f32[64,8,128]{2,1,0:T(8,128)}), f32[64,8,128]{2,1,0:T(8,128)S(1)}, u32[]{:S(2)}, u32[]{:S(2)}) async-start(f32[64,8,128]{2,1,0:T(8,128)} %shard_map.106), calls=%async_computation.5 | async-start | bytes 524288 | tf_op jit(solution)/shard_map/all_to_all | solution.py:1014
  153.7 22.2 %collective-permute-start.13 = (f32[256,256]{1,0:T(8,128)S(1)}, f32[256,256]{1,0:T(8,128)S(1)}, u32[]{:S(2)}, u32[]{:S(2)}) collective-permute-start(f32[256,256]{1,0:T(8,128)S(1)} %get-tuple-element.123), channel_id=1, source_target_pairs={{0,4},{1,5},{2,6},{3,7},{4,0},{5,1},{6,2},{7,3},{8,12},{9,13},{10,... | collective-permute-start | bytes 786440 | tf_op jit(solution)/shard_map/ppermute | solution.py:970
  167.6 1.0 copy-start.4
  175.9 29.9 %copy-start.3 = (bf16[1024,256]{1,0:T(8,128)(2,1)S(1)}, bf16[1024,256]{1,0:T(8,128)(2,1)}, u32[]{:S(2)}) copy-start(bf16[1024,256]{1,0:T(8,128)(2,1)} %refs_5_.1) | copy-start | bytes 1572868
  175.9 29.9 %copy-start.13 = (s32[4,96]{1,0:T(4,128)S(1)}, s32[4,96]{1,0:T(4,128)}, u32[]{:S(2)}) copy-start(s32[4,96]{1,0:T(4,128)} %mask.3) | copy-start | bytes 4612
  184.3 25.6 %copy-start.10 = (f32[1,8192]{1,0:T(1,128)S(1)}, f32[1,8192]{1,0:T(1,128)}, u32[]{:S(2)}) copy-start(f32[1,8192]{1,0:T(1,128)} %copy-done.9) | copy-start | bytes 98308
  184.3 25.6 %all-to-all-start.6 = ((f32[32,72,128]{2,1,0:T(8,128)}), f32[32,72,128]{2,1,0:T(8,128)S(1)}, u32[]{:S(2)}, u32[]{:S(2)}) async-start(f32[32,72,128]{2,1,0:T(8,128)} %shard_map.109), calls=%async_computation.6 | async-start | bytes 2359296 | tf_op jit(solution)/shard_map/all_to_all | solution.py:1022
  192.3 7.1 %collective-permute-start.15 = (f32[128,256]{1,0:T(8,128)S(1)}, f32[128,256]{1,0:T(8,128)S(1)}, u32[]{:S(2)}, u32[]{:S(2)}) collective-permute-start(f32[128,256]{1,0:T(8,128)S(1)} %get-tuple-element.135.refs_0_), channel_id=1, source_target_pairs={{0,1},{1,0},{2,3},{3,2},{4,5},{5,4},{6,7},{7,6},{8,9},{9,8},{10,11... | collective-permute-start | bytes 393224 | tf_op jit(solution)/shard_map/ppermute | solution.py:970
  193.9 12.0 %collective-permute-start.16 = (f32[128,256]{1,0:T(8,128)S(1)}, f32[128,256]{1,0:T(8,128)S(1)}, u32[]{:S(2)}, u32[]{:S(2)}) collective-permute-start(f32[128,256]{1,0:T(8,128)S(1)} %get-tuple-element.136), channel_id=1, source_target_pairs={{0,3},{1,2},{2,1},{3,0},{4,7},{5,6},{6,5},{7,4},{8,11},{9,10},{10,... | collective-permute-start | bytes 393224 | tf_op jit(solution)/shard_map/ppermute | solution.py:970
  193.9 12.0 %collective-permute-start.14 = (f32[128,256]{1,0:T(8,128)S(1)}, f32[128,256]{1,0:T(8,128)S(1)}, u32[]{:S(2)}, u32[]{:S(2)}) collective-permute-start(f32[128,256]{1,0:T(8,128)S(1)} %get-tuple-element.136), channel_id=1, source_target_pairs={{0,2},{1,3},{2,0},{3,1},{4,6},{5,7},{6,4},{7,5},{8,10},{9,11},{10,... | collective-permute-start | bytes 393224 | tf_op jit(solution)/shard_map/ppermute | solution.py:970
  (7 other events, 5.8 us)

commit v8 on v7

--- a/solution.py
+++ b/solution.py
@@ -18,13 +18,12 @@
 BN = 512
 F32 = jnp.float32
 BF16 = jnp.bfloat16
-VMEM_LIMIT = 52 * 1024 * 1024
 SMEM = pl.BlockSpec(memory_space=pltpu.SMEM)
 VMEM = pl.BlockSpec(memory_space=pltpu.VMEM)
 HBM = pl.BlockSpec(memory_space=pltpu.HBM)
 
 
-def call(kernel, out_shape, args, specs, outs="", scratch=(), flops=0, traffic=0):
+def call(kernel, out_shape, args, specs, outs="", scratch=(), flops=0, traffic=0, limit=52):
     spaces = {"s": SMEM, "v": VMEM, "h": HBM}
     if not isinstance(out_shape, list):
         out_specs = VMEM
@@ -36,7 +35,7 @@
         out_specs=out_specs,
         in_specs=[spaces[letter] for letter in specs],
         scratch_shapes=list(scratch),
-        compiler_params=pltpu.CompilerParams(vmem_limit_bytes=VMEM_LIMIT),
+        compiler_params=pltpu.CompilerParams(vmem_limit_bytes=limit * 1024 * 1024),
         cost_estimate=pl.CostEstimate(flops=flops, bytes_accessed=traffic, transcendentals=0),
     )(*args)
 
@@ -107,6 +106,7 @@
         array((2 * half, tcrops.shape[1])),
         [tcrops, tpatch, scrops, spatch, mask],
         "hhhhv",
+        limit=58,
         scratch=[pltpu.VMEM(a.shape, BF16) for a in (tcrops, tpatch, scrops, spatch)]
         + [pltpu.SemaphoreType.DMA((4,))],
     )
@@ -990,13 +990,12 @@
     all_totals = [totals] + [lax.ppermute(totals, "y", shifted(ny, s)) for s in range(1, ny)]
     mine, theirs = part_pass(idx, mix, totals, crops)
     p_keep, p_send = pack_half_pass(idx, mine, lax.ppermute(theirs, "c", swap), nz, crops)
-    colparts, p_send = tie(colparts, p_send)
     p_came = across(p_send, nz // 2)
+    colparts, p_came = tie(colparts, p_came)
     sums = row_pass(expo, colparts, None, crops, 2 * nz)
     sums, *ring = tie(sums, *ring)
     gathered = ring + [other] + [lax.ppermute(rows, "c", swap) for rows in ring[1:]]
     rowparts = lax.all_to_all(sums, ("c", "z"), 0, 0)
-    rowparts, p_came = tie(rowparts, p_came)
     sums = column_pass(expo, rowparts, crops, nx * ny)
 
     colparts = lax.all_to_all(sums, ("x", "y"), 0, 0)

time: 217 us -> 211 us (0.972)
  blocking collectives: 0 us -> 10.4 us
  waiting for transfers between devices: 50 us -> 44.1 us
  local copies, waits for them, and re-layouts: 10 us -> 4.17 us
  starting transfers between devices: 65.2 us -> 60.3 us
    all_to_all x0 -> x1, blocking collectives: none -> 10.4 us  [local(): rowparts = lax.all_to_all(sums, ('c', 'z'), 0, 0)]
    all_to_all x2 -> x1, starting transfers between devices: 15 us -> 8.6 us  [local(): rowparts = lax.all_to_all(sums, ('c', 'z'), 0, 0)]
    unnamed x30 -> x16, local copies, waits for them, and re-layouts: 10 us -> 4.17 us
    ppermute x5, waiting for transfers between devices: 27.5 us -> 21.9 us  [across(): return lax.ppermute(value, 'z', [(i, i ^ bit) for i in range(nz)])]
    all_to_all x2 -> x1, waiting for transfers between devices: 5.76 us -> 5.85 us  [local(): rowparts = lax.all_to_all(sums, ('c', 'z'), 0, 0)]
  transfers between devices with their start and end apart: 24 -> 23, of which waited for: 12 -> 11; matrix products, arithmetic and copies ran while one was open for 0% -> 0% of each run, Pallas kernels for 31% -> 29%
where the time goes in v8:
time: 211 us; the launch traced here: 207 us
  Pallas kernels  87 us (41%)
  starting transfers between devices  60.3 us (29%)
  waiting for transfers between devices  44.1 us (21%)
  blocking collectives  10.4 us (5%)
  local copies, waits for them, and re-layouts  4.17 us (2%)
    pallas_call x19, Pallas kernels, call(): pl.pallas_call(kernel, out_shape=out_shape, out_specs=out_specs, in_specs...  87 us
    ppermute x5, waiting for transfers between devices, across(): return lax.ppermute(value, 'z', [(i, i ^ bit) for i in range(nz)])  21.9 us
    all_to_all x3, starting transfers between devices, local(): colparts = lax.all_to_all(sums, ('x', 'y'), 0, 0)  18.5 us
    ppermute x5, starting transfers between devices, across(): return lax.ppermute(value, 'z', [(i, i ^ bit) for i in range(nz)])  11 us
    all_to_all x3, waiting for transfers between devices, local(): colparts = lax.all_to_all(sums, ('x', 'y'), 0, 0)  11 us
    all_to_all x1, blocking collectives, local(): rowparts = lax.all_to_all(sums, ('c', 'z'), 0, 0)  10.4 us
    all_to_all x1, starting transfers between devices, local(): rowparts = lax.all_to_all(sums, ('c', 'z'), 0, 0)  8.6 us
    all_to_all x1, starting transfers between devices, local(): parts = lax.all_to_all(outgoing, ('x', 'y', 'c'), 0, 0)  7.21 us
  transfers between devices with their start and end apart: 23, of which 11 were waited for; matrix products, arithmetic and copies ran while one was open for 0% of the time, Pallas kernels for 29%

profile of v8, /device:TPU:32, one launch (start us, length us, event | category | flops | bytes accessed | tf_op | source)
XLA Modules:
  0.0 207.2 jit_solution(15431311910936631105)
XLA Ops:
  0.6 3.5 %shard_map.94.own.refs_0_ = f32[1024,256]{1,0:T(8,128)} custom-call(bf16[128,256]{1,0:T(8,128)(2,1)} %tcrops.1, bf16[1024,256]{1,0:T(8,128)(2,1)} %tpatch.1, bf16[128,256]{1,0:T(8,128)(2,1)} %refs_4_.1, bf16[1024,256]{1,0:T(8,128)(2,1)} %refs_5_.1, s32[4,96]{1,0:T(4,128)} %mask.3), custom_call_target="tpu_custom_call" | custom-call | tf_op jit(solution)/shard_map/pallas_call | solution.py:32
  4.2 3.1 %collective-permute-start.2 = (f32[1024,256]{1,0:T(8,128)}, f32[1024,256]{1,0:T(8,128)}, u32[]{:S(2)}, u32[]{:S(2)}) collective-permute-start(f32[1024,256]{1,0:T(8,128)} %shard_map.94.own.refs_0_), channel_id=1, source_target_pairs={{0,48},{16,0},{32,16},{48,32},{1,49},{17,1},{33,17},{49,33},{2,50}... | collective-permute-start | bytes 3145736 | tf_op jit(solution)/shard_map/ppermute | solution.py:963
  9.6 8.9 %shard_map.95 = (bf16[1024,4096]{1,0:T(8,128)(2,1)}, f32[16,64,128]{2,1,0:T(8,128)}) custom-call(s32[4]{0:T(128)S(1)} %pad_add_fusion.idx, f32[1024,256]{1,0:T(8,128)S(1)} %copy-done, f32[1024,256]{1,0:T(8,128)} %copy-done.7, bf16[256,8192]{1,0:T(8,128)(2,1)} %protos.9), custom_call_target="tpu_custom_call" | custom-call | flops 2147483648 | bytes 8388608 | tf_op jit(solution)/shard_map/pallas_call | solution.py:32
  18.5 7.1 %all-to-all-start = ((f32[16,64,128]{2,1,0:T(8,128)}), f32[16,64,128]{2,1,0:T(8,128)S(1)}, u32[]{:S(2)}, u32[]{:S(2)}) async-start(f32[16,64,128]{2,1,0:T(8,128)} %get-tuple-element.70), calls=%async_computation | async-start | bytes 1048576 | tf_op jit(solution)/shard_map/all_to_all | solution.py:972
  25.6 8.7 %shard_map.96 = (f32[8,128]{1,0:T(8,128)S(1)}, f32[1024,256]{1,0:T(8,128)S(1)}) custom-call(s32[4]{0:T(128)S(1)} %pad_add_fusion.idx, f32[1024,256]{1,0:T(8,128)} %shard_map.94.own.refs_0_, f32[1024,256]{1,0:T(8,128)} %copy-done.7, bf16[256,8192]{1,0:T(8,128)(2,1)} %protos.12), custom_call_target="tpu_custom_call" | custom-call | flops 4294967296 | bytes 2097152 | tf_op jit(solution)/shard_map/pallas_call | solution.py:32
  35.9 3.4 %collective-permute-done.1.refs_1_ = f32[1024,256]{1,0:T(8,128)} collective-permute-done((f32[1024,256]{1,0:T(8,128)}, f32[1024,256]{1,0:T(8,128)}, u32[]{:S(2)}, u32[]{:S(2)}) %collective-permute-start.1) | collective-permute-done | bytes 1048608 | tf_op jit(solution)/shard_map/ppermute | solution.py:962
  39.6 5.1 %shard_map.97 = f32[16,16,128]{2,1,0:T(8,128)} custom-call(bf16[1024,4096]{1,0:T(8,128)(2,1)} %get-tuple-element.69.expo, f32[16,64,128]{2,1,0:T(8,128)S(1)} %all-to-all-done.colparts, f32[8,128]{1,0:T(8,128)S(1)} %get-tuple-element.73.refs_0_), custom_call_target="tpu_custom_call" | custom-call | flops 8388608 | bytes 8388608 | tf_op jit(solution)/shard_map/pallas_call | solution.py:32
  44.7 8.6 %all-to-all-start.1 = ((f32[16,16,128]{2,1,0:T(8,128)}), f32[16,16,128]{2,1,0:T(8,128)S(1)}, u32[]{:S(2)}, u32[]{:S(2)}) async-start(f32[16,16,128]{2,1,0:T(8,128)} %shard_map.97), calls=%async_computation.1 | async-start | bytes 262144 | tf_op jit(solution)/shard_map/all_to_all | solution.py:981
  53.3 2.3 %shard_map.98.winv = f32[1,8192]{1,0:T(1,128)S(1)} custom-call(bf16[256,8192]{1,0:T(8,128)(2,1)} %protos.12), custom_call_target="tpu_custom_call" | custom-call | flops 6291456 | bytes 4194304 | tf_op jit(solution)/shard_map/pallas_call | solution.py:32
  55.7 5.9 %all-to-all-done.1.rowparts = f32[16,16,128]{2,1,0:T(8,128)S(1)} async-done(((f32[16,16,128]{2,1,0:T(8,128)}), f32[16,16,128]{2,1,0:T(8,128)S(1)}, u32[]{:S(2)}, u32[]{:S(2)}) %all-to-all-start.1) | async-done | bytes 131104 | tf_op jit(solution)/shard_map/all_to_all | solution.py:981
  61.5 4.6 %shard_map.99 = f32[16,64,128]{2,1,0:T(8,128)} custom-call(bf16[1024,4096]{1,0:T(8,128)(2,1)} %get-tuple-element.69.expo, f32[16,16,128]{2,1,0:T(8,128)S(1)} %all-to-all-done.1.rowparts), custom_call_target="tpu_custom_call" | custom-call | flops 8388608 | bytes 8388608 | tf_op jit(solution)/shard_map/pallas_call | solution.py:32
  67.8 4.5 %all-to-all-start.2 = ((f32[16,64,128]{2,1,0:T(8,128)}), f32[16,64,128]{2,1,0:T(8,128)S(1)}, u32[]{:S(2)}, u32[]{:S(2)}) async-start(f32[16,64,128]{2,1,0:T(8,128)} %shard_map.99), calls=%async_computation.2 | async-start | bytes 1048576 | tf_op jit(solution)/shard_map/all_to_all | solution.py:988
  74.9 10.6 %all-to-all-done.2.colparts = f32[16,64,128]{2,1,0:T(8,128)S(1)} async-done(((f32[16,64,128]{2,1,0:T(8,128)}), f32[16,64,128]{2,1,0:T(8,128)S(1)}, u32[]{:S(2)}, u32[]{:S(2)}) %all-to-all-start.2) | async-done | bytes 524320 | tf_op jit(solution)/shard_map/all_to_all | solution.py:988
  85.6 5.6 %collective-permute-done.4.prob_came = f32[256,256]{1,0:T(8,128)S(1)} collective-permute-done((f32[256,256]{1,0:T(8,128)S(1)}, f32[256,256]{1,0:T(8,128)S(1)}, u32[]{:S(2)}, u32[]{:S(2)}) %collective-permute-start.4) | collective-permute-done | bytes 262176 | tf_op jit(solution)/shard_map/ppermute | solution.py:970
  91.1 4.5 %shard_map.102 = f32[16,8,128]{2,1,0:T(8,128)S(1)} custom-call(bf16[1024,4096]{1,0:T(8,128)(2,1)} %get-tuple-element.69.expo, f32[16,64,128]{2,1,0:T(8,128)S(1)} %all-to-all-done.2.colparts), custom_call_target="tpu_custom_call" | custom-call | flops 8388608 | bytes 8388608 | tf_op jit(solution)/shard_map/pallas_call | solution.py:32
  96.3 10.4 %all_to_all.35.rowparts = f32[16,8,128]{2,1,0:T(8,128)S(1)} all-to-all(f32[16,8,128]{2,1,0:T(8,128)S(1)} %shard_map.102), channel_id=1, replica_groups=mesh['x'=4,'y'=4,'c'=2,'z'=8] {'c','z'}, dimensions={0} | all-to-all | bytes 131072 | tf_op jit(solution)/shard_map/all_to_all | solution.py:998
  106.7 4.7 %shard_map.103 = f32[16,64,128]{2,1,0:T(8,128)} custom-call(bf16[1024,4096]{1,0:T(8,128)(2,1)} %get-tuple-element.69.expo, f32[16,8,128]{2,1,0:T(8,128)S(1)} %all_to_all.35.rowparts), custom_call_target="tpu_custom_call" | custom-call | flops 8388608 | bytes 8388608 | tf_op jit(solution)/shard_map/pallas_call | solution.py:32
  111.5 6.9 %all-to-all-start.4 = ((f32[16,64,128]{2,1,0:T(8,128)}), f32[16,64,128]{2,1,0:T(8,128)S(1)}, u32[]{:S(2)}, u32[]{:S(2)}) async-start(f32[16,64,128]{2,1,0:T(8,128)} %shard_map.103), calls=%async_computation.4 | async-start | bytes 1048576 | tf_op jit(solution)/shard_map/all_to_all | solution.py:1001
  118.4 3.1 %collective-permute-start.11 = (f32[8,128]{1,0:T(8,128)S(1)}, f32[8,128]{1,0:T(8,128)S(1)}, u32[]{:S(2)}, u32[]{:S(2)}) collective-permute-start(f32[8,128]{1,0:T(8,128)S(1)} %slice_reduce_fusion.totals.refs_8_), channel_id=1, source_target_pairs={{0,48},{16,0},{32,16},{48,32},{1,49},{17,1},{33,17},{49,33},{2,50}... | collective-permute-start | bytes 12296 | tf_op jit(solution)/shard_map/ppermute | solution.py:990
  123.3 6.4 %shard_map.104 = (bf16[1024,1024]{1,0:T(8,128)(2,1)}, bf16[3072,1024]{1,0:T(8,128)(2,1)}) custom-call(s32[4]{0:T(128)S(1)} %pad_add_fusion.idx, bf16[256,8192]{1,0:T(8,128)(2,1)} %protos.9, f32[1024,256]{1,0:T(8,128)S(1)} %copy-done.1, f32[1024,256]{1,0:T(8,128)} %collective-permute-done.1.refs_1_, f32[1024,256]{1,0:T(8,128)} %collective-permute-done.5.refs_2_, ...), custom_call_target="tpu_custom_call" | custom-call | flops 2147483648 | bytes 4194304 | tf_op jit(solution)/shard_map/pallas_call | solution.py:32
  129.9 6.6 %shard_map.105 = (f32[512,256]{1,0:T(8,128)S(1)}, f32[512,256]{1,0:T(8,128)S(1)}) custom-call(s32[4]{0:T(128)S(1)} %pad_add_fusion.idx, bf16[1024,4096]{1,0:T(8,128)(2,1)} %get-tuple-element.69.expo, f32[16,64,128]{2,1,0:T(8,128)S(1)} %all-to-all-done.4.colparts, bf16[256,8192]{1,0:T(8,128)(2,1)} %protos.12), custom_call_target="tpu_custom_call" | custom-call | flops 2147483648 | bytes 8388608 | tf_op jit(solution)/shard_map/pallas_call | solution.py:32
  136.8 5.3 %shard_map.106 = f32[64,8,128]{2,1,0:T(8,128)} custom-call(bf16[1024,4096]{1,0:T(8,128)(2,1)} %get-tuple-element.69.expo, f32[16,64,128]{2,1,0:T(8,128)S(1)} %all-to-all-done.4.colparts), custom_call_target="tpu_custom_call" | custom-call | flops 8388608 | bytes 8388608 | tf_op jit(solution)/shard_map/pallas_call | solution.py:32
  142.7 5.8 %all-to-all-start.5 = ((f32[64,8,128]{2,1,0:T(8,128)}), f32[64,8,128]{2,1,0:T(8,128)S(1)}, u32[]{:S(2)}, u32[]{:S(2)}) async-start(f32[64,8,128]{2,1,0:T(8,128)} %shard_map.106), calls=%async_computation.5 | async-start | bytes 524288 | tf_op jit(solution)/shard_map/all_to_all | solution.py:1013
  148.5 4.6 %collective-permute-start.13 = (f32[256,256]{1,0:T(8,128)S(1)}, f32[256,256]{1,0:T(8,128)S(1)}, u32[]{:S(2)}, u32[]{:S(2)}) collective-permute-start(f32[256,256]{1,0:T(8,128)S(1)} %get-tuple-element.119), channel_id=1, source_target_pairs={{0,4},{1,5},{2,6},{3,7},{4,0},{5,1},{6,2},{7,3},{8,12},{9,13},{10,... | collective-permute-start | bytes 786440 | tf_op jit(solution)/shard_map/ppermute | solution.py:970
  153.1 9.3 %shard_map.108 = (f32[256,1024]{1,0:T(8,128)S(1)}, f32[256,1024]{1,0:T(8,128)}, bf16[256,1024]{1,0:T(8,128)(2,1)S(1)}, bf16[256,3072]{1,0:T(8,128)(2,1)}) custom-call(s32[4]{0:T(128)S(1)} %pad_add_fusion.idx, bf16[256,8192]{1,0:T(8,128)(2,1)} %protos.12, f32[1024,256]{1,0:T(8,128)} %shard_map.94.own.refs_0_, f32[1024,256]{1,0:T(8,128)} %collective-permute-done.1.refs_1_, ...), custom_call_target="tpu_custom_call" | custom-call | flops 4294967296 | bytes 4194304 | tf_op jit(solution)/shard_map/pallas_call | solution.py:32
  163.4 7.3 %collective-permute-done.13.target_came = f32[256,256]{1,0:T(8,128)S(1)} collective-permute-done((f32[256,256]{1,0:T(8,128)S(1)}, f32[256,256]{1,0:T(8,128)S(1)}, u32[]{:S(2)}, u32[]{:S(2)}) %collective-permute-start.13) | collective-permute-done | bytes 262176 | tf_op jit(solution)/shard_map/ppermute | solution.py:970
  170.7 8.4 %shard_map.109 = f32[32,72,128]{2,1,0:T(8,128)} custom-call(s32[4]{0:T(128)S(1)} %pad_add_fusion.idx, f32[256,1024]{1,0:T(8,128)} %copy-done.3, f32[256,1024]{1,0:T(8,128)} %get-tuple-element.121.wnorm_in, bf16[256,1024]{1,0:T(8,128)(2,1)S(1)} %get-tuple-element.122.turned_d_in, bf16[256,3072]{1,0:T(8,128)(2,1)} %get-tuple-element.123.turned_i_in, ...), custom_call_target="tpu_custom_call" | custom-call | flops 2147483648 | bytes 8388608 | tf_op jit(solution)/shard_map/pallas_call | solution.py:32
  179.1 7.2 %all-to-all-start.6 = ((f32[32,72,128]{2,1,0:T(8,128)}), f32[32,72,128]{2,1,0:T(8,128)S(1)}, u32[]{:S(2)}, u32[]{:S(2)}) async-start(f32[32,72,128]{2,1,0:T(8,128)} %shard_map.109), calls=%async_computation.6 | async-start | bytes 2359296 | tf_op jit(solution)/shard_map/all_to_all | solution.py:1021
  188.6 2.9 %collective-permute-start.14 = (f32[128,256]{1,0:T(8,128)S(1)}, f32[128,256]{1,0:T(8,128)S(1)}, u32[]{:S(2)}, u32[]{:S(2)}) collective-permute-start(f32[128,256]{1,0:T(8,128)S(1)} %get-tuple-element.132), channel_id=1, source_target_pairs={{0,2},{1,3},{2,0},{3,1},{4,6},{5,7},{6,4},{7,5},{8,10},{9,11},{10,... | collective-permute-start | bytes 393224 | tf_op jit(solution)/shard_map/ppermute | solution.py:970
  191.6 2.6 %collective-permute-done.15.refs_2_ = f32[128,256]{1,0:T(8,128)S(1)} collective-permute-done((f32[128,256]{1,0:T(8,128)S(1)}, f32[128,256]{1,0:T(8,128)S(1)}, u32[]{:S(2)}, u32[]{:S(2)}) %collective-permute-start.15) | collective-permute-done | bytes 131104 | tf_op jit(solution)/shard_map/ppermute | solution.py:970
  194.2 6.4 %collective-permute-done.16.refs_3_ = f32[128,256]{1,0:T(8,128)S(1)} collective-permute-done((f32[128,256]{1,0:T(8,128)S(1)}, f32[128,256]{1,0:T(8,128)S(1)}, u32[]{:S(2)}, u32[]{:S(2)}) %collective-permute-start.16) | collective-permute-done | bytes 131104 | tf_op jit(solution)/shard_map/ppermute | solution.py:970
  200.6 2.7 %shard_map.112 = (f32[16,256]{1,0:T(8,128)}, f32[128,256]{1,0:T(8,128)}) custom-call(s32[4]{0:T(128)S(1)} %pad_add_fusion.idx, s32[4,96]{1,0:T(4,128)S(1)} %copy-done.6, f32[128,256]{1,0:T(8,128)S(1)} %get-tuple-element.131.refs_0_, f32[128,256]{1,0:T(8,128)S(1)} %collective-permute-done.14.refs_1_, f32[128,256]{1,0:T(8,128)S(1)} %collective-permute-done.15.refs_2_, ...), custom_call_target="tpu_custom_call" | custom-call | tf_op jit(solution)/shard_map/pallas_call | solution.py:32
  (52 shorter events, 18.9 us)
Async XLA Ops:
  4.1 3.3 %collective-permute-start = (f32[1024,256]{1,0:T(8,128)}, f32[1024,256]{1,0:T(8,128)S(1)}, u32[]{:S(2)}, u32[]{:S(2)}) collective-permute-start(f32[1024,256]{1,0:T(8,128)} %shard_map.94.own.refs_0_), channel_id=1, source_target_pairs={{0,8},{8,0},{1,9},{9,1},{2,10},{10,2},{3,11},{11,3},{4,12},{12,4},... | collective-permute-start | bytes 3145736 | tf_op jit(solution)/shard_map/ppermute | solution.py:960
  4.2 31.7 %collective-permute-start.2 = (f32[1024,256]{1,0:T(8,128)}, f32[1024,256]{1,0:T(8,128)}, u32[]{:S(2)}, u32[]{:S(2)}) collective-permute-start(f32[1024,256]{1,0:T(8,128)} %shard_map.94.own.refs_0_), channel_id=1, source_target_pairs={{0,48},{16,0},{32,16},{48,32},{1,49},{17,1},{33,17},{49,33},{2,50}... | collective-permute-start | bytes 3145736 | tf_op jit(solution)/shard_map/ppermute | solution.py:963
  7.3 32.0 %collective-permute-start.1 = (f32[1024,256]{1,0:T(8,128)}, f32[1024,256]{1,0:T(8,128)}, u32[]{:S(2)}, u32[]{:S(2)}) collective-permute-start(f32[1024,256]{1,0:T(8,128)} %shard_map.94.own.refs_0_), channel_id=1, source_target_pairs={{0,16},{16,32},{32,48},{48,0},{1,17},{17,33},{33,49},{49,1},{2,18}... | collective-permute-start | bytes 3145736 | tf_op jit(solution)/shard_map/ppermute | solution.py:962
  7.4 1.0 copy-start.7
  8.4 1.2 copy-start
  18.5 21.0 %all-to-all-start = ((f32[16,64,128]{2,1,0:T(8,128)}), f32[16,64,128]{2,1,0:T(8,128)S(1)}, u32[]{:S(2)}, u32[]{:S(2)}) async-start(f32[16,64,128]{2,1,0:T(8,128)} %get-tuple-element.70), calls=%async_computation | async-start | bytes 1048576 | tf_op jit(solution)/shard_map/all_to_all | solution.py:972
  34.3 1.0 copy-start.4
  44.7 16.8 %all-to-all-start.1 = ((f32[16,16,128]{2,1,0:T(8,128)}), f32[16,16,128]{2,1,0:T(8,128)S(1)}, u32[]{:S(2)}, u32[]{:S(2)}) async-start(f32[16,16,128]{2,1,0:T(8,128)} %shard_map.97), calls=%async_computation.1 | async-start | bytes 262144 | tf_op jit(solution)/shard_map/all_to_all | solution.py:981
  53.3 42.3 %collective-permute-start.5 = (f32[1024,256]{1,0:T(8,128)}, f32[1024,256]{1,0:T(8,128)}, u32[]{:S(2)}, u32[]{:S(2)}) collective-permute-start(f32[1024,256]{1,0:T(8,128)} %collective-permute-done.1.refs_1_), channel_id=1, source_target_pairs={{0,16},{16,32},{32,48},{48,0},{1,17},{17,33},{33,49},{49,1},{2,18}... | collective-permute-start | bytes 3145736 | tf_op jit(solution)/shard_map/ppermute | solution.py:977
  67.7 4.6 %collective-permute-start.3 = (f32[512,256]{1,0:T(8,128)S(1)}, f32[512,256]{1,0:T(8,128)S(1)}, u32[]{:S(2)}, u32[]{:S(2)}) collective-permute-start(f32[512,256]{1,0:T(8,128)S(1)} %get-tuple-element.79), channel_id=1, source_target_pairs={{0,8},{8,0},{1,9},{9,1},{2,10},{10,2},{3,11},{11,3},{4,12},{12,4},... | collective-permute-start | bytes 1572872 | tf_op jit(solution)/shard_map/ppermute | solution.py:992
  67.8 17.8 %all-to-all-start.2 = ((f32[16,64,128]{2,1,0:T(8,128)}), f32[16,64,128]{2,1,0:T(8,128)S(1)}, u32[]{:S(2)}, u32[]{:S(2)}) async-start(f32[16,64,128]{2,1,0:T(8,128)} %shard_map.99), calls=%async_computation.2 | async-start | bytes 1048576 | tf_op jit(solution)/shard_map/all_to_all | solution.py:988
  72.9 18.2 %collective-permute-start.4 = (f32[256,256]{1,0:T(8,128)S(1)}, f32[256,256]{1,0:T(8,128)S(1)}, u32[]{:S(2)}, u32[]{:S(2)}) collective-permute-start(f32[256,256]{1,0:T(8,128)S(1)} %get-tuple-element.80), channel_id=1, source_target_pairs={{0,4},{1,5},{2,6},{3,7},{4,0},{5,1},{6,2},{7,3},{8,12},{9,13},{10,... | collective-permute-start | bytes 786440 | tf_op jit(solution)/shard_map/ppermute | solution.py:970
  95.6 26.8 %collective-permute-start.6 = (f32[1024,256]{1,0:T(8,128)}, f32[1024,256]{1,0:T(8,128)}, u32[]{:S(2)}, u32[]{:S(2)}) collective-permute-start(f32[1024,256]{1,0:T(8,128)} %collective-permute-done.1.refs_1_), channel_id=1, source_target_pairs={{0,8},{8,0},{1,9},{9,1},{2,10},{10,2},{3,11},{11,3},{4,12},{12,4},... | collective-permute-start | bytes 3145736 | tf_op jit(solution)/shard_map/ppermute | solution.py:997
  95.7 27.5 %collective-permute-start.7 = (f32[1024,256]{1,0:T(8,128)}, f32[1024,256]{1,0:T(8,128)}, u32[]{:S(2)}, u32[]{:S(2)}) collective-permute-start(f32[1024,256]{1,0:T(8,128)} %collective-permute-done.5.refs_2_), channel_id=1, source_target_pairs={{0,8},{8,0},{1,9},{9,1},{2,10},{10,2},{3,11},{11,3},{4,12},{12,4},... | collective-permute-start | bytes 3145736 | tf_op jit(solution)/shard_map/ppermute | solution.py:997
  96.2 27.0 %collective-permute-start.8 = (f32[1024,256]{1,0:T(8,128)}, f32[1024,256]{1,0:T(8,128)}, u32[]{:S(2)}, u32[]{:S(2)}) collective-permute-start(f32[1024,256]{1,0:T(8,128)} %collective-permute-done.2.refs_3_), channel_id=1, source_target_pairs={{0,8},{8,0},{1,9},{9,1},{2,10},{10,2},{3,11},{11,3},{4,12},{12,4},... | collective-permute-start | bytes 3145736 | tf_op jit(solution)/shard_map/ppermute | solution.py:997
  106.7 16.6 %copy-start.1 = (f32[1024,256]{1,0:T(8,128)S(1)}, f32[1024,256]{1,0:T(8,128)}, u32[]{:S(2)}) copy-start(f32[1024,256]{1,0:T(8,128)} %shard_map.94.own.refs_0_) | copy-start | bytes 3145732
  111.5 18.4 %all-to-all-start.4 = ((f32[16,64,128]{2,1,0:T(8,128)}), f32[16,64,128]{2,1,0:T(8,128)S(1)}, u32[]{:S(2)}, u32[]{:S(2)}) async-start(f32[16,64,128]{2,1,0:T(8,128)} %shard_map.103), calls=%async_computation.4 | async-start | bytes 1048576 | tf_op jit(solution)/shard_map/all_to_all | solution.py:1001
  118.4 11.3 %collective-permute-start.11 = (f32[8,128]{1,0:T(8,128)S(1)}, f32[8,128]{1,0:T(8,128)S(1)}, u32[]{:S(2)}, u32[]{:S(2)}) collective-permute-start(f32[8,128]{1,0:T(8,128)S(1)} %slice_reduce_fusion.totals.refs_8_), channel_id=1, source_target_pairs={{0,48},{16,0},{32,16},{48,32},{1,49},{17,1},{33,17},{49,33},{2,50}... | collective-permute-start | bytes 12296 | tf_op jit(solution)/shard_map/ppermute | solution.py:990
  121.5 8.2 %collective-permute-start.10 = (f32[8,128]{1,0:T(8,128)S(1)}, f32[8,128]{1,0:T(8,128)S(1)}, u32[]{:S(2)}, u32[]{:S(2)}) collective-permute-start(f32[8,128]{1,0:T(8,128)S(1)} %slice_reduce_fusion.totals.refs_8_), channel_id=1, source_target_pairs={{0,32},{16,48},{32,0},{48,16},{1,33},{17,49},{33,1},{49,17},{2,34}... | collective-permute-start | bytes 12296 | tf_op jit(solution)/shard_map/ppermute | solution.py:990
  122.4 7.3 %collective-permute-start.9 = (f32[8,128]{1,0:T(8,128)S(1)}, f32[8,128]{1,0:T(8,128)S(1)}, u32[]{:S(2)}, u32[]{:S(2)}) collective-permute-start(f32[8,128]{1,0:T(8,128)S(1)} %slice_reduce_fusion.totals.refs_8_), channel_id=1, source_target_pairs={{0,16},{16,32},{32,48},{48,0},{1,17},{17,33},{33,49},{49,1},{2,18}... | collective-permute-start | bytes 12296 | tf_op jit(solution)/shard_map/ppermute | solution.py:990
  136.4 5.6 %collective-permute-start.12 = (f32[512,256]{1,0:T(8,128)S(1)}, f32[512,256]{1,0:T(8,128)S(1)}, u32[]{:S(2)}, u32[]{:S(2)}) collective-permute-start(f32[512,256]{1,0:T(8,128)S(1)} %get-tuple-element.103), channel_id=1, source_target_pairs={{0,8},{8,0},{1,9},{9,1},{2,10},{10,2},{3,11},{11,3},{4,12},{12,4},... | collective-permute-start | bytes 1572872 | tf_op jit(solution)/shard_map/ppermute | solution.py:1010
  142.7 28.0 %all-to-all-start.5 = ((f32[64,8,128]{2,1,0:T(8,128)}), f32[64,8,128]{2,1,0:T(8,128)S(1)}, u32[]{:S(2)}, u32[]{:S(2)}) async-start(f32[64,8,128]{2,1,0:T(8,128)} %shard_map.106), calls=%async_computation.5 | async-start | bytes 524288 | tf_op jit(solution)/shard_map/all_to_all | solution.py:1013
  148.5 22.2 %collective-permute-start.13 = (f32[256,256]{1,0:T(8,128)S(1)}, f32[256,256]{1,0:T(8,128)S(1)}, u32[]{:S(2)}, u32[]{:S(2)}) collective-permute-start(f32[256,256]{1,0:T(8,128)S(1)} %get-tuple-element.119), channel_id=1, source_target_pairs={{0,4},{1,5},{2,6},{3,7},{4,0},{5,1},{6,2},{7,3},{8,12},{9,13},{10,... | collective-permute-start | bytes 786440 | tf_op jit(solution)/shard_map/ppermute | solution.py:970
  162.4 1.0 copy-start.3
  170.7 29.9 %copy-start.2 = (bf16[1024,256]{1,0:T(8,128)(2,1)S(1)}, bf16[1024,256]{1,0:T(8,128)(2,1)}, u32[]{:S(2)}) copy-start(bf16[1024,256]{1,0:T(8,128)(2,1)} %refs_5_.1) | copy-start | bytes 1572868
  170.7 29.9 %copy-start.5 = (bf16[128,256]{1,0:T(8,128)(2,1)S(1)}, bf16[128,256]{1,0:T(8,128)(2,1)}, u32[]{:S(2)}) copy-start(bf16[128,256]{1,0:T(8,128)(2,1)} %refs_4_.1) | copy-start | bytes 196612
  170.7 29.9 %copy-start.6 = (s32[4,96]{1,0:T(4,128)S(1)}, s32[4,96]{1,0:T(4,128)}, u32[]{:S(2)}) copy-start(s32[4,96]{1,0:T(4,128)} %mask.3) | copy-start | bytes 4612
  179.1 25.6 %all-to-all-start.6 = ((f32[32,72,128]{2,1,0:T(8,128)}), f32[32,72,128]{2,1,0:T(8,128)S(1)}, u32[]{:S(2)}, u32[]{:S(2)}) async-start(f32[32,72,128]{2,1,0:T(8,128)} %shard_map.109), calls=%async_computation.6 | async-start | bytes 2359296 | tf_op jit(solution)/shard_map/all_to_all | solution.py:1021
  187.1 7.1 %collective-permute-start.15 = (f32[128,256]{1,0:T(8,128)S(1)}, f32[128,256]{1,0:T(8,128)S(1)}, u32[]{:S(2)}, u32[]{:S(2)}) collective-permute-start(f32[128,256]{1,0:T(8,128)S(1)} %get-tuple-element.131.refs_0_), channel_id=1, source_target_pairs={{0,1},{1,0},{2,3},{3,2},{4,5},{5,4},{6,7},{7,6},{8,9},{9,8},{10,11... | collective-permute-start | bytes 393224 | tf_op jit(solution)/shard_map/ppermute | solution.py:970
  188.6 12.0 %collective-permute-start.16 = (f32[128,256]{1,0:T(8,128)S(1)}, f32[128,256]{1,0:T(8,128)S(1)}, u32[]{:S(2)}, u32[]{:S(2)}) collective-permute-start(f32[128,256]{1,0:T(8,128)S(1)} %get-tuple-element.132), channel_id=1, source_target_pairs={{0,3},{1,2},{2,1},{3,0},{4,7},{5,6},{6,5},{7,4},{8,11},{9,10},{10,... | collective-permute-start | bytes 393224 | tf_op jit(solution)/shard_map/ppermute | solution.py:970
  188.6 12.0 %collective-permute-start.14 = (f32[128,256]{1,0:T(8,128)S(1)}, f32[128,256]{1,0:T(8,128)S(1)}, u32[]{:S(2)}, u32[]{:S(2)}) collective-permute-start(f32[128,256]{1,0:T(8,128)S(1)} %get-tuple-element.132), channel_id=1, source_target_pairs={{0,2},{1,3},{2,0},{3,1},{4,6},{5,7},{6,4},{7,5},{8,10},{9,11},{10,... | collective-permute-start | bytes 393224 | tf_op jit(solution)/shard_map/ppermute | solution.py:970

commit v9 on v8

--- a/solution.py
+++ b/solution.py
@@ -1012,9 +1012,8 @@
     sums, send = tie(sums, send)
     rowparts = lax.all_to_all(sums, ("y", "c", "z"), 0, 0)
     came = across(send, nz // 2)
-    *gathered, _ = tie(*gathered, sums)
+    *gathered, came, _ = tie(*gathered, came, sums)
     prob, wnorm, *turned = wide_student_pass(idx, gathered, student_protos, all_totals, crops)
-    prob, came = tie(prob, came)
     outgoing = weight_pass(
         idx, prob, wnorm, turned, wide_expo, colparts, rowparts, crops, ny, nx * ny * 2
     )

time: 211 us -> 210 us (level)
    all_to_all x1, starting transfers between devices: 5.82 us -> 8.83 us  [local(): rowparts = lax.all_to_all(sums, ('y', 'c', 'z'), 0, 0)]
    ppermute x5, starting transfers between devices: 11 us -> 8.32 us  [across(): return lax.ppermute(value, 'z', [(i, i ^ bit) for i in range(nz)])]
  transfers between devices with their start and end apart: 23 -> 23, of which waited for: 11 -> 12; matrix products, arithmetic and copies ran while one was open for 0% -> 0% of each run, Pallas kernels for 29% -> 29%
where the time goes in v9:
time: 210 us; the launch traced here: 208 us
  Pallas kernels  87 us (41%)
  starting transfers between devices  59.6 us (28%)
  waiting for transfers between devices  45.5 us (22%)
  blocking collectives  10.4 us (5%)
  local copies, waits for them, and re-layouts  4.17 us (2%)
    pallas_call x19, Pallas kernels, call(): pl.pallas_call(kernel, out_shape=out_shape, out_specs=out_specs, in_specs...  87 us
    ppermute x5, waiting for transfers between devices, across(): return lax.ppermute(value, 'z', [(i, i ^ bit) for i in range(nz)])  22.4 us
    all_to_all x3, starting transfers between devices, local(): colparts = lax.all_to_all(sums, ('x', 'y'), 0, 0)  18.5 us
    all_to_all x3, waiting for transfers between devices, local(): colparts = lax.all_to_all(sums, ('x', 'y'), 0, 0)  11 us
    all_to_all x1, blocking collectives, local(): rowparts = lax.all_to_all(sums, ('c', 'z'), 0, 0)  10.4 us
    all_to_all x1, starting transfers between devices, local(): rowparts = lax.all_to_all(sums, ('y', 'c', 'z'), 0, 0)  8.83 us
    all_to_all x1, starting transfers between devices, local(): rowparts = lax.all_to_all(sums, ('c', 'z'), 0, 0)  8.6 us
    ppermute x5, starting transfers between devices, across(): return lax.ppermute(value, 'z', [(i, i ^ bit) for i in range(nz)])  8.32 us
  transfers between devices with their start and end apart: 23, of which 12 were waited for; matrix products, arithmetic and copies ran while one was open for 0% of the time, Pallas kernels for 29%

profile of v9, /device:TPU:32, one launch (start us, length us, event | category | flops | bytes accessed | tf_op | source)
XLA Modules:
  0.0 207.8 jit_solution(17991185092030705897)
XLA Ops:
  0.6 3.5 %shard_map.94.own.refs_0_ = f32[1024,256]{1,0:T(8,128)} custom-call(bf16[128,256]{1,0:T(8,128)(2,1)} %tcrops.1, bf16[1024,256]{1,0:T(8,128)(2,1)} %tpatch.1, bf16[128,256]{1,0:T(8,128)(2,1)} %refs_4_.1, bf16[1024,256]{1,0:T(8,128)(2,1)} %refs_5_.1, s32[4,96]{1,0:T(4,128)} %mask.3), custom_call_target="tpu_custom_call" | custom-call | tf_op jit(solution)/shard_map/pallas_call | solution.py:32
  4.2 3.1 %collective-permute-start.2 = (f32[1024,256]{1,0:T(8,128)}, f32[1024,256]{1,0:T(8,128)}, u32[]{:S(2)}, u32[]{:S(2)}) collective-permute-start(f32[1024,256]{1,0:T(8,128)} %shard_map.94.own.refs_0_), channel_id=1, source_target_pairs={{0,48},{16,0},{32,16},{48,32},{1,49},{17,1},{33,17},{49,33},{2,50}... | collective-permute-start | bytes 3145736 | tf_op jit(solution)/shard_map/ppermute | solution.py:963
  9.6 8.9 %shard_map.95 = (bf16[1024,4096]{1,0:T(8,128)(2,1)}, f32[16,64,128]{2,1,0:T(8,128)}) custom-call(s32[4]{0:T(128)S(1)} %pad_add_fusion.idx, f32[1024,256]{1,0:T(8,128)S(1)} %copy-done, f32[1024,256]{1,0:T(8,128)} %copy-done.7, bf16[256,8192]{1,0:T(8,128)(2,1)} %protos.9), custom_call_target="tpu_custom_call" | custom-call | flops 2147483648 | bytes 8388608 | tf_op jit(solution)/shard_map/pallas_call | solution.py:32
  18.5 7.1 %all-to-all-start = ((f32[16,64,128]{2,1,0:T(8,128)}), f32[16,64,128]{2,1,0:T(8,128)S(1)}, u32[]{:S(2)}, u32[]{:S(2)}) async-start(f32[16,64,128]{2,1,0:T(8,128)} %get-tuple-element.69), calls=%async_computation | async-start | bytes 1048576 | tf_op jit(solution)/shard_map/all_to_all | solution.py:972
  25.6 8.7 %shard_map.96 = (f32[8,128]{1,0:T(8,128)S(1)}, f32[1024,256]{1,0:T(8,128)S(1)}) custom-call(s32[4]{0:T(128)S(1)} %pad_add_fusion.idx, f32[1024,256]{1,0:T(8,128)} %shard_map.94.own.refs_0_, f32[1024,256]{1,0:T(8,128)} %copy-done.7, bf16[256,8192]{1,0:T(8,128)(2,1)} %protos.12), custom_call_target="tpu_custom_call" | custom-call | flops 4294967296 | bytes 2097152 | tf_op jit(solution)/shard_map/pallas_call | solution.py:32
  35.9 3.4 %collective-permute-done.1.refs_1_ = f32[1024,256]{1,0:T(8,128)} collective-permute-done((f32[1024,256]{1,0:T(8,128)}, f32[1024,256]{1,0:T(8,128)}, u32[]{:S(2)}, u32[]{:S(2)}) %collective-permute-start.1) | collective-permute-done | bytes 1048608 | tf_op jit(solution)/shard_map/ppermute | solution.py:962
  39.6 5.1 %shard_map.97 = f32[16,16,128]{2,1,0:T(8,128)} custom-call(bf16[1024,4096]{1,0:T(8,128)(2,1)} %get-tuple-element.68.expo, f32[16,64,128]{2,1,0:T(8,128)S(1)} %all-to-all-done.colparts, f32[8,128]{1,0:T(8,128)S(1)} %get-tuple-element.72.refs_0_), custom_call_target="tpu_custom_call" | custom-call | flops 8388608 | bytes 8388608 | tf_op jit(solution)/shard_map/pallas_call | solution.py:32
  44.7 8.6 %all-to-all-start.1 = ((f32[16,16,128]{2,1,0:T(8,128)}), f32[16,16,128]{2,1,0:T(8,128)S(1)}, u32[]{:S(2)}, u32[]{:S(2)}) async-start(f32[16,16,128]{2,1,0:T(8,128)} %shard_map.97), calls=%async_computation.1 | async-start | bytes 262144 | tf_op jit(solution)/shard_map/all_to_all | solution.py:981
  53.3 2.3 %shard_map.98.winv = f32[1,8192]{1,0:T(1,128)S(1)} custom-call(bf16[256,8192]{1,0:T(8,128)(2,1)} %protos.12), custom_call_target="tpu_custom_call" | custom-call | flops 6291456 | bytes 4194304 | tf_op jit(solution)/shard_map/pallas_call | solution.py:32
  55.7 5.9 %all-to-all-done.1.rowparts = f32[16,16,128]{2,1,0:T(8,128)S(1)} async-done(((f32[16,16,128]{2,1,0:T(8,128)}), f32[16,16,128]{2,1,0:T(8,128)S(1)}, u32[]{:S(2)}, u32[]{:S(2)}) %all-to-all-start.1) | async-done | bytes 131104 | tf_op jit(solution)/shard_map/all_to_all | solution.py:981
  61.5 4.6 %shard_map.99 = f32[16,64,128]{2,1,0:T(8,128)} custom-call(bf16[1024,4096]{1,0:T(8,128)(2,1)} %get-tuple-element.68.expo, f32[16,16,128]{2,1,0:T(8,128)S(1)} %all-to-all-done.1.rowparts), custom_call_target="tpu_custom_call" | custom-call | flops 8388608 | bytes 8388608 | tf_op jit(solution)/shard_map/pallas_call | solution.py:32
  67.8 4.5 %all-to-all-start.2 = ((f32[16,64,128]{2,1,0:T(8,128)}), f32[16,64,128]{2,1,0:T(8,128)S(1)}, u32[]{:S(2)}, u32[]{:S(2)}) async-start(f32[16,64,128]{2,1,0:T(8,128)} %shard_map.99), calls=%async_computation.2 | async-start | bytes 1048576 | tf_op jit(solution)/shard_map/all_to_all | solution.py:988
  74.9 10.6 %all-to-all-done.2.colparts = f32[16,64,128]{2,1,0:T(8,128)S(1)} async-done(((f32[16,64,128]{2,1,0:T(8,128)}), f32[16,64,128]{2,1,0:T(8,128)S(1)}, u32[]{:S(2)}, u32[]{:S(2)}) %all-to-all-start.2) | async-done | bytes 524320 | tf_op jit(solution)/shard_map/all_to_all | solution.py:988
  85.6 5.6 %collective-permute-done.4.prob_came = f32[256,256]{1,0:T(8,128)S(1)} collective-permute-done((f32[256,256]{1,0:T(8,128)S(1)}, f32[256,256]{1,0:T(8,128)S(1)}, u32[]{:S(2)}, u32[]{:S(2)}) %collective-permute-start.4) | collective-permute-done | bytes 262176 | tf_op jit(solution)/shard_map/ppermute | solution.py:970
  91.1 4.5 %shard_map.102 = f32[16,8,128]{2,1,0:T(8,128)S(1)} custom-call(bf16[1024,4096]{1,0:T(8,128)(2,1)} %get-tuple-element.68.expo, f32[16,64,128]{2,1,0:T(8,128)S(1)} %all-to-all-done.2.colparts), custom_call_target="tpu_custom_call" | custom-call | flops 8388608 | bytes 8388608 | tf_op jit(solution)/shard_map/pallas_call | solution.py:32
  96.3 10.4 %all_to_all.35.rowparts = f32[16,8,128]{2,1,0:T(8,128)S(1)} all-to-all(f32[16,8,128]{2,1,0:T(8,128)S(1)} %shard_map.102), channel_id=1, replica_groups=mesh['x'=4,'y'=4,'c'=2,'z'=8] {'c','z'}, dimensions={0} | all-to-all | bytes 131072 | tf_op jit(solution)/shard_map/all_to_all | solution.py:998
  106.7 4.7 %shard_map.103 = f32[16,64,128]{2,1,0:T(8,128)} custom-call(bf16[1024,4096]{1,0:T(8,128)(2,1)} %get-tuple-element.68.expo, f32[16,8,128]{2,1,0:T(8,128)S(1)} %all_to_all.35.rowparts), custom_call_target="tpu_custom_call" | custom-call | flops 8388608 | bytes 8388608 | tf_op jit(solution)/shard_map/pallas_call | solution.py:32
  111.5 6.9 %all-to-all-start.4 = ((f32[16,64,128]{2,1,0:T(8,128)}), f32[16,64,128]{2,1,0:T(8,128)S(1)}, u32[]{:S(2)}, u32[]{:S(2)}) async-start(f32[16,64,128]{2,1,0:T(8,128)} %shard_map.103), calls=%async_computation.4 | async-start | bytes 1048576 | tf_op jit(solution)/shard_map/all_to_all | solution.py:1001
  118.4 3.1 %collective-permute-start.11 = (f32[8,128]{1,0:T(8,128)S(1)}, f32[8,128]{1,0:T(8,128)S(1)}, u32[]{:S(2)}, u32[]{:S(2)}) collective-permute-start(f32[8,128]{1,0:T(8,128)S(1)} %slice_reduce_fusion.totals.refs_8_), channel_id=1, source_target_pairs={{0,48},{16,0},{32,16},{48,32},{1,49},{17,1},{33,17},{49,33},{2,50}... | collective-permute-start | bytes 12296 | tf_op jit(solution)/shard_map/ppermute | solution.py:990
  123.3 6.4 %shard_map.104 = (bf16[1024,1024]{1,0:T(8,128)(2,1)}, bf16[3072,1024]{1,0:T(8,128)(2,1)}) custom-call(s32[4]{0:T(128)S(1)} %pad_add_fusion.idx, bf16[256,8192]{1,0:T(8,128)(2,1)} %protos.9, f32[1024,256]{1,0:T(8,128)S(1)} %copy-done.1, f32[1024,256]{1,0:T(8,128)} %collective-permute-done.1.refs_1_, f32[1024,256]{1,0:T(8,128)} %collective-permute-done.5.refs_2_, ...), custom_call_target="tpu_custom_call" | custom-call | flops 2147483648 | bytes 4194304 | tf_op jit(solution)/shard_map/pallas_call | solution.py:32
  129.9 6.6 %shard_map.105 = (f32[512,256]{1,0:T(8,128)S(1)}, f32[512,256]{1,0:T(8,128)S(1)}) custom-call(s32[4]{0:T(128)S(1)} %pad_add_fusion.idx, bf16[1024,4096]{1,0:T(8,128)(2,1)} %get-tuple-element.68.expo, f32[16,64,128]{2,1,0:T(8,128)S(1)} %all-to-all-done.4.colparts, bf16[256,8192]{1,0:T(8,128)(2,1)} %protos.12), custom_call_target="tpu_custom_call" | custom-call | flops 2147483648 | bytes 8388608 | tf_op jit(solution)/shard_map/pallas_call | solution.py:32
  136.8 5.3 %shard_map.106 = f32[64,8,128]{2,1,0:T(8,128)} custom-call(bf16[1024,4096]{1,0:T(8,128)(2,1)} %get-tuple-element.68.expo, f32[16,64,128]{2,1,0:T(8,128)S(1)} %all-to-all-done.4.colparts), custom_call_target="tpu_custom_call" | custom-call | flops 8388608 | bytes 8388608 | tf_op jit(solution)/shard_map/pallas_call | solution.py:32
  144.6 8.8 %all-to-all-start.5 = ((f32[64,8,128]{2,1,0:T(8,128)}), f32[64,8,128]{2,1,0:T(8,128)S(1)}, u32[]{:S(2)}, u32[]{:S(2)}) async-start(f32[64,8,128]{2,1,0:T(8,128)} %shard_map.106), calls=%async_computation.5 | async-start | bytes 524288 | tf_op jit(solution)/shard_map/all_to_all | solution.py:1013
  153.4 8.7 %collective-permute-done.13.target_came = f32[256,256]{1,0:T(8,128)S(1)} collective-permute-done((f32[256,256]{1,0:T(8,128)S(1)}, f32[256,256]{1,0:T(8,128)S(1)}, u32[]{:S(2)}, u32[]{:S(2)}) %collective-permute-start.13) | collective-permute-done | bytes 262176 | tf_op jit(solution)/shard_map/ppermute | solution.py:970
  162.1 9.3 %shard_map.108 = (f32[256,1024]{1,0:T(8,128)S(1)}, f32[256,1024]{1,0:T(8,128)}, bf16[256,1024]{1,0:T(8,128)(2,1)S(1)}, bf16[256,3072]{1,0:T(8,128)(2,1)}) custom-call(s32[4]{0:T(128)S(1)} %pad_add_fusion.idx, bf16[256,8192]{1,0:T(8,128)(2,1)} %protos.12, f32[1024,256]{1,0:T(8,128)} %shard_map.94.own.refs_0_, f32[1024,256]{1,0:T(8,128)} %collective-permute-done.1.refs_1_, ...), custom_call_target="tpu_custom_call" | custom-call | flops 4294967296 | bytes 4194304 | tf_op jit(solution)/shard_map/pallas_call | solution.py:32
  172.4 8.4 %shard_map.109 = f32[32,72,128]{2,1,0:T(8,128)} custom-call(s32[4]{0:T(128)S(1)} %pad_add_fusion.idx, f32[256,1024]{1,0:T(8,128)} %copy-done.3, f32[256,1024]{1,0:T(8,128)} %get-tuple-element.119.wnorm_in, bf16[256,1024]{1,0:T(8,128)(2,1)S(1)} %get-tuple-element.120.turned_d_in, bf16[256,3072]{1,0:T(8,128)(2,1)} %get-tuple-element.121.turned_i_in, ...), custom_call_target="tpu_custom_call" | custom-call | flops 2147483648 | bytes 8388608 | tf_op jit(solution)/shard_map/pallas_call | solution.py:32
  180.8 6.2 %all-to-all-start.6 = ((f32[32,72,128]{2,1,0:T(8,128)}), f32[32,72,128]{2,1,0:T(8,128)S(1)}, u32[]{:S(2)}, u32[]{:S(2)}) async-start(f32[32,72,128]{2,1,0:T(8,128)} %shard_map.109), calls=%async_computation.6 | async-start | bytes 2359296 | tf_op jit(solution)/shard_map/all_to_all | solution.py:1020
  188.3 3.9 %collective-permute-start.14 = (f32[128,256]{1,0:T(8,128)S(1)}, f32[128,256]{1,0:T(8,128)S(1)}, u32[]{:S(2)}, u32[]{:S(2)}) collective-permute-start(f32[128,256]{1,0:T(8,128)S(1)} %get-tuple-element.130), channel_id=1, source_target_pairs={{0,2},{1,3},{2,0},{3,1},{4,6},{5,7},{6,4},{7,5},{8,10},{9,11},{10,... | collective-permute-start | bytes 393224 | tf_op jit(solution)/shard_map/ppermute | solution.py:970
  194.1 5.7 %collective-permute-done.16.refs_3_ = f32[128,256]{1,0:T(8,128)S(1)} collective-permute-done((f32[128,256]{1,0:T(8,128)S(1)}, f32[128,256]{1,0:T(8,128)S(1)}, u32[]{:S(2)}, u32[]{:S(2)}) %collective-permute-start.16) | collective-permute-done | bytes 131104 | tf_op jit(solution)/shard_map/ppermute | solution.py:970
  200.4 2.7 %shard_map.112 = (f32[16,256]{1,0:T(8,128)}, f32[128,256]{1,0:T(8,128)}) custom-call(s32[4]{0:T(128)S(1)} %pad_add_fusion.idx, s32[4,96]{1,0:T(4,128)S(1)} %copy-done.6, f32[128,256]{1,0:T(8,128)S(1)} %get-tuple-element.129.refs_0_, f32[128,256]{1,0:T(8,128)S(1)} %collective-permute-done.14.refs_1_, f32[128,256]{1,0:T(8,128)S(1)} %collective-permute-done.15.refs_2_, ...), custom_call_target="tpu_custom_call" | custom-call | tf_op jit(solution)/shard_map/pallas_call | solution.py:32
  203.1 2.2 %all-to-all-done.6.parts = f32[32,72,128]{2,1,0:T(8,128)S(1)} async-done(((f32[32,72,128]{2,1,0:T(8,128)}), f32[32,72,128]{2,1,0:T(8,128)S(1)}, u32[]{:S(2)}, u32[]{:S(2)}) %all-to-all-start.6) | async-done | bytes 1179680 | tf_op jit(solution)/shard_map/all_to_all | solution.py:1020
  205.3 2.3 %shard_map.110 = f32[8,8192]{1,0:T(8,128)} custom-call(s32[4]{0:T(128)S(1)} %pad_add_fusion.idx, f32[32,72,128]{2,1,0:T(8,128)S(1)} %all-to-all-done.6.parts, bf16[256,8192]{1,0:T(8,128)(2,1)} %protos.12, f32[1,8192]{1,0:T(1,128)S(1)} %shard_map.98.winv), custom_call_target="tpu_custom_call" | custom-call | tf_op jit(solution)/shard_map/pallas_call | solution.py:32
  (52 shorter events, 18.5 us)
Async XLA Ops:
  4.1 3.3 %collective-permute-start = (f32[1024,256]{1,0:T(8,128)}, f32[1024,256]{1,0:T(8,128)S(1)}, u32[]{:S(2)}, u32[]{:S(2)}) collective-permute-start(f32[1024,256]{1,0:T(8,128)} %shard_map.94.own.refs_0_), channel_id=1, source_target_pairs={{0,8},{8,0},{1,9},{9,1},{2,10},{10,2},{3,11},{11,3},{4,12},{12,4},... | collective-permute-start | bytes 3145736 | tf_op jit(solution)/shard_map/ppermute | solution.py:960
  4.2 31.7 %collective-permute-start.2 = (f32[1024,256]{1,0:T(8,128)}, f32[1024,256]{1,0:T(8,128)}, u32[]{:S(2)}, u32[]{:S(2)}) collective-permute-start(f32[1024,256]{1,0:T(8,128)} %shard_map.94.own.refs_0_), channel_id=1, source_target_pairs={{0,48},{16,0},{32,16},{48,32},{1,49},{17,1},{33,17},{49,33},{2,50}... | collective-permute-start | bytes 3145736 | tf_op jit(solution)/shard_map/ppermute | solution.py:963
  7.3 32.0 %collective-permute-start.1 = (f32[1024,256]{1,0:T(8,128)}, f32[1024,256]{1,0:T(8,128)}, u32[]{:S(2)}, u32[]{:S(2)}) collective-permute-start(f32[1024,256]{1,0:T(8,128)} %shard_map.94.own.refs_0_), channel_id=1, source_target_pairs={{0,16},{16,32},{32,48},{48,0},{1,17},{17,33},{33,49},{49,1},{2,18}... | collective-permute-start | bytes 3145736 | tf_op jit(solution)/shard_map/ppermute | solution.py:962
  7.4 1.0 copy-start.7
  8.4 1.2 copy-start
  18.5 21.0 %all-to-all-start = ((f32[16,64,128]{2,1,0:T(8,128)}), f32[16,64,128]{2,1,0:T(8,128)S(1)}, u32[]{:S(2)}, u32[]{:S(2)}) async-start(f32[16,64,128]{2,1,0:T(8,128)} %get-tuple-element.69), calls=%async_computation | async-start | bytes 1048576 | tf_op jit(solution)/shard_map/all_to_all | solution.py:972
  34.3 1.0 copy-start.4
  44.7 16.8 %all-to-all-start.1 = ((f32[16,16,128]{2,1,0:T(8,128)}), f32[16,16,128]{2,1,0:T(8,128)S(1)}, u32[]{:S(2)}, u32[]{:S(2)}) async-start(f32[16,16,128]{2,1,0:T(8,128)} %shard_map.97), calls=%async_computation.1 | async-start | bytes 262144 | tf_op jit(solution)/shard_map/all_to_all | solution.py:981
  53.3 42.3 %collective-permute-start.5 = (f32[1024,256]{1,0:T(8,128)}, f32[1024,256]{1,0:T(8,128)}, u32[]{:S(2)}, u32[]{:S(2)}) collective-permute-start(f32[1024,256]{1,0:T(8,128)} %collective-permute-done.1.refs_1_), channel_id=1, source_target_pairs={{0,16},{16,32},{32,48},{48,0},{1,17},{17,33},{33,49},{49,1},{2,18}... | collective-permute-start | bytes 3145736 | tf_op jit(solution)/shard_map/ppermute | solution.py:977
  67.7 4.6 %collective-permute-start.3 = (f32[512,256]{1,0:T(8,128)S(1)}, f32[512,256]{1,0:T(8,128)S(1)}, u32[]{:S(2)}, u32[]{:S(2)}) collective-permute-start(f32[512,256]{1,0:T(8,128)S(1)} %get-tuple-element.78), channel_id=1, source_target_pairs={{0,8},{8,0},{1,9},{9,1},{2,10},{10,2},{3,11},{11,3},{4,12},{12,4},... | collective-permute-start | bytes 1572872 | tf_op jit(solution)/shard_map/ppermute | solution.py:992
  67.8 17.8 %all-to-all-start.2 = ((f32[16,64,128]{2,1,0:T(8,128)}), f32[16,64,128]{2,1,0:T(8,128)S(1)}, u32[]{:S(2)}, u32[]{:S(2)}) async-start(f32[16,64,128]{2,1,0:T(8,128)} %shard_map.99), calls=%async_computation.2 | async-start | bytes 1048576 | tf_op jit(solution)/shard_map/all_to_all | solution.py:988
  72.9 18.2 %collective-permute-start.4 = (f32[256,256]{1,0:T(8,128)S(1)}, f32[256,256]{1,0:T(8,128)S(1)}, u32[]{:S(2)}, u32[]{:S(2)}) collective-permute-start(f32[256,256]{1,0:T(8,128)S(1)} %get-tuple-element.79), channel_id=1, source_target_pairs={{0,4},{1,5},{2,6},{3,7},{4,0},{5,1},{6,2},{7,3},{8,12},{9,13},{10,... | collective-permute-start | bytes 786440 | tf_op jit(solution)/shard_map/ppermute | solution.py:970
  95.6 26.8 %collective-permute-start.6 = (f32[1024,256]{1,0:T(8,128)}, f32[1024,256]{1,0:T(8,128)}, u32[]{:S(2)}, u32[]{:S(2)}) collective-permute-start(f32[1024,256]{1,0:T(8,128)} %collective-permute-done.1.refs_1_), channel_id=1, source_target_pairs={{0,8},{8,0},{1,9},{9,1},{2,10},{10,2},{3,11},{11,3},{4,12},{12,4},... | collective-permute-start | bytes 3145736 | tf_op jit(solution)/shard_map/ppermute | solution.py:997
  95.7 27.5 %collective-permute-start.7 = (f32[1024,256]{1,0:T(8,128)}, f32[1024,256]{1,0:T(8,128)}, u32[]{:S(2)}, u32[]{:S(2)}) collective-permute-start(f32[1024,256]{1,0:T(8,128)} %collective-permute-done.5.refs_2_), channel_id=1, source_target_pairs={{0,8},{8,0},{1,9},{9,1},{2,10},{10,2},{3,11},{11,3},{4,12},{12,4},... | collective-permute-start | bytes 3145736 | tf_op jit(solution)/shard_map/ppermute | solution.py:997
  96.2 27.0 %collective-permute-start.8 = (f32[1024,256]{1,0:T(8,128)}, f32[1024,256]{1,0:T(8,128)}, u32[]{:S(2)}, u32[]{:S(2)}) collective-permute-start(f32[1024,256]{1,0:T(8,128)} %collective-permute-done.2.refs_3_), channel_id=1, source_target_pairs={{0,8},{8,0},{1,9},{9,1},{2,10},{10,2},{3,11},{11,3},{4,12},{12,4},... | collective-permute-start | bytes 3145736 | tf_op jit(solution)/shard_map/ppermute | solution.py:997
  106.7 16.6 %copy-start.1 = (f32[1024,256]{1,0:T(8,128)S(1)}, f32[1024,256]{1,0:T(8,128)}, u32[]{:S(2)}) copy-start(f32[1024,256]{1,0:T(8,128)} %shard_map.94.own.refs_0_) | copy-start | bytes 3145732
  111.5 18.4 %all-to-all-start.4 = ((f32[16,64,128]{2,1,0:T(8,128)}), f32[16,64,128]{2,1,0:T(8,128)S(1)}, u32[]{:S(2)}, u32[]{:S(2)}) async-start(f32[16,64,128]{2,1,0:T(8,128)} %shard_map.103), calls=%async_computation.4 | async-start | bytes 1048576 | tf_op jit(solution)/shard_map/all_to_all | solution.py:1001
  118.4 11.3 %collective-permute-start.11 = (f32[8,128]{1,0:T(8,128)S(1)}, f32[8,128]{1,0:T(8,128)S(1)}, u32[]{:S(2)}, u32[]{:S(2)}) collective-permute-start(f32[8,128]{1,0:T(8,128)S(1)} %slice_reduce_fusion.totals.refs_8_), channel_id=1, source_target_pairs={{0,48},{16,0},{32,16},{48,32},{1,49},{17,1},{33,17},{49,33},{2,50}... | collective-permute-start | bytes 12296 | tf_op jit(solution)/shard_map/ppermute | solution.py:990
  121.5 8.2 %collective-permute-start.10 = (f32[8,128]{1,0:T(8,128)S(1)}, f32[8,128]{1,0:T(8,128)S(1)}, u32[]{:S(2)}, u32[]{:S(2)}) collective-permute-start(f32[8,128]{1,0:T(8,128)S(1)} %slice_reduce_fusion.totals.refs_8_), channel_id=1, source_target_pairs={{0,32},{16,48},{32,0},{48,16},{1,33},{17,49},{33,1},{49,17},{2,34}... | collective-permute-start | bytes 12296 | tf_op jit(solution)/shard_map/ppermute | solution.py:990
  122.4 7.3 %collective-permute-start.9 = (f32[8,128]{1,0:T(8,128)S(1)}, f32[8,128]{1,0:T(8,128)S(1)}, u32[]{:S(2)}, u32[]{:S(2)}) collective-permute-start(f32[8,128]{1,0:T(8,128)S(1)} %slice_reduce_fusion.totals.refs_8_), channel_id=1, source_target_pairs={{0,16},{16,32},{32,48},{48,0},{1,17},{17,33},{33,49},{49,1},{2,18}... | collective-permute-start | bytes 12296 | tf_op jit(solution)/shard_map/ppermute | solution.py:990
  136.4 5.6 %collective-permute-start.12 = (f32[512,256]{1,0:T(8,128)S(1)}, f32[512,256]{1,0:T(8,128)S(1)}, u32[]{:S(2)}, u32[]{:S(2)}) collective-permute-start(f32[512,256]{1,0:T(8,128)S(1)} %get-tuple-element.102), channel_id=1, source_target_pairs={{0,8},{8,0},{1,9},{9,1},{2,10},{10,2},{3,11},{11,3},{4,12},{12,4},... | collective-permute-start | bytes 1572872 | tf_op jit(solution)/shard_map/ppermute | solution.py:1010
  142.7 19.4 %collective-permute-start.13 = (f32[256,256]{1,0:T(8,128)S(1)}, f32[256,256]{1,0:T(8,128)S(1)}, u32[]{:S(2)}, u32[]{:S(2)}) collective-permute-start(f32[256,256]{1,0:T(8,128)S(1)} %get-tuple-element.104), channel_id=1, source_target_pairs={{0,4},{1,5},{2,6},{3,7},{4,0},{5,1},{6,2},{7,3},{8,12},{9,13},{10,... | collective-permute-start | bytes 786440 | tf_op jit(solution)/shard_map/ppermute | solution.py:970
  144.6 27.8 %all-to-all-start.5 = ((f32[64,8,128]{2,1,0:T(8,128)}), f32[64,8,128]{2,1,0:T(8,128)S(1)}, u32[]{:S(2)}, u32[]{:S(2)}) async-start(f32[64,8,128]{2,1,0:T(8,128)} %shard_map.106), calls=%async_computation.5 | async-start | bytes 524288 | tf_op jit(solution)/shard_map/all_to_all | solution.py:1013
  171.4 1.0 copy-start.3
  172.4 28.0 %copy-start.2 = (bf16[1024,256]{1,0:T(8,128)(2,1)S(1)}, bf16[1024,256]{1,0:T(8,128)(2,1)}, u32[]{:S(2)}) copy-start(bf16[1024,256]{1,0:T(8,128)(2,1)} %refs_5_.1) | copy-start | bytes 1572868
  172.4 28.0 %copy-start.5 = (bf16[128,256]{1,0:T(8,128)(2,1)S(1)}, bf16[128,256]{1,0:T(8,128)(2,1)}, u32[]{:S(2)}) copy-start(bf16[128,256]{1,0:T(8,128)(2,1)} %refs_4_.1) | copy-start | bytes 196612
  172.4 28.0 %copy-start.6 = (s32[4,96]{1,0:T(4,128)S(1)}, s32[4,96]{1,0:T(4,128)}, u32[]{:S(2)}) copy-start(s32[4,96]{1,0:T(4,128)} %mask.3) | copy-start | bytes 4612
  180.8 24.6 %all-to-all-start.6 = ((f32[32,72,128]{2,1,0:T(8,128)}), f32[32,72,128]{2,1,0:T(8,128)S(1)}, u32[]{:S(2)}, u32[]{:S(2)}) async-start(f32[32,72,128]{2,1,0:T(8,128)} %shard_map.109), calls=%async_computation.6 | async-start | bytes 2359296 | tf_op jit(solution)/shard_map/all_to_all | solution.py:1020
  187.7 6.4 %collective-permute-start.15 = (f32[128,256]{1,0:T(8,128)S(1)}, f32[128,256]{1,0:T(8,128)S(1)}, u32[]{:S(2)}, u32[]{:S(2)}) collective-permute-start(f32[128,256]{1,0:T(8,128)S(1)} %get-tuple-element.129.refs_0_), channel_id=1, source_target_pairs={{0,1},{1,0},{2,3},{3,2},{4,5},{5,4},{6,7},{7,6},{8,9},{9,8},{10,11... | collective-permute-start | bytes 393224 | tf_op jit(solution)/shard_map/ppermute | solution.py:970
  187.8 12.0 %collective-permute-start.16 = (f32[128,256]{1,0:T(8,128)S(1)}, f32[128,256]{1,0:T(8,128)S(1)}, u32[]{:S(2)}, u32[]{:S(2)}) collective-permute-start(f32[128,256]{1,0:T(8,128)S(1)} %get-tuple-element.130), channel_id=1, source_target_pairs={{0,3},{1,2},{2,1},{3,0},{4,7},{5,6},{6,5},{7,4},{8,11},{9,10},{10,... | collective-permute-start | bytes 393224 | tf_op jit(solution)/shard_map/ppermute | solution.py:970
  188.3 12.1 %collective-permute-start.14 = (f32[128,256]{1,0:T(8,128)S(1)}, f32[128,256]{1,0:T(8,128)S(1)}, u32[]{:S(2)}, u32[]{:S(2)}) collective-permute-start(f32[128,256]{1,0:T(8,128)S(1)} %get-tuple-element.130), channel_id=1, source_target_pairs={{0,2},{1,3},{2,0},{3,1},{4,6},{5,7},{6,4},{7,5},{8,10},{9,11},{10,... | collective-permute-start | bytes 393224 | tf_op jit(solution)/shard_map/ppermute | solution.py:970
